TPU v7x, 32 devices: a whole 2x2x4 slice. The times are simulated.
32 devices in a mesh: ulysses: 4 (over y, x), blk: 4 (over z), tensor: 2 (over core).
Axes of the slice: x: 2, y: 2, z: 4, core: 2. Of those that a mesh axis runs over, the one named last changes fastest.
Arguments:
- tokens: bfloat16 [1024, 3072], P(('ulysses', 'blk'), 'tensor'), may hold values from -12 to 12
- cond: bfloat16 [3072], replicated, may hold values from -4 to 4
- mod_weight: bfloat16 [3072, 18432], P(None, ('ulysses', 'blk', 'tensor')), may hold values from -0.109375 to 0.109375
- qkv_weight: bfloat16 [3072, 3, 3072], P('tensor', None, 'ulysses'), as said below
- q_gain: float32 [128], replicated, may hold values from 1.2 to 3.4, as said below
- k_gain: float32 [128], replicated, may hold values from 1.2 to 3.4, as said below
- out_weight: bfloat16 [3072, 3072], P('ulysses', 'tensor'), may hold values from -0.109375 to 0.109375
- up_weight: bfloat16 [3072, 12288], P('tensor', 'ulysses'), may hold values from -0.109375 to 0.109375
- down_weight: bfloat16 [12288, 3072], P('ulysses', 'tensor'), may hold values from -0.0546875 to 0.0546875
Outputs:
- block_out: float32 [1024, 3072], P(('ulysses', 'blk'), 'tensor')
Inputs may be any that keep to these rules, and one draw needn't show every extreme that they name: `qkv_weight`: entries lie within four times 3072 ** -0.5 of zero. `q_gain`: positive gains. `k_gain`: positive gains.
All inputs are finite; a program needn't handle non-finite values.
Results may differ from a plain program's by a relative error of at most 0.011.
Values may be sent and summed in bfloat16 or wider, within the bound.
No kernel may reach another device: no remote copies, remote signals or barrier semaphores. Data moves between devices by JAX's collectives and lax.ppermute only.
A program may use at most 128 MiB of HBM per device.

v0:
```python
import math

import jax
import jax.numpy as jnp
from jax import lax
from jax.sharding import PartitionSpec as P


def joined(array, axis, combine):
    everything = jax.tree.map(
        lambda part, kind: lax.all_gather(part.astype(kind), axis),
        array,
        jax.tree.map(lambda a: jnp.bfloat16 if a.dtype == jnp.float32 else a.dtype, array),
    )

    def take(k):
        return jax.tree.map(lambda part, own: part[k].astype(own.dtype), everything, array)

    return lax.fori_loop(
        1, lax.axis_size(axis), lambda k, so_far: combine(so_far, take(k)), take(0)
    )


def moments_norm(values, shift_row, scale_row, features):
    sums = lax.psum((jnp.sum(values, axis=-1), jnp.sum(values * values, axis=-1)), "tensor")
    average = sums[0][:, None] / features
    variance = sums[1][:, None] / features - average * average
    normal_rows = (values - average) * lax.rsqrt(variance + 1e-06)
    return (normal_rows * (1.0 + scale_row) + shift_row).astype(jnp.bfloat16)


def spread_rows(values):
    return lax.all_gather(values, "ulysses", axis=0, tiled=True)


def head_norm(values, gains):
    return values * lax.rsqrt(jnp.mean(values * values, axis=-1, keepdims=True) + 1e-06) * gains


def make_absorb(queries, score_scale, running, kv_block):
    keys_part, values_part = kv_block
    top_score, total_weight, summed = running
    scores = (
        jnp.einsum("qhd,khd->qhk", queries, keys_part, preferred_element_type=jnp.float32)
        * score_scale
    )
    new_top = jnp.max(scores, axis=-1)
    decay = jnp.exp(top_score - new_top)
    weights = jnp.exp(scores - new_top[..., None])
    total_weight = total_weight * decay + jnp.sum(weights, axis=-1)
    summed = summed * decay[..., None] + jnp.einsum(
        "qhk,khd->qhd",
        weights.astype(jnp.bfloat16),
        values_part,
        preferred_element_type=jnp.float32,
    )
    return (new_top, total_weight, summed)


def empty_state(row_count, heads_local, head_size):
    return (
        jnp.full((row_count, heads_local), -jnp.inf, jnp.float32),
        jnp.zeros((row_count, heads_local), jnp.float32),
        jnp.zeros((row_count, heads_local, head_size), jnp.float32),
    )


def combine_parts(first_part, second_part):
    top_score = jnp.maximum(first_part[0], second_part[0])
    first_decay = jnp.exp(first_part[0] - top_score)
    second_decay = jnp.exp(second_part[0] - top_score)
    total_weight = first_part[1] * first_decay + second_part[1] * second_decay
    summed = first_part[2] * first_decay[..., None] + second_part[2] * second_decay[..., None]
    return (top_score, total_weight, summed)


def on_device(
    tokens, cond, mod_weight, qkv_weight, q_gain, k_gain, out_weight, up_weight, down_weight
):
    tensor_size = lax.axis_size("tensor")
    tensor_pos = lax.axis_index("tensor")
    width = tokens.shape[1]
    features = width * tensor_size
    activated = jax.nn.silu(cond.astype(jnp.float32)).astype(jnp.bfloat16)
    local_mod = jnp.dot(activated[None, :], mod_weight, preferred_element_type=jnp.float32)[0]
    full_mod = lax.all_gather(local_mod, ("ulysses", "blk", "tensor"), axis=0, tiled=True).reshape(
        6, features
    )
    own_mod = lax.dynamic_slice_in_dim(full_mod, tensor_pos * width, width, 1)
    resid = tokens.astype(jnp.float32)
    normed = moments_norm(resid, own_mod[0], own_mod[1], features)
    gathered = spread_rows(normed)
    group_rows = gathered.shape[0]
    attn_rows = group_rows // tensor_size
    inner_local = qkv_weight.shape[2]
    head_size = q_gain.shape[0]
    heads_local = inner_local // head_size
    flat_qkv = qkv_weight.reshape(width, 3 * inner_local)
    projected = (
        lax.psum_scatter(
            jnp.dot(gathered, flat_qkv, preferred_element_type=jnp.float32).astype(jnp.bfloat16),
            "tensor",
            scatter_dimension=0,
            tiled=True,
        )
        .astype(jnp.float32)
        .reshape(attn_rows, 3, heads_local, head_size)
    )
    queries = head_norm(projected[:, 0], q_gain).astype(jnp.bfloat16)
    keys_local = head_norm(projected[:, 1], k_gain).astype(jnp.bfloat16)
    values_local = projected[:, 2].astype(jnp.bfloat16)
    score_scale = 1.0 / math.sqrt(head_size)
    all_queries = lax.all_gather(queries, "tensor", axis=0, tiled=True)
    state = make_absorb(
        all_queries,
        score_scale,
        empty_state(group_rows, heads_local, head_size),
        (
            lax.all_gather(keys_local, "blk", axis=0, tiled=True),
            lax.all_gather(values_local, "blk", axis=0, tiled=True),
        ),
    )
    merged = joined(state, "tensor", combine_parts)
    context = (
        (merged[2] / merged[1][..., None]).astype(jnp.bfloat16).reshape(group_rows, inner_local)
    )
    attended = lax.psum_scatter(
        jnp.dot(context, out_weight, preferred_element_type=jnp.float32).astype(jnp.bfloat16),
        "ulysses",
        scatter_dimension=0,
        tiled=True,
    ).astype(jnp.float32)
    mixed = resid + own_mod[2] * attended
    normed_two = moments_norm(mixed, own_mod[3], own_mod[4], features)
    gathered_two = spread_rows(normed_two)
    hidden = lax.psum_scatter(
        jnp.dot(gathered_two, up_weight, preferred_element_type=jnp.float32).astype(jnp.bfloat16),
        "tensor",
        scatter_dimension=0,
        tiled=True,
    ).astype(jnp.float32)
    activ = jax.nn.gelu(hidden, approximate=True).astype(jnp.bfloat16)
    activ_rows = lax.all_gather(activ, "tensor", axis=0, tiled=True)
    feedforward = lax.psum_scatter(
        jnp.dot(activ_rows, down_weight, preferred_element_type=jnp.float32).astype(jnp.bfloat16),
        "ulysses",
        scatter_dimension=0,
        tiled=True,
    ).astype(jnp.float32)
    return mixed + own_mod[5] * feedforward


def solution(mesh):
    return jax.shard_map(
        on_device,
        mesh=mesh,
        in_specs=(
            P(("ulysses", "blk"), "tensor"),
            P(),
            P(None, ("ulysses", "blk", "tensor")),
            P("tensor", None, "ulysses"),
            P(),
            P(),
            P("ulysses", "tensor"),
            P("tensor", "ulysses"),
            P("ulysses", "tensor"),
        ),
        out_specs=P(("ulysses", "blk"), "tensor"),
        check_vma=False,
    )
```

profile of v0, /device:TPU:0, one launch (start us, length us, event | category | flops | bytes accessed | tf_op | source)
XLA Modules:
  0.0 342.6 jit_solution(6586532953156883643)
XLA Ops:
  6.5 0.9 fusion.32
  7.4 1.1 copy-done
  8.6 1.0 convolution_reduce_fusion
  9.6 0.6 broadcast.92
  10.2 1.4 dynamic-update-slice
  11.6 1.5 reshape.152
  13.3 1.1 convert_reduce_fusion
  14.3 2.6 all-reduce.3
  16.9 0.6 broadcast_multiply_fusion.1
  17.5 10.3 %copy.13 = bf16[1536,3,768]{0,2,1:T(8,128)(2,1)} copy(bf16[1536,3,768]{2,0,1:T(8,128)(2,1)} %param.12) | data formatting | bytes 14155776 | tf_op args[3]
  27.8 108.8 %all-reduce.6.cloned.1.call-done = f32[6,3072]{1,0:T(8,128)} async-done(((f32[6,3072]{1,0:T(8,128)}), f32[6,3072]{1,0:T(8,128)}) %all-reduce.6.cloned.1.call-update) | async-done | bytes 73744
  136.6 1.8 dynamic-slice_reduce_fusion.1
  138.4 1.1 fusion.26
  139.5 11.3 %all_gather.36 = bf16[256,1536]{1,0:T(8,128)(2,1)S(1)} all-gather(bf16[64,1536]{1,0:T(8,128)(2,1)S(1)} %fusion.26), channel_id=1, replica_groups=mesh['ulysses'=4,'blk'=4,'tensor'=2] {'ulysses'}, dimensions={0}, use_global_device_ids=true | all-gather | bytes 983040 | tf_op jit(solution)/shard_map/all_gather | solution.py:33
  150.8 6.1 %convolution_convert_fusion.1 = bf16[256,2304]{1,0:T(8,128)(2,1)} fusion(bf16[256,1536]{1,0:T(8,128)(2,1)S(1)} %all_gather.36, bf16[1536,2304]{0,1:T(8,128)(2,1)} %bitcast.52), kind=kOutput, calls=%fused_computation.1 | convolution fusion | flops 1812529152 | bytes 9043968 | tf_op jit(solution)/shard_map/dot_general | solution.py:101
  157.0 0.0 reduce-scatter.7.cloned.1.call-start
  157.0 10.1 %reduce-scatter.5.cloned.1.call-done = bf16[128,2304]{1,0:T(8,128)(2,1)} async-done(((bf16[256,2304]{1,0:T(8,128)(2,1)}), bf16[128,2304]{1,0:T(8,128)(2,1)}) %reduce-scatter.5.cloned.1.call-update) | async-done | bytes 589840 | tf_op jit(solution)/shard_map/reduce_scatter | solution.py:100
  167.1 2.1 copy.14
  169.2 1.6 slice.60
  170.8 2.1 copy.15
  172.9 1.2 reshape.155
  174.2 0.3 multiply_reduce_fusion.1
  174.5 0.9 multiply_convert_fusion
  175.4 2.1 all_gather.38
  177.5 19.0 %all-gather = bf16[512,1,6,128]{0,3,2,1:T(8,128)(2,1)S(1)} all-gather(bf16[128,1,6,128]{0,3,2,1:T(8,128)(2,1)S(1)} %copy-done.2), channel_id=2, replica_groups=mesh['ulysses'=4,'blk'=4,'tensor'=2] {'blk'}, dimensions={0}, use_global_device_ids=true | all-gather | bytes 983040 | tf_op jit(solution)/shard_map/all_gather | solution.py:120
  196.5 17.8 %all_gather.37 = bf16[512,6,128]{2,0,1:T(8,128)(2,1)S(1)} all-gather(bf16[128,6,128]{2,0,1:T(8,128)(2,1)S(1)} %get-tuple-element.46), channel_id=1, replica_groups=mesh['ulysses'=4,'blk'=4,'tensor'=2] {'blk'}, dimensions={0}, use_global_device_ids=true | all-gather | bytes 983040 | tf_op jit(solution)/shard_map/all_gather | solution.py:119
  214.3 0.6 bitcast_reduce_fusion
  214.9 0.5 fusion.1
  215.4 1.8 all-gather.2
  217.2 1.8 all-gather.3
  219.0 0.7 fusion.19
  219.8 2.4 all-gather.1
  222.1 0.2 divide_convert_fusion
  222.3 1.7 convolution_convert_fusion.3
  224.1 25.5 %reduce-scatter.7.cloned.1.call-done = bf16[64,1536]{1,0:T(8,128)(2,1)} async-done(((bf16[256,1536]{1,0:T(8,128)(2,1)}), bf16[64,1536]{1,0:T(8,128)(2,1)}) %reduce-scatter.7.cloned.1.call-update) | async-done | bytes 196624 | tf_op jit(solution)/shard_map/reduce_scatter | solution.py:127
  249.6 1.8 fusion.28
  251.4 3.1 all-reduce.2
  254.5 0.7 broadcast_multiply_fusion
  255.1 1.2 add_convert_fusion
  256.3 12.0 %all_gather.44 = bf16[256,1536]{1,0:T(8,128)(2,1)S(1)} all-gather(bf16[64,1536]{1,0:T(8,128)(2,1)S(1)} %add_convert_fusion), channel_id=1, replica_groups=mesh['ulysses'=4,'blk'=4,'tensor'=2] {'ulysses'}, dimensions={0}, use_global_device_ids=true | all-gather | bytes 983040 | tf_op jit(solution)/shard_map/all_gather | solution.py:33
  268.3 7.4 %convolution_convert_fusion = bf16[256,3072]{1,0:T(8,128)(2,1)} fusion(bf16[256,1536]{1,0:T(8,128)(2,1)S(1)} %all_gather.44, bf16[1536,3072]{1,0:T(8,128)(2,1)} %param.16), kind=kOutput, calls=%fused_computation | convolution fusion | flops 2416705536 | bytes 11796480 | tf_op jit(solution)/shard_map/dot_general | solution.py:137
  275.7 0.0 all-gather.6.cloned.1.call-start
  275.8 9.2 %reduce-scatter.9.cloned.1.call-done = bf16[128,3072]{1,0:T(8,128)(2,1)} async-done(((bf16[256,3072]{1,0:T(8,128)(2,1)}), bf16[128,3072]{1,0:T(8,128)(2,1)}) %reduce-scatter.9.cloned.1.call-update) | async-done | bytes 786448 | tf_op jit(solution)/shard_map/reduce_scatter | solution.py:136
  285.0 2.6 fusion.10
  287.6 11.1 %all-gather.6.cloned.1.call-done = bf16[256,3072]{1,0:T(8,128)(2,1)} async-done(((bf16[128,3072]{1,0:T(8,128)(2,1)}), bf16[256,3072]{1,0:T(8,128)(2,1)}) %all-gather.6.cloned.1.call-update) | async-done | bytes 1572880 | tf_op jit(solution)/shard_map/all_gather | solution.py:143
  298.7 7.7 %convolution_convert_fusion.2 = bf16[256,1536]{1,0:T(8,128)(2,1)} fusion(bf16[256,3072]{1,0:T(8,128)(2,1)} %all-gather.6.cloned.1.call-done, bf16[3072,1536]{1,0:T(8,128)(2,1)} %param.17), kind=kOutput, calls=%fused_computation.9 | convolution fusion | flops 2416312320 | bytes 11796480 | tf_op jit(solution)/shard_map/dot_general | solution.py:145
  306.4 27.4 %reduce-scatter.11.cloned.1.call-done = bf16[64,1536]{1,0:T(8,128)(2,1)} async-done(((bf16[256,1536]{1,0:T(8,128)(2,1)}), bf16[64,1536]{1,0:T(8,128)(2,1)}) %reduce-scatter.11.cloned.1.call-update) | async-done | bytes 196624 | tf_op jit(solution)/shard_map/reduce_scatter | solution.py:144
  333.8 2.0 multiply_add_fusion
  (19 shorter events, 0.3 us)
Async XLA Ops:
  6.5 2.0 copy-start
  6.5 130.1 %all-reduce.6.cloned.1.call-start = ((), (), s32[]{:S(2)}) async-start(), calls=%async_computation.9 | async-start | bytes 196608
  13.2 153.9 %reduce-scatter.5.cloned.1.call-start = ((), (), s32[]{:S(2)}) async-start(), calls=%async_computation.4 | async-start | bytes 1769472 | tf_op jit(solution)/shard_map/reduce_scatter | solution.py:100
  157.0 92.6 %reduce-scatter.7.cloned.1.call-start = ((), (), s32[]{:S(2)}) async-start(), calls=%async_computation.5 | async-start | bytes 983040 | tf_op jit(solution)/shard_map/reduce_scatter | solution.py:127
  172.9 4.6 %copy-start.2 = (bf16[128,1,6,128]{0,3,2,1:T(8,128)(2,1)S(1)}, bf16[128,1,6,128]{0,3,2,1:T(8,128)(2,1)}, u32[]{:S(2)}) copy-start(bf16[128,1,6,128]{0,3,2,1:T(8,128)(2,1)} %slice.60) | copy-start | bytes 589828
  219.0 3.3 copy-start.1
  224.0 60.9 %reduce-scatter.9.cloned.1.call-start = ((), (), s32[]{:S(2)}) async-start(), calls=%async_computation.6 | async-start | bytes 2359296 | tf_op jit(solution)/shard_map/reduce_scatter | solution.py:136
  275.7 23.0 %all-gather.6.cloned.1.call-start = ((), (), s32[]{:S(2)}) async-start(), calls=%async_computation.7 | async-start | bytes 2359296 | tf_op jit(solution)/shard_map/all_gather | solution.py:143
  287.6 46.2 %reduce-scatter.11.cloned.1.call-start = ((), (), s32[]{:S(2)}) async-start(), calls=%async_computation.8 | async-start | bytes 983040 | tf_op jit(solution)/shard_map/reduce_scatter | solution.py:144
Sparse Core Ops, SparseCore 0:
  13.3 123.2 all-reduce.5
  157.1 9.9 reduce-scatter.4
  224.2 25.3 reduce-scatter.6
  275.8 9.0 reduce-scatter.8
  287.7 10.9 all-gather.5
  306.5 27.2 reduce-scatter.10
where the time goes:
time: 344 us; the launch traced here: 343 us
  waiting for transfers between devices  192 us (56%)
  blocking collectives  73.8 us (21%)
  matrix products  25.2 us (7%)
  local copies, waits for them, and re-layouts  20.9 us (6%)
  other arithmetic  16.8 us (5%)
  between operations  13.6 us (4%)
    unnamed x7, waiting for transfers between devices  109 us
    reduce_scatter x1, waiting for transfers between devices, on_device(): lax.psum_scatter(jnp.dot(activ_rows, down_weight, preferred_element_type=...  27.4 us
    reduce_scatter x1, waiting for transfers between devices, on_device(): lax.psum_scatter(jnp.dot(context, out_weight, preferred_element_type=jnp....  25.5 us
    all_gather x2, blocking collectives, spread_rows(): return lax.all_gather(values, 'ulysses', axis=0, tiled=True)  23.3 us
    all_gather x1, blocking collectives, on_device(): lax.all_gather(values_local, 'blk', axis=0, tiled=True)  19 us
    all_gather x1, blocking collectives, on_device(): lax.all_gather(keys_local, 'blk', axis=0, tiled=True)  17.8 us
    unnamed x9, local copies, waits for them, and re-layouts  13.5 us
    all_gather x1, waiting for transfers between devices, on_device(): activ_rows = lax.all_gather(activ, 'tensor', axis=0, tiled=True)  11.1 us
  transfers between devices with their start and end apart: 6, of which 6 were waited for; matrix products, arithmetic and copies ran while one was open for 3% of the time, Pallas kernels for 0%

commit v1 on v0

--- a/solution.py
+++ b/solution.py
@@ -150,9 +150,148 @@
     return mixed + own_mod[5] * feedforward
 
 
+def partners(axis):
+    size = lax.axis_size(axis)
+    return [[(i, i ^ k) for i in range(size)] for k in range(1, size)]
+
+
+def from_all(values, axis):
+    return [values] + [lax.ppermute(values, axis, pairs) for pairs in partners(axis)]
+
+
+def to_all(blocks, axis):
+    return [blocks[0]] + [
+        lax.ppermute(block, axis, pairs) for block, pairs in zip(blocks[1:], partners(axis))
+    ]
+
+
+def swapped(values):
+    return lax.ppermute(values, "tensor", [(0, 1), (1, 0)])
+
+
+def in_order(pieces, axis):
+    position = lax.axis_index(axis)
+    bit = 1
+    while bit < len(pieces):
+        flip = (position & bit) != 0
+        pieces = [jnp.where(flip, pieces[i ^ bit], pieces[i]) for i in range(len(pieces))]
+        bit *= 2
+    return jnp.concatenate(pieces, axis=0)
+
+
+def modulation_rows(cond, mod_weight, features, width):
+    activated = jax.nn.silu(cond.astype(jnp.float32)).astype(jnp.bfloat16)
+    piece = jnp.dot(activated[None, :], mod_weight, preferred_element_type=jnp.float32)[0]
+    for axis in ("tensor", "blk", "ulysses"):
+        piece = in_order(from_all(piece, axis), axis)
+    rows = piece.reshape(6, features)
+    return lax.dynamic_slice_in_dim(rows, lax.axis_index("tensor") * width, width, 1)
+
+
+def row_sums(values):
+    return jnp.stack([jnp.sum(values, axis=-1), jnp.sum(values * values, axis=-1)])
+
+
+def apply_norm(values, sums, shift_row, scale_row, features):
+    average = sums[0][:, None] / features
+    variance = sums[1][:, None] / features - average * average
+    normal_rows = (values - average) * lax.rsqrt(variance + 1e-06)
+    return (normal_rows * (1.0 + scale_row) + shift_row).astype(jnp.bfloat16)
+
+
+def product(left, right):
+    return jnp.dot(left, right, preferred_element_type=jnp.float32).astype(jnp.bfloat16)
+
+
+def added(blocks):
+    total = blocks[0].astype(jnp.float32)
+    for block in blocks[1:]:
+        total = total + block.astype(jnp.float32)
+    return total
+
+
+def on_pair(
+    tokens, cond, mod_weight, qkv_weight, q_gain, k_gain, out_weight, up_weight, down_weight
+):
+    tensor_pos = lax.axis_index("tensor")
+    rows, width = tokens.shape
+    features = width * lax.axis_size("tensor")
+    head_size = q_gain.shape[0]
+    inner_local = qkv_weight.shape[2]
+    half = inner_local // 2
+    heads = half // head_size
+
+    chunks = [from_all(block, "ulysses") for block in from_all(tokens, "blk")]
+    own_mod = modulation_rows(cond, mod_weight, features, width)
+
+    def half_weight(position):
+        part = lax.dynamic_slice_in_dim(qkv_weight, position * half, half, 2)
+        return part.reshape(width, 3 * half)
+
+    weight_own = half_weight(tensor_pos)
+    weight_other = half_weight(1 - tensor_pos)
+
+    queries, keys, values = None, [], []
+    for index, blocks in enumerate(chunks):
+        chunk = jnp.concatenate(blocks, axis=0).astype(jnp.float32)
+        sums = row_sums(chunk)
+        sums = sums + swapped(sums)
+        normed = apply_norm(chunk, sums, own_mod[0], own_mod[1], features)
+        first = 0 if index == 0 else half
+        arrived = swapped(product(normed, weight_other[:, first:]))
+        projected = added([product(normed, weight_own[:, first:]), arrived])
+        projected = projected.reshape(projected.shape[0], -1, heads, head_size)
+        if index == 0:
+            queries = head_norm(projected[:, 0], q_gain).astype(jnp.bfloat16)
+        keys.append(head_norm(projected[:, -2], k_gain).astype(jnp.bfloat16))
+        values.append(projected[:, -1].astype(jnp.bfloat16))
+
+    scores = jnp.einsum(
+        "qhd,khd->hqk", queries, jnp.concatenate(keys, 0), preferred_element_type=jnp.float32
+    ) * (1.0 / math.sqrt(head_size))
+    weights = jnp.exp(scores - jnp.max(scores, axis=-1, keepdims=True))
+    denominator = jnp.sum(weights, axis=-1)
+    summed = jnp.einsum(
+        "hqk,khd->qhd",
+        weights.astype(jnp.bfloat16),
+        jnp.concatenate(values, 0),
+        preferred_element_type=jnp.float32,
+    )
+    context = (summed / denominator.T[..., None]).astype(jnp.bfloat16)
+    context = context.reshape(context.shape[0], half)
+    context = in_order_columns(context, tensor_pos)
+
+    resid = tokens.astype(jnp.float32)
+    attended = reduced_rows(product(context, out_weight), rows)
+    mixed = resid + own_mod[2] * attended
+    sums = row_sums(mixed)
+    sums = sums + swapped(sums)
+    normed_two = apply_norm(mixed, sums, own_mod[3], own_mod[4], features)
+    gathered_two = jnp.concatenate(from_all(normed_two, "ulysses"), axis=0)
+    partial = product(gathered_two, up_weight)
+    hidden = added([partial, swapped(partial)])
+    activ = jax.nn.gelu(hidden, approximate=True).astype(jnp.bfloat16)
+    feedforward = reduced_rows(product(activ, down_weight), rows)
+    return mixed + own_mod[5] * feedforward
+
+
+def in_order_columns(values, tensor_pos):
+    other = swapped(values)
+    first = jnp.where(tensor_pos == 0, values, other)
+    second = jnp.where(tensor_pos == 0, other, values)
+    return jnp.concatenate([first, second], axis=1)
+
+
+def reduced_rows(partial, rows):
+    blocks = [partial[i : i + rows] for i in range(0, partial.shape[0], rows)]
+    return added(to_all(blocks, "ulysses"))
+
+
 def solution(mesh):
+    sizes = [mesh.shape[axis] for axis in ("ulysses", "blk")]
+    pairs = mesh.shape["tensor"] == 2 and all(size & (size - 1) == 0 for size in sizes)
     return jax.shard_map(
-        on_device,
+        on_pair if pairs else on_device,
         mesh=mesh,
         in_specs=(
             P(("ulysses", "blk"), "tensor"),

time: 344 us -> 164 us (0.48)
  waiting for transfers between devices: 192 us -> 48.4 us
  blocking collectives: 73.8 us -> 0 us
  starting transfers between devices: 0.21 us -> 42.4 us
  between operations: 13.6 us -> 0.84 us
  matrix products: 25.2 us -> 32.2 us
  local copies, waits for them, and re-layouts: 20.9 us -> 27.3 us
  other arithmetic: 16.8 us -> 12.5 us
    unnamed x7 -> x0, waiting for transfers between devices: 109 us -> none
    reduce_scatter x4 -> x0, waiting for transfers between devices: 72.1 us -> none  [the longest x1 27.4 us: on_device(): lax.psum_scatter(jnp.dot(activ_rows, down_weight, preferred_element_type=...]
    all_gather x8 -> x0, blocking collectives: 68.2 us -> none  [the longest x2 23.3 us: spread_rows(): return lax.all_gather(values, 'ulysses', axis=0, tiled=True)]
    ppermute x0 -> x42, waiting for transfers between devices: none -> 48.4 us  [the longest x25 25.6 us: from_all(): lax.ppermute(values, axis, pairs)]
    ppermute x0 -> x42, starting transfers between devices: none -> 42.4 us  [the longest x25 33.3 us: from_all(): lax.ppermute(values, axis, pairs)]
    all_gather x1 -> x0, waiting for transfers between devices: 11.1 us -> none  [on_device(): activ_rows = lax.all_gather(activ, 'tensor', axis=0, tiled=True)]
    dot_general x7 -> x14, matrix products: 25.2 us -> 32.2 us  [the longest x11 29.6 us: product(): jnp.dot(left, right, preferred_element_type=jnp.float32)]
    psum x2 -> x0, blocking collectives: 5.67 us -> none  [moments_norm(): lax.psum((jnp.sum(values, axis=-1), jnp.sum(values * values, axis=-1)), '...]
  transfers between devices with their start and end apart: 6 -> 42, of which waited for: 6 -> 18; matrix products, arithmetic and copies ran while one was open for 3% -> 25% of each run, Pallas kernels for 0% -> 0%
where the time goes in v1:
time: 164 us
  waiting for transfers between devices  48.4 us (30%)
  starting transfers between devices  42.4 us (26%)
  matrix products  32.2 us (20%)
  local copies, waits for them, and re-layouts  27.3 us (17%)
  other arithmetic  12.5 us (8%)
    ppermute x25, starting transfers between devices, from_all(): lax.ppermute(values, axis, pairs)  33.3 us
    dot_general x11, matrix products, product(): jnp.dot(left, right, preferred_element_type=jnp.float32)  29.6 us
    ppermute x25, waiting for transfers between devices, from_all(): lax.ppermute(values, axis, pairs)  25.6 us
    ppermute x6, waiting for transfers between devices, to_all(): lax.ppermute(block, axis, pairs)  17.2 us
    unnamed x84, local copies, waits for them, and re-layouts  14.9 us
    ppermute x6, starting transfers between devices, to_all(): lax.ppermute(block, axis, pairs)  7.12 us
    ppermute x11, waiting for transfers between devices, swapped(): return lax.ppermute(values, 'tensor', [(0, 1), (1, 0)])  5.61 us
    dynamic_slice x1, local copies, waits for them, and re-layouts, half_weight(): part = lax.dynamic_slice_in_dim(qkv_weight, position * half, half, 2)  5.54 us
  transfers between devices with their start and end apart: 42, of which 18 were waited for; matrix products, arithmetic and copies ran while one was open for 25% of the time, Pallas kernels for 0%

profile of v1, /device:TPU:0, one launch (start us, length us, event | category | flops | bytes accessed | tf_op | source)
XLA Modules:
  0.0 163.7 jit_solution(2745825970096114311)
XLA Ops:
  4.5 4.9 %collective-permute-start.1 = (f32[1152]{0:T(1024)S(1)}, f32[1152]{0:T(1024)S(1)}, u32[]{:S(2)}, u32[]{:S(2)}) collective-permute-start(f32[1152]{0:T(1024)S(1)} %pad_maximum_fusion.6), channel_id=1, source_target_pairs={{0,6},{2,4},{4,2},{6,0},{1,7},{3,5},{5,3},{7,1},{8,14},{10,12},{12... | collective-permute-start | bytes 13832 | tf_op jit(solution)/shard_map/ppermute | solution.py:159
  10.0 2.3 %collective-permute-start.18 = (bf16[64,1536]{1,0:T(8,128)(2,1)}, bf16[64,1536]{1,0:T(8,128)(2,1)}, u32[]{:S(2)}, u32[]{:S(2)}) collective-permute-start(bf16[64,1536]{1,0:T(8,128)(2,1)} %param.9), channel_id=1, source_target_pairs={{0,4},{2,6},{4,0},{6,2},{1,5},{3,7},{5,1},{7,3},{8,12},{10,14},{12... | collective-permute-start | bytes 589832 | tf_op jit(solution)/shard_map/ppermute | solution.py:159
  12.3 1.5 collective-permute-start.24
  14.7 2.4 %collective-permute-start.4 = (f32[4608]{0:T(1024)}, f32[4608]{0:T(1024)}, u32[]{:S(2)}, u32[]{:S(2)}) collective-permute-start(f32[4608]{0:T(1024)} %pad_maximum_fusion.5), channel_id=1, source_target_pairs={{0,24},{8,16},{16,8},{24,0},{1,25},{9,17},{17,9},{25,1},{2,26},{10... | collective-permute-start | bytes 55304 | tf_op jit(solution)/shard_map/ppermute | solution.py:159
  18.2 5.5 %constant_dynamic-slice_fusion = (bf16[1536,3,384]{2,0,1:T(8,128)(2,1)}, bf16[1536,3,384]{2,0,1:T(8,128)(2,1)S(1)}) fusion(bf16[1536,3,768]{2,0,1:T(8,128)(2,1)} %param.12, s32[]{:T(128)S(6)} %select_n.135, s32[]{:T(128)S(6)} %select_n.134), kind=kLoop, calls=%fused_computation.212 | loop fusion | bytes 14155784 | tf_op jit(solution)/shard_map/dynamic_slice | solution.py:228
  23.7 6.1 %copy.32 = bf16[1536,3,384]{0,2,1:T(8,128)(2,1)} copy(bf16[1536,3,384]{2,0,1:T(8,128)(2,1)} %get-tuple-element.22) | data formatting | bytes 7077888
  29.8 3.8 %copy.31 = bf16[1536,3,384]{0,2,1:T(8,128)(2,1)} copy(bf16[1536,3,384]{2,0,1:T(8,128)(2,1)S(1)} %get-tuple-element.23) | data formatting | bytes 7077888
  33.6 1.5 collective-permute-start.7
  35.1 1.5 collective-permute-start.8
  37.9 3.1 %collective-permute-done.7 = bf16[64,1536]{1,0:T(8,128)(2,1)S(1)} collective-permute-done((bf16[64,1536]{1,0:T(8,128)(2,1)}, bf16[64,1536]{1,0:T(8,128)(2,1)S(1)}, u32[]{:S(2)}, u32[]{:S(2)}) %collective-permute-start.7) | collective-permute-done | bytes 196640 | tf_op jit(solution)/shard_map/ppermute | solution.py:159
  41.6 2.8 %collective-permute-done.8 = bf16[64,1536]{1,0:T(8,128)(2,1)S(1)} collective-permute-done((bf16[64,1536]{1,0:T(8,128)(2,1)}, bf16[64,1536]{1,0:T(8,128)(2,1)S(1)}, u32[]{:S(2)}, u32[]{:S(2)}) %collective-permute-start.8) | collective-permute-done | bytes 196640 | tf_op jit(solution)/shard_map/ppermute | solution.py:159
  44.4 1.4 convert_reduce_fusion.3
  48.4 1.8 %collective-permute-start.21 = (bf16[64,1536]{1,0:T(8,128)(2,1)}, bf16[64,1536]{1,0:T(8,128)(2,1)S(1)}, u32[]{:S(2)}, u32[]{:S(2)}) collective-permute-start(bf16[64,1536]{1,0:T(8,128)(2,1)} %collective-permute-done.18), channel_id=1, source_target_pairs={{0,24},{8,16},{16,8},{24,0},{1,25},{9,17},{17,9},{25,1},{2,26},{10... | collective-permute-start | bytes 589832 | tf_op jit(solution)/shard_map/ppermute | solution.py:159
  51.1 3.8 %convolution_convert_fusion.3 = bf16[256,1152]{1,0:T(8,128)(2,1)S(1)} fusion(bf16[1536,1152]{0,1:T(8,128)(2,1)} %bitcast.112, f32[1536]{0:T(1024)S(1)} %get-tuple-element.17, f32[1536]{0:T(1024)S(1)} %get-tuple-element.18, f32[256]{0:T(256)S(1)} %add_rsqrt_fusion.8, f32[256]{0:T(256)S(1)} %bitcast.145, bf16[64,1536]{1,0:T(8,128)(2,1)} %copy-done.10, ...), kind=kOutput, calls=%fused_computation.14 | convolution fusion | flops 911376384 | bytes 4929536 | tf_op jit(solution)/shard_map/dot_general | solution.py:203
  55.8 1.8 %collective-permute-start.27 = (bf16[64,1536]{1,0:T(8,128)(2,1)}, bf16[64,1536]{1,0:T(8,128)(2,1)S(1)}, u32[]{:S(2)}, u32[]{:S(2)}) collective-permute-start(bf16[64,1536]{1,0:T(8,128)(2,1)} %collective-permute-done.24), channel_id=1, source_target_pairs={{0,24},{8,16},{16,8},{24,0},{1,25},{9,17},{17,9},{25,1},{2,26},{10... | collective-permute-start | bytes 589832 | tf_op jit(solution)/shard_map/ppermute | solution.py:159
  57.6 3.0 %collective-permute-start.13 = (bf16[64,1536]{1,0:T(8,128)(2,1)S(1)}, bf16[64,1536]{1,0:T(8,128)(2,1)S(1)}, u32[]{:S(2)}, u32[]{:S(2)}) collective-permute-start(bf16[64,1536]{1,0:T(8,128)(2,1)S(1)} %collective-permute-done.12), channel_id=1, source_target_pairs={{0,8},{8,0},{16,24},{24,16},{1,9},{9,1},{17,25},{25,17},{2,10},{10... | collective-permute-start | bytes 589832 | tf_op jit(solution)/shard_map/ppermute | solution.py:159
  60.6 1.2 collective-permute-start.14
  61.8 1.3 convert_reduce_fusion.1
  64.2 3.7 %collective-permute-done.27 = bf16[64,1536]{1,0:T(8,128)(2,1)S(1)} collective-permute-done((bf16[64,1536]{1,0:T(8,128)(2,1)}, bf16[64,1536]{1,0:T(8,128)(2,1)S(1)}, u32[]{:S(2)}, u32[]{:S(2)}) %collective-permute-start.27) | collective-permute-done | bytes 196640 | tf_op jit(solution)/shard_map/ppermute | solution.py:159
  67.9 1.3 convert_reduce_fusion
  69.3 2.2 %collective-permute-done.13 = bf16[64,1536]{1,0:T(8,128)(2,1)S(1)} collective-permute-done((bf16[64,1536]{1,0:T(8,128)(2,1)S(1)}, bf16[64,1536]{1,0:T(8,128)(2,1)S(1)}, u32[]{:S(2)}, u32[]{:S(2)}) %collective-permute-start.13) | collective-permute-done | bytes 196640 | tf_op jit(solution)/shard_map/ppermute | solution.py:159
  72.0 3.9 %collective-permute-done.15 = bf16[64,1536]{1,0:T(8,128)(2,1)S(1)} collective-permute-done((bf16[64,1536]{1,0:T(8,128)(2,1)S(1)}, bf16[64,1536]{1,0:T(8,128)(2,1)S(1)}, u32[]{:S(2)}, u32[]{:S(2)}) %collective-permute-start.15) | collective-permute-done | bytes 196640 | tf_op jit(solution)/shard_map/ppermute | solution.py:159
  76.4 1.8 %fusion.64 = bf16[256,768]{1,0:T(8,128)(2,1)S(1)} fusion(bf16[1536,1152]{0,1:T(8,128)(2,1)S(1)} %bitcast.113, f32[256]{0:T(256)S(1)} %add_rsqrt_fusion.6, f32[256]{0:T(256)S(1)} %bitcast.151, f32[1536]{0:T(1024)S(1)} %get-tuple-element.17, f32[1536]{0:T(1024)S(1)} %get-tuple-element.18, bf16[64,1536]{1,0:T(8,128)(2,1)S(1)} %collective-permute-done.21, ...), kind=kOutput, calls=%fused_computation.74 | convolution fusion | flops 609288192 | bytes 3557376 | tf_op jit(solution)/shard_map/dot_general | solution.py:203
  78.9 2.6 %fusion.67 = bf16[256,768]{1,0:T(8,128)(2,1)} fusion(bf16[1536,1152]{0,1:T(8,128)(2,1)S(1)} %bitcast.114, f32[256]{0:T(256)S(1)} %add_rsqrt_fusion.5, f32[256]{0:T(256)S(1)} %bitcast.148, f32[1536]{0:T(1024)S(1)} %get-tuple-element.17, f32[1536]{0:T(1024)S(1)} %get-tuple-element.18, bf16[64,1536]{1,0:T(8,128)(2,1)S(1)} %collective-permute-done.27, ...), kind=kOutput, calls=%fused_computation.75 | convolution fusion | flops 609288192 | bytes 3557376 | tf_op jit(solution)/shard_map/dot_general | solution.py:203
  83.7 2.3 %convert_add_fusion = f32[256,1152]{1,0:T(8,128)} fusion(bf16[256,1152]{1,0:T(8,128)(2,1)S(1)} %collective-permute-done.11, bf16[1536,1152]{0,1:T(8,128)(2,1)S(1)} %bitcast.109, f32[1536]{0:T(1024)S(1)} %get-tuple-element.17, f32[1536]{0:T(1024)S(1)} %get-tuple-element.18, f32[256]{0:T(256)S(1)} %add_rsqrt_fusion.8, f32[256]{0:T(256)S(1)} %bitcast.146, ...), kind=kOutput, calls=%fused_computation.84 | convolution fusion | flops 912261120 | bytes 6109184 | tf_op jit(solution)/shard_map/dot_general | solution.py:203
  86.0 1.8 %fusion.79 = f32[256,768]{1,0:T(8,128)S(1)} fusion(bf16[1536,1152]{0,1:T(8,128)(2,1)S(1)} %bitcast.110, bf16[256,768]{1,0:T(8,128)(2,1)S(1)} %collective-permute-done.23, f32[256]{0:T(256)S(1)} %add_rsqrt_fusion.6, f32[256]{0:T(256)S(1)} %bitcast.152, f32[1536]{0:T(1024)S(1)} %get-tuple-element.17, f32[1536]{0:T(1024)S(1)} %get-tuple-element.18, ...), kind=kOutput, calls=%fused_computation.79 | convolution fusion | flops 609878016 | bytes 4343808 | tf_op jit(solution)/shard_map/dot_general | solution.py:203
  90.2 1.6 copy.21
  93.4 3.5 %fusion.73 = f32[256,768]{1,0:T(8,128)} fusion(bf16[1536,1152]{0,1:T(8,128)(2,1)} %bitcast.108, bf16[256,768]{1,0:T(8,128)(2,1)} %collective-permute-done.29, f32[256]{0:T(256)S(1)} %copy-done.34, f32[256]{0:T(256)S(1)} %bitcast.149, f32[1536]{0:T(1024)S(1)} %copy-done.28, f32[1536]{0:T(1024)S(1)} %copy-done.30, bf16[64,1536]{1,0:T(8,128)(2,1)S(1)} %copy-done.17, ...), kind=kOutput, calls=%fused_computation.77 | convolution fusion | flops 609878016 | bytes 4339712 | tf_op jit(solution)/shard_map/dot_general | solution.py:203
  97.0 1.4 copy.24
  99.9 1.1 copy.35
  101.3 1.2 copy.36
  109.3 2.5 %convolution_convert_fusion.2 = bf16[256,1536]{1,0:T(8,128)(2,1)S(1)} fusion(bf16[768,1536]{1,0:T(8,128)(2,1)} %param.15, bf16[256,384]{0,1:T(8,128)(2,1)S(1)} %get-tuple-element.31, bf16[256,384]{0,1:T(8,128)(2,1)S(1)} %get-tuple-element.30), kind=kOutput, calls=%fused_computation.13 | convolution fusion | flops 605159424 | bytes 3538944 | tf_op jit(solution)/shard_map/dot_general | solution.py:203
  111.9 1.2 collective-permute-start.31
  113.0 1.2 collective-permute-start.32
  114.2 1.2 collective-permute-start.33
  115.4 4.2 %collective-permute-done.31 = bf16[64,1536]{1,0:T(8,128)(2,1)S(1)} collective-permute-done((bf16[64,1536]{1,0:T(8,128)(2,1)S(1)}, bf16[64,1536]{1,0:T(8,128)(2,1)S(1)}, u32[]{:S(2)}, u32[]{:S(2)}) %collective-permute-start.31) | collective-permute-done | bytes 196640 | tf_op jit(solution)/shard_map/ppermute | solution.py:164
  119.7 4.5 %collective-permute-done.32 = bf16[64,1536]{1,0:T(8,128)(2,1)S(1)} collective-permute-done((bf16[64,1536]{1,0:T(8,128)(2,1)S(1)}, bf16[64,1536]{1,0:T(8,128)(2,1)S(1)}, u32[]{:S(2)}, u32[]{:S(2)}) %collective-permute-start.32) | collective-permute-done | bytes 196640 | tf_op jit(solution)/shard_map/ppermute | solution.py:164
  127.7 1.7 %collective-permute-start.37 = (bf16[64,1536]{1,0:T(8,128)(2,1)S(1)}, bf16[64,1536]{1,0:T(8,128)(2,1)S(1)}, u32[]{:S(2)}, u32[]{:S(2)}) collective-permute-start(bf16[64,1536]{1,0:T(8,128)(2,1)S(1)} %add_convert_fusion), channel_id=1, source_target_pairs={{0,24},{8,16},{16,8},{24,0},{1,25},{9,17},{17,9},{25,1},{2,26},{10... | collective-permute-start | bytes 589832 | tf_op jit(solution)/shard_map/ppermute | solution.py:159
  129.4 4.3 %collective-permute-done.35 = bf16[64,1536]{1,0:T(8,128)(2,1)S(1)} collective-permute-done((bf16[64,1536]{1,0:T(8,128)(2,1)S(1)}, bf16[64,1536]{1,0:T(8,128)(2,1)S(1)}, u32[]{:S(2)}, u32[]{:S(2)}) %collective-permute-start.35) | collective-permute-done | bytes 196640 | tf_op jit(solution)/shard_map/ppermute | solution.py:159
  134.3 3.5 %collective-permute-done.37 = bf16[64,1536]{1,0:T(8,128)(2,1)S(1)} collective-permute-done((bf16[64,1536]{1,0:T(8,128)(2,1)S(1)}, bf16[64,1536]{1,0:T(8,128)(2,1)S(1)}, u32[]{:S(2)}, u32[]{:S(2)}) %collective-permute-start.37) | collective-permute-done | bytes 196640 | tf_op jit(solution)/shard_map/ppermute | solution.py:159
  137.8 6.3 %convolution_convert_fusion = bf16[256,3072]{1,0:T(8,128)(2,1)S(1)} fusion(bf16[1536,3072]{1,0:T(8,128)(2,1)} %param.16, bf16[64,1536]{1,0:T(8,128)(2,1)S(1)} %collective-permute-done.37, bf16[64,1536]{1,0:T(8,128)(2,1)S(1)} %collective-permute-done.36, bf16[64,1536]{1,0:T(8,128)(2,1)S(1)} %collective-permute-done.35, bf16[64,1536]{1,0:T(8,128)(2,1)S(1)} %add_convert_fusion), kind=kOutput, calls=%fused_computation.1 | convolution fusion | flops 2419851264 | bytes 11796480 | tf_op jit(solution)/shard_map/dot_general | solution.py:203
  144.1 3.4 %collective-permute-done.38 = bf16[256,3072]{1,0:T(8,128)(2,1)S(1)} collective-permute-done((bf16[256,3072]{1,0:T(8,128)(2,1)S(1)}, bf16[256,3072]{1,0:T(8,128)(2,1)S(1)}, u32[]{:S(2)}, u32[]{:S(2)}) %collective-permute-start.38) | collective-permute-done | bytes 1572896 | tf_op jit(solution)/shard_map/ppermute | solution.py:169
  147.6 3.1 %convolution_convert_fusion.1 = bf16[256,1536]{1,0:T(8,128)(2,1)S(1)} fusion(bf16[3072,1536]{1,0:T(8,128)(2,1)S(1)} %bitcast.161, bf16[256,3072]{1,0:T(8,128)(2,1)S(1)} %collective-permute-done.38, bf16[256,3072]{1,0:T(8,128)(2,1)S(1)} %convolution_convert_fusion), kind=kOutput, calls=%fused_computation.12 | convolution fusion | flops 2425749504 | bytes 13369344 | tf_op jit(solution)/shard_map/dot_general | solution.py:203
  150.7 1.2 collective-permute-start.39
  151.9 1.2 collective-permute-start.40
  153.1 1.2 collective-permute-start.41
  154.3 4.3 %collective-permute-done.39 = bf16[64,1536]{1,0:T(8,128)(2,1)S(1)} collective-permute-done((bf16[64,1536]{1,0:T(8,128)(2,1)S(1)}, bf16[64,1536]{1,0:T(8,128)(2,1)S(1)}, u32[]{:S(2)}, u32[]{:S(2)}) %collective-permute-start.39) | collective-permute-done | bytes 196640 | tf_op jit(solution)/shard_map/ppermute | solution.py:164
  158.6 4.2 %collective-permute-done.40 = bf16[64,1536]{1,0:T(8,128)(2,1)S(1)} collective-permute-done((bf16[64,1536]{1,0:T(8,128)(2,1)S(1)}, bf16[64,1536]{1,0:T(8,128)(2,1)S(1)}, u32[]{:S(2)}, u32[]{:S(2)}) %collective-permute-start.40) | collective-permute-done | bytes 196640 | tf_op jit(solution)/shard_map/ppermute | solution.py:164
  (196 shorter events, 35.5 us)
Async XLA Ops:
  3.0 1.3 collective-permute-start
  4.5 9.3 %collective-permute-start.1 = (f32[1152]{0:T(1024)S(1)}, f32[1152]{0:T(1024)S(1)}, u32[]{:S(2)}, u32[]{:S(2)}) collective-permute-start(f32[1152]{0:T(1024)S(1)} %pad_maximum_fusion.6), channel_id=1, source_target_pairs={{0,6},{2,4},{4,2},{6,0},{1,7},{3,5},{5,3},{7,1},{8,14},{10,12},{12... | collective-permute-start | bytes 13832 | tf_op jit(solution)/shard_map/ppermute | solution.py:159
  9.4 4.6 %collective-permute-start.2 = (f32[1152]{0:T(1024)S(1)}, f32[1152]{0:T(1024)S(1)}, u32[]{:S(2)}, u32[]{:S(2)}) collective-permute-start(f32[1152]{0:T(1024)S(1)} %pad_maximum_fusion.6), channel_id=1, source_target_pairs={{0,4},{2,6},{4,0},{6,2},{1,5},{3,7},{5,1},{7,3},{8,12},{10,14},{12... | collective-permute-start | bytes 13832 | tf_op jit(solution)/shard_map/ppermute | solution.py:159
  9.4 4.6 %collective-permute-start.3 = (f32[1152]{0:T(1024)S(1)}, f32[1152]{0:T(1024)S(1)}, u32[]{:S(2)}, u32[]{:S(2)}) collective-permute-start(f32[1152]{0:T(1024)S(1)} %pad_maximum_fusion.6), channel_id=1, source_target_pairs={{0,2},{2,0},{4,6},{6,4},{1,3},{3,1},{5,7},{7,5},{8,10},{10,8},{12,... | collective-permute-start | bytes 13832 | tf_op jit(solution)/shard_map/ppermute | solution.py:159
  10.0 36.6 %collective-permute-start.18 = (bf16[64,1536]{1,0:T(8,128)(2,1)}, bf16[64,1536]{1,0:T(8,128)(2,1)}, u32[]{:S(2)}, u32[]{:S(2)}) collective-permute-start(bf16[64,1536]{1,0:T(8,128)(2,1)} %param.9), channel_id=1, source_target_pairs={{0,4},{2,6},{4,0},{6,2},{1,5},{3,7},{5,1},{7,3},{8,12},{10,14},{12... | collective-permute-start | bytes 589832 | tf_op jit(solution)/shard_map/ppermute | solution.py:159
  12.3 36.1 %collective-permute-start.24 = (bf16[64,1536]{1,0:T(8,128)(2,1)}, bf16[64,1536]{1,0:T(8,128)(2,1)}, u32[]{:S(2)}, u32[]{:S(2)}) collective-permute-start(bf16[64,1536]{1,0:T(8,128)(2,1)} %param.9), channel_id=1, source_target_pairs={{0,6},{2,4},{4,2},{6,0},{1,7},{3,5},{5,3},{7,1},{8,14},{10,12},{12... | collective-permute-start | bytes 589832 | tf_op jit(solution)/shard_map/ppermute | solution.py:159
  14.7 18.9 %collective-permute-start.4 = (f32[4608]{0:T(1024)}, f32[4608]{0:T(1024)}, u32[]{:S(2)}, u32[]{:S(2)}) collective-permute-start(f32[4608]{0:T(1024)} %pad_maximum_fusion.5), channel_id=1, source_target_pairs={{0,24},{8,16},{16,8},{24,0},{1,25},{9,17},{17,9},{25,1},{2,26},{10... | collective-permute-start | bytes 55304 | tf_op jit(solution)/shard_map/ppermute | solution.py:159
  17.1 18.0 %collective-permute-start.5 = (f32[4608]{0:T(1024)}, f32[4608]{0:T(1024)}, u32[]{:S(2)}, u32[]{:S(2)}) collective-permute-start(f32[4608]{0:T(1024)} %pad_maximum_fusion.5), channel_id=1, source_target_pairs={{0,16},{8,24},{16,0},{24,8},{1,17},{9,25},{17,1},{25,9},{2,18},{10... | collective-permute-start | bytes 55304 | tf_op jit(solution)/shard_map/ppermute | solution.py:159
  17.6 19.0 %collective-permute-start.6 = (f32[4608]{0:T(1024)}, f32[4608]{0:T(1024)}, u32[]{:S(2)}, u32[]{:S(2)}) collective-permute-start(f32[4608]{0:T(1024)} %pad_maximum_fusion.5), channel_id=1, source_target_pairs={{0,8},{8,0},{16,24},{24,16},{1,9},{9,1},{17,25},{25,17},{2,10},{10... | collective-permute-start | bytes 55304 | tf_op jit(solution)/shard_map/ppermute | solution.py:159
  33.6 7.5 %collective-permute-start.7 = (bf16[64,1536]{1,0:T(8,128)(2,1)}, bf16[64,1536]{1,0:T(8,128)(2,1)S(1)}, u32[]{:S(2)}, u32[]{:S(2)}) collective-permute-start(bf16[64,1536]{1,0:T(8,128)(2,1)} %param.9), channel_id=1, source_target_pairs={{0,8},{8,0},{16,24},{24,16},{1,9},{9,1},{17,25},{25,17},{2,10},{10... | collective-permute-start | bytes 589832 | tf_op jit(solution)/shard_map/ppermute | solution.py:159
  35.1 9.3 %collective-permute-start.8 = (bf16[64,1536]{1,0:T(8,128)(2,1)}, bf16[64,1536]{1,0:T(8,128)(2,1)S(1)}, u32[]{:S(2)}, u32[]{:S(2)}) collective-permute-start(bf16[64,1536]{1,0:T(8,128)(2,1)} %param.9), channel_id=1, source_target_pairs={{0,16},{8,24},{16,0},{24,8},{1,17},{9,25},{17,1},{25,9},{2,18},{10... | collective-permute-start | bytes 589832 | tf_op jit(solution)/shard_map/ppermute | solution.py:159
  36.6 7.8 %collective-permute-start.9 = (bf16[64,1536]{1,0:T(8,128)(2,1)}, bf16[64,1536]{1,0:T(8,128)(2,1)S(1)}, u32[]{:S(2)}, u32[]{:S(2)}) collective-permute-start(bf16[64,1536]{1,0:T(8,128)(2,1)} %param.9), channel_id=1, source_target_pairs={{0,24},{8,16},{16,8},{24,0},{1,25},{9,17},{17,9},{25,1},{2,26},{10... | collective-permute-start | bytes 589832 | tf_op jit(solution)/shard_map/ppermute | solution.py:159
  41.0 13.8 %collective-permute-start.12 = (bf16[64,1536]{1,0:T(8,128)(2,1)}, bf16[64,1536]{1,0:T(8,128)(2,1)S(1)}, u32[]{:S(2)}, u32[]{:S(2)}) collective-permute-start(bf16[64,1536]{1,0:T(8,128)(2,1)} %param.9), channel_id=1, source_target_pairs={{0,2},{2,0},{4,6},{6,4},{1,3},{3,1},{5,7},{7,5},{8,10},{10,8},{12,... | collective-permute-start | bytes 589832 | tf_op jit(solution)/shard_map/ppermute | solution.py:159
  45.9 4.3 %collective-permute-start.10 = (f32[2,256]{1,0:T(2,128)S(1)}, f32[2,256]{1,0:T(2,128)S(1)}, u32[]{:S(2)}, u32[]{:S(2)}) collective-permute-start(f32[2,256]{1,0:T(2,128)S(1)} %pad_maximum_fusion.7), channel_id=1, source_target_pairs={{0,1},{1,0},{2,3},{3,2},{4,5},{5,4},{6,7},{7,6},{8,9},{9,8},{10,11... | collective-permute-start | bytes 6152 | tf_op jit(solution)/shard_map/ppermute | solution.py:169
  46.7 41.2 %copy-start.27 = (f32[1536]{0:T(1024)}, f32[1536]{0:T(1024)S(1)}, u32[]{:S(2)}) copy-start(f32[1536]{0:T(1024)S(1)} %get-tuple-element.17) | copy-start | bytes 18436
  46.7 41.2 %copy-start.29 = (f32[1536]{0:T(1024)}, f32[1536]{0:T(1024)S(1)}, u32[]{:S(2)}) copy-start(f32[1536]{0:T(1024)S(1)} %get-tuple-element.18) | copy-start | bytes 18436
  46.7 9.2 %collective-permute-start.19 = (bf16[64,1536]{1,0:T(8,128)(2,1)}, bf16[64,1536]{1,0:T(8,128)(2,1)S(1)}, u32[]{:S(2)}, u32[]{:S(2)}) collective-permute-start(bf16[64,1536]{1,0:T(8,128)(2,1)} %collective-permute-done.18), channel_id=1, source_target_pairs={{0,8},{8,0},{16,24},{24,16},{1,9},{9,1},{17,25},{25,17},{2,10},{10... | collective-permute-start | bytes 589832 | tf_op jit(solution)/shard_map/ppermute | solution.py:159
  47.5 10.1 %collective-permute-start.20 = (bf16[64,1536]{1,0:T(8,128)(2,1)}, bf16[64,1536]{1,0:T(8,128)(2,1)S(1)}, u32[]{:S(2)}, u32[]{:S(2)}) collective-permute-start(bf16[64,1536]{1,0:T(8,128)(2,1)} %collective-permute-done.18), channel_id=1, source_target_pairs={{0,16},{8,24},{16,0},{24,8},{1,17},{9,25},{17,1},{25,9},{2,18},{10... | collective-permute-start | bytes 589832 | tf_op jit(solution)/shard_map/ppermute | solution.py:159
  48.4 12.2 %collective-permute-start.21 = (bf16[64,1536]{1,0:T(8,128)(2,1)}, bf16[64,1536]{1,0:T(8,128)(2,1)S(1)}, u32[]{:S(2)}, u32[]{:S(2)}) collective-permute-start(bf16[64,1536]{1,0:T(8,128)(2,1)} %collective-permute-done.18), channel_id=1, source_target_pairs={{0,24},{8,16},{16,8},{24,0},{1,25},{9,17},{17,9},{25,1},{2,26},{10... | collective-permute-start | bytes 589832 | tf_op jit(solution)/shard_map/ppermute | solution.py:159
  50.2 12.9 %collective-permute-start.25 = (bf16[64,1536]{1,0:T(8,128)(2,1)}, bf16[64,1536]{1,0:T(8,128)(2,1)S(1)}, u32[]{:S(2)}, u32[]{:S(2)}) collective-permute-start(bf16[64,1536]{1,0:T(8,128)(2,1)} %collective-permute-done.24), channel_id=1, source_target_pairs={{0,8},{8,0},{16,24},{24,16},{1,9},{9,1},{17,25},{25,17},{2,10},{10... | collective-permute-start | bytes 589832 | tf_op jit(solution)/shard_map/ppermute | solution.py:159
  51.1 25.3 %copy-start.3 = (bf16[1536,3,384]{0,2,1:T(8,128)(2,1)S(1)}, bf16[1536,3,384]{0,2,1:T(8,128)(2,1)}, u32[]{:S(2)}) copy-start(bf16[1536,3,384]{0,2,1:T(8,128)(2,1)} %copy.32) | copy-start | bytes 10616836
  54.9 9.3 %collective-permute-start.26 = (bf16[64,1536]{1,0:T(8,128)(2,1)}, bf16[64,1536]{1,0:T(8,128)(2,1)S(1)}, u32[]{:S(2)}, u32[]{:S(2)}) collective-permute-start(bf16[64,1536]{1,0:T(8,128)(2,1)} %collective-permute-done.24), channel_id=1, source_target_pairs={{0,16},{8,24},{16,0},{24,8},{1,17},{9,25},{17,1},{25,9},{2,18},{10... | collective-permute-start | bytes 589832 | tf_op jit(solution)/shard_map/ppermute | solution.py:159
  55.8 12.0 %collective-permute-start.27 = (bf16[64,1536]{1,0:T(8,128)(2,1)}, bf16[64,1536]{1,0:T(8,128)(2,1)S(1)}, u32[]{:S(2)}, u32[]{:S(2)}) collective-permute-start(bf16[64,1536]{1,0:T(8,128)(2,1)} %collective-permute-done.24), channel_id=1, source_target_pairs={{0,24},{8,16},{16,8},{24,0},{1,25},{9,17},{17,9},{25,1},{2,26},{10... | collective-permute-start | bytes 589832 | tf_op jit(solution)/shard_map/ppermute | solution.py:159
  57.6 13.9 %collective-permute-start.13 = (bf16[64,1536]{1,0:T(8,128)(2,1)S(1)}, bf16[64,1536]{1,0:T(8,128)(2,1)S(1)}, u32[]{:S(2)}, u32[]{:S(2)}) collective-permute-start(bf16[64,1536]{1,0:T(8,128)(2,1)S(1)} %collective-permute-done.12), channel_id=1, source_target_pairs={{0,8},{8,0},{16,24},{24,16},{1,9},{9,1},{17,25},{25,17},{2,10},{10... | collective-permute-start | bytes 589832 | tf_op jit(solution)/shard_map/ppermute | solution.py:159
  60.6 11.4 %collective-permute-start.14 = (bf16[64,1536]{1,0:T(8,128)(2,1)S(1)}, bf16[64,1536]{1,0:T(8,128)(2,1)S(1)}, u32[]{:S(2)}, u32[]{:S(2)}) collective-permute-start(bf16[64,1536]{1,0:T(8,128)(2,1)S(1)} %collective-permute-done.12), channel_id=1, source_target_pairs={{0,16},{8,24},{16,0},{24,8},{1,17},{9,25},{17,1},{25,9},{2,18},{10... | collective-permute-start | bytes 589832 | tf_op jit(solution)/shard_map/ppermute | solution.py:159
  63.1 12.8 %collective-permute-start.15 = (bf16[64,1536]{1,0:T(8,128)(2,1)S(1)}, bf16[64,1536]{1,0:T(8,128)(2,1)S(1)}, u32[]{:S(2)}, u32[]{:S(2)}) collective-permute-start(bf16[64,1536]{1,0:T(8,128)(2,1)S(1)} %collective-permute-done.12), channel_id=1, source_target_pairs={{0,24},{8,16},{16,8},{24,0},{1,25},{9,17},{17,9},{25,1},{2,26},{10... | collective-permute-start | bytes 589832 | tf_op jit(solution)/shard_map/ppermute | solution.py:159
  64.2 18.8 %collective-permute-start.11 = (bf16[256,1152]{1,0:T(8,128)(2,1)S(1)}, bf16[256,1152]{1,0:T(8,128)(2,1)S(1)}, u32[]{:S(2)}, u32[]{:S(2)}) collective-permute-start(bf16[256,1152]{1,0:T(8,128)(2,1)S(1)} %convolution_convert_fusion.3), channel_id=1, source_target_pairs={{0,1},{1,0},{2,3},{3,2},{4,5},{5,4},{6,7},{7,6},{8,9},{9,8},{10,11... | collective-permute-start | bytes 1769480 | tf_op jit(solution)/shard_map/ppermute | solution.py:169
  67.9 8.4 %collective-permute-start.22 = (f32[2,256]{1,0:T(2,128)S(1)}, f32[2,256]{1,0:T(2,128)S(1)}, u32[]{:S(2)}, u32[]{:S(2)}) collective-permute-start(f32[2,256]{1,0:T(2,128)S(1)} %pad_maximum_fusion.9), channel_id=1, source_target_pairs={{0,1},{1,0},{2,3},{3,2},{4,5},{5,4},{6,7},{7,6},{8,9},{9,8},{10,11... | collective-permute-start | bytes 6152 | tf_op jit(solution)/shard_map/ppermute | solution.py:169
  71.5 7.3 %collective-permute-start.28 = (f32[2,256]{1,0:T(2,128)S(1)}, f32[2,256]{1,0:T(2,128)S(1)}, u32[]{:S(2)}, u32[]{:S(2)}) collective-permute-start(f32[2,256]{1,0:T(2,128)S(1)} %pad_maximum_fusion.10), channel_id=1, source_target_pairs={{0,1},{1,0},{2,3},{3,2},{4,5},{5,4},{6,7},{7,6},{8,9},{9,8},{10,11... | collective-permute-start | bytes 6152 | tf_op jit(solution)/shard_map/ppermute | solution.py:169
  76.3 5.2 %collective-permute-start.16 = (f32[2,256]{1,0:T(2,128)S(1)}, f32[2,256]{1,0:T(2,128)S(1)}, u32[]{:S(2)}, u32[]{:S(2)}) collective-permute-start(f32[2,256]{1,0:T(2,128)S(1)} %pad_maximum_fusion.8), channel_id=1, source_target_pairs={{0,1},{1,0},{2,3},{3,2},{4,5},{5,4},{6,7},{7,6},{8,9},{9,8},{10,11... | collective-permute-start | bytes 6152 | tf_op jit(solution)/shard_map/ppermute | solution.py:169
  78.2 7.8 %collective-permute-start.23 = (bf16[256,768]{1,0:T(8,128)(2,1)S(1)}, bf16[256,768]{1,0:T(8,128)(2,1)S(1)}, u32[]{:S(2)}, u32[]{:S(2)}) collective-permute-start(bf16[256,768]{1,0:T(8,128)(2,1)S(1)} %fusion.64), channel_id=1, source_target_pairs={{0,1},{1,0},{2,3},{3,2},{4,5},{5,4},{6,7},{7,6},{8,9},{9,8},{10,11... | collective-permute-start | bytes 1179656 | tf_op jit(solution)/shard_map/ppermute | solution.py:169
  81.5 11.9 %collective-permute-start.29 = (bf16[256,768]{1,0:T(8,128)(2,1)}, bf16[256,768]{1,0:T(8,128)(2,1)}, u32[]{:S(2)}, u32[]{:S(2)}) collective-permute-start(bf16[256,768]{1,0:T(8,128)(2,1)} %fusion.67), channel_id=1, source_target_pairs={{0,1},{1,0},{2,3},{3,2},{4,5},{5,4},{6,7},{7,6},{8,9},{9,8},{10,11... | collective-permute-start | bytes 1179656 | tf_op jit(solution)/shard_map/ppermute | solution.py:169
  82.5 5.3 %collective-permute-start.17 = (bf16[256,768]{1,0:T(8,128)(2,1)S(1)}, bf16[256,768]{1,0:T(8,128)(2,1)S(1)}, u32[]{:S(2)}, u32[]{:S(2)}) collective-permute-start(bf16[256,768]{1,0:T(8,128)(2,1)S(1)} %fusion.61), channel_id=1, source_target_pairs={{0,1},{1,0},{2,3},{3,2},{4,5},{5,4},{6,7},{7,6},{8,9},{9,8},{10,11... | collective-permute-start | bytes 1179656 | tf_op jit(solution)/shard_map/ppermute | solution.py:169
  107.6 1.6 collective-permute-start.30
  111.9 7.8 %collective-permute-start.31 = (bf16[64,1536]{1,0:T(8,128)(2,1)S(1)}, bf16[64,1536]{1,0:T(8,128)(2,1)S(1)}, u32[]{:S(2)}, u32[]{:S(2)}) collective-permute-start(bf16[64,1536]{1,0:T(8,128)(2,1)S(1)} %get-tuple-element.27), channel_id=1, source_target_pairs={{0,8},{8,0},{16,24},{24,16},{1,9},{9,1},{17,25},{25,17},{2,10},{10... | collective-permute-start | bytes 589832 | tf_op jit(solution)/shard_map/ppermute | solution.py:164
  113.0 11.1 %collective-permute-start.32 = (bf16[64,1536]{1,0:T(8,128)(2,1)S(1)}, bf16[64,1536]{1,0:T(8,128)(2,1)S(1)}, u32[]{:S(2)}, u32[]{:S(2)}) collective-permute-start(bf16[64,1536]{1,0:T(8,128)(2,1)S(1)} %get-tuple-element.29), channel_id=1, source_target_pairs={{0,16},{8,24},{16,0},{24,8},{1,17},{9,25},{17,1},{25,9},{2,18},{10... | collective-permute-start | bytes 589832 | tf_op jit(solution)/shard_map/ppermute | solution.py:164
  114.2 9.9 %collective-permute-start.33 = (bf16[64,1536]{1,0:T(8,128)(2,1)S(1)}, bf16[64,1536]{1,0:T(8,128)(2,1)S(1)}, u32[]{:S(2)}, u32[]{:S(2)}) collective-permute-start(bf16[64,1536]{1,0:T(8,128)(2,1)S(1)} %get-tuple-element.28), channel_id=1, source_target_pairs={{0,24},{8,16},{16,8},{24,0},{1,25},{9,17},{17,9},{25,1},{2,26},{10... | collective-permute-start | bytes 589832 | tf_op jit(solution)/shard_map/ppermute | solution.py:164
  124.4 1.2 collective-permute-start.34
  125.7 21.9 %slice-start = ((s8[9437184]{0:T(1024)(128)(4,1)}), s8[4194304]{0:T(1024)(128)(4,1)S(1)}, s32[]{:S(2)}) async-start(s8[9437184]{0:T(1024)(128)(4,1)} %bitcast.160), calls=%async_computation | async-start | bytes 8388608
  125.8 21.7 %slice-start.1 = ((s8[9437184]{0:T(1024)(128)(4,1)}), s8[4194304]{0:T(1024)(128)(4,1)S(1)}, s32[]{:S(2)}) async-start(s8[9437184]{0:T(1024)(128)(4,1)} %bitcast.160), calls=%async_computation.1 | async-start | bytes 8388608
  125.8 21.7 %slice-start.2 = ((s8[9437184]{0:T(1024)(128)(4,1)}), s8[1048576]{0:T(1024)(128)(4,1)S(1)}, s32[]{:S(2)}) async-start(s8[9437184]{0:T(1024)(128)(4,1)} %bitcast.160), calls=%async_computation.2 | async-start | bytes 2097152
  125.9 7.8 %collective-permute-start.35 = (bf16[64,1536]{1,0:T(8,128)(2,1)S(1)}, bf16[64,1536]{1,0:T(8,128)(2,1)S(1)}, u32[]{:S(2)}, u32[]{:S(2)}) collective-permute-start(bf16[64,1536]{1,0:T(8,128)(2,1)S(1)} %add_convert_fusion), channel_id=1, source_target_pairs={{0,8},{8,0},{16,24},{24,16},{1,9},{9,1},{17,25},{25,17},{2,10},{10... | collective-permute-start | bytes 589832 | tf_op jit(solution)/shard_map/ppermute | solution.py:159
  126.8 7.5 %collective-permute-start.36 = (bf16[64,1536]{1,0:T(8,128)(2,1)S(1)}, bf16[64,1536]{1,0:T(8,128)(2,1)S(1)}, u32[]{:S(2)}, u32[]{:S(2)}) collective-permute-start(bf16[64,1536]{1,0:T(8,128)(2,1)S(1)} %add_convert_fusion), channel_id=1, source_target_pairs={{0,16},{8,24},{16,0},{24,8},{1,17},{9,25},{17,1},{25,9},{2,18},{10... | collective-permute-start | bytes 589832 | tf_op jit(solution)/shard_map/ppermute | solution.py:159
  127.7 10.1 %collective-permute-start.37 = (bf16[64,1536]{1,0:T(8,128)(2,1)S(1)}, bf16[64,1536]{1,0:T(8,128)(2,1)S(1)}, u32[]{:S(2)}, u32[]{:S(2)}) collective-permute-start(bf16[64,1536]{1,0:T(8,128)(2,1)S(1)} %add_convert_fusion), channel_id=1, source_target_pairs={{0,24},{8,16},{16,8},{24,0},{1,25},{9,17},{17,9},{25,1},{2,26},{10... | collective-permute-start | bytes 589832 | tf_op jit(solution)/shard_map/ppermute | solution.py:159
  144.1 3.5 %collective-permute-start.38 = (bf16[256,3072]{1,0:T(8,128)(2,1)S(1)}, bf16[256,3072]{1,0:T(8,128)(2,1)S(1)}, u32[]{:S(2)}, u32[]{:S(2)}) collective-permute-start(bf16[256,3072]{1,0:T(8,128)(2,1)S(1)} %convolution_convert_fusion), channel_id=1, source_target_pairs={{0,1},{1,0},{2,3},{3,2},{4,5},{5,4},{6,7},{7,6},{8,9},{9,8},{10,11... | collective-permute-start | bytes 4718600 | tf_op jit(solution)/shard_map/ppermute | solution.py:169
  150.7 7.8 %collective-permute-start.39 = (bf16[64,1536]{1,0:T(8,128)(2,1)S(1)}, bf16[64,1536]{1,0:T(8,128)(2,1)S(1)}, u32[]{:S(2)}, u32[]{:S(2)}) collective-permute-start(bf16[64,1536]{1,0:T(8,128)(2,1)S(1)} %get-tuple-element.24), channel_id=1, source_target_pairs={{0,8},{8,0},{16,24},{24,16},{1,9},{9,1},{17,25},{25,17},{2,10},{10... | collective-permute-start | bytes 589832 | tf_op jit(solution)/shard_map/ppermute | solution.py:164
  151.9 10.9 %collective-permute-start.40 = (bf16[64,1536]{1,0:T(8,128)(2,1)S(1)}, bf16[64,1536]{1,0:T(8,128)(2,1)S(1)}, u32[]{:S(2)}, u32[]{:S(2)}) collective-permute-start(bf16[64,1536]{1,0:T(8,128)(2,1)S(1)} %get-tuple-element.26), channel_id=1, source_target_pairs={{0,16},{8,24},{16,0},{24,8},{1,17},{9,25},{17,1},{25,9},{2,18},{10... | collective-permute-start | bytes 589832 | tf_op jit(solution)/shard_map/ppermute | solution.py:164
  153.1 9.7 %collective-permute-start.41 = (bf16[64,1536]{1,0:T(8,128)(2,1)S(1)}, bf16[64,1536]{1,0:T(8,128)(2,1)S(1)}, u32[]{:S(2)}, u32[]{:S(2)}) collective-permute-start(bf16[64,1536]{1,0:T(8,128)(2,1)S(1)} %get-tuple-element.25), channel_id=1, source_target_pairs={{0,24},{8,16},{16,8},{24,0},{1,25},{9,17},{17,9},{25,1},{2,26},{10... | collective-permute-start | bytes 589832 | tf_op jit(solution)/shard_map/ppermute | solution.py:164
  (33 other events, 166.5 us)

commit v2 on v0

--- a/solution.py
+++ b/solution.py
@@ -3,6 +3,8 @@
 import jax
 import jax.numpy as jnp
 from jax import lax
+from jax.experimental import pallas as pl
+from jax.experimental.pallas import tpu as pltpu
 from jax.sharding import PartitionSpec as P
 
 
@@ -150,9 +152,262 @@
     return mixed + own_mod[5] * feedforward
 
 
+VMEM_BYTES = 48 * 1024 * 1024
+
+
+def permuted(values, axis, distance):
+    size = lax.axis_size(axis)
+    return lax.ppermute(values, axis, [(i, i ^ distance) for i in range(size)])
+
+
+def from_all(values, axis):
+    return [values] + [permuted(values, axis, k) for k in range(1, lax.axis_size(axis))]
+
+
+def to_all(blocks, axis):
+    return [blocks[0]] + [permuted(blocks[k], axis, k) for k in range(1, len(blocks))]
+
+
+def doubled(piece, axis):
+    position = lax.axis_index(axis)
+    distance = 1
+    while distance < lax.axis_size(axis):
+        other = permuted(piece, axis, distance)
+        upper = (position & distance) != 0
+        piece = jnp.concatenate(
+            [jnp.where(upper, other, piece), jnp.where(upper, piece, other)], axis=0
+        )
+        distance *= 2
+    return piece
+
+
+def modulation_rows(cond, mod_weight, features, width):
+    activated = jax.nn.silu(cond.astype(jnp.float32)).astype(jnp.bfloat16)
+    piece = jnp.dot(activated[None, :], mod_weight, preferred_element_type=jnp.float32)[0]
+    for axis in ("tensor", "blk", "ulysses"):
+        piece = doubled(piece, axis)
+    rows = piece.reshape(6, features)
+    return lax.dynamic_slice_in_dim(rows, lax.axis_index("tensor") * width, width, 1)
+
+
+def standardized(values, features):
+    sums = jnp.stack([jnp.sum(values, axis=-1), jnp.sum(values * values, axis=-1)])
+    sums = sums + permuted(sums, "tensor", 1)
+    average = sums[0][:, None] / features
+    variance = sums[1][:, None] / features - average * average
+    return (values - average) * lax.rsqrt(variance + 1e-06)
+
+
+def product(left, right):
+    return jnp.dot(left, right, preferred_element_type=jnp.float32).astype(jnp.bfloat16)
+
+
+def added(blocks):
+    total = blocks[0].astype(jnp.float32)
+    for block in blocks[1:]:
+        total = total + block.astype(jnp.float32)
+    return total
+
+
+def project_kernel(pick, *refs):
+    *block_refs, shift_ref, scale_ref, weight_ref, out_ref, normed_ref = refs
+
+    @pl.when(pl.program_id(0) == 0)
+    def _():
+        rows = block_refs[0].shape[0]
+        for k, block_ref in enumerate(block_refs):
+            values = block_ref[...].astype(jnp.float32)
+            values = values * (1.0 + scale_ref[...]) + shift_ref[...]
+            normed_ref[k * rows : (k + 1) * rows, :] = values.astype(jnp.bfloat16)
+
+    out_ref[...] = jnp.dot(
+        normed_ref[...], weight_ref[0], preferred_element_type=jnp.float32
+    ).astype(jnp.bfloat16)
+
+
+def projected(blocks, shift_row, scale_row, weights, first, half, pick):
+    rows, width = blocks[0].shape
+    all_rows = rows * len(blocks)
+    count = weights.shape[0] - first
+    whole = lambda shape: pl.BlockSpec(shape, lambda j, pick: (0, 0))
+    return pl.pallas_call(
+        project_kernel,
+        grid_spec=pltpu.PrefetchScalarGridSpec(
+            num_scalar_prefetch=1,
+            grid=(count,),
+            in_specs=[whole((rows, width)) for _ in blocks]
+            + [whole((1, width)), whole((1, width))]
+            + [pl.BlockSpec((1, width, half), lambda j, pick: (j + first, 0, pick[0]))],
+            out_specs=pl.BlockSpec((all_rows, half), lambda j, pick: (0, j)),
+            scratch_shapes=[pltpu.VMEM((all_rows, width), jnp.bfloat16)],
+        ),
+        out_shape=jax.ShapeDtypeStruct((all_rows, count * half), jnp.bfloat16),
+        compiler_params=pltpu.CompilerParams(vmem_limit_bytes=VMEM_BYTES // 2),
+        cost_estimate=pl.CostEstimate(
+            flops=2 * all_rows * width * count * half,
+            bytes_accessed=2 * width * count * half,
+            transcendentals=0,
+        ),
+        name="projected",
+    )(pick, *blocks, shift_row, scale_row, weights)
+
+
+def heads_kernel(count, head_size, own_ref, arrived_ref, q_gain_ref, k_gain_ref, *out_refs):
+    half = own_ref.shape[1] // count
+    total = lambda lo: (
+        own_ref[:, lo : lo + head_size].astype(jnp.float32)
+        + arrived_ref[:, lo : lo + head_size].astype(jnp.float32)
+    )
+
+    def normal(lo, gain_ref):
+        values = total(lo)
+        spread = jnp.mean(values * values, axis=-1, keepdims=True) + 1e-06
+        return (values * lax.rsqrt(spread) * gain_ref[...]).astype(jnp.bfloat16)
+
+    for lo in range(0, half, head_size):
+        if count == 3:
+            out_refs[1][:, lo : lo + head_size] = normal(lo, q_gain_ref)
+        key_lo = (count - 2) * half + lo
+        out_refs[0][:, lo : lo + head_size] = normal(key_lo, k_gain_ref)
+        out_refs[0][:, half + lo : half + lo + head_size] = total(key_lo + half).astype(
+            jnp.bfloat16
+        )
+
+
+def split_heads(own, arrived, q_gain, k_gain, count):
+    rows, columns = own.shape
+    half = columns // count
+    head_size = q_gain.shape[0]
+    shapes = [jax.ShapeDtypeStruct((rows, 2 * half), jnp.bfloat16)]
+    if count == 3:
+        shapes.append(jax.ShapeDtypeStruct((rows, half), jnp.bfloat16))
+    return pl.pallas_call(
+        lambda *refs: heads_kernel(count, head_size, *refs),
+        out_shape=shapes,
+        compiler_params=pltpu.CompilerParams(vmem_limit_bytes=VMEM_BYTES // 4),
+        cost_estimate=pl.CostEstimate(
+            flops=8 * rows * columns, bytes_accessed=6 * rows * columns, transcendentals=rows * 6
+        ),
+        name="split_heads",
+    )(own, arrived, q_gain[None, :], k_gain[None, :])
+
+
+def attention_kernel(head_size, query_ref, *refs):
+    *kv_refs, out_ref = refs
+    half = query_ref.shape[1]
+    score_scale = 1.0 / math.sqrt(head_size)
+    for lo in range(0, half, head_size):
+        query = query_ref[:, lo : lo + head_size]
+        scores = [
+            lax.dot_general(
+                query,
+                kv_ref[:, lo : lo + head_size],
+                (((1,), (1,)), ((), ())),
+                preferred_element_type=jnp.float32,
+            )
+            * score_scale
+            for kv_ref in kv_refs
+        ]
+        top = jnp.max(scores[0], axis=-1, keepdims=True)
+        for part in scores[1:]:
+            top = jnp.maximum(top, jnp.max(part, axis=-1, keepdims=True))
+        denominator, summed = 0.0, 0.0
+        for part, kv_ref in zip(scores, kv_refs):
+            weights = jnp.exp(part - top)
+            denominator = denominator + jnp.sum(weights, axis=-1, keepdims=True)
+            summed = summed + jnp.dot(
+                weights.astype(jnp.bfloat16),
+                kv_ref[:, half + lo : half + lo + head_size],
+                preferred_element_type=jnp.float32,
+            )
+        out_ref[:, lo : lo + head_size] = (summed / denominator).astype(jnp.bfloat16)
+
+
+def attention(queries, kv_parts, head_size):
+    rows, half = queries.shape
+    keys = sum(part.shape[0] for part in kv_parts)
+    return pl.pallas_call(
+        lambda *refs: attention_kernel(head_size, *refs),
+        out_shape=jax.ShapeDtypeStruct((rows, half), jnp.bfloat16),
+        compiler_params=pltpu.CompilerParams(vmem_limit_bytes=VMEM_BYTES),
+        cost_estimate=pl.CostEstimate(
+            flops=4 * rows * keys * half,
+            bytes_accessed=4 * keys * half,
+            transcendentals=rows * keys * half // head_size,
+        ),
+        name="attention",
+    )(queries, *kv_parts)
+
+
+def on_pair(
+    tokens, cond, mod_weight, qkv_weight, q_gain, k_gain, out_weight, up_weight, down_weight
+):
+    tensor_pos = lax.axis_index("tensor")
+    rows, width = tokens.shape
+    features = width * lax.axis_size("tensor")
+    head_size = q_gain.shape[0]
+    half = qkv_weight.shape[2] // 2
+    blocks_z = lax.axis_size("blk")
+
+    resid = tokens.astype(jnp.float32)
+    normal = standardized(resid, features).astype(jnp.bfloat16)
+    remote = {0: normal}
+    for k in range(2, blocks_z):
+        remote[k] = permuted(remote[k - 1] if k % 2 else normal, "blk", 1 if k % 2 else k)
+    chunks = [from_all(remote[k], "ulysses") for k in sorted(remote)]
+
+    own_mod = modulation_rows(cond, mod_weight, features, width)
+    weights = jnp.moveaxis(qkv_weight, 1, 0)
+    pick_own = tensor_pos.reshape(1).astype(jnp.int32)
+    shift_row, scale_row = own_mod[0:1], own_mod[1:2]
+
+    queries, kv_parts = None, []
+    for index, blocks in enumerate(chunks):
+        first = 0 if index == 0 else 1
+        arrived = permuted(
+            projected(blocks, shift_row, scale_row, weights, first, half, 1 - pick_own),
+            "tensor",
+            1,
+        )
+        own = projected(blocks, shift_row, scale_row, weights, first, half, pick_own)
+        outs = split_heads(own, arrived, q_gain, k_gain, 3 - first)
+        kv_parts.append(outs[0])
+        if index == 0:
+            queries = outs[1]
+            if blocks_z > 1:
+                kv_parts.append(permuted(outs[0], "blk", 1))
+
+    context = attention(queries, kv_parts, head_size)
+    other = permuted(context, "tensor", 1)
+    context = jnp.concatenate(
+        [
+            jnp.where(tensor_pos == 0, context, other),
+            jnp.where(tensor_pos == 0, other, context),
+        ],
+        axis=1,
+    )
+
+    attended = reduced_rows(product(context, out_weight), rows)
+    mixed = resid + own_mod[2] * attended
+    normed_two = standardized(mixed, features) * (1.0 + own_mod[4]) + own_mod[3]
+    gathered_two = jnp.concatenate(from_all(normed_two.astype(jnp.bfloat16), "ulysses"), axis=0)
+    partial = product(gathered_two, up_weight)
+    hidden = added([partial, permuted(partial, "tensor", 1)])
+    activ = jax.nn.gelu(hidden, approximate=True).astype(jnp.bfloat16)
+    feedforward = reduced_rows(product(activ, down_weight), rows)
+    return mixed + own_mod[5] * feedforward
+
+
+def reduced_rows(partial, rows):
+    blocks = [partial[i : i + rows] for i in range(0, partial.shape[0], rows)]
+    return added(to_all(blocks, "ulysses"))
+
+
 def solution(mesh):
+    sizes = [mesh.shape[axis] for axis in ("ulysses", "blk")]
+    pairs = mesh.shape["tensor"] == 2 and all(size & (size - 1) == 0 for size in sizes)
     return jax.shard_map(
-        on_device,
+        on_pair if pairs else on_device,
         mesh=mesh,
         in_specs=(
             P(("ulysses", "blk"), "tensor"),

time: 344 us -> 138 us (0.40)
  waiting for transfers between devices: 192 us -> 53.3 us
  blocking collectives: 73.8 us -> 0 us
  starting transfers between devices: 0.21 us -> 36.6 us
  Pallas kernels: 0 us -> 18.7 us
  local copies, waits for them, and re-layouts: 20.9 us -> 7.09 us
  between operations: 13.6 us -> 0.34 us
  matrix products: 25.2 us -> 13 us
  other arithmetic: 16.8 us -> 8.72 us
    unnamed x7 -> x0, waiting for transfers between devices: 109 us -> none
    reduce_scatter x4 -> x0, waiting for transfers between devices: 72.1 us -> none  [the longest x1 27.4 us: on_device(): lax.psum_scatter(jnp.dot(activ_rows, down_weight, preferred_element_type=...]
    all_gather x8 -> x0, blocking collectives: 68.2 us -> none  [the longest x2 23.3 us: spread_rows(): return lax.all_gather(values, 'ulysses', axis=0, tiled=True)]
    ppermute x0 -> x33, waiting for transfers between devices: none -> 53.3 us  [permuted(): return lax.ppermute(values, axis, [(i, i ^ distance) for i in range(size)])]
    ppermute x0 -> x33, starting transfers between devices: none -> 36.6 us  [permuted(): return lax.ppermute(values, axis, [(i, i ^ distance) for i in range(size)])]
    pallas_call x0 -> x10, Pallas kernels: none -> 18.7 us  [the longest x6 15.6 us: projected(): pl.pallas_call(project_kernel, grid_spec=pltpu.PrefetchScalarGridSpec(num...]
    dot_general x7 -> x4, matrix products: 25.2 us -> 13 us  [the longest x3 12 us: product(): jnp.dot(left, right, preferred_element_type=jnp.float32)]
    all_gather x1 -> x0, waiting for transfers between devices: 11.1 us -> none  [on_device(): activ_rows = lax.all_gather(activ, 'tensor', axis=0, tiled=True)]
  transfers between devices with their start and end apart: 6 -> 33, of which waited for: 6 -> 20; matrix products, arithmetic and copies ran while one was open for 3% -> 6% of each run, Pallas kernels for 0% -> 12%
where the time goes in v2:
time: 138 us
  waiting for transfers between devices  53.3 us (39%)
  starting transfers between devices  36.6 us (27%)
  Pallas kernels  18.7 us (14%)
  matrix products  13 us (9%)
  other arithmetic  8.72 us (6%)
  local copies, waits for them, and re-layouts  7.09 us (5%)
    ppermute x33, waiting for transfers between devices, permuted(): return lax.ppermute(values, axis, [(i, i ^ distance) for i in range(size)])  53.3 us
    ppermute x33, starting transfers between devices, permuted(): return lax.ppermute(values, axis, [(i, i ^ distance) for i in range(size)])  36.6 us
    pallas_call x6, Pallas kernels, projected(): pl.pallas_call(project_kernel, grid_spec=pltpu.PrefetchScalarGridSpec(num...  15.6 us
    dot_general x3, matrix products, product(): jnp.dot(left, right, preferred_element_type=jnp.float32)  12 us
    unnamed x24, local copies, waits for them, and re-layouts  4.2 us
    concatenate x2, local copies, waits for them, and re-layouts, doubled(): jnp.concatenate([jnp.where(upper, other, piece), jnp.where(upper, piece,...  2.8 us
  transfers between devices with their start and end apart: 33, of which 20 were waited for; matrix products, arithmetic and copies ran while one was open for 6% of the time, Pallas kernels for 12%

profile of v2, /device:TPU:0, one launch (start us, length us, event | category | flops | bytes accessed | tf_op | source)
XLA Modules:
  0.0 137.7 jit_solution(13410703848079668268)
XLA Ops:
  0.9 1.1 copy-done
  4.5 3.0 %collective-permute-start.1 = (f32[1152]{0:T(1024)S(1)}, f32[1152]{0:T(1024)S(1)}, u32[]{:S(2)}, u32[]{:S(2)}) collective-permute-start(f32[1152]{0:T(1024)S(1)} %pad_maximum_fusion.3), channel_id=1, source_target_pairs={{0,2},{2,0},{4,6},{6,4},{1,3},{3,1},{5,7},{7,5},{8,10},{10,8},{12,... | collective-permute-start | bytes 13832 | tf_op jit(solution)/shard_map/ppermute | solution.py:160
  9.2 3.1 %collective-permute-start.2 = (f32[2304]{0:T(1024)S(1)}, f32[2304]{0:T(1024)S(1)}, u32[]{:S(2)}, u32[]{:S(2)}) collective-permute-start(f32[2304]{0:T(1024)S(1)} %pad_maximum_fusion.2), channel_id=1, source_target_pairs={{0,4},{2,6},{4,0},{6,2},{1,5},{3,7},{5,1},{7,3},{8,12},{10,14},{12... | collective-permute-start | bytes 27656 | tf_op jit(solution)/shard_map/ppermute | solution.py:160
  12.3 1.7 %collective-permute-done.2 = f32[2304]{0:T(1024)S(1)} collective-permute-done((f32[2304]{0:T(1024)S(1)}, f32[2304]{0:T(1024)S(1)}, u32[]{:S(2)}, u32[]{:S(2)}) %collective-permute-start.2) | collective-permute-done | bytes 9248 | tf_op jit(solution)/shard_map/ppermute | solution.py:160
  13.9 1.9 %collective-permute-start.3 = (f32[4608]{0:T(1024)S(1)}, f32[4608]{0:T(1024)S(1)}, u32[]{:S(2)}, u32[]{:S(2)}) collective-permute-start(f32[4608]{0:T(1024)S(1)} %pad_maximum_fusion.1), channel_id=1, source_target_pairs={{0,8},{8,0},{16,24},{24,16},{1,9},{9,1},{17,25},{25,17},{2,10},{10... | collective-permute-start | bytes 55304 | tf_op jit(solution)/shard_map/ppermute | solution.py:160
  15.8 2.0 %collective-permute-done.3 = f32[4608]{0:T(1024)S(1)} collective-permute-done((f32[4608]{0:T(1024)S(1)}, f32[4608]{0:T(1024)S(1)}, u32[]{:S(2)}, u32[]{:S(2)}) %collective-permute-start.3) | collective-permute-done | bytes 18464 | tf_op jit(solution)/shard_map/ppermute | solution.py:160
  17.8 1.9 %collective-permute-start.4 = (f32[9216]{0:T(1024)S(1)}, f32[9216]{0:T(1024)S(1)}, u32[]{:S(2)}, u32[]{:S(2)}) collective-permute-start(f32[9216]{0:T(1024)S(1)} %pad_maximum_fusion), channel_id=1, source_target_pairs={{0,16},{8,24},{16,0},{24,8},{1,17},{9,25},{17,1},{25,9},{2,18},{10... | collective-permute-start | bytes 110600 | tf_op jit(solution)/shard_map/ppermute | solution.py:160
  19.7 1.7 %fusion.22.refs_0_ = bf16[64,1536]{1,0:T(8,128)(2,1)} fusion(bf16[64,1536]{1,0:T(8,128)(2,1)} %param.9, f32[64]{0:T(128)S(1)} %fusion.35, f32[64]{0:T(128)S(1)} %multiply_bitcast_fusion.1), kind=kLoop, calls=%fused_computation.30 | loop fusion | flops 393216 | bytes 393728 | tf_op jit(solution)/shard_map/convert_element_type | solution.py:353
  21.5 2.6 %collective-permute-start.11 = (bf16[64,1536]{1,0:T(8,128)(2,1)}, bf16[64,1536]{1,0:T(8,128)(2,1)}, u32[]{:S(2)}, u32[]{:S(2)}) collective-permute-start(bf16[64,1536]{1,0:T(8,128)(2,1)} %fusion.22.refs_0_), channel_id=1, source_target_pairs={{0,4},{2,6},{4,0},{6,2},{1,5},{3,7},{5,1},{7,3},{8,12},{10,14},{12... | collective-permute-start | bytes 589832 | tf_op jit(solution)/shard_map/ppermute | solution.py:160
  24.1 1.4 %collective-permute-start.8 = (bf16[64,1536]{1,0:T(8,128)(2,1)}, bf16[64,1536]{1,0:T(8,128)(2,1)}, u32[]{:S(2)}, u32[]{:S(2)}) collective-permute-start(bf16[64,1536]{1,0:T(8,128)(2,1)} %fusion.22.refs_0_), channel_id=1, source_target_pairs={{0,24},{8,16},{16,8},{24,0},{1,25},{9,17},{17,9},{25,1},{2,26},{10... | collective-permute-start | bytes 589832 | tf_op jit(solution)/shard_map/ppermute | solution.py:160
  25.5 1.5 %collective-permute-start.7 = (bf16[64,1536]{1,0:T(8,128)(2,1)}, bf16[64,1536]{1,0:T(8,128)(2,1)}, u32[]{:S(2)}, u32[]{:S(2)}) collective-permute-start(bf16[64,1536]{1,0:T(8,128)(2,1)} %fusion.22.refs_0_), channel_id=1, source_target_pairs={{0,16},{8,24},{16,0},{24,8},{1,17},{9,25},{17,1},{25,9},{2,18},{10... | collective-permute-start | bytes 589832 | tf_op jit(solution)/shard_map/ppermute | solution.py:160
  28.2 1.4 %concatenate.31 = f32[3,3072]{1,0:T(4,128)} reshape(f32[9216]{0:T(1024)} %get-tuple-element.26) | data formatting | bytes 73728 | tf_op jit(solution)/shard_map/concatenate | solution.py:177
  29.6 1.4 %concatenate.30 = f32[3,3072]{1,0:T(4,128)} reshape(f32[9216]{0:T(1024)} %get-tuple-element.27) | data formatting | bytes 73728 | tf_op jit(solution)/shard_map/concatenate | solution.py:177
  33.0 3.0 %copy-done.1 = bf16[1536,3,768]{2,0,1:T(8,128)(2,1)S(1)} copy-done((bf16[1536,3,768]{2,0,1:T(8,128)(2,1)S(1)}, bf16[1536,3,768]{2,0,1:T(8,128)(2,1)}, u32[]{:S(2)}) %copy-start.1) | copy-done | bytes 7077912
  36.1 3.6 %projected.7 = bf16[256,1152]{1,0:T(8,128)(2,1)S(1)} custom-call(s32[1]{0:T(128)S(6)} %sub.40.pick, bf16[64,1536]{1,0:T(8,128)(2,1)} %fusion.22.refs_0_, bf16[64,1536]{1,0:T(8,128)(2,1)} %collective-permute-done.6.refs_1_, bf16[64,1536]{1,0:T(8,128)(2,1)} %collective-permute-done.7.refs_2_, bf16[64,1536]{1,0:T(8,128)(2,1)} %collective-permute-done.8.refs_3_, ...), custom_call_target="tpu_custom_call" | custom-call | flops 905969664 | bytes 3538944 | tf_op jit(solution)/shard_map/projected/pallas_call | solution.py:233
  39.8 1.7 %collective-permute-start.16 = (bf16[64,1536]{1,0:T(8,128)(2,1)}, bf16[64,1536]{1,0:T(8,128)(2,1)S(1)}, u32[]{:S(2)}, u32[]{:S(2)}) collective-permute-start(bf16[64,1536]{1,0:T(8,128)(2,1)} %collective-permute-done.11.refs_0_), channel_id=1, source_target_pairs={{0,2},{2,0},{4,6},{6,4},{1,3},{3,1},{5,7},{7,5},{8,10},{10,8},{12,... | collective-permute-start | bytes 589832 | tf_op jit(solution)/shard_map/ppermute | solution.py:160
  41.5 1.5 %collective-permute-start.14 = (bf16[64,1536]{1,0:T(8,128)(2,1)}, bf16[64,1536]{1,0:T(8,128)(2,1)S(1)}, u32[]{:S(2)}, u32[]{:S(2)}) collective-permute-start(bf16[64,1536]{1,0:T(8,128)(2,1)} %collective-permute-done.11.refs_0_), channel_id=1, source_target_pairs={{0,24},{8,16},{16,8},{24,0},{1,25},{9,17},{17,9},{25,1},{2,26},{10... | collective-permute-start | bytes 589832 | tf_op jit(solution)/shard_map/ppermute | solution.py:160
  44.9 2.4 %collective-permute-done.16.refs_0_ = bf16[64,1536]{1,0:T(8,128)(2,1)S(1)} collective-permute-done((bf16[64,1536]{1,0:T(8,128)(2,1)}, bf16[64,1536]{1,0:T(8,128)(2,1)S(1)}, u32[]{:S(2)}, u32[]{:S(2)}) %collective-permute-start.16) | collective-permute-done | bytes 196640 | tf_op jit(solution)/shard_map/ppermute | solution.py:160
  47.3 1.5 %collective-permute-start.19 = (bf16[64,1536]{1,0:T(8,128)(2,1)S(1)}, bf16[64,1536]{1,0:T(8,128)(2,1)S(1)}, u32[]{:S(2)}, u32[]{:S(2)}) collective-permute-start(bf16[64,1536]{1,0:T(8,128)(2,1)S(1)} %collective-permute-done.16.refs_0_), channel_id=1, source_target_pairs={{0,24},{8,16},{16,8},{24,0},{1,25},{9,17},{17,9},{25,1},{2,26},{10... | collective-permute-start | bytes 589832 | tf_op jit(solution)/shard_map/ppermute | solution.py:160
  48.8 1.5 %collective-permute-done.14.refs_3_ = bf16[64,1536]{1,0:T(8,128)(2,1)S(1)} collective-permute-done((bf16[64,1536]{1,0:T(8,128)(2,1)}, bf16[64,1536]{1,0:T(8,128)(2,1)S(1)}, u32[]{:S(2)}, u32[]{:S(2)}) %collective-permute-start.14) | collective-permute-done | bytes 196640 | tf_op jit(solution)/shard_map/ppermute | solution.py:160
  50.9 3.7 %collective-permute-done.13.refs_2_ = bf16[64,1536]{1,0:T(8,128)(2,1)S(1)} collective-permute-done((bf16[64,1536]{1,0:T(8,128)(2,1)}, bf16[64,1536]{1,0:T(8,128)(2,1)S(1)}, u32[]{:S(2)}, u32[]{:S(2)}) %collective-permute-start.13) | collective-permute-done | bytes 196640 | tf_op jit(solution)/shard_map/ppermute | solution.py:160
  55.7 3.5 %projected.6.refs_0_ = bf16[256,1152]{1,0:T(8,128)(2,1)S(1)} custom-call(s32[1]{0:T(128)} %bitcast.pick, bf16[64,1536]{1,0:T(8,128)(2,1)} %fusion.22.refs_0_, bf16[64,1536]{1,0:T(8,128)(2,1)} %collective-permute-done.6.refs_1_, bf16[64,1536]{1,0:T(8,128)(2,1)} %collective-permute-done.7.refs_2_, bf16[64,1536]{1,0:T(8,128)(2,1)} %collective-permute-done.8.refs_3_, ...), custom_call_target="tpu_custom_call" | custom-call | flops 905969664 | bytes 3538944 | tf_op jit(solution)/shard_map/projected/pallas_call | solution.py:233
  59.2 2.5 %projected.9 = bf16[256,768]{1,0:T(8,128)(2,1)S(1)} custom-call(s32[1]{0:T(128)S(6)} %sub.40.pick, bf16[64,1536]{1,0:T(8,128)(2,1)} %collective-permute-done.11.refs_0_, bf16[64,1536]{1,0:T(8,128)(2,1)S(1)} %collective-permute-done.12.refs_1_, bf16[64,1536]{1,0:T(8,128)(2,1)S(1)} %collective-permute-done.13.refs_2_, ...), custom_call_target="tpu_custom_call" | custom-call | flops 603979776 | bytes 2359296 | tf_op jit(solution)/shard_map/projected/pallas_call | solution.py:233
  62.2 1.7 %projected.11 = bf16[256,768]{1,0:T(8,128)(2,1)S(1)} custom-call(s32[1]{0:T(128)S(6)} %sub.40.pick, bf16[64,1536]{1,0:T(8,128)(2,1)S(1)} %collective-permute-done.16.refs_0_, bf16[64,1536]{1,0:T(8,128)(2,1)S(1)} %collective-permute-done.17.refs_1_, bf16[64,1536]{1,0:T(8,128)(2,1)S(1)} %collective-permute-done.18.refs_2_, ...), custom_call_target="tpu_custom_call" | custom-call | flops 603979776 | bytes 2359296 | tf_op jit(solution)/shard_map/projected/pallas_call | solution.py:233
  64.9 2.4 %projected.8.refs_0_ = bf16[256,768]{1,0:T(8,128)(2,1)S(1)} custom-call(s32[1]{0:T(128)} %bitcast.pick, bf16[64,1536]{1,0:T(8,128)(2,1)} %collective-permute-done.11.refs_0_, bf16[64,1536]{1,0:T(8,128)(2,1)S(1)} %collective-permute-done.12.refs_1_, bf16[64,1536]{1,0:T(8,128)(2,1)S(1)} %collective-permute-done.13.refs_2_, ...), custom_call_target="tpu_custom_call" | custom-call | flops 603979776 | bytes 2359296 | tf_op jit(solution)/shard_map/projected/pallas_call | solution.py:233
  67.4 1.9 %projected.10.refs_0_ = bf16[256,768]{1,0:T(8,128)(2,1)S(1)} custom-call(s32[1]{0:T(128)} %bitcast.pick, bf16[64,1536]{1,0:T(8,128)(2,1)S(1)} %collective-permute-done.16.refs_0_, bf16[64,1536]{1,0:T(8,128)(2,1)S(1)} %collective-permute-done.17.refs_1_, bf16[64,1536]{1,0:T(8,128)(2,1)S(1)} %collective-permute-done.18.refs_2_, ...), custom_call_target="tpu_custom_call" | custom-call | flops 603979776 | bytes 2359296 | tf_op jit(solution)/shard_map/projected/pallas_call | solution.py:233
  69.8 6.1 %collective-permute-done.10.refs_2_ = bf16[256,768]{1,0:T(8,128)(2,1)S(1)} collective-permute-done((bf16[256,768]{1,0:T(8,128)(2,1)S(1)}, bf16[256,768]{1,0:T(8,128)(2,1)S(1)}, u32[]{:S(2)}, u32[]{:S(2)}) %collective-permute-start.10) | collective-permute-done | bytes 393248 | tf_op jit(solution)/shard_map/ppermute | solution.py:160
  75.9 2.3 %attention.1 = bf16[256,384]{1,0:T(8,128)(2,1)} custom-call(bf16[256,384]{1,0:T(8,128)(2,1)S(1)} %get-tuple-element.7.refs_0_, bf16[256,768]{1,0:T(8,128)(2,1)S(1)} %get-tuple-element.8.refs_1_, bf16[256,768]{1,0:T(8,128)(2,1)S(1)} %collective-permute-done.10.refs_2_, bf16[256,768]{1,0:T(8,128)(2,1)S(1)} %split_heads.4.refs_3_, ...), custom_call_target="tpu_custom_call" | custom-call | flops 402653184 | bytes 1572864 | tf_op jit(solution)/shard_map/attention/pallas_call | solution.py:329
  78.2 1.8 %collective-permute-done.21 = bf16[256,384]{1,0:T(8,128)(2,1)} collective-permute-done((bf16[256,384]{1,0:T(8,128)(2,1)}, bf16[256,384]{1,0:T(8,128)(2,1)}, u32[]{:S(2)}, u32[]{:S(2)}) %collective-permute-start.21) | collective-permute-done | bytes 196640 | tf_op jit(solution)/shard_map/ppermute | solution.py:160
  81.0 2.4 %convolution_convert_fusion.2 = bf16[256,1536]{1,0:T(8,128)(2,1)S(1)} fusion(bf16[768,1536]{1,0:T(8,128)(2,1)} %param.15, bf16[256,384]{1,0:T(8,128)(2,1)S(1)} %get-tuple-element.25, bf16[256,384]{1,0:T(8,128)(2,1)S(1)} %get-tuple-element.24), kind=kOutput, calls=%fused_computation.11 | convolution fusion | flops 605159424 | bytes 3538944 | tf_op jit(solution)/shard_map/dot_general | solution.py:202
  84.5 1.3 collective-permute-start.24
  85.8 1.3 collective-permute-start.23
  87.1 4.3 %collective-permute-done.22 = bf16[64,1536]{1,0:T(8,128)(2,1)S(1)} collective-permute-done((bf16[64,1536]{1,0:T(8,128)(2,1)S(1)}, bf16[64,1536]{1,0:T(8,128)(2,1)S(1)}, u32[]{:S(2)}, u32[]{:S(2)}) %collective-permute-start.22) | collective-permute-done | bytes 196640 | tf_op jit(solution)/shard_map/ppermute | solution.py:160
  91.3 3.7 %collective-permute-done.24 = bf16[64,1536]{1,0:T(8,128)(2,1)S(1)} collective-permute-done((bf16[64,1536]{1,0:T(8,128)(2,1)S(1)}, bf16[64,1536]{1,0:T(8,128)(2,1)S(1)}, u32[]{:S(2)}, u32[]{:S(2)}) %collective-permute-start.24) | collective-permute-done | bytes 196640 | tf_op jit(solution)/shard_map/ppermute | solution.py:160
  95.0 1.4 collective-permute-done.23
  96.7 1.1 collective-permute-done.25
  98.1 1.7 %collective-permute-start.28 = (bf16[64,1536]{1,0:T(8,128)(2,1)S(1)}, bf16[64,1536]{1,0:T(8,128)(2,1)S(1)}, u32[]{:S(2)}, u32[]{:S(2)}) collective-permute-start(bf16[64,1536]{1,0:T(8,128)(2,1)S(1)} %add_convert_fusion), channel_id=1, source_target_pairs={{0,24},{8,16},{16,8},{24,0},{1,25},{9,17},{17,9},{25,1},{2,26},{10... | collective-permute-start | bytes 589832 | tf_op jit(solution)/shard_map/ppermute | solution.py:160
  99.8 1.2 collective-permute-start.27
  101.6 5.2 %collective-permute-done.28 = bf16[64,1536]{1,0:T(8,128)(2,1)S(1)} collective-permute-done((bf16[64,1536]{1,0:T(8,128)(2,1)S(1)}, bf16[64,1536]{1,0:T(8,128)(2,1)S(1)}, u32[]{:S(2)}, u32[]{:S(2)}) %collective-permute-start.28) | collective-permute-done | bytes 196640 | tf_op jit(solution)/shard_map/ppermute | solution.py:160
  106.8 3.4 %collective-permute-done.27 = bf16[64,1536]{1,0:T(8,128)(2,1)S(1)} collective-permute-done((bf16[64,1536]{1,0:T(8,128)(2,1)S(1)}, bf16[64,1536]{1,0:T(8,128)(2,1)S(1)}, u32[]{:S(2)}, u32[]{:S(2)}) %collective-permute-start.27) | collective-permute-done | bytes 196640 | tf_op jit(solution)/shard_map/ppermute | solution.py:160
  110.3 6.4 %convolution_convert_fusion = bf16[256,3072]{1,0:T(8,128)(2,1)S(1)} fusion(bf16[1536,3072]{1,0:T(8,128)(2,1)} %param.16, bf16[64,1536]{1,0:T(8,128)(2,1)S(1)} %collective-permute-done.28, bf16[64,1536]{1,0:T(8,128)(2,1)S(1)} %collective-permute-done.27, bf16[64,1536]{1,0:T(8,128)(2,1)S(1)} %collective-permute-done.26, bf16[64,1536]{1,0:T(8,128)(2,1)S(1)} %add_convert_fusion), kind=kOutput, calls=%fused_computation.1 | convolution fusion | flops 2419851264 | bytes 11796480 | tf_op jit(solution)/shard_map/dot_general | solution.py:202
  116.8 3.4 %collective-permute-done.29 = bf16[256,3072]{1,0:T(8,128)(2,1)S(1)} collective-permute-done((bf16[256,3072]{1,0:T(8,128)(2,1)S(1)}, bf16[256,3072]{1,0:T(8,128)(2,1)S(1)}, u32[]{:S(2)}, u32[]{:S(2)}) %collective-permute-start.29) | collective-permute-done | bytes 1572896 | tf_op jit(solution)/shard_map/ppermute | solution.py:160
  120.2 3.1 %convolution_convert_fusion.1 = bf16[256,1536]{1,0:T(8,128)(2,1)S(1)} fusion(bf16[3072,1536]{1,0:T(8,128)(2,1)S(1)} %bitcast.54, bf16[256,3072]{1,0:T(8,128)(2,1)S(1)} %collective-permute-done.29, bf16[256,3072]{1,0:T(8,128)(2,1)S(1)} %convolution_convert_fusion), kind=kOutput, calls=%fused_computation.10 | convolution fusion | flops 2425749504 | bytes 13369344 | tf_op jit(solution)/shard_map/dot_general | solution.py:202
  123.4 1.5 %collective-permute-start.30 = (bf16[64,1536]{1,0:T(8,128)(2,1)S(1)}, bf16[64,1536]{1,0:T(8,128)(2,1)S(1)}, u32[]{:S(2)}, u32[]{:S(2)}) collective-permute-start(bf16[64,1536]{1,0:T(8,128)(2,1)S(1)} %get-tuple-element.18), channel_id=1, source_target_pairs={{0,8},{8,0},{16,24},{24,16},{1,9},{9,1},{17,25},{25,17},{2,10},{10... | collective-permute-start | bytes 589832 | tf_op jit(solution)/shard_map/ppermute | solution.py:160
  124.9 1.4 %collective-permute-start.32 = (bf16[64,1536]{1,0:T(8,128)(2,1)S(1)}, bf16[64,1536]{1,0:T(8,128)(2,1)S(1)}, u32[]{:S(2)}, u32[]{:S(2)}) collective-permute-start(bf16[64,1536]{1,0:T(8,128)(2,1)S(1)} %get-tuple-element.19), channel_id=1, source_target_pairs={{0,24},{8,16},{16,8},{24,0},{1,25},{9,17},{17,9},{25,1},{2,26},{10... | collective-permute-start | bytes 589832 | tf_op jit(solution)/shard_map/ppermute | solution.py:160
  127.0 4.3 %collective-permute-done.30 = bf16[64,1536]{1,0:T(8,128)(2,1)S(1)} collective-permute-done((bf16[64,1536]{1,0:T(8,128)(2,1)S(1)}, bf16[64,1536]{1,0:T(8,128)(2,1)S(1)}, u32[]{:S(2)}, u32[]{:S(2)}) %collective-permute-start.30) | collective-permute-done | bytes 196640 | tf_op jit(solution)/shard_map/ppermute | solution.py:160
  131.2 4.3 %collective-permute-done.32 = bf16[64,1536]{1,0:T(8,128)(2,1)S(1)} collective-permute-done((bf16[64,1536]{1,0:T(8,128)(2,1)S(1)}, bf16[64,1536]{1,0:T(8,128)(2,1)S(1)}, u32[]{:S(2)}, u32[]{:S(2)}) %collective-permute-start.32) | collective-permute-done | bytes 196640 | tf_op jit(solution)/shard_map/ppermute | solution.py:160
  135.5 1.4 collective-permute-done.31
  (88 shorter events, 18.9 us)
Async XLA Ops:
  0.0 2.0 %copy-start = (bf16[3072,576]{0,1:T(8,128)(2,1)S(1)}, bf16[3072,576]{0,1:T(8,128)(2,1)}, u32[]{:S(2)}) copy-start(bf16[3072,576]{0,1:T(8,128)(2,1)} %param.11) | copy-start | bytes 10616836
  0.0 3.5 %copy-start.5 = (bf16[64,1536]{1,0:T(8,128)(2,1)S(1)}, bf16[64,1536]{1,0:T(8,128)(2,1)}, u32[]{:S(2)}) copy-start(bf16[64,1536]{1,0:T(8,128)(2,1)} %param.9) | copy-start | bytes 589828
  3.0 1.3 collective-permute-start
  4.3 3.2 %collective-permute-start.5 = (f32[2,64]{1,0:T(2,128)}, f32[2,64]{1,0:T(2,128)}, u32[]{:S(2)}, u32[]{:S(2)}) collective-permute-start(f32[2,64]{1,0:T(2,128)} %pad_maximum_fusion.4), channel_id=1, source_target_pairs={{0,1},{1,0},{2,3},{3,2},{4,5},{5,4},{6,7},{7,6},{8,9},{9,8},{10,11... | collective-permute-start | bytes 1544 | tf_op jit(solution)/shard_map/ppermute | solution.py:160
  4.5 4.6 %collective-permute-start.1 = (f32[1152]{0:T(1024)S(1)}, f32[1152]{0:T(1024)S(1)}, u32[]{:S(2)}, u32[]{:S(2)}) collective-permute-start(f32[1152]{0:T(1024)S(1)} %pad_maximum_fusion.3), channel_id=1, source_target_pairs={{0,2},{2,0},{4,6},{6,4},{1,3},{3,1},{5,7},{7,5},{8,10},{10,8},{12,... | collective-permute-start | bytes 13832 | tf_op jit(solution)/shard_map/ppermute | solution.py:160
  9.2 4.8 %collective-permute-start.2 = (f32[2304]{0:T(1024)S(1)}, f32[2304]{0:T(1024)S(1)}, u32[]{:S(2)}, u32[]{:S(2)}) collective-permute-start(f32[2304]{0:T(1024)S(1)} %pad_maximum_fusion.2), channel_id=1, source_target_pairs={{0,4},{2,6},{4,0},{6,2},{1,5},{3,7},{5,1},{7,3},{8,12},{10,14},{12... | collective-permute-start | bytes 27656 | tf_op jit(solution)/shard_map/ppermute | solution.py:160
  13.9 3.8 %collective-permute-start.3 = (f32[4608]{0:T(1024)S(1)}, f32[4608]{0:T(1024)S(1)}, u32[]{:S(2)}, u32[]{:S(2)}) collective-permute-start(f32[4608]{0:T(1024)S(1)} %pad_maximum_fusion.1), channel_id=1, source_target_pairs={{0,8},{8,0},{16,24},{24,16},{1,9},{9,1},{17,25},{25,17},{2,10},{10... | collective-permute-start | bytes 55304 | tf_op jit(solution)/shard_map/ppermute | solution.py:160
  17.8 9.7 %collective-permute-start.4 = (f32[9216]{0:T(1024)S(1)}, f32[9216]{0:T(1024)S(1)}, u32[]{:S(2)}, u32[]{:S(2)}) collective-permute-start(f32[9216]{0:T(1024)S(1)} %pad_maximum_fusion), channel_id=1, source_target_pairs={{0,16},{8,24},{16,0},{24,8},{1,17},{9,25},{17,1},{25,9},{2,18},{10... | collective-permute-start | bytes 110600 | tf_op jit(solution)/shard_map/ppermute | solution.py:160
  21.5 18.3 %collective-permute-start.11 = (bf16[64,1536]{1,0:T(8,128)(2,1)}, bf16[64,1536]{1,0:T(8,128)(2,1)}, u32[]{:S(2)}, u32[]{:S(2)}) collective-permute-start(bf16[64,1536]{1,0:T(8,128)(2,1)} %fusion.22.refs_0_), channel_id=1, source_target_pairs={{0,4},{2,6},{4,0},{6,2},{1,5},{3,7},{5,1},{7,3},{8,12},{10,14},{12... | collective-permute-start | bytes 589832 | tf_op jit(solution)/shard_map/ppermute | solution.py:160
  24.1 8.5 %collective-permute-start.8 = (bf16[64,1536]{1,0:T(8,128)(2,1)}, bf16[64,1536]{1,0:T(8,128)(2,1)}, u32[]{:S(2)}, u32[]{:S(2)}) collective-permute-start(bf16[64,1536]{1,0:T(8,128)(2,1)} %fusion.22.refs_0_), channel_id=1, source_target_pairs={{0,24},{8,16},{16,8},{24,0},{1,25},{9,17},{17,9},{25,1},{2,26},{10... | collective-permute-start | bytes 589832 | tf_op jit(solution)/shard_map/ppermute | solution.py:160
  25.5 7.6 %collective-permute-start.7 = (bf16[64,1536]{1,0:T(8,128)(2,1)}, bf16[64,1536]{1,0:T(8,128)(2,1)}, u32[]{:S(2)}, u32[]{:S(2)}) collective-permute-start(bf16[64,1536]{1,0:T(8,128)(2,1)} %fusion.22.refs_0_), channel_id=1, source_target_pairs={{0,16},{8,24},{16,0},{24,8},{1,17},{9,25},{17,1},{25,9},{2,18},{10... | collective-permute-start | bytes 589832 | tf_op jit(solution)/shard_map/ppermute | solution.py:160
  27.0 6.0 %collective-permute-start.6 = (bf16[64,1536]{1,0:T(8,128)(2,1)}, bf16[64,1536]{1,0:T(8,128)(2,1)}, u32[]{:S(2)}, u32[]{:S(2)}) collective-permute-start(bf16[64,1536]{1,0:T(8,128)(2,1)} %fusion.22.refs_0_), channel_id=1, source_target_pairs={{0,8},{8,0},{16,24},{24,16},{1,9},{9,1},{17,25},{25,17},{2,10},{10... | collective-permute-start | bytes 589832 | tf_op jit(solution)/shard_map/ppermute | solution.py:160
  33.0 3.0 %copy-start.1 = (bf16[1536,3,768]{2,0,1:T(8,128)(2,1)S(1)}, bf16[1536,3,768]{2,0,1:T(8,128)(2,1)}, u32[]{:S(2)}) copy-start(bf16[1536,3,768]{2,0,1:T(8,128)(2,1)} %param.12) | copy-start | bytes 21233668
  36.1 19.6 %copy-start.2 = (bf16[1536,3,768]{2,0,1:T(8,128)(2,1)S(1)}, bf16[1536,3,768]{2,0,1:T(8,128)(2,1)}, u32[]{:S(2)}) copy-start(bf16[1536,3,768]{2,0,1:T(8,128)(2,1)} %param.12) | copy-start | bytes 21233668
  39.7 24.4 %collective-permute-start.9 = (bf16[256,1152]{1,0:T(8,128)(2,1)S(1)}, bf16[256,1152]{1,0:T(8,128)(2,1)S(1)}, u32[]{:S(2)}, u32[]{:S(2)}) collective-permute-start(bf16[256,1152]{1,0:T(8,128)(2,1)S(1)} %projected.7), channel_id=1, source_target_pairs={{0,1},{1,0},{2,3},{3,2},{4,5},{5,4},{6,7},{7,6},{8,9},{9,8},{10,11... | collective-permute-start | bytes 1769480 | tf_op jit(solution)/shard_map/ppermute | solution.py:160
  39.8 7.5 %collective-permute-start.16 = (bf16[64,1536]{1,0:T(8,128)(2,1)}, bf16[64,1536]{1,0:T(8,128)(2,1)S(1)}, u32[]{:S(2)}, u32[]{:S(2)}) collective-permute-start(bf16[64,1536]{1,0:T(8,128)(2,1)} %collective-permute-done.11.refs_0_), channel_id=1, source_target_pairs={{0,2},{2,0},{4,6},{6,4},{1,3},{3,1},{5,7},{7,5},{8,10},{10,8},{12,... | collective-permute-start | bytes 589832 | tf_op jit(solution)/shard_map/ppermute | solution.py:160
  41.5 8.9 %collective-permute-start.14 = (bf16[64,1536]{1,0:T(8,128)(2,1)}, bf16[64,1536]{1,0:T(8,128)(2,1)S(1)}, u32[]{:S(2)}, u32[]{:S(2)}) collective-permute-start(bf16[64,1536]{1,0:T(8,128)(2,1)} %collective-permute-done.11.refs_0_), channel_id=1, source_target_pairs={{0,24},{8,16},{16,8},{24,0},{1,25},{9,17},{17,9},{25,1},{2,26},{10... | collective-permute-start | bytes 589832 | tf_op jit(solution)/shard_map/ppermute | solution.py:160
  43.0 11.6 %collective-permute-start.13 = (bf16[64,1536]{1,0:T(8,128)(2,1)}, bf16[64,1536]{1,0:T(8,128)(2,1)S(1)}, u32[]{:S(2)}, u32[]{:S(2)}) collective-permute-start(bf16[64,1536]{1,0:T(8,128)(2,1)} %collective-permute-done.11.refs_0_), channel_id=1, source_target_pairs={{0,16},{8,24},{16,0},{24,8},{1,17},{9,25},{17,1},{25,9},{2,18},{10... | collective-permute-start | bytes 589832 | tf_op jit(solution)/shard_map/ppermute | solution.py:160
  44.0 15.2 %collective-permute-start.12 = (bf16[64,1536]{1,0:T(8,128)(2,1)}, bf16[64,1536]{1,0:T(8,128)(2,1)S(1)}, u32[]{:S(2)}, u32[]{:S(2)}) collective-permute-start(bf16[64,1536]{1,0:T(8,128)(2,1)} %collective-permute-done.11.refs_0_), channel_id=1, source_target_pairs={{0,8},{8,0},{16,24},{24,16},{1,9},{9,1},{17,25},{25,17},{2,10},{10... | collective-permute-start | bytes 589832 | tf_op jit(solution)/shard_map/ppermute | solution.py:160
  47.3 14.5 %collective-permute-start.19 = (bf16[64,1536]{1,0:T(8,128)(2,1)S(1)}, bf16[64,1536]{1,0:T(8,128)(2,1)S(1)}, u32[]{:S(2)}, u32[]{:S(2)}) collective-permute-start(bf16[64,1536]{1,0:T(8,128)(2,1)S(1)} %collective-permute-done.16.refs_0_), channel_id=1, source_target_pairs={{0,24},{8,16},{16,8},{24,0},{1,25},{9,17},{17,9},{25,1},{2,26},{10... | collective-permute-start | bytes 589832 | tf_op jit(solution)/shard_map/ppermute | solution.py:160
  50.3 11.8 %collective-permute-start.18 = (bf16[64,1536]{1,0:T(8,128)(2,1)S(1)}, bf16[64,1536]{1,0:T(8,128)(2,1)S(1)}, u32[]{:S(2)}, u32[]{:S(2)}) collective-permute-start(bf16[64,1536]{1,0:T(8,128)(2,1)S(1)} %collective-permute-done.16.refs_0_), channel_id=1, source_target_pairs={{0,16},{8,24},{16,0},{24,8},{1,17},{9,25},{17,1},{25,9},{2,18},{10... | collective-permute-start | bytes 589832 | tf_op jit(solution)/shard_map/ppermute | solution.py:160
  54.6 7.5 %collective-permute-start.17 = (bf16[64,1536]{1,0:T(8,128)(2,1)S(1)}, bf16[64,1536]{1,0:T(8,128)(2,1)S(1)}, u32[]{:S(2)}, u32[]{:S(2)}) collective-permute-start(bf16[64,1536]{1,0:T(8,128)(2,1)S(1)} %collective-permute-done.16.refs_0_), channel_id=1, source_target_pairs={{0,8},{8,0},{16,24},{24,16},{1,9},{9,1},{17,25},{25,17},{2,10},{10... | collective-permute-start | bytes 589832 | tf_op jit(solution)/shard_map/ppermute | solution.py:160
  61.7 2.4 %copy-start.3 = (f32[128]{0:T(128)S(1)}, f32[128]{0:T(128)}, u32[]{:S(2)}) copy-start(f32[128]{0:T(128)} %param.13) | copy-start | bytes 1540
  61.7 2.4 %copy-start.4 = (f32[128]{0:T(128)S(1)}, f32[128]{0:T(128)}, u32[]{:S(2)}) copy-start(f32[128]{0:T(128)} %param.14) | copy-start | bytes 1540
  61.7 7.5 %collective-permute-start.15 = (bf16[256,768]{1,0:T(8,128)(2,1)S(1)}, bf16[256,768]{1,0:T(8,128)(2,1)S(1)}, u32[]{:S(2)}, u32[]{:S(2)}) collective-permute-start(bf16[256,768]{1,0:T(8,128)(2,1)S(1)} %projected.9), channel_id=1, source_target_pairs={{0,1},{1,0},{2,3},{3,2},{4,5},{5,4},{6,7},{7,6},{8,9},{9,8},{10,11... | collective-permute-start | bytes 1179656 | tf_op jit(solution)/shard_map/ppermute | solution.py:160
  63.8 5.7 %collective-permute-start.20 = (bf16[256,768]{1,0:T(8,128)(2,1)S(1)}, bf16[256,768]{1,0:T(8,128)(2,1)S(1)}, u32[]{:S(2)}, u32[]{:S(2)}) collective-permute-start(bf16[256,768]{1,0:T(8,128)(2,1)S(1)} %projected.11), channel_id=1, source_target_pairs={{0,1},{1,0},{2,3},{3,2},{4,5},{5,4},{6,7},{7,6},{8,9},{9,8},{10,11... | collective-permute-start | bytes 1179656 | tf_op jit(solution)/shard_map/ppermute | solution.py:160
  64.4 11.4 %collective-permute-start.10 = (bf16[256,768]{1,0:T(8,128)(2,1)S(1)}, bf16[256,768]{1,0:T(8,128)(2,1)S(1)}, u32[]{:S(2)}, u32[]{:S(2)}) collective-permute-start(bf16[256,768]{1,0:T(8,128)(2,1)S(1)} %get-tuple-element.8.refs_1_), channel_id=1, source_target_pairs={{0,2},{2,0},{4,6},{6,4},{1,3},{3,1},{5,7},{7,5},{8,10},{10,8},{12,... | collective-permute-start | bytes 1179656 | tf_op jit(solution)/shard_map/ppermute | solution.py:160
  78.2 1.8 %collective-permute-start.21 = (bf16[256,384]{1,0:T(8,128)(2,1)}, bf16[256,384]{1,0:T(8,128)(2,1)}, u32[]{:S(2)}, u32[]{:S(2)}) collective-permute-start(bf16[256,384]{1,0:T(8,128)(2,1)} %attention.1), channel_id=1, source_target_pairs={{0,1},{1,0},{2,3},{3,2},{4,5},{5,4},{6,7},{7,6},{8,9},{9,8},{10,11... | collective-permute-start | bytes 589832 | tf_op jit(solution)/shard_map/ppermute | solution.py:160
  78.2 18.2 %copy-start.6 = (bf16[64,1536]{1,0:T(8,128)(2,1)S(1)}, bf16[64,1536]{1,0:T(8,128)(2,1)}, u32[]{:S(2)}) copy-start(bf16[64,1536]{1,0:T(8,128)(2,1)} %param.9) | copy-start | bytes 589828
  78.2 18.2 %copy-start.8 = (f32[1536]{0:T(1024)S(1)}, f32[1536]{0:T(1024)}, u32[]{:S(2)}) copy-start(f32[1536]{0:T(1024)} %get-tuple-element.15) | copy-start | bytes 18436
  81.0 16.9 %copy-start.7 = (f32[1536]{0:T(1024)S(1)}, f32[1536]{0:T(1024)}, u32[]{:S(2)}) copy-start(f32[1536]{0:T(1024)} %get-tuple-element.16) | copy-start | bytes 18436
  83.5 7.8 %collective-permute-start.22 = (bf16[64,1536]{1,0:T(8,128)(2,1)S(1)}, bf16[64,1536]{1,0:T(8,128)(2,1)S(1)}, u32[]{:S(2)}, u32[]{:S(2)}) collective-permute-start(bf16[64,1536]{1,0:T(8,128)(2,1)S(1)} %get-tuple-element.21), channel_id=1, source_target_pairs={{0,8},{8,0},{16,24},{24,16},{1,9},{9,1},{17,25},{25,17},{2,10},{10... | collective-permute-start | bytes 589832 | tf_op jit(solution)/shard_map/ppermute | solution.py:160
  84.5 10.6 %collective-permute-start.24 = (bf16[64,1536]{1,0:T(8,128)(2,1)S(1)}, bf16[64,1536]{1,0:T(8,128)(2,1)S(1)}, u32[]{:S(2)}, u32[]{:S(2)}) collective-permute-start(bf16[64,1536]{1,0:T(8,128)(2,1)S(1)} %get-tuple-element.22), channel_id=1, source_target_pairs={{0,24},{8,16},{16,8},{24,0},{1,25},{9,17},{17,9},{25,1},{2,26},{10... | collective-permute-start | bytes 589832 | tf_op jit(solution)/shard_map/ppermute | solution.py:160
  85.8 10.6 %collective-permute-start.23 = (bf16[64,1536]{1,0:T(8,128)(2,1)S(1)}, bf16[64,1536]{1,0:T(8,128)(2,1)S(1)}, u32[]{:S(2)}, u32[]{:S(2)}) collective-permute-start(bf16[64,1536]{1,0:T(8,128)(2,1)S(1)} %get-tuple-element.23), channel_id=1, source_target_pairs={{0,16},{8,24},{16,0},{24,8},{1,17},{9,25},{17,1},{25,9},{2,18},{10... | collective-permute-start | bytes 589832 | tf_op jit(solution)/shard_map/ppermute | solution.py:160
  96.7 1.2 collective-permute-start.25
  97.9 22.3 %slice-start = ((s8[9437184]{0:T(1024)(128)(4,1)}), s8[4194304]{0:T(1024)(128)(4,1)S(1)}, s32[]{:S(2)}) async-start(s8[9437184]{0:T(1024)(128)(4,1)} %bitcast.53), calls=%async_computation | async-start | bytes 8388608
  98.1 22.1 %slice-start.1 = ((s8[9437184]{0:T(1024)(128)(4,1)}), s8[4194304]{0:T(1024)(128)(4,1)S(1)}, s32[]{:S(2)}) async-start(s8[9437184]{0:T(1024)(128)(4,1)} %bitcast.53), calls=%async_computation.1 | async-start | bytes 8388608
  98.1 22.1 %slice-start.2 = ((s8[9437184]{0:T(1024)(128)(4,1)}), s8[1048576]{0:T(1024)(128)(4,1)S(1)}, s32[]{:S(2)}) async-start(s8[9437184]{0:T(1024)(128)(4,1)} %bitcast.53), calls=%async_computation.2 | async-start | bytes 2097152
  98.1 8.7 %collective-permute-start.28 = (bf16[64,1536]{1,0:T(8,128)(2,1)S(1)}, bf16[64,1536]{1,0:T(8,128)(2,1)S(1)}, u32[]{:S(2)}, u32[]{:S(2)}) collective-permute-start(bf16[64,1536]{1,0:T(8,128)(2,1)S(1)} %add_convert_fusion), channel_id=1, source_target_pairs={{0,24},{8,16},{16,8},{24,0},{1,25},{9,17},{17,9},{25,1},{2,26},{10... | collective-permute-start | bytes 589832 | tf_op jit(solution)/shard_map/ppermute | solution.py:160
  99.8 10.5 %collective-permute-start.27 = (bf16[64,1536]{1,0:T(8,128)(2,1)S(1)}, bf16[64,1536]{1,0:T(8,128)(2,1)S(1)}, u32[]{:S(2)}, u32[]{:S(2)}) collective-permute-start(bf16[64,1536]{1,0:T(8,128)(2,1)S(1)} %add_convert_fusion), channel_id=1, source_target_pairs={{0,16},{8,24},{16,0},{24,8},{1,17},{9,25},{17,1},{25,9},{2,18},{10... | collective-permute-start | bytes 589832 | tf_op jit(solution)/shard_map/ppermute | solution.py:160
  101.0 9.3 %collective-permute-start.26 = (bf16[64,1536]{1,0:T(8,128)(2,1)S(1)}, bf16[64,1536]{1,0:T(8,128)(2,1)S(1)}, u32[]{:S(2)}, u32[]{:S(2)}) collective-permute-start(bf16[64,1536]{1,0:T(8,128)(2,1)S(1)} %add_convert_fusion), channel_id=1, source_target_pairs={{0,8},{8,0},{16,24},{24,16},{1,9},{9,1},{17,25},{25,17},{2,10},{10... | collective-permute-start | bytes 589832 | tf_op jit(solution)/shard_map/ppermute | solution.py:160
  116.7 3.5 %collective-permute-start.29 = (bf16[256,3072]{1,0:T(8,128)(2,1)S(1)}, bf16[256,3072]{1,0:T(8,128)(2,1)S(1)}, u32[]{:S(2)}, u32[]{:S(2)}) collective-permute-start(bf16[256,3072]{1,0:T(8,128)(2,1)S(1)} %convolution_convert_fusion), channel_id=1, source_target_pairs={{0,1},{1,0},{2,3},{3,2},{4,5},{5,4},{6,7},{7,6},{8,9},{9,8},{10,11... | collective-permute-start | bytes 4718600 | tf_op jit(solution)/shard_map/ppermute | solution.py:160
  123.4 7.8 %collective-permute-start.30 = (bf16[64,1536]{1,0:T(8,128)(2,1)S(1)}, bf16[64,1536]{1,0:T(8,128)(2,1)S(1)}, u32[]{:S(2)}, u32[]{:S(2)}) collective-permute-start(bf16[64,1536]{1,0:T(8,128)(2,1)S(1)} %get-tuple-element.18), channel_id=1, source_target_pairs={{0,8},{8,0},{16,24},{24,16},{1,9},{9,1},{17,25},{25,17},{2,10},{10... | collective-permute-start | bytes 589832 | tf_op jit(solution)/shard_map/ppermute | solution.py:160
  124.9 10.6 %collective-permute-start.32 = (bf16[64,1536]{1,0:T(8,128)(2,1)S(1)}, bf16[64,1536]{1,0:T(8,128)(2,1)S(1)}, u32[]{:S(2)}, u32[]{:S(2)}) collective-permute-start(bf16[64,1536]{1,0:T(8,128)(2,1)S(1)} %get-tuple-element.19), channel_id=1, source_target_pairs={{0,24},{8,16},{16,8},{24,0},{1,25},{9,17},{17,9},{25,1},{2,26},{10... | collective-permute-start | bytes 589832 | tf_op jit(solution)/shard_map/ppermute | solution.py:160
  126.2 10.6 %collective-permute-start.31 = (bf16[64,1536]{1,0:T(8,128)(2,1)S(1)}, bf16[64,1536]{1,0:T(8,128)(2,1)S(1)}, u32[]{:S(2)}, u32[]{:S(2)}) collective-permute-start(bf16[64,1536]{1,0:T(8,128)(2,1)S(1)} %get-tuple-element.20), channel_id=1, source_target_pairs={{0,16},{8,24},{16,0},{24,8},{1,17},{9,25},{17,1},{25,9},{2,18},{10... | collective-permute-start | bytes 589832 | tf_op jit(solution)/shard_map/ppermute | solution.py:160

commit v3 on v2

--- a/solution.py
+++ b/solution.py
@@ -152,7 +152,8 @@
     return mixed + own_mod[5] * feedforward
 
 
-VMEM_BYTES = 48 * 1024 * 1024
+VMEM_BYTES = 1024 * 1024
+NO_COST = pl.CostEstimate(flops=0, bytes_accessed=0, transcendentals=0)
 
 
 def permuted(values, axis, distance):
@@ -168,29 +169,114 @@
     return [blocks[0]] + [permuted(blocks[k], axis, k) for k in range(1, len(blocks))]
 
 
-def doubled(piece, axis):
-    position = lax.axis_index(axis)
-    distance = 1
-    while distance < lax.axis_size(axis):
-        other = permuted(piece, axis, distance)
-        upper = (position & distance) != 0
-        piece = jnp.concatenate(
-            [jnp.where(upper, other, piece), jnp.where(upper, piece, other)], axis=0
-        )
-        distance *= 2
-    return piece
-
-
-def modulation_rows(cond, mod_weight, features, width):
-    activated = jax.nn.silu(cond.astype(jnp.float32)).astype(jnp.bfloat16)
-    piece = jnp.dot(activated[None, :], mod_weight, preferred_element_type=jnp.float32)[0]
-    for axis in ("tensor", "blk", "ulysses"):
-        piece = doubled(piece, axis)
-    rows = piece.reshape(6, features)
-    return lax.dynamic_slice_in_dim(rows, lax.axis_index("tensor") * width, width, 1)
+def after_specs(after):
+    return [pl.BlockSpec((16, 128), lambda j: (0, 0)) for _ in after]
+
+
+def merge_kernel(axis, distance, own_ref, other_ref, *refs):
+    out_ref = refs[-1]
+    rows = own_ref.shape[0]
+    upper = (lax.axis_index(axis) & distance) != 0
+    out_ref[:rows, :] = jnp.where(upper, other_ref[...], own_ref[...])
+    out_ref[rows:, :] = jnp.where(upper, own_ref[...], other_ref[...])
+
+
+def doubled_once(piece, axis, distance, after):
+    other = permuted(piece, axis, distance)
+    rows, length = piece.shape
+    block = pl.BlockSpec((rows, length), lambda j: (0, 0))
+    return pl.pallas_call(
+        lambda *refs: merge_kernel(axis, distance, *refs),
+        grid=(1,),
+        in_specs=[block, block] + after_specs(after),
+        out_specs=pl.BlockSpec((2 * rows, length), lambda j: (0, 0)),
+        out_shape=jax.ShapeDtypeStruct((2 * rows, length), piece.dtype),
+        compiler_params=pltpu.CompilerParams(vmem_limit_bytes=VMEM_BYTES),
+        cost_estimate=NO_COST,
+        name="merged",
+    )(piece, other, *after)
+
+
+def assemble_kernel(pieces_ref, out_ref):
+    length = pieces_ref.shape[1]
+    width = out_ref.shape[1]
+    vectors = out_ref.shape[0]
+    halves = pieces_ref.shape[0] * length // (vectors * width)
+    for half in range(halves):
+
+        @pl.when(lax.axis_index("tensor") == half)
+        def _(half=half):
+            for vector in range(vectors):
+                at = (vector * halves + half) * width
+                end = at + width
+                parts = []
+                while at < end:
+                    row, low = divmod(at, length)
+                    high = min(length, low + end - at)
+                    parts.append(pieces_ref[row : row + 1, low:high])
+                    at += high - low
+                out_ref[vector : vector + 1, :] = jnp.concatenate(parts, axis=1)
+
+
+def assembled(pieces, width):
+    return pl.pallas_call(
+        assemble_kernel,
+        out_shape=jax.ShapeDtypeStruct((6, width), jnp.float32),
+        compiler_params=pltpu.CompilerParams(vmem_limit_bytes=VMEM_BYTES),
+        cost_estimate=NO_COST,
+        name="assembled",
+    )(pieces)
+
+
+def row_sums_kernel(values_ref, out_ref, copy_ref):
+    values = values_ref[...].astype(jnp.float32)
+    lane = lax.broadcasted_iota(jnp.int32, out_ref.shape, 1)
+    out_ref[...] = jnp.where(
+        lane < out_ref.shape[1] // 2,
+        jnp.sum(values, axis=-1, keepdims=True),
+        jnp.sum(values * values, axis=-1, keepdims=True),
+    )
+    copy_ref[...] = values_ref[...]
+
+
+def row_sums(values):
+    rows = values.shape[0]
+    return pl.pallas_call(
+        row_sums_kernel,
+        out_shape=[
+            jax.ShapeDtypeStruct((rows, 128), jnp.float32),
+            jax.ShapeDtypeStruct(values.shape, values.dtype),
+        ],
+        compiler_params=pltpu.CompilerParams(vmem_limit_bytes=VMEM_BYTES * 2),
+        cost_estimate=NO_COST,
+        name="row_sums",
+    )(values)
+
+
+def centered(values, own, arrived, features):
+    total = own + arrived
+    average = total[:, :1] / features
+    variance = total[:, total.shape[1] // 2 :][:, :1] / features - average * average
+    return (values - average) * lax.rsqrt(variance + 1e-06)
+
+
+def standardize_kernel(features, values_ref, own_ref, arrived_ref, out_ref):
+    values = values_ref[...].astype(jnp.float32)
+    out_ref[...] = centered(values, own_ref[...], arrived_ref[...], features).astype(jnp.bfloat16)
 
 
 def standardized(values, features):
+    own, values = row_sums(values)
+    return pl.pallas_call(
+        lambda *refs: standardize_kernel(features, *refs),
+        out_shape=jax.ShapeDtypeStruct(values.shape, jnp.bfloat16),
+        compiler_params=pltpu.CompilerParams(vmem_limit_bytes=VMEM_BYTES * 2),
+        cost_estimate=NO_COST,
+        name="standardized",
+    )(values, own, permuted(own, "tensor", 1))
+
+
+def normalized(values, features):
     sums = jnp.stack([jnp.sum(values, axis=-1), jnp.sum(values * values, axis=-1)])
     sums = sums + permuted(sums, "tensor", 1)
     average = sums[0][:, None] / features
@@ -209,8 +295,9 @@
     return total
 
 
-def project_kernel(pick, *refs):
-    *block_refs, shift_ref, scale_ref, weight_ref, out_ref, normed_ref = refs
+def project_kernel(count, *refs):
+    block_refs, (shift_ref, scale_ref, weight_ref) = refs[:count], refs[count : count + 3]
+    out_ref, normed_ref = refs[-2:]
 
     @pl.when(pl.program_id(0) == 0)
     def _():
@@ -225,31 +312,29 @@
     ).astype(jnp.bfloat16)
 
 
-def projected(blocks, shift_row, scale_row, weights, first, half, pick):
+def projected(blocks, shift_row, scale_row, weights, first, half, other, after=()):
     rows, width = blocks[0].shape
     all_rows = rows * len(blocks)
     count = weights.shape[0] - first
-    whole = lambda shape: pl.BlockSpec(shape, lambda j, pick: (0, 0))
-    return pl.pallas_call(
-        project_kernel,
-        grid_spec=pltpu.PrefetchScalarGridSpec(
-            num_scalar_prefetch=1,
-            grid=(count,),
-            in_specs=[whole((rows, width)) for _ in blocks]
-            + [whole((1, width)), whole((1, width))]
-            + [pl.BlockSpec((1, width, half), lambda j, pick: (j + first, 0, pick[0]))],
-            out_specs=pl.BlockSpec((all_rows, half), lambda j, pick: (0, j)),
-            scratch_shapes=[pltpu.VMEM((all_rows, width), jnp.bfloat16)],
-        ),
+
+    def columns(j):
+        position = lax.axis_index("tensor")
+        return (j + first, 0, 1 - position if other else position)
+
+    whole = lambda shape: pl.BlockSpec(shape, lambda j: (0, 0))
+    return pl.pallas_call(
+        lambda *refs: project_kernel(len(blocks), *refs),
+        grid=(count,),
+        in_specs=[whole((rows, width)) for _ in blocks]
+        + [whole((1, width)), whole((1, width)), pl.BlockSpec((1, width, half), columns)]
+        + after_specs(after),
+        out_specs=pl.BlockSpec((all_rows, half), lambda j: (0, j)),
         out_shape=jax.ShapeDtypeStruct((all_rows, count * half), jnp.bfloat16),
-        compiler_params=pltpu.CompilerParams(vmem_limit_bytes=VMEM_BYTES // 2),
-        cost_estimate=pl.CostEstimate(
-            flops=2 * all_rows * width * count * half,
-            bytes_accessed=2 * width * count * half,
-            transcendentals=0,
-        ),
+        scratch_shapes=[pltpu.VMEM((all_rows, width), jnp.bfloat16)],
+        compiler_params=pltpu.CompilerParams(vmem_limit_bytes=VMEM_BYTES * 8),
+        cost_estimate=NO_COST,
         name="projected",
-    )(pick, *blocks, shift_row, scale_row, weights)
+    )(*blocks, shift_row, scale_row, weights, *after)
 
 
 def heads_kernel(count, head_size, own_ref, arrived_ref, q_gain_ref, k_gain_ref, *out_refs):
@@ -284,7 +369,7 @@
     return pl.pallas_call(
         lambda *refs: heads_kernel(count, head_size, *refs),
         out_shape=shapes,
-        compiler_params=pltpu.CompilerParams(vmem_limit_bytes=VMEM_BYTES // 4),
+        compiler_params=pltpu.CompilerParams(vmem_limit_bytes=VMEM_BYTES * 8),
         cost_estimate=pl.CostEstimate(
             flops=8 * rows * columns, bytes_accessed=6 * rows * columns, transcendentals=rows * 6
         ),
@@ -329,7 +414,7 @@
     return pl.pallas_call(
         lambda *refs: attention_kernel(head_size, *refs),
         out_shape=jax.ShapeDtypeStruct((rows, half), jnp.bfloat16),
-        compiler_params=pltpu.CompilerParams(vmem_limit_bytes=VMEM_BYTES),
+        compiler_params=pltpu.CompilerParams(vmem_limit_bytes=VMEM_BYTES * 12),
         cost_estimate=pl.CostEstimate(
             flops=4 * rows * keys * half,
             bytes_accessed=4 * keys * half,
@@ -339,37 +424,181 @@
     )(queries, *kv_parts)
 
 
+def row_blocks(values, out_refs):
+    rows = out_refs[0].shape[0]
+    for k, out_ref in enumerate(out_refs):
+        out_ref[...] = values[k * rows : (k + 1) * rows].astype(jnp.bfloat16)
+
+
+def out_kernel(own_ref, arrived_ref, own_weight_ref, other_weight_ref, *out_refs):
+    total = jnp.dot(own_ref[...], own_weight_ref[...], preferred_element_type=jnp.float32)
+    total = total + jnp.dot(
+        arrived_ref[...], other_weight_ref[...], preferred_element_type=jnp.float32
+    )
+    row_blocks(total, out_refs)
+
+
+def out_projected(own, arrived, weight, rows):
+    all_rows, half = own.shape
+    width = weight.shape[1]
+    tile = width // 3 if width % 384 == 0 else width
+    whole = pl.BlockSpec((all_rows, half), lambda j: (0, 0))
+    return pl.pallas_call(
+        out_kernel,
+        grid=(width // tile,),
+        in_specs=[
+            whole,
+            whole,
+            pl.BlockSpec((half, tile), lambda j: (lax.axis_index("tensor"), j)),
+            pl.BlockSpec((half, tile), lambda j: (1 - lax.axis_index("tensor"), j)),
+        ],
+        out_specs=[pl.BlockSpec((rows, tile), lambda j: (0, j))] * (all_rows // rows),
+        out_shape=[jax.ShapeDtypeStruct((rows, width), jnp.bfloat16)] * (all_rows // rows),
+        compiler_params=pltpu.CompilerParams(vmem_limit_bytes=VMEM_BYTES * 8),
+        cost_estimate=NO_COST,
+        name="out_projected",
+    )(own, arrived, weight, weight)
+
+
+def up_kernel(*refs):
+    *block_refs, weight_ref, out_ref, joined_ref = refs
+
+    @pl.when(pl.program_id(0) == 0)
+    def _():
+        rows = block_refs[0].shape[0]
+        for k, block_ref in enumerate(block_refs):
+            joined_ref[k * rows : (k + 1) * rows, :] = block_ref[...]
+
+    out_ref[...] = jnp.dot(
+        joined_ref[...], weight_ref[...], preferred_element_type=jnp.float32
+    ).astype(jnp.bfloat16)
+
+
+def up_projected(blocks, weight, part, parts):
+    rows, width = blocks[0].shape
+    all_rows = rows * len(blocks)
+    columns = weight.shape[1] // parts
+    tile = columns // 3 if columns % 384 == 0 else columns
+    first = part * columns // tile
+    return pl.pallas_call(
+        up_kernel,
+        grid=(columns // tile,),
+        in_specs=[pl.BlockSpec((rows, width), lambda j: (0, 0)) for _ in blocks]
+        + [pl.BlockSpec((width, tile), lambda j: (0, j + first))],
+        out_specs=pl.BlockSpec((all_rows, tile), lambda j: (0, j)),
+        out_shape=jax.ShapeDtypeStruct((all_rows, columns), jnp.bfloat16),
+        scratch_shapes=[pltpu.VMEM((all_rows, width), jnp.bfloat16)],
+        compiler_params=pltpu.CompilerParams(vmem_limit_bytes=VMEM_BYTES * 8),
+        cost_estimate=pl.CostEstimate(
+            flops=2 * all_rows * width * columns,
+            bytes_accessed=2 * width * columns,
+            transcendentals=0,
+        ),
+        name="up_projected",
+    )(*blocks, weight)
+
+
+def down_kernel(last, own_ref, arrived_ref, weight_ref, *refs):
+    step = pl.program_id(0)
+    out_refs, total_ref = refs[:-1], refs[-1]
+    hidden = own_ref[...].astype(jnp.float32) + arrived_ref[...].astype(jnp.float32)
+    activ = jax.nn.gelu(hidden, approximate=True).astype(jnp.bfloat16)
+    partial = jnp.dot(activ, weight_ref[...], preferred_element_type=jnp.float32)
+    if last:
+        before_ref, *out_refs = out_refs
+    else:
+        total_ref = out_refs[0]
+
+    @pl.when(step == 0)
+    def _():
+        total_ref[...] = partial + before_ref[...] if last else partial
+
+    @pl.when(step > 0)
+    def _():
+        total_ref[...] += partial
+
+    if last:
+
+        @pl.when(step == pl.num_programs(0) - 1)
+        def _():
+            row_blocks(total_ref[...], out_refs)
+
+
+def down_projected(own, arrived, weight, part, parts, before, rows):
+    all_rows, columns = own.shape
+    width = weight.shape[1]
+    tile = columns // 3 if columns % 384 == 0 else columns
+    first = part * columns // tile
+    last = before is not None
+    whole = pl.BlockSpec((all_rows, width), lambda j: (0, 0))
+    if last:
+        shapes = [jax.ShapeDtypeStruct((rows, width), jnp.bfloat16)] * (all_rows // rows)
+        out_specs = [pl.BlockSpec((rows, width), lambda j: (0, 0))] * (all_rows // rows)
+    else:
+        shapes = [jax.ShapeDtypeStruct((all_rows, width), jnp.float32)]
+        out_specs = [whole]
+    scratch = pltpu.VMEM((all_rows, width) if last else (8, 128), jnp.float32)
+    return pl.pallas_call(
+        lambda *refs: down_kernel(last, *refs),
+        grid=(columns // tile,),
+        in_specs=[
+            pl.BlockSpec((all_rows, tile), lambda j: (0, j)),
+            pl.BlockSpec((all_rows, tile), lambda j: (0, j)),
+            pl.BlockSpec((tile, width), lambda j: (j + first, 0)),
+        ]
+        + [whole] * last,
+        out_specs=out_specs,
+        out_shape=shapes,
+        scratch_shapes=[scratch],
+        compiler_params=pltpu.CompilerParams(vmem_limit_bytes=VMEM_BYTES * 12),
+        cost_estimate=pl.CostEstimate(
+            flops=2 * all_rows * width * columns,
+            bytes_accessed=2 * width * columns,
+            transcendentals=all_rows * columns,
+        ),
+        name="down_projected",
+    )(own, arrived, weight, *([before] * last))
+
+
 def on_pair(
     tokens, cond, mod_weight, qkv_weight, q_gain, k_gain, out_weight, up_weight, down_weight
 ):
-    tensor_pos = lax.axis_index("tensor")
+    stages = [
+        (axis, 1 << bit)
+        for axis in ("tensor", "blk", "ulysses")
+        for bit in range(lax.axis_size(axis).bit_length() - 1)
+    ]
     rows, width = tokens.shape
     features = width * lax.axis_size("tensor")
     head_size = q_gain.shape[0]
     half = qkv_weight.shape[2] // 2
     blocks_z = lax.axis_size("blk")
 
-    resid = tokens.astype(jnp.float32)
-    normal = standardized(resid, features).astype(jnp.bfloat16)
+    normal = standardized(tokens, features)
     remote = {0: normal}
     for k in range(2, blocks_z):
         remote[k] = permuted(remote[k - 1] if k % 2 else normal, "blk", 1 if k % 2 else k)
     chunks = [from_all(remote[k], "ulysses") for k in sorted(remote)]
 
-    own_mod = modulation_rows(cond, mod_weight, features, width)
+    activated = jax.nn.silu(cond.astype(jnp.float32)).astype(jnp.bfloat16)
+    pieces = jnp.dot(activated[None, :], mod_weight, preferred_element_type=jnp.float32)
+    after = {("blk", 1): [normal], ("blk", 2): chunks[0][1:3], ("ulysses", 1): chunks[0][3:]}
+    after[("ulysses", 2)] = [remote[k] for k in remote if k > 0 and k % 2 == 0]
+    for stage in stages:
+        pieces = doubled_once(pieces, *stage, after.get(stage, []))
+    own_mod = assembled(pieces, width)
     weights = jnp.moveaxis(qkv_weight, 1, 0)
-    pick_own = tensor_pos.reshape(1).astype(jnp.int32)
     shift_row, scale_row = own_mod[0:1], own_mod[1:2]
 
     queries, kv_parts = None, []
     for index, blocks in enumerate(chunks):
         first = 0 if index == 0 else 1
-        arrived = permuted(
-            projected(blocks, shift_row, scale_row, weights, first, half, 1 - pick_own),
-            "tensor",
-            1,
-        )
-        own = projected(blocks, shift_row, scale_row, weights, first, half, pick_own)
+        after = [kv_parts[-1]] if index == 2 else []
+        if index == len(chunks) - 1 and index > 0:
+            after = after + [kv_parts[1]]
+        common = (shift_row, scale_row, weights, first, half)
+        arrived = permuted(projected(blocks, *common, True, after), "tensor", 1)
+        own = projected(blocks, *common, False)
         outs = split_heads(own, arrived, q_gain, k_gain, 3 - first)
         kv_parts.append(outs[0])
         if index == 0:
@@ -378,29 +607,19 @@
                 kv_parts.append(permuted(outs[0], "blk", 1))
 
     context = attention(queries, kv_parts, head_size)
-    other = permuted(context, "tensor", 1)
-    context = jnp.concatenate(
-        [
-            jnp.where(tensor_pos == 0, context, other),
-            jnp.where(tensor_pos == 0, other, context),
-        ],
-        axis=1,
-    )
-
-    attended = reduced_rows(product(context, out_weight), rows)
-    mixed = resid + own_mod[2] * attended
-    normed_two = standardized(mixed, features) * (1.0 + own_mod[4]) + own_mod[3]
-    gathered_two = jnp.concatenate(from_all(normed_two.astype(jnp.bfloat16), "ulysses"), axis=0)
-    partial = product(gathered_two, up_weight)
-    hidden = added([partial, permuted(partial, "tensor", 1)])
-    activ = jax.nn.gelu(hidden, approximate=True).astype(jnp.bfloat16)
-    feedforward = reduced_rows(product(activ, down_weight), rows)
+    partial = out_projected(context, permuted(context, "tensor", 1), out_weight, rows)
+    attended = added(to_all(partial, "ulysses"))
+    mixed = tokens.astype(jnp.float32) + own_mod[2] * attended
+    normed_two = normalized(mixed, features) * (1.0 + own_mod[4]) + own_mod[3]
+    blocks = from_all(normed_two.astype(jnp.bfloat16), "ulysses")
+    first = up_projected(blocks, up_weight, 0, 2)
+    first_arrived = permuted(first, "tensor", 1)
+    second = up_projected(blocks, up_weight, 1, 2)
+    second_arrived = permuted(second, "tensor", 1)
+    before = down_projected(first, first_arrived, down_weight, 0, 2, None, rows)[0]
+    partial = down_projected(second, second_arrived, down_weight, 1, 2, before, rows)
+    feedforward = added(to_all(partial, "ulysses"))
     return mixed + own_mod[5] * feedforward
-
-
-def reduced_rows(partial, rows):
-    blocks = [partial[i : i + rows] for i in range(0, partial.shape[0], rows)]
-    return added(to_all(blocks, "ulysses"))
 
 
 def solution(mesh):

time: 138 us -> 121 us (0.88)
  matrix products: 13 us -> 1.01 us
  Pallas kernels: 18.7 us -> 25.7 us
  other arithmetic: 8.72 us -> 2.08 us
  local copies, waits for them, and re-layouts: 7.09 us -> 4.17 us
  starting transfers between devices: 36.6 us -> 34.2 us
    dot_general x4 -> x1, matrix products: 13 us -> 1.01 us  [on_pair(): jnp.dot(activated[None, :], mod_weight, preferred_element_type=jnp.float32)]
    pallas_call x6 -> x19, Pallas kernels: 15.6 us -> 23.2 us  [the longest x6 11.5 us: projected(): pl.pallas_call(lambda *refs: project_kernel(len(blocks), *refs), grid=(co...]
    concatenate x2 -> x0, local copies, waits for them, and re-layouts: 2.8 us -> none  [doubled(): jnp.concatenate([jnp.where(upper, other, piece), jnp.where(upper, piece,...]
    ppermute x33 -> x34, starting transfers between devices: 36.6 us -> 34.2 us  [permuted(): return lax.ppermute(values, axis, [(i, i ^ distance) for i in range(size)])]
    convert_element_type x3 -> x2, other arithmetic: 2.71 us -> 0.84 us  [the longest x1 0.7 us: on_pair(): activated = jax.nn.silu(cond.astype(jnp.float32)).astype(jnp.bfloat16)]
    select_n x6 -> x0, other arithmetic: 1.81 us -> none  [the longest x1 1.06 us: on_pair(): jnp.where(tensor_pos == 0, context, other)]
    ppermute x33 -> x34, waiting for transfers between devices: 53.3 us -> 53 us  [permuted(): return lax.ppermute(values, axis, [(i, i ^ distance) for i in range(size)])]
    unnamed x24 -> x30, local copies, waits for them, and re-layouts: 4.2 us -> 4.16 us
  transfers between devices with their start and end apart: 33 -> 34, of which waited for: 20 -> 20; matrix products, arithmetic and copies ran while one was open for 6% -> 1% of each run, Pallas kernels for 12% -> 11%
where the time goes in v3:
time: 121 us
  waiting for transfers between devices  53 us (44%)
  starting transfers between devices  34.2 us (28%)
  Pallas kernels  25.7 us (21%)
  local copies, waits for them, and re-layouts  4.17 us (3%)
  other arithmetic  2.08 us (2%)
    ppermute x34, waiting for transfers between devices, permuted(): return lax.ppermute(values, axis, [(i, i ^ distance) for i in range(size)])  53 us
    ppermute x34, starting transfers between devices, permuted(): return lax.ppermute(values, axis, [(i, i ^ distance) for i in range(size)])  34.2 us
    pallas_call x6, Pallas kernels, projected(): pl.pallas_call(lambda *refs: project_kernel(len(blocks), *refs), grid=(co...  11.5 us
    pallas_call x2, Pallas kernels, down_projected(): pl.pallas_call(lambda *refs: down_kernel(last, *refs), grid=(columns // t...  5.21 us
    pallas_call x2, Pallas kernels, up_projected(): pl.pallas_call(up_kernel, grid=(columns // tile,), in_specs=[pl.BlockSpec...  4.35 us
    unnamed x30, local copies, waits for them, and re-layouts  4.16 us
  transfers between devices with their start and end apart: 34, of which 20 were waited for; matrix products, arithmetic and copies ran while one was open for 1% of the time, Pallas kernels for 11%

profile of v3, /device:TPU:0, one launch (start us, length us, event | category | flops | bytes accessed | tf_op | source)
XLA Modules:
  0.0 120.6 jit_solution(2569397146845865194)
XLA Ops:
  0.0 1.1 copy-done.3
  2.8 2.9 %collective-permute-start.4 = (bf16[64,1536]{1,0:T(8,128)(2,1)S(1)}, bf16[64,1536]{1,0:T(8,128)(2,1)S(1)}, u32[]{:S(2)}, u32[]{:S(2)}) collective-permute-start(bf16[64,1536]{1,0:T(8,128)(2,1)S(1)} %standardized.1.refs_2_.refs_0_), channel_id=1, source_target_pairs={{0,8},{8,0},{16,24},{24,16},{1,9},{9,1},{17,25},{25,17},{2,10},{10... | collective-permute-start | bytes 589832 | tf_op jit(solution)/shard_map/ppermute | solution.py:161
  5.7 1.5 %collective-permute-start.5 = (bf16[64,1536]{1,0:T(8,128)(2,1)S(1)}, bf16[64,1536]{1,0:T(8,128)(2,1)S(1)}, u32[]{:S(2)}, u32[]{:S(2)}) collective-permute-start(bf16[64,1536]{1,0:T(8,128)(2,1)S(1)} %standardized.1.refs_2_.refs_0_), channel_id=1, source_target_pairs={{0,16},{8,24},{16,0},{24,8},{1,17},{9,25},{17,1},{25,9},{2,18},{10... | collective-permute-start | bytes 589832 | tf_op jit(solution)/shard_map/ppermute | solution.py:161
  7.2 3.0 %collective-permute-start.9 = (bf16[64,1536]{1,0:T(8,128)(2,1)S(1)}, bf16[64,1536]{1,0:T(8,128)(2,1)S(1)}, u32[]{:S(2)}, u32[]{:S(2)}) collective-permute-start(bf16[64,1536]{1,0:T(8,128)(2,1)S(1)} %standardized.1.refs_2_.refs_0_), channel_id=1, source_target_pairs={{0,4},{2,6},{4,0},{6,2},{1,5},{3,7},{5,1},{7,3},{8,12},{10,14},{12... | collective-permute-start | bytes 589832 | tf_op jit(solution)/shard_map/ppermute | solution.py:161
  11.3 1.2 collective-permute-done.refs_1_
  12.4 1.6 %collective-permute-start.1 = (f32[2,576]{1,0:T(2,128)S(1)}, f32[2,576]{1,0:T(2,128)S(1)}, u32[]{:S(2)}, u32[]{:S(2)}) collective-permute-start(f32[2,576]{1,0:T(2,128)S(1)} %merged.5.refs_0_), channel_id=1, source_target_pairs={{0,2},{2,0},{4,6},{6,4},{1,3},{3,1},{5,7},{7,5},{8,10},{10,8},{12,... | collective-permute-start | bytes 13832 | tf_op jit(solution)/shard_map/ppermute | solution.py:161
  14.0 2.5 %collective-permute-done.1.refs_1_ = f32[2,576]{1,0:T(2,128)S(1)} collective-permute-done((f32[2,576]{1,0:T(2,128)S(1)}, f32[2,576]{1,0:T(2,128)S(1)}, u32[]{:S(2)}, u32[]{:S(2)}) %collective-permute-start.1) | collective-permute-done | bytes 4640 | tf_op jit(solution)/shard_map/ppermute | solution.py:161
  16.7 4.6 %collective-permute-done.3.refs_1_ = f32[4,576]{1,0:T(4,128)S(1)} collective-permute-done((f32[4,576]{1,0:T(4,128)S(1)}, f32[4,576]{1,0:T(4,128)S(1)}, u32[]{:S(2)}, u32[]{:S(2)}) %collective-permute-start.3) | collective-permute-done | bytes 9248 | tf_op jit(solution)/shard_map/ppermute | solution.py:161
  21.2 1.6 %collective-permute-start.6 = (f32[8,576]{1,0:T(8,128)S(1)}, f32[8,576]{1,0:T(8,128)S(1)}, u32[]{:S(2)}, u32[]{:S(2)}) collective-permute-start(f32[8,576]{1,0:T(8,128)S(1)} %merged.7.refs_0_), channel_id=1, source_target_pairs={{0,8},{8,0},{16,24},{24,16},{1,9},{9,1},{17,25},{25,17},{2,10},{10... | collective-permute-start | bytes 55304 | tf_op jit(solution)/shard_map/ppermute | solution.py:161
  22.8 2.3 %collective-permute-done.6.refs_1_ = f32[8,576]{1,0:T(8,128)S(1)} collective-permute-done((f32[8,576]{1,0:T(8,128)S(1)}, f32[8,576]{1,0:T(8,128)S(1)}, u32[]{:S(2)}, u32[]{:S(2)}) %collective-permute-start.6) | collective-permute-done | bytes 18464 | tf_op jit(solution)/shard_map/ppermute | solution.py:161
  25.1 1.6 %collective-permute-start.8 = (f32[16,576]{1,0:T(8,128)S(1)}, f32[16,576]{1,0:T(8,128)S(1)}, u32[]{:S(2)}, u32[]{:S(2)}) collective-permute-start(f32[16,576]{1,0:T(8,128)S(1)} %merged.8.refs_0_), channel_id=1, source_target_pairs={{0,16},{8,24},{16,0},{24,8},{1,17},{9,25},{17,1},{25,9},{2,18},{10... | collective-permute-start | bytes 110600 | tf_op jit(solution)/shard_map/ppermute | solution.py:161
  26.7 2.5 %collective-permute-done.8.refs_1_ = f32[16,576]{1,0:T(8,128)S(1)} collective-permute-done((f32[16,576]{1,0:T(8,128)S(1)}, f32[16,576]{1,0:T(8,128)S(1)}, u32[]{:S(2)}, u32[]{:S(2)}) %collective-permute-start.8) | collective-permute-done | bytes 36896 | tf_op jit(solution)/shard_map/ppermute | solution.py:161
  29.4 3.0 %copy-done.1 = bf16[1536,3,768]{2,0,1:T(8,128)(2,1)S(1)} copy-done((bf16[1536,3,768]{2,0,1:T(8,128)(2,1)S(1)}, bf16[1536,3,768]{2,0,1:T(8,128)(2,1)}, u32[]{:S(2)}) %copy-start.1) | copy-done | bytes 7077912
  32.4 2.4 %projected.7 = bf16[256,1152]{1,0:T(8,128)(2,1)S(1)} custom-call(bf16[64,1536]{1,0:T(8,128)(2,1)S(1)} %standardized.1.refs_2_.refs_0_, bf16[64,1536]{1,0:T(8,128)(2,1)S(1)} %collective-permute-done.4.refs_2_.refs_1_, bf16[64,1536]{1,0:T(8,128)(2,1)S(1)} %collective-permute-done.5.refs_3_.refs_2_, ...), custom_call_target="tpu_custom_call" | custom-call | tf_op jit(solution)/shard_map/projected/pallas_call | solution.py:325
  34.9 1.6 %collective-permute-start.12 = (bf16[64,1536]{1,0:T(8,128)(2,1)S(1)}, bf16[64,1536]{1,0:T(8,128)(2,1)S(1)}, u32[]{:S(2)}, u32[]{:S(2)}) collective-permute-start(bf16[64,1536]{1,0:T(8,128)(2,1)S(1)} %collective-permute-done.9.refs_2_.refs_0_), channel_id=1, source_target_pairs={{0,8},{8,0},{16,24},{24,16},{1,9},{9,1},{17,25},{25,17},{2,10},{10... | collective-permute-start | bytes 589832 | tf_op jit(solution)/shard_map/ppermute | solution.py:161
  36.5 1.5 %collective-permute-start.13 = (bf16[64,1536]{1,0:T(8,128)(2,1)S(1)}, bf16[64,1536]{1,0:T(8,128)(2,1)S(1)}, u32[]{:S(2)}, u32[]{:S(2)}) collective-permute-start(bf16[64,1536]{1,0:T(8,128)(2,1)S(1)} %collective-permute-done.9.refs_2_.refs_0_), channel_id=1, source_target_pairs={{0,16},{8,24},{16,0},{24,8},{1,17},{9,25},{17,1},{25,9},{2,18},{10... | collective-permute-start | bytes 589832 | tf_op jit(solution)/shard_map/ppermute | solution.py:161
  39.5 2.4 %projected.6.refs_0_ = bf16[256,1152]{1,0:T(8,128)(2,1)S(1)} custom-call(bf16[64,1536]{1,0:T(8,128)(2,1)S(1)} %standardized.1.refs_2_.refs_0_, bf16[64,1536]{1,0:T(8,128)(2,1)S(1)} %collective-permute-done.4.refs_2_.refs_1_, bf16[64,1536]{1,0:T(8,128)(2,1)S(1)} %collective-permute-done.5.refs_3_.refs_2_, ...), custom_call_target="tpu_custom_call" | custom-call | tf_op jit(solution)/shard_map/projected/pallas_call | solution.py:325
  42.7 5.0 %collective-permute-done.13.refs_2_ = bf16[64,1536]{1,0:T(8,128)(2,1)S(1)} collective-permute-done((bf16[64,1536]{1,0:T(8,128)(2,1)S(1)}, bf16[64,1536]{1,0:T(8,128)(2,1)S(1)}, u32[]{:S(2)}, u32[]{:S(2)}) %collective-permute-start.13) | collective-permute-done | bytes 196640 | tf_op jit(solution)/shard_map/ppermute | solution.py:161
  47.7 1.7 %projected.9 = bf16[256,768]{1,0:T(8,128)(2,1)S(1)} custom-call(bf16[64,1536]{1,0:T(8,128)(2,1)S(1)} %collective-permute-done.9.refs_2_.refs_0_, bf16[64,1536]{1,0:T(8,128)(2,1)S(1)} %collective-permute-done.12.refs_1_, bf16[64,1536]{1,0:T(8,128)(2,1)S(1)} %collective-permute-done.13.refs_2_, bf16[64,1536]{1,0:T(8,128)(2,1)S(1)} %collective-permute-done.14.refs_3_, ...), custom_call_target="tpu_custom_call" | custom-call | tf_op jit(solution)/shard_map/projected/pallas_call | solution.py:325
  49.8 1.1 collective-permute-start.11
  51.0 1.2 collective-permute-start.17
  53.0 1.4 %collective-permute-start.19 = (bf16[64,1536]{1,0:T(8,128)(2,1)S(1)}, bf16[64,1536]{1,0:T(8,128)(2,1)S(1)}, u32[]{:S(2)}, u32[]{:S(2)}) collective-permute-start(bf16[64,1536]{1,0:T(8,128)(2,1)S(1)} %collective-permute-done.16.refs_0_), channel_id=1, source_target_pairs={{0,24},{8,16},{16,8},{24,0},{1,25},{9,17},{17,9},{25,1},{2,26},{10... | collective-permute-start | bytes 589832 | tf_op jit(solution)/shard_map/ppermute | solution.py:161
  54.5 1.7 %projected.8.refs_0_ = bf16[256,768]{1,0:T(8,128)(2,1)S(1)} custom-call(bf16[64,1536]{1,0:T(8,128)(2,1)S(1)} %collective-permute-done.9.refs_2_.refs_0_, bf16[64,1536]{1,0:T(8,128)(2,1)S(1)} %collective-permute-done.12.refs_1_, bf16[64,1536]{1,0:T(8,128)(2,1)S(1)} %collective-permute-done.13.refs_2_, bf16[64,1536]{1,0:T(8,128)(2,1)S(1)} %collective-permute-done.14.refs_3_, ...), custom_call_target="tpu_custom_call" | custom-call | tf_op jit(solution)/shard_map/projected/pallas_call | solution.py:325
  56.4 2.3 %collective-permute-done.17.refs_1_ = bf16[64,1536]{1,0:T(8,128)(2,1)S(1)} collective-permute-done((bf16[64,1536]{1,0:T(8,128)(2,1)S(1)}, bf16[64,1536]{1,0:T(8,128)(2,1)S(1)}, u32[]{:S(2)}, u32[]{:S(2)}) %collective-permute-start.17) | collective-permute-done | bytes 196640 | tf_op jit(solution)/shard_map/ppermute | solution.py:161
  58.7 2.8 %collective-permute-done.18.refs_2_ = bf16[64,1536]{1,0:T(8,128)(2,1)S(1)} collective-permute-done((bf16[64,1536]{1,0:T(8,128)(2,1)S(1)}, bf16[64,1536]{1,0:T(8,128)(2,1)S(1)}, u32[]{:S(2)}, u32[]{:S(2)}) %collective-permute-start.18) | collective-permute-done | bytes 196640 | tf_op jit(solution)/shard_map/ppermute | solution.py:161
  61.5 1.6 %collective-permute-done.19.refs_3_ = bf16[64,1536]{1,0:T(8,128)(2,1)S(1)} collective-permute-done((bf16[64,1536]{1,0:T(8,128)(2,1)S(1)}, bf16[64,1536]{1,0:T(8,128)(2,1)S(1)}, u32[]{:S(2)}, u32[]{:S(2)}) %collective-permute-start.19) | collective-permute-done | bytes 196640 | tf_op jit(solution)/shard_map/ppermute | solution.py:161
  63.2 1.7 %projected.11 = bf16[256,768]{1,0:T(8,128)(2,1)S(1)} custom-call(bf16[64,1536]{1,0:T(8,128)(2,1)S(1)} %collective-permute-done.16.refs_0_, bf16[64,1536]{1,0:T(8,128)(2,1)S(1)} %collective-permute-done.17.refs_1_, bf16[64,1536]{1,0:T(8,128)(2,1)S(1)} %collective-permute-done.18.refs_2_, bf16[64,1536]{1,0:T(8,128)(2,1)S(1)} %collective-permute-done.19.refs_3_, ...), custom_call_target="tpu_custom_call" | custom-call | tf_op jit(solution)/shard_map/projected/pallas_call | solution.py:325
  64.9 1.7 %projected.10.refs_0_ = bf16[256,768]{1,0:T(8,128)(2,1)S(1)} custom-call(bf16[64,1536]{1,0:T(8,128)(2,1)S(1)} %collective-permute-done.16.refs_0_, bf16[64,1536]{1,0:T(8,128)(2,1)S(1)} %collective-permute-done.17.refs_1_, bf16[64,1536]{1,0:T(8,128)(2,1)S(1)} %collective-permute-done.18.refs_2_, bf16[64,1536]{1,0:T(8,128)(2,1)S(1)} %collective-permute-done.19.refs_3_, ...), custom_call_target="tpu_custom_call" | custom-call | tf_op jit(solution)/shard_map/projected/pallas_call | solution.py:325
  66.9 1.6 %attention.1.own_ref = bf16[256,384]{1,0:T(8,128)(2,1)S(1)} custom-call(bf16[256,384]{1,0:T(8,128)(2,1)S(1)} %get-tuple-element.19.refs_0_, bf16[256,768]{1,0:T(8,128)(2,1)S(1)} %get-tuple-element.20.refs_1_, bf16[256,768]{1,0:T(8,128)(2,1)S(1)} %collective-permute-done.11.refs_8_.refs_2_, bf16[256,768]{1,0:T(8,128)(2,1)S(1)} %split_heads.4.refs_7_.refs_3_, ...), custom_call_target="tpu_custom_call" | custom-call | flops 402653184 | bytes 1572864 | tf_op jit(solution)/shard_map/attention/pallas_call | solution.py:414
  70.2 1.7 %out_projected.1 = (bf16[64,1536]{1,0:T(8,128)(2,1)S(1)}, bf16[64,1536]{1,0:T(8,128)(2,1)S(1)}, bf16[64,1536]{1,0:T(8,128)(2,1)S(1)}, bf16[64,1536]{1,0:T(8,128)(2,1)S(1)}) custom-call(bf16[256,384]{1,0:T(8,128)(2,1)S(1)} %attention.1.own_ref, bf16[256,384]{1,0:T(8,128)(2,1)S(1)} %collective-permute-done.21.arrived_ref, bf16[768,1536]{1,0:T(8,128)(2,1)S(1)} %copy-done.2, ...), custom_call_target="tpu_custom_call" | custom-call | tf_op jit(solution)/shard_map/out_projected/pallas_call | solution.py:446
  72.8 1.5 %collective-permute-start.23 = (bf16[64,1536]{1,0:T(8,128)(2,1)S(1)}, bf16[64,1536]{1,0:T(8,128)(2,1)S(1)}, u32[]{:S(2)}, u32[]{:S(2)}) collective-permute-start(bf16[64,1536]{1,0:T(8,128)(2,1)S(1)} %get-tuple-element.23), channel_id=1, source_target_pairs={{0,16},{8,24},{16,0},{24,8},{1,17},{9,25},{17,1},{25,9},{2,18},{10... | collective-permute-start | bytes 589832 | tf_op jit(solution)/shard_map/ppermute | solution.py:161
  74.3 1.1 collective-permute-start.24
  75.4 4.2 %collective-permute-done.22 = bf16[64,1536]{1,0:T(8,128)(2,1)S(1)} collective-permute-done((bf16[64,1536]{1,0:T(8,128)(2,1)S(1)}, bf16[64,1536]{1,0:T(8,128)(2,1)S(1)}, u32[]{:S(2)}, u32[]{:S(2)}) %collective-permute-start.22) | collective-permute-done | bytes 196640 | tf_op jit(solution)/shard_map/ppermute | solution.py:161
  79.7 4.2 %collective-permute-done.23 = bf16[64,1536]{1,0:T(8,128)(2,1)S(1)} collective-permute-done((bf16[64,1536]{1,0:T(8,128)(2,1)S(1)}, bf16[64,1536]{1,0:T(8,128)(2,1)S(1)}, u32[]{:S(2)}, u32[]{:S(2)}) %collective-permute-start.23) | collective-permute-done | bytes 196640 | tf_op jit(solution)/shard_map/ppermute | solution.py:161
  84.2 1.1 collective-permute-done.25
  85.5 1.3 %collective-permute-start.26 = (bf16[64,1536]{1,0:T(8,128)(2,1)S(1)}, bf16[64,1536]{1,0:T(8,128)(2,1)S(1)}, u32[]{:S(2)}, u32[]{:S(2)}) collective-permute-start(bf16[64,1536]{1,0:T(8,128)(2,1)S(1)} %add_convert_fusion.refs_0_), channel_id=1, source_target_pairs={{0,8},{8,0},{16,24},{24,16},{1,9},{9,1},{17,25},{25,17},{2,10},{10... | collective-permute-start | bytes 589832 | tf_op jit(solution)/shard_map/ppermute | solution.py:161
  87.7 1.4 %collective-permute-start.28 = (bf16[64,1536]{1,0:T(8,128)(2,1)S(1)}, bf16[64,1536]{1,0:T(8,128)(2,1)S(1)}, u32[]{:S(2)}, u32[]{:S(2)}) collective-permute-start(bf16[64,1536]{1,0:T(8,128)(2,1)S(1)} %add_convert_fusion.refs_0_), channel_id=1, source_target_pairs={{0,24},{8,16},{16,8},{24,0},{1,25},{9,17},{17,9},{25,1},{2,26},{10... | collective-permute-start | bytes 589832 | tf_op jit(solution)/shard_map/ppermute | solution.py:161
  89.1 4.3 %collective-permute-done.26.refs_1_ = bf16[64,1536]{1,0:T(8,128)(2,1)S(1)} collective-permute-done((bf16[64,1536]{1,0:T(8,128)(2,1)S(1)}, bf16[64,1536]{1,0:T(8,128)(2,1)S(1)}, u32[]{:S(2)}, u32[]{:S(2)}) %collective-permute-start.26) | collective-permute-done | bytes 196640 | tf_op jit(solution)/shard_map/ppermute | solution.py:161
  93.3 2.8 %collective-permute-done.27.refs_2_ = bf16[64,1536]{1,0:T(8,128)(2,1)S(1)} collective-permute-done((bf16[64,1536]{1,0:T(8,128)(2,1)S(1)}, bf16[64,1536]{1,0:T(8,128)(2,1)S(1)}, u32[]{:S(2)}, u32[]{:S(2)}) %collective-permute-start.27) | collective-permute-done | bytes 196640 | tf_op jit(solution)/shard_map/ppermute | solution.py:161
  96.1 1.6 %collective-permute-done.28.refs_3_ = bf16[64,1536]{1,0:T(8,128)(2,1)S(1)} collective-permute-done((bf16[64,1536]{1,0:T(8,128)(2,1)S(1)}, bf16[64,1536]{1,0:T(8,128)(2,1)S(1)}, u32[]{:S(2)}, u32[]{:S(2)}) %collective-permute-start.28) | collective-permute-done | bytes 196640 | tf_op jit(solution)/shard_map/ppermute | solution.py:161
  97.8 2.2 %up_projected.3.refs_0_ = bf16[256,1536]{1,0:T(8,128)(2,1)S(1)} custom-call(bf16[64,1536]{1,0:T(8,128)(2,1)S(1)} %add_convert_fusion.refs_0_, bf16[64,1536]{1,0:T(8,128)(2,1)S(1)} %collective-permute-done.26.refs_1_, bf16[64,1536]{1,0:T(8,128)(2,1)S(1)} %collective-permute-done.27.refs_2_, bf16[64,1536]{1,0:T(8,128)(2,1)S(1)} %collective-permute-done.28.refs_3_, ...), custom_call_target="tpu_custom_call" | custom-call | flops 1207959552 | bytes 4718592 | tf_op jit(solution)/shard_map/up_projected/pallas_call | solution.py:483
  100.1 2.2 %up_projected.2.refs_0_ = bf16[256,1536]{1,0:T(8,128)(2,1)S(1)} custom-call(bf16[64,1536]{1,0:T(8,128)(2,1)S(1)} %add_convert_fusion.refs_0_, bf16[64,1536]{1,0:T(8,128)(2,1)S(1)} %collective-permute-done.26.refs_1_, bf16[64,1536]{1,0:T(8,128)(2,1)S(1)} %collective-permute-done.27.refs_2_, bf16[64,1536]{1,0:T(8,128)(2,1)S(1)} %collective-permute-done.28.refs_3_, ...), custom_call_target="tpu_custom_call" | custom-call | flops 1207959552 | bytes 4718592 | tf_op jit(solution)/shard_map/up_projected/pallas_call | solution.py:483
  102.8 2.5 %down_projected.2.refs_3_ = f32[256,1536]{1,0:T(8,128)S(1)} custom-call(bf16[256,1536]{1,0:T(8,128)(2,1)S(1)} %up_projected.3.refs_0_, bf16[256,1536]{1,0:T(8,128)(2,1)S(1)} %collective-permute-done.30.refs_1_, bf16[3072,1536]{1,0:T(8,128)(2,1)S(1)} %bitcast.28), custom_call_target="tpu_custom_call" | custom-call | flops 1207959552 | bytes 4718592 | tf_op jit(solution)/shard_map/down_projected/pallas_call | solution.py:541
  105.4 2.7 %down_projected.3 = (bf16[64,1536]{1,0:T(8,128)(2,1)S(1)}, bf16[64,1536]{1,0:T(8,128)(2,1)S(1)}, bf16[64,1536]{1,0:T(8,128)(2,1)S(1)}, bf16[64,1536]{1,0:T(8,128)(2,1)S(1)}) custom-call(bf16[256,1536]{1,0:T(8,128)(2,1)S(1)} %up_projected.2.refs_0_, bf16[256,1536]{1,0:T(8,128)(2,1)S(1)} %collective-permute-done.29.refs_1_, bf16[3072,1536]{1,0:T(8,128)(2,1)S(1)} %bitcast.28, ...), custom_call_target="tpu_custom_call" | custom-call | flops 1207959552 | bytes 4718592 | tf_op jit(solution)/shard_map/down_projected/pallas_call | solution.py:541
  109.0 1.5 %collective-permute-start.32 = (bf16[64,1536]{1,0:T(8,128)(2,1)S(1)}, bf16[64,1536]{1,0:T(8,128)(2,1)S(1)}, u32[]{:S(2)}, u32[]{:S(2)}) collective-permute-start(bf16[64,1536]{1,0:T(8,128)(2,1)S(1)} %get-tuple-element.27), channel_id=1, source_target_pairs={{0,16},{8,24},{16,0},{24,8},{1,17},{9,25},{17,1},{25,9},{2,18},{10... | collective-permute-start | bytes 589832 | tf_op jit(solution)/shard_map/ppermute | solution.py:161
  110.5 1.2 collective-permute-start.33
  111.6 4.3 %collective-permute-done.31 = bf16[64,1536]{1,0:T(8,128)(2,1)S(1)} collective-permute-done((bf16[64,1536]{1,0:T(8,128)(2,1)S(1)}, bf16[64,1536]{1,0:T(8,128)(2,1)S(1)}, u32[]{:S(2)}, u32[]{:S(2)}) %collective-permute-start.31) | collective-permute-done | bytes 196640 | tf_op jit(solution)/shard_map/ppermute | solution.py:161
  115.9 3.8 %collective-permute-done.32 = bf16[64,1536]{1,0:T(8,128)(2,1)S(1)} collective-permute-done((bf16[64,1536]{1,0:T(8,128)(2,1)S(1)}, bf16[64,1536]{1,0:T(8,128)(2,1)S(1)}, u32[]{:S(2)}, u32[]{:S(2)}) %collective-permute-start.32) | collective-permute-done | bytes 196640 | tf_op jit(solution)/shard_map/ppermute | solution.py:161
  (87 shorter events, 13.5 us)
Async XLA Ops:
  0.0 10.2 %copy-start = (bf16[3072,576]{0,1:T(8,128)(2,1)S(1)}, bf16[3072,576]{0,1:T(8,128)(2,1)}, u32[]{:S(2)}) copy-start(bf16[3072,576]{0,1:T(8,128)(2,1)} %param.11) | copy-start | bytes 10616836
  1.2 1.4 %collective-permute-start.2 = (f32[64,128]{1,0:T(8,128)S(1)}, f32[64,128]{1,0:T(8,128)S(1)}, u32[]{:S(2)}, u32[]{:S(2)}) collective-permute-start(f32[64,128]{1,0:T(8,128)S(1)} %get-tuple-element.18.refs_1_), channel_id=1, source_target_pairs={{0,1},{1,0},{2,3},{3,2},{4,5},{5,4},{6,7},{7,6},{8,9},{9,8},{10,11... | collective-permute-start | bytes 98312 | tf_op jit(solution)/shard_map/ppermute | solution.py:161
  2.8 18.5 %collective-permute-start.4 = (bf16[64,1536]{1,0:T(8,128)(2,1)S(1)}, bf16[64,1536]{1,0:T(8,128)(2,1)S(1)}, u32[]{:S(2)}, u32[]{:S(2)}) collective-permute-start(bf16[64,1536]{1,0:T(8,128)(2,1)S(1)} %standardized.1.refs_2_.refs_0_), channel_id=1, source_target_pairs={{0,8},{8,0},{16,24},{24,16},{1,9},{9,1},{17,25},{25,17},{2,10},{10... | collective-permute-start | bytes 589832 | tf_op jit(solution)/shard_map/ppermute | solution.py:161
  5.7 15.6 %collective-permute-start.5 = (bf16[64,1536]{1,0:T(8,128)(2,1)S(1)}, bf16[64,1536]{1,0:T(8,128)(2,1)S(1)}, u32[]{:S(2)}, u32[]{:S(2)}) collective-permute-start(bf16[64,1536]{1,0:T(8,128)(2,1)S(1)} %standardized.1.refs_2_.refs_0_), channel_id=1, source_target_pairs={{0,16},{8,24},{16,0},{24,8},{1,17},{9,25},{17,1},{25,9},{2,18},{10... | collective-permute-start | bytes 589832 | tf_op jit(solution)/shard_map/ppermute | solution.py:161
  7.2 15.6 %collective-permute-start.7 = (bf16[64,1536]{1,0:T(8,128)(2,1)S(1)}, bf16[64,1536]{1,0:T(8,128)(2,1)S(1)}, u32[]{:S(2)}, u32[]{:S(2)}) collective-permute-start(bf16[64,1536]{1,0:T(8,128)(2,1)S(1)} %standardized.1.refs_2_.refs_0_), channel_id=1, source_target_pairs={{0,24},{8,16},{16,8},{24,0},{1,25},{9,17},{17,9},{25,1},{2,26},{10... | collective-permute-start | bytes 589832 | tf_op jit(solution)/shard_map/ppermute | solution.py:161
  7.2 19.5 %collective-permute-start.9 = (bf16[64,1536]{1,0:T(8,128)(2,1)S(1)}, bf16[64,1536]{1,0:T(8,128)(2,1)S(1)}, u32[]{:S(2)}, u32[]{:S(2)}) collective-permute-start(bf16[64,1536]{1,0:T(8,128)(2,1)S(1)} %standardized.1.refs_2_.refs_0_), channel_id=1, source_target_pairs={{0,4},{2,6},{4,0},{6,2},{1,5},{3,7},{5,1},{7,3},{8,12},{10,14},{12... | collective-permute-start | bytes 589832 | tf_op jit(solution)/shard_map/ppermute | solution.py:161
  11.3 1.2 collective-permute-start
  12.4 4.1 %collective-permute-start.1 = (f32[2,576]{1,0:T(2,128)S(1)}, f32[2,576]{1,0:T(2,128)S(1)}, u32[]{:S(2)}, u32[]{:S(2)}) collective-permute-start(f32[2,576]{1,0:T(2,128)S(1)} %merged.5.refs_0_), channel_id=1, source_target_pairs={{0,2},{2,0},{4,6},{6,4},{1,3},{3,1},{5,7},{7,5},{8,10},{10,8},{12,... | collective-permute-start | bytes 13832 | tf_op jit(solution)/shard_map/ppermute | solution.py:161
  16.6 4.6 %collective-permute-start.3 = (f32[4,576]{1,0:T(4,128)S(1)}, f32[4,576]{1,0:T(4,128)S(1)}, u32[]{:S(2)}, u32[]{:S(2)}) collective-permute-start(f32[4,576]{1,0:T(4,128)S(1)} %merged.6.refs_0_), channel_id=1, source_target_pairs={{0,4},{2,6},{4,0},{6,2},{1,5},{3,7},{5,1},{7,3},{8,12},{10,14},{12... | collective-permute-start | bytes 27656 | tf_op jit(solution)/shard_map/ppermute | solution.py:161
  21.2 3.8 %collective-permute-start.6 = (f32[8,576]{1,0:T(8,128)S(1)}, f32[8,576]{1,0:T(8,128)S(1)}, u32[]{:S(2)}, u32[]{:S(2)}) collective-permute-start(f32[8,576]{1,0:T(8,128)S(1)} %merged.7.refs_0_), channel_id=1, source_target_pairs={{0,8},{8,0},{16,24},{24,16},{1,9},{9,1},{17,25},{25,17},{2,10},{10... | collective-permute-start | bytes 55304 | tf_op jit(solution)/shard_map/ppermute | solution.py:161
  25.1 4.1 %collective-permute-start.8 = (f32[16,576]{1,0:T(8,128)S(1)}, f32[16,576]{1,0:T(8,128)S(1)}, u32[]{:S(2)}, u32[]{:S(2)}) collective-permute-start(f32[16,576]{1,0:T(8,128)S(1)} %merged.8.refs_0_), channel_id=1, source_target_pairs={{0,16},{8,24},{16,0},{24,8},{1,17},{9,25},{17,1},{25,9},{2,18},{10... | collective-permute-start | bytes 110600 | tf_op jit(solution)/shard_map/ppermute | solution.py:161
  29.4 3.0 %copy-start.1 = (bf16[1536,3,768]{2,0,1:T(8,128)(2,1)S(1)}, bf16[1536,3,768]{2,0,1:T(8,128)(2,1)}, u32[]{:S(2)}) copy-start(bf16[1536,3,768]{2,0,1:T(8,128)(2,1)} %param.12) | copy-start | bytes 21233668
  32.4 15.2 %slice-start = ((s8[7077888]{0:T(1024)(128)(4,1)}), s8[4194304]{0:T(1024)(128)(4,1)S(1)}, s32[]{:S(2)}) async-start(s8[7077888]{0:T(1024)(128)(4,1)} %bitcast.19), calls=%async_computation | async-start | bytes 8388608
  34.8 12.8 %slice-start.1 = ((s8[7077888]{0:T(1024)(128)(4,1)}), s8[2883584]{0:T(1024)(128)(4,1)S(1)}, s32[]{:S(2)}) async-start(s8[7077888]{0:T(1024)(128)(4,1)} %bitcast.19), calls=%async_computation.1 | async-start | bytes 5767168
  34.8 14.6 %collective-permute-start.10 = (bf16[256,1152]{1,0:T(8,128)(2,1)S(1)}, bf16[256,1152]{1,0:T(8,128)(2,1)S(1)}, u32[]{:S(2)}, u32[]{:S(2)}) collective-permute-start(bf16[256,1152]{1,0:T(8,128)(2,1)S(1)} %projected.7), channel_id=1, source_target_pairs={{0,1},{1,0},{2,3},{3,2},{4,5},{5,4},{6,7},{7,6},{8,9},{9,8},{10,11... | collective-permute-start | bytes 1769480 | tf_op jit(solution)/shard_map/ppermute | solution.py:161
  34.9 7.8 %collective-permute-start.12 = (bf16[64,1536]{1,0:T(8,128)(2,1)S(1)}, bf16[64,1536]{1,0:T(8,128)(2,1)S(1)}, u32[]{:S(2)}, u32[]{:S(2)}) collective-permute-start(bf16[64,1536]{1,0:T(8,128)(2,1)S(1)} %collective-permute-done.9.refs_2_.refs_0_), channel_id=1, source_target_pairs={{0,8},{8,0},{16,24},{24,16},{1,9},{9,1},{17,25},{25,17},{2,10},{10... | collective-permute-start | bytes 589832 | tf_op jit(solution)/shard_map/ppermute | solution.py:161
  36.5 11.2 %collective-permute-start.13 = (bf16[64,1536]{1,0:T(8,128)(2,1)S(1)}, bf16[64,1536]{1,0:T(8,128)(2,1)S(1)}, u32[]{:S(2)}, u32[]{:S(2)}) collective-permute-start(bf16[64,1536]{1,0:T(8,128)(2,1)S(1)} %collective-permute-done.9.refs_2_.refs_0_), channel_id=1, source_target_pairs={{0,16},{8,24},{16,0},{24,8},{1,17},{9,25},{17,1},{25,9},{2,18},{10... | collective-permute-start | bytes 589832 | tf_op jit(solution)/shard_map/ppermute | solution.py:161
  38.0 9.7 %collective-permute-start.14 = (bf16[64,1536]{1,0:T(8,128)(2,1)S(1)}, bf16[64,1536]{1,0:T(8,128)(2,1)S(1)}, u32[]{:S(2)}, u32[]{:S(2)}) collective-permute-start(bf16[64,1536]{1,0:T(8,128)(2,1)S(1)} %collective-permute-done.9.refs_2_.refs_0_), channel_id=1, source_target_pairs={{0,24},{8,16},{16,8},{24,0},{1,25},{9,17},{17,9},{25,1},{2,26},{10... | collective-permute-start | bytes 589832 | tf_op jit(solution)/shard_map/ppermute | solution.py:161
  38.5 12.5 %collective-permute-start.16 = (bf16[64,1536]{1,0:T(8,128)(2,1)S(1)}, bf16[64,1536]{1,0:T(8,128)(2,1)S(1)}, u32[]{:S(2)}, u32[]{:S(2)}) collective-permute-start(bf16[64,1536]{1,0:T(8,128)(2,1)S(1)} %collective-permute-done.9.refs_2_.refs_0_), channel_id=1, source_target_pairs={{0,2},{2,0},{4,6},{6,4},{1,3},{3,1},{5,7},{7,5},{8,10},{10,8},{12,... | collective-permute-start | bytes 589832 | tf_op jit(solution)/shard_map/ppermute | solution.py:161
  41.9 7.5 %copy-start.5 = (f32[128]{0:T(128)S(1)}, f32[128]{0:T(128)}, u32[]{:S(2)}) copy-start(f32[128]{0:T(128)} %param.13) | copy-start | bytes 1540
  41.9 7.5 %copy-start.6 = (f32[128]{0:T(128)S(1)}, f32[128]{0:T(128)}, u32[]{:S(2)}) copy-start(f32[128]{0:T(128)} %param.14) | copy-start | bytes 1540
  49.4 6.8 %collective-permute-start.15 = (bf16[256,768]{1,0:T(8,128)(2,1)S(1)}, bf16[256,768]{1,0:T(8,128)(2,1)S(1)}, u32[]{:S(2)}, u32[]{:S(2)}) collective-permute-start(bf16[256,768]{1,0:T(8,128)(2,1)S(1)} %projected.9), channel_id=1, source_target_pairs={{0,1},{1,0},{2,3},{3,2},{4,5},{5,4},{6,7},{7,6},{8,9},{9,8},{10,11... | collective-permute-start | bytes 1179656 | tf_op jit(solution)/shard_map/ppermute | solution.py:161
  49.8 13.3 %collective-permute-start.11 = (bf16[256,768]{1,0:T(8,128)(2,1)S(1)}, bf16[256,768]{1,0:T(8,128)(2,1)S(1)}, u32[]{:S(2)}, u32[]{:S(2)}) collective-permute-start(bf16[256,768]{1,0:T(8,128)(2,1)S(1)} %get-tuple-element.20.refs_1_), channel_id=1, source_target_pairs={{0,2},{2,0},{4,6},{6,4},{1,3},{3,1},{5,7},{7,5},{8,10},{10,8},{12,... | collective-permute-start | bytes 1179656 | tf_op jit(solution)/shard_map/ppermute | solution.py:161
  51.0 7.7 %collective-permute-start.17 = (bf16[64,1536]{1,0:T(8,128)(2,1)S(1)}, bf16[64,1536]{1,0:T(8,128)(2,1)S(1)}, u32[]{:S(2)}, u32[]{:S(2)}) collective-permute-start(bf16[64,1536]{1,0:T(8,128)(2,1)S(1)} %collective-permute-done.16.refs_0_), channel_id=1, source_target_pairs={{0,8},{8,0},{16,24},{24,16},{1,9},{9,1},{17,25},{25,17},{2,10},{10... | collective-permute-start | bytes 589832 | tf_op jit(solution)/shard_map/ppermute | solution.py:161
  52.2 9.3 %collective-permute-start.18 = (bf16[64,1536]{1,0:T(8,128)(2,1)S(1)}, bf16[64,1536]{1,0:T(8,128)(2,1)S(1)}, u32[]{:S(2)}, u32[]{:S(2)}) collective-permute-start(bf16[64,1536]{1,0:T(8,128)(2,1)S(1)} %collective-permute-done.16.refs_0_), channel_id=1, source_target_pairs={{0,16},{8,24},{16,0},{24,8},{1,17},{9,25},{17,1},{25,9},{2,18},{10... | collective-permute-start | bytes 589832 | tf_op jit(solution)/shard_map/ppermute | solution.py:161
  53.0 10.1 %collective-permute-start.19 = (bf16[64,1536]{1,0:T(8,128)(2,1)S(1)}, bf16[64,1536]{1,0:T(8,128)(2,1)S(1)}, u32[]{:S(2)}, u32[]{:S(2)}) collective-permute-start(bf16[64,1536]{1,0:T(8,128)(2,1)S(1)} %collective-permute-done.16.refs_0_), channel_id=1, source_target_pairs={{0,24},{8,16},{16,8},{24,0},{1,25},{9,17},{17,9},{25,1},{2,26},{10... | collective-permute-start | bytes 589832 | tf_op jit(solution)/shard_map/ppermute | solution.py:161
  63.2 34.6 %slice-start.2 = ((s8[9437184]{0:T(1024)(128)(4,1)}), s8[1048576]{0:T(1024)(128)(4,1)S(1)}, s32[]{:S(2)}) async-start(s8[9437184]{0:T(1024)(128)(4,1)} %bitcast.25), calls=%async_computation.2 | async-start | bytes 2097152
  64.8 32.9 %slice-start.3 = ((s8[9437184]{0:T(1024)(128)(4,1)}), s8[4194304]{0:T(1024)(128)(4,1)S(1)}, s32[]{:S(2)}) async-start(s8[9437184]{0:T(1024)(128)(4,1)} %bitcast.25), calls=%async_computation.3 | async-start | bytes 8388608
  64.8 1.8 %collective-permute-start.20 = (bf16[256,768]{1,0:T(8,128)(2,1)S(1)}, bf16[256,768]{1,0:T(8,128)(2,1)S(1)}, u32[]{:S(2)}, u32[]{:S(2)}) collective-permute-start(bf16[256,768]{1,0:T(8,128)(2,1)S(1)} %projected.11), channel_id=1, source_target_pairs={{0,1},{1,0},{2,3},{3,2},{4,5},{5,4},{6,7},{7,6},{8,9},{9,8},{10,11... | collective-permute-start | bytes 1179656 | tf_op jit(solution)/shard_map/ppermute | solution.py:161
  64.9 5.2 %copy-start.2 = (bf16[768,1536]{1,0:T(8,128)(2,1)S(1)}, bf16[768,1536]{1,0:T(8,128)(2,1)}, u32[]{:S(2)}) copy-start(bf16[768,1536]{1,0:T(8,128)(2,1)} %other_weight_ref.1) | copy-start | bytes 7077892
  66.6 31.1 %slice-start.4 = ((s8[9437184]{0:T(1024)(128)(4,1)}), s8[4194304]{0:T(1024)(128)(4,1)S(1)}, s32[]{:S(2)}) async-start(s8[9437184]{0:T(1024)(128)(4,1)} %bitcast.25), calls=%async_computation.4 | async-start | bytes 8388608
  66.9 17.0 %copy-start.4 = (bf16[64,1536]{1,0:T(8,128)(2,1)S(1)}, bf16[64,1536]{1,0:T(8,128)(2,1)}, u32[]{:S(2)}) copy-start(bf16[64,1536]{1,0:T(8,128)(2,1)} %values_ref.1) | copy-start | bytes 589828
  68.6 1.6 %collective-permute-start.21 = (bf16[256,384]{1,0:T(8,128)(2,1)S(1)}, bf16[256,384]{1,0:T(8,128)(2,1)S(1)}, u32[]{:S(2)}, u32[]{:S(2)}) collective-permute-start(bf16[256,384]{1,0:T(8,128)(2,1)S(1)} %attention.1.own_ref), channel_id=1, source_target_pairs={{0,1},{1,0},{2,3},{3,2},{4,5},{5,4},{6,7},{7,6},{8,9},{9,8},{10,11... | collective-permute-start | bytes 589832 | tf_op jit(solution)/shard_map/ppermute | solution.py:161
  71.9 7.8 %collective-permute-start.22 = (bf16[64,1536]{1,0:T(8,128)(2,1)S(1)}, bf16[64,1536]{1,0:T(8,128)(2,1)S(1)}, u32[]{:S(2)}, u32[]{:S(2)}) collective-permute-start(bf16[64,1536]{1,0:T(8,128)(2,1)S(1)} %get-tuple-element.22), channel_id=1, source_target_pairs={{0,8},{8,0},{16,24},{24,16},{1,9},{9,1},{17,25},{25,17},{2,10},{10... | collective-permute-start | bytes 589832 | tf_op jit(solution)/shard_map/ppermute | solution.py:161
  72.8 11.1 %collective-permute-start.23 = (bf16[64,1536]{1,0:T(8,128)(2,1)S(1)}, bf16[64,1536]{1,0:T(8,128)(2,1)S(1)}, u32[]{:S(2)}, u32[]{:S(2)}) collective-permute-start(bf16[64,1536]{1,0:T(8,128)(2,1)S(1)} %get-tuple-element.23), channel_id=1, source_target_pairs={{0,16},{8,24},{16,0},{24,8},{1,17},{9,25},{17,1},{25,9},{2,18},{10... | collective-permute-start | bytes 589832 | tf_op jit(solution)/shard_map/ppermute | solution.py:161
  74.3 9.6 %collective-permute-start.24 = (bf16[64,1536]{1,0:T(8,128)(2,1)S(1)}, bf16[64,1536]{1,0:T(8,128)(2,1)S(1)}, u32[]{:S(2)}, u32[]{:S(2)}) collective-permute-start(bf16[64,1536]{1,0:T(8,128)(2,1)S(1)} %get-tuple-element.24), channel_id=1, source_target_pairs={{0,24},{8,16},{16,8},{24,0},{1,25},{9,17},{17,9},{25,1},{2,26},{10... | collective-permute-start | bytes 589832 | tf_op jit(solution)/shard_map/ppermute | solution.py:161
  84.2 1.2 collective-permute-start.25
  85.5 7.8 %collective-permute-start.26 = (bf16[64,1536]{1,0:T(8,128)(2,1)S(1)}, bf16[64,1536]{1,0:T(8,128)(2,1)S(1)}, u32[]{:S(2)}, u32[]{:S(2)}) collective-permute-start(bf16[64,1536]{1,0:T(8,128)(2,1)S(1)} %add_convert_fusion.refs_0_), channel_id=1, source_target_pairs={{0,8},{8,0},{16,24},{24,16},{1,9},{9,1},{17,25},{25,17},{2,10},{10... | collective-permute-start | bytes 589832 | tf_op jit(solution)/shard_map/ppermute | solution.py:161
  86.8 9.3 %collective-permute-start.27 = (bf16[64,1536]{1,0:T(8,128)(2,1)S(1)}, bf16[64,1536]{1,0:T(8,128)(2,1)S(1)}, u32[]{:S(2)}, u32[]{:S(2)}) collective-permute-start(bf16[64,1536]{1,0:T(8,128)(2,1)S(1)} %add_convert_fusion.refs_0_), channel_id=1, source_target_pairs={{0,16},{8,24},{16,0},{24,8},{1,17},{9,25},{17,1},{25,9},{2,18},{10... | collective-permute-start | bytes 589832 | tf_op jit(solution)/shard_map/ppermute | solution.py:161
  87.7 10.1 %collective-permute-start.28 = (bf16[64,1536]{1,0:T(8,128)(2,1)S(1)}, bf16[64,1536]{1,0:T(8,128)(2,1)S(1)}, u32[]{:S(2)}, u32[]{:S(2)}) collective-permute-start(bf16[64,1536]{1,0:T(8,128)(2,1)S(1)} %add_convert_fusion.refs_0_), channel_id=1, source_target_pairs={{0,24},{8,16},{16,8},{24,0},{1,25},{9,17},{17,9},{25,1},{2,26},{10... | collective-permute-start | bytes 589832 | tf_op jit(solution)/shard_map/ppermute | solution.py:161
  97.8 5.0 %slice-start.5 = ((s8[9437184]{0:T(1024)(128)(4,1)}), s8[4194304]{0:T(1024)(128)(4,1)S(1)}, s32[]{:S(2)}) async-start(s8[9437184]{0:T(1024)(128)(4,1)} %bitcast.27), calls=%async_computation.5 | async-start | bytes 8388608
  97.8 5.0 %slice-start.6 = ((s8[9437184]{0:T(1024)(128)(4,1)}), s8[4194304]{0:T(1024)(128)(4,1)S(1)}, s32[]{:S(2)}) async-start(s8[9437184]{0:T(1024)(128)(4,1)} %bitcast.27), calls=%async_computation.6 | async-start | bytes 8388608
  100.0 2.8 %slice-start.7 = ((s8[9437184]{0:T(1024)(128)(4,1)}), s8[1048576]{0:T(1024)(128)(4,1)S(1)}, s32[]{:S(2)}) async-start(s8[9437184]{0:T(1024)(128)(4,1)} %bitcast.27), calls=%async_computation.7 | async-start | bytes 2097152
  100.0 2.8 %collective-permute-start.30 = (bf16[256,1536]{1,0:T(8,128)(2,1)S(1)}, bf16[256,1536]{1,0:T(8,128)(2,1)S(1)}, u32[]{:S(2)}, u32[]{:S(2)}) collective-permute-start(bf16[256,1536]{1,0:T(8,128)(2,1)S(1)} %up_projected.3.refs_0_), channel_id=1, source_target_pairs={{0,1},{1,0},{2,3},{3,2},{4,5},{5,4},{6,7},{7,6},{8,9},{9,8},{10,11... | collective-permute-start | bytes 2359304 | tf_op jit(solution)/shard_map/ppermute | solution.py:161
  102.3 3.1 %collective-permute-start.29 = (bf16[256,1536]{1,0:T(8,128)(2,1)S(1)}, bf16[256,1536]{1,0:T(8,128)(2,1)S(1)}, u32[]{:S(2)}, u32[]{:S(2)}) collective-permute-start(bf16[256,1536]{1,0:T(8,128)(2,1)S(1)} %up_projected.2.refs_0_), channel_id=1, source_target_pairs={{0,1},{1,0},{2,3},{3,2},{4,5},{5,4},{6,7},{7,6},{8,9},{9,8},{10,11... | collective-permute-start | bytes 2359304 | tf_op jit(solution)/shard_map/ppermute | solution.py:161
  108.1 7.8 %collective-permute-start.31 = (bf16[64,1536]{1,0:T(8,128)(2,1)S(1)}, bf16[64,1536]{1,0:T(8,128)(2,1)S(1)}, u32[]{:S(2)}, u32[]{:S(2)}) collective-permute-start(bf16[64,1536]{1,0:T(8,128)(2,1)S(1)} %get-tuple-element.26), channel_id=1, source_target_pairs={{0,8},{8,0},{16,24},{24,16},{1,9},{9,1},{17,25},{25,17},{2,10},{10... | collective-permute-start | bytes 589832 | tf_op jit(solution)/shard_map/ppermute | solution.py:161
  109.0 10.8 %collective-permute-start.32 = (bf16[64,1536]{1,0:T(8,128)(2,1)S(1)}, bf16[64,1536]{1,0:T(8,128)(2,1)S(1)}, u32[]{:S(2)}, u32[]{:S(2)}) collective-permute-start(bf16[64,1536]{1,0:T(8,128)(2,1)S(1)} %get-tuple-element.27), channel_id=1, source_target_pairs={{0,16},{8,24},{16,0},{24,8},{1,17},{9,25},{17,1},{25,9},{2,18},{10... | collective-permute-start | bytes 589832 | tf_op jit(solution)/shard_map/ppermute | solution.py:161
  110.5 9.3 %collective-permute-start.33 = (bf16[64,1536]{1,0:T(8,128)(2,1)S(1)}, bf16[64,1536]{1,0:T(8,128)(2,1)S(1)}, u32[]{:S(2)}, u32[]{:S(2)}) collective-permute-start(bf16[64,1536]{1,0:T(8,128)(2,1)S(1)} %get-tuple-element.28), channel_id=1, source_target_pairs={{0,24},{8,16},{16,8},{24,0},{1,25},{9,17},{17,9},{25,1},{2,26},{10... | collective-permute-start | bytes 589832 | tf_op jit(solution)/shard_map/ppermute | solution.py:161
  (1 other events, 1.1 us)

commit v4 on v3

--- a/solution.py
+++ b/solution.py
@@ -153,6 +153,8 @@
 
 
 VMEM_BYTES = 1024 * 1024
+COPY_AT = 1
+LONG = pl.CostEstimate(flops=10**10, bytes_accessed=0, transcendentals=0)
 NO_COST = pl.CostEstimate(flops=0, bytes_accessed=0, transcendentals=0)
 
 
@@ -170,7 +172,8 @@
 
 
 def after_specs(after):
-    return [pl.BlockSpec((16, 128), lambda j: (0, 0)) for _ in after]
+    shapes = [(1,) * (dep.ndim - 2) + (min(16, dep.shape[-2]), 128) for dep in after]
+    return [pl.BlockSpec(shape, lambda j, n=len(shape): (0,) * n) for shape in shapes]
 
 
 def merge_kernel(axis, distance, own_ref, other_ref, *refs):
@@ -197,11 +200,63 @@
     )(piece, other, *after)
 
 
-def assemble_kernel(pieces_ref, out_ref):
-    length = pieces_ref.shape[1]
+def lane_tiles(rows, count, length):
+    return -(-(-(-length // 128)) // (rows // count))
+
+
+def pack_kernel(values_ref, pieces_ref, out_ref):
+    rows, width = values_ref.shape
+    count, length = pieces_ref.shape
+    per = rows // count
+    out_ref[:, :width] = values_ref[...]
+    for tile in range((out_ref.shape[1] - width) // 128):
+        lines = []
+        for row in range(count):
+            for low in range(tile * per * 128, (tile + 1) * per * 128, 128):
+                size = max(0, min(128, length - low))
+                line = jnp.zeros((1, 128 - size), jnp.float32)
+                if size:
+                    part = pieces_ref[row : row + 1, low : low + size]
+                    line = jnp.concatenate([part, line], axis=1) if size < 128 else part
+                lines.append(line)
+        columns = slice(width + tile * 128, width + (tile + 1) * 128)
+        out_ref[:, columns] = jnp.concatenate(lines, axis=0).astype(jnp.bfloat16)
+
+
+def packed(values, pieces):
+    rows, width = values.shape
+    columns = width + 128 * lane_tiles(rows, *pieces.shape)
+    return pl.pallas_call(
+        pack_kernel,
+        out_shape=jax.ShapeDtypeStruct((rows, columns), jnp.bfloat16),
+        compiler_params=pltpu.CompilerParams(vmem_limit_bytes=VMEM_BYTES * 2),
+        cost_estimate=NO_COST,
+        name="packed",
+    )(values, pieces)
+
+
+def assemble_kernel(axis, count, length, *refs):
+    *tile_refs, out_ref, pieces_ref = refs
+    position = lax.axis_index(axis)
+    tiles = [ref[...].astype(jnp.float32) for ref in tile_refs]
+    bit = 1
+    while bit < len(tiles):
+        flip = (position & bit) != 0
+        tiles = [jnp.where(flip, tiles[i ^ bit], tiles[i]) for i in range(len(tiles))]
+        bit *= 2
+    per = tiles[0].shape[0] // count
+    for block, tile in enumerate(tiles):
+        for row in range(count):
+            for low in range(0, length, 128):
+                line = row * per + low // 128 % per
+                columns = low // 128 // per * 128
+                size = min(128, length - low)
+                pieces_ref[block * count + row : block * count + row + 1, low : low + size] = tile[
+                    line : line + 1, columns : columns + size
+                ]
     width = out_ref.shape[1]
     vectors = out_ref.shape[0]
-    halves = pieces_ref.shape[0] * length // (vectors * width)
+    halves = len(tiles) * count * length // (vectors * width)
     for half in range(halves):
 
         @pl.when(lax.axis_index("tensor") == half)
@@ -218,62 +273,72 @@
                 out_ref[vector : vector + 1, :] = jnp.concatenate(parts, axis=1)
 
 
-def assembled(pieces, width):
-    return pl.pallas_call(
-        assemble_kernel,
+def assembled(blocks, axis, count, length, width):
+    rows, columns = blocks[0].shape
+    extra = columns - width
+    return pl.pallas_call(
+        lambda *refs: assemble_kernel(axis, count, length, *refs),
+        grid=(1,),
+        in_specs=[pl.BlockSpec((rows, extra), lambda j: (0, width // extra)) for _ in blocks],
+        out_specs=pl.BlockSpec((6, width), lambda j: (0, 0)),
         out_shape=jax.ShapeDtypeStruct((6, width), jnp.float32),
+        scratch_shapes=[pltpu.VMEM((len(blocks) * count, -(-length // 128) * 128), jnp.float32)],
         compiler_params=pltpu.CompilerParams(vmem_limit_bytes=VMEM_BYTES),
         cost_estimate=NO_COST,
         name="assembled",
-    )(pieces)
-
-
-def row_sums_kernel(values_ref, out_ref, copy_ref):
-    values = values_ref[...].astype(jnp.float32)
-    lane = lax.broadcasted_iota(jnp.int32, out_ref.shape, 1)
-    out_ref[...] = jnp.where(
-        lane < out_ref.shape[1] // 2,
-        jnp.sum(values, axis=-1, keepdims=True),
-        jnp.sum(values * values, axis=-1, keepdims=True),
-    )
-    copy_ref[...] = values_ref[...]
-
-
-def row_sums(values):
-    rows = values.shape[0]
-    return pl.pallas_call(
-        row_sums_kernel,
-        out_shape=[
-            jax.ShapeDtypeStruct((rows, 128), jnp.float32),
-            jax.ShapeDtypeStruct(values.shape, values.dtype),
-        ],
-        compiler_params=pltpu.CompilerParams(vmem_limit_bytes=VMEM_BYTES * 2),
+    )(*blocks)
+
+
+def row_sums_kernel(count, *refs):
+    block_refs, out_ref = refs[:count], refs[-1]
+    rows = block_refs[0].shape[0]
+    for k, block_ref in enumerate(block_refs):
+        values = block_ref[...].astype(jnp.float32)
+        lane = lax.broadcasted_iota(jnp.int32, (rows, out_ref.shape[1]), 1)
+        out_ref[k * rows : (k + 1) * rows, :] = jnp.where(
+            lane < out_ref.shape[1] // 2,
+            jnp.sum(values, axis=-1, keepdims=True),
+            jnp.sum(values * values, axis=-1, keepdims=True),
+        )
+
+
+def row_sums(blocks, width, after):
+    rows = blocks[0].shape[0]
+    whole = lambda *shape: pl.BlockSpec(shape, lambda j: (0, 0))
+    return pl.pallas_call(
+        lambda *refs: row_sums_kernel(len(blocks), *refs),
+        grid=(1,),
+        in_specs=[whole(rows, width)] * len(blocks) + after_specs(after),
+        out_specs=whole(rows * len(blocks), 128),
+        out_shape=jax.ShapeDtypeStruct((rows * len(blocks), 128), jnp.float32),
+        compiler_params=pltpu.CompilerParams(vmem_limit_bytes=VMEM_BYTES * 4),
         cost_estimate=NO_COST,
         name="row_sums",
-    )(values)
-
-
-def centered(values, own, arrived, features):
-    total = own + arrived
+    )(*blocks, *after)
+
+
+def copied_kernel(values_ref, after_ref, out_ref):
+    out_ref[...] = values_ref[...]
+
+
+def copied(values, after, cost):
+    whole = pl.BlockSpec(values.shape, lambda j: (0, 0))
+    return pl.pallas_call(
+        copied_kernel,
+        grid=(1,),
+        in_specs=[whole] + after_specs([after]),
+        out_specs=whole,
+        out_shape=jax.ShapeDtypeStruct(values.shape, values.dtype),
+        compiler_params=pltpu.CompilerParams(vmem_limit_bytes=VMEM_BYTES * 2),
+        cost_estimate=cost,
+        name="copied",
+    )(values, after)
+
+
+def centered(values, total, features):
     average = total[:, :1] / features
     variance = total[:, total.shape[1] // 2 :][:, :1] / features - average * average
     return (values - average) * lax.rsqrt(variance + 1e-06)
-
-
-def standardize_kernel(features, values_ref, own_ref, arrived_ref, out_ref):
-    values = values_ref[...].astype(jnp.float32)
-    out_ref[...] = centered(values, own_ref[...], arrived_ref[...], features).astype(jnp.bfloat16)
-
-
-def standardized(values, features):
-    own, values = row_sums(values)
-    return pl.pallas_call(
-        lambda *refs: standardize_kernel(features, *refs),
-        out_shape=jax.ShapeDtypeStruct(values.shape, jnp.bfloat16),
-        compiler_params=pltpu.CompilerParams(vmem_limit_bytes=VMEM_BYTES * 2),
-        cost_estimate=NO_COST,
-        name="standardized",
-    )(values, own, permuted(own, "tensor", 1))
 
 
 def normalized(values, features):
@@ -295,25 +360,39 @@
     return total
 
 
-def project_kernel(count, *refs):
-    block_refs, (shift_ref, scale_ref, weight_ref) = refs[:count], refs[count : count + 3]
-    out_ref, normed_ref = refs[-2:]
+def project_kernel(count, features, parts, *refs):
+    block_refs = refs[:count]
+    own_ref, arrived_ref, shift_ref, scale_ref, weight_ref = refs[count : count + 5]
+    normed_ref = refs[-1]
 
     @pl.when(pl.program_id(0) == 0)
     def _():
         rows = block_refs[0].shape[0]
         for k, block_ref in enumerate(block_refs):
-            values = block_ref[...].astype(jnp.float32)
+            here = slice(k * rows, (k + 1) * rows)
+            total = own_ref[here, :] + arrived_ref[here, :]
+            values = centered(block_ref[...].astype(jnp.float32), total, features)
             values = values * (1.0 + scale_ref[...]) + shift_ref[...]
-            normed_ref[k * rows : (k + 1) * rows, :] = values.astype(jnp.bfloat16)
-
-    out_ref[...] = jnp.dot(
-        normed_ref[...], weight_ref[0], preferred_element_type=jnp.float32
-    ).astype(jnp.bfloat16)
-
-
-def projected(blocks, shift_row, scale_row, weights, first, half, other, after=()):
-    rows, width = blocks[0].shape
+            normed_ref[here, :] = values.astype(jnp.bfloat16)
+
+    project_part(normed_ref, weight_ref, refs[-1 - parts : -1])
+
+
+def project_part(normed_ref, weight_ref, out_refs):
+    product = jnp.dot(normed_ref[...], weight_ref[0], preferred_element_type=jnp.float32)
+    for k, out_ref in enumerate(out_refs):
+
+        @pl.when(pl.program_id(0) == k)
+        def _(out_ref=out_ref):
+            out_ref[...] = product.astype(jnp.bfloat16)
+
+
+def project_again_kernel(parts, normed_ref, weight_ref, *refs):
+    project_part(normed_ref, weight_ref, refs[-parts:])
+
+
+def projected(blocks, small, weights, first, half, other, after=()):
+    rows, width = blocks[0].shape[0], weights.shape[1]
     all_rows = rows * len(blocks)
     count = weights.shape[0] - first
 
@@ -322,59 +401,90 @@
         return (j + first, 0, 1 - position if other else position)
 
     whole = lambda shape: pl.BlockSpec(shape, lambda j: (0, 0))
-    return pl.pallas_call(
-        lambda *refs: project_kernel(len(blocks), *refs),
+    shapes = [(all_rows, half)] * count + [(all_rows, width)] * bool(small)
+    return pl.pallas_call(
+        (lambda *refs: project_kernel(len(blocks), 2 * width, count, *refs))
+        if small
+        else (lambda *refs: project_again_kernel(count, *refs)),
         grid=(count,),
         in_specs=[whole((rows, width)) for _ in blocks]
-        + [whole((1, width)), whole((1, width)), pl.BlockSpec((1, width, half), columns)]
+        + [whole(array.shape) for array in small]
+        + [pl.BlockSpec((1, width, half), columns)]
         + after_specs(after),
-        out_specs=pl.BlockSpec((all_rows, half), lambda j: (0, j)),
-        out_shape=jax.ShapeDtypeStruct((all_rows, count * half), jnp.bfloat16),
-        scratch_shapes=[pltpu.VMEM((all_rows, width), jnp.bfloat16)],
-        compiler_params=pltpu.CompilerParams(vmem_limit_bytes=VMEM_BYTES * 8),
+        out_specs=[whole(shape) for shape in shapes],
+        out_shape=[jax.ShapeDtypeStruct(shape, jnp.bfloat16) for shape in shapes],
+        compiler_params=pltpu.CompilerParams(vmem_limit_bytes=VMEM_BYTES * 9),
         cost_estimate=NO_COST,
         name="projected",
-    )(*blocks, shift_row, scale_row, weights, *after)
-
-
-def heads_kernel(count, head_size, own_ref, arrived_ref, q_gain_ref, k_gain_ref, *out_refs):
-    half = own_ref.shape[1] // count
-    total = lambda lo: (
-        own_ref[:, lo : lo + head_size].astype(jnp.float32)
-        + arrived_ref[:, lo : lo + head_size].astype(jnp.float32)
-    )
-
-    def normal(lo, gain_ref):
-        values = total(lo)
+    )(*blocks, *small, weights, *after)
+
+
+def staged(weights, after):
+    block = pl.BlockSpec(memory_space=pl.ANY)
+    count, width, columns = weights.shape
+
+    def kernel(weight_ref, after_ref, out_ref, sem):
+        copy = pltpu.make_async_copy(weight_ref, out_ref, sem)
+        copy.start()
+        copy.wait()
+
+    return pl.pallas_call(
+        kernel,
+        in_specs=[block, pl.BlockSpec(memory_space=pltpu.VMEM)],
+        out_specs=pl.BlockSpec(memory_space=pltpu.VMEM),
+        out_shape=pltpu.VMEM(weights.shape, weights.dtype),
+        scratch_shapes=[pltpu.SemaphoreType.DMA],
+        compiler_params=pltpu.CompilerParams(vmem_limit_bytes=VMEM_BYTES * 9),
+        cost_estimate=pl.CostEstimate(
+            flops=0, bytes_accessed=2 * weights.size, transcendentals=0
+        ),
+        name="staged",
+    )(weights, after)
+
+
+def heads_kernel(count, head_size, *refs):
+    own_refs, arrived_refs = refs[:count], refs[count : 2 * count]
+    q_gain_ref, k_gain_ref = refs[2 * count : 2 * count + 2]
+    out_refs = refs[-1:] if count == 2 else refs[-2:]
+    half = own_refs[0].shape[1]
+
+    def total(part, here):
+        return own_refs[part][:, here].astype(jnp.float32) + arrived_refs[part][:, here].astype(
+            jnp.float32
+        )
+
+    def normal(values, gain_ref):
         spread = jnp.mean(values * values, axis=-1, keepdims=True) + 1e-06
         return (values * lax.rsqrt(spread) * gain_ref[...]).astype(jnp.bfloat16)
 
-    for lo in range(0, half, head_size):
+    for low in range(0, half, head_size):
+        here = slice(low, low + head_size)
         if count == 3:
-            out_refs[1][:, lo : lo + head_size] = normal(lo, q_gain_ref)
-        key_lo = (count - 2) * half + lo
-        out_refs[0][:, lo : lo + head_size] = normal(key_lo, k_gain_ref)
-        out_refs[0][:, half + lo : half + lo + head_size] = total(key_lo + half).astype(
+            out_refs[1][:, here] = normal(total(0, here), q_gain_ref)
+        out_refs[0][:, here] = normal(total(count - 2, here), k_gain_ref)
+        out_refs[0][:, half + low : half + low + head_size] = total(count - 1, here).astype(
             jnp.bfloat16
         )
 
 
-def split_heads(own, arrived, q_gain, k_gain, count):
-    rows, columns = own.shape
-    half = columns // count
+def split_heads(own, arrived, q_gain, k_gain, after=()):
+    count = len(own)
+    rows, half = own[0].shape
     head_size = q_gain.shape[0]
-    shapes = [jax.ShapeDtypeStruct((rows, 2 * half), jnp.bfloat16)]
-    if count == 3:
-        shapes.append(jax.ShapeDtypeStruct((rows, half), jnp.bfloat16))
+    widths = [2 * half] if count == 2 else [2 * half, half]
+    whole = lambda *shape: pl.BlockSpec(shape, lambda j: (0, 0))
     return pl.pallas_call(
         lambda *refs: heads_kernel(count, head_size, *refs),
-        out_shape=shapes,
-        compiler_params=pltpu.CompilerParams(vmem_limit_bytes=VMEM_BYTES * 8),
-        cost_estimate=pl.CostEstimate(
-            flops=8 * rows * columns, bytes_accessed=6 * rows * columns, transcendentals=rows * 6
-        ),
+        grid=(1,),
+        in_specs=[whole(rows, half)] * (2 * count)
+        + [whole(1, head_size)] * 2
+        + after_specs(after),
+        out_specs=[whole(rows, width) for width in widths],
+        out_shape=[jax.ShapeDtypeStruct((rows, width), jnp.bfloat16) for width in widths],
+        compiler_params=pltpu.CompilerParams(vmem_limit_bytes=VMEM_BYTES * 5),
+        cost_estimate=NO_COST,
         name="split_heads",
-    )(own, arrived, q_gain[None, :], k_gain[None, :])
+    )(*own, *arrived, q_gain[None, :], k_gain[None, :], *after)
 
 
 def attention_kernel(head_size, query_ref, *refs):
@@ -565,7 +675,7 @@
 ):
     stages = [
         (axis, 1 << bit)
-        for axis in ("tensor", "blk", "ulysses")
+        for axis in ("tensor", "blk")
         for bit in range(lax.axis_size(axis).bit_length() - 1)
     ]
     rows, width = tokens.shape
@@ -574,37 +684,40 @@
     half = qkv_weight.shape[2] // 2
     blocks_z = lax.axis_size("blk")
 
-    normal = standardized(tokens, features)
-    remote = {0: normal}
-    for k in range(2, blocks_z):
-        remote[k] = permuted(remote[k - 1] if k % 2 else normal, "blk", 1 if k % 2 else k)
-    chunks = [from_all(remote[k], "ulysses") for k in sorted(remote)]
-
     activated = jax.nn.silu(cond.astype(jnp.float32)).astype(jnp.bfloat16)
     pieces = jnp.dot(activated[None, :], mod_weight, preferred_element_type=jnp.float32)
-    after = {("blk", 1): [normal], ("blk", 2): chunks[0][1:3], ("ulysses", 1): chunks[0][3:]}
-    after[("ulysses", 2)] = [remote[k] for k in remote if k > 0 and k % 2 == 0]
+    weights = jnp.moveaxis(qkv_weight, 1, 0)
+    start = copied(tokens, pieces, NO_COST)
+    remote = [permuted(start, "blk", k) for k in range(2, blocks_z, 2)]
     for stage in stages:
-        pieces = doubled_once(pieces, *stage, after.get(stage, []))
-    own_mod = assembled(pieces, width)
-    weights = jnp.moveaxis(qkv_weight, 1, 0)
-    shift_row, scale_row = own_mod[0:1], own_mod[1:2]
-
-    queries, kv_parts = None, []
+        after = remote if stage == ("blk", 2) else []
+        pieces = doubled_once(pieces, *stage, after)
+    own = packed(tokens, pieces)
+    weights = staged(pltpu.with_memory_space_constraint(weights, pltpu.HBM), own)
+    chunks = [from_all(own, "ulysses")]
+    chunks += [from_all(block, "ulysses") for block in remote]
+    own_mod = assembled(chunks[0], "ulysses", *pieces.shape, width)
+    mod_rows = [own_mod[0:1], own_mod[1:2]]
+
+    far = [block for blocks in chunks[1:] for block in blocks[1:]]
+    kv_parts = []
     for index, blocks in enumerate(chunks):
-        first = 0 if index == 0 else 1
-        after = [kv_parts[-1]] if index == 2 else []
-        if index == len(chunks) - 1 and index > 0:
-            after = after + [kv_parts[1]]
-        common = (shift_row, scale_row, weights, first, half)
-        arrived = permuted(projected(blocks, *common, True, after), "tensor", 1)
-        own = projected(blocks, *common, False)
-        outs = split_heads(own, arrived, q_gain, k_gain, 3 - first)
+        first = min(index, 1)
+        after = [[], [], far]
+        if index:
+            after = [[own[0]], [kv_parts[0]], []]
+        sums = row_sums(blocks, width, after[0])
+        small = [sums, permuted(sums, "tensor", 1), *mod_rows]
+        *partial, normed = projected(blocks, small, weights, first, half, True, after[1])
+        arrived = [permuted(part, "tensor", 1) for part in partial]
+        own = projected([normed], [], weights, first, half, False)
+        outs = split_heads(own, arrived, q_gain, k_gain, after[2])
         kv_parts.append(outs[0])
         if index == 0:
             queries = outs[1]
-            if blocks_z > 1:
-                kv_parts.append(permuted(outs[0], "blk", 1))
+        if blocks_z > 1:
+            arrived = permuted(outs[0], "blk", 1)
+            kv_parts.append(arrived if index else copied(arrived, arrived, LONG))
 
     context = attention(queries, kv_parts, head_size)
     partial = out_projected(context, permuted(context, "tensor", 1), out_weight, rows)

time: 121 us -> 113 us (0.934)
  starting transfers between devices: 34.2 us -> 30.5 us
  local copies, waits for them, and re-layouts: 4.17 us -> 1.21 us
  waiting for transfers between devices: 53 us -> 51.4 us
    ppermute x34 -> x32, starting transfers between devices: 34.2 us -> 30.5 us  [permuted(): return lax.ppermute(values, axis, [(i, i ^ distance) for i in range(size)])]
    unnamed x30 -> x22, local copies, waits for them, and re-layouts: 4.16 us -> 1.2 us
    ppermute x34 -> x32, waiting for transfers between devices: 53 us -> 51.4 us  [permuted(): return lax.ppermute(values, axis, [(i, i ^ distance) for i in range(size)])]
    pallas_call x12 -> x13, Pallas kernels: 12.7 us -> 12.8 us  [the longest x4 8.37 us: projected(): pl.pallas_call((lambda *refs: project_kernel(len(blocks), 2 * width, coun...]
  transfers between devices with their start and end apart: 34 -> 32, of which waited for: 20 -> 17; matrix products, arithmetic and copies ran while one was open for 1% -> 0% of each run, Pallas kernels for 11% -> 15%
where the time goes in v4:
time: 113 us; the launch traced here: 112 us
  waiting for transfers between devices  51.4 us (45%)
  starting transfers between devices  30.5 us (27%)
  Pallas kernels  25.7 us (23%)
  other arithmetic  2.23 us (2%)
  local copies, waits for them, and re-layouts  1.21 us (1%)
    ppermute x32, waiting for transfers between devices, permuted(): return lax.ppermute(values, axis, [(i, i ^ distance) for i in range(size)])  51.4 us
    ppermute x32, starting transfers between devices, permuted(): return lax.ppermute(values, axis, [(i, i ^ distance) for i in range(size)])  30.5 us
    pallas_call x4, Pallas kernels, projected(): pl.pallas_call((lambda *refs: project_kernel(len(blocks), 2 * width, coun...  8.37 us
    pallas_call x2, Pallas kernels, down_projected(): pl.pallas_call(lambda *refs: down_kernel(last, *refs), grid=(columns // t...  5.21 us
    pallas_call x2, Pallas kernels, up_projected(): pl.pallas_call(up_kernel, grid=(columns // tile,), in_specs=[pl.BlockSpec...  4.35 us
    pallas_call x1, Pallas kernels, staged(): pl.pallas_call(kernel, in_specs=[block, pl.BlockSpec(memory_space=pltpu.V...  3.02 us
  transfers between devices with their start and end apart: 32, of which 17 were waited for; matrix products, arithmetic and copies ran while one was open for 0% of the time, Pallas kernels for 15%

profile of v4, /device:TPU:0, one launch (start us, length us, event | category | flops | bytes accessed | tf_op | source)
XLA Modules:
  0.0 112.4 jit_solution(9134775528748779096)
XLA Ops:
  0.0 0.9 fusion.3
  0.9 1.1 %copy-done = bf16[3072,576]{0,1:T(8,128)(2,1)S(1)} copy-done((bf16[3072,576]{0,1:T(8,128)(2,1)S(1)}, bf16[3072,576]{0,1:T(8,128)(2,1)}, u32[]{:S(2)}) %copy-start) | copy-done | bytes 3538968
  2.0 1.0 fusion.9.refs_0_.after_ref
  3.1 4.1 %collective-permute-start.3 = (bf16[64,1536]{1,0:T(8,128)(2,1)S(1)}, bf16[64,1536]{1,0:T(8,128)(2,1)S(1)}, u32[]{:S(2)}, u32[]{:S(2)}) collective-permute-start(bf16[64,1536]{1,0:T(8,128)(2,1)S(1)} %copied.2), channel_id=1, source_target_pairs={{0,4},{2,6},{4,0},{6,2},{1,5},{3,7},{5,1},{7,3},{8,12},{10,14},{12... | collective-permute-start | bytes 589832 | tf_op jit(solution)/shard_map/ppermute | solution.py:163
  7.2 1.2 %collective-permute-done.refs_1_ = f32[1,576]{1,0:T(1,128)S(1)} collective-permute-done((f32[1,576]{1,0:T(1,128)S(1)}, f32[1,576]{1,0:T(1,128)S(1)}, u32[]{:S(2)}, u32[]{:S(2)}) %collective-permute-start) | collective-permute-done | bytes 2336 | tf_op jit(solution)/shard_map/ppermute | solution.py:163
  8.3 1.6 %collective-permute-start.1 = (f32[2,576]{1,0:T(2,128)S(1)}, f32[2,576]{1,0:T(2,128)S(1)}, u32[]{:S(2)}, u32[]{:S(2)}) collective-permute-start(f32[2,576]{1,0:T(2,128)S(1)} %merged.3.refs_0_), channel_id=1, source_target_pairs={{0,2},{2,0},{4,6},{6,4},{1,3},{3,1},{5,7},{7,5},{8,10},{10,8},{12,... | collective-permute-start | bytes 13832 | tf_op jit(solution)/shard_map/ppermute | solution.py:163
  9.9 2.0 %collective-permute-done.1.refs_1_ = f32[2,576]{1,0:T(2,128)S(1)} collective-permute-done((f32[2,576]{1,0:T(2,128)S(1)}, f32[2,576]{1,0:T(2,128)S(1)}, u32[]{:S(2)}, u32[]{:S(2)}) %collective-permute-start.1) | collective-permute-done | bytes 4640 | tf_op jit(solution)/shard_map/ppermute | solution.py:163
  12.0 2.0 %collective-permute-start.2 = (f32[4,576]{1,0:T(4,128)S(1)}, f32[4,576]{1,0:T(4,128)S(1)}, u32[]{:S(2)}, u32[]{:S(2)}) collective-permute-start(f32[4,576]{1,0:T(4,128)S(1)} %merged.4.refs_0_), channel_id=1, source_target_pairs={{0,4},{2,6},{4,0},{6,2},{1,5},{3,7},{5,1},{7,3},{8,12},{10,14},{12... | collective-permute-start | bytes 27656 | tf_op jit(solution)/shard_map/ppermute | solution.py:163
  13.9 2.7 %collective-permute-done.2.refs_1_ = f32[4,576]{1,0:T(4,128)S(1)} collective-permute-done((f32[4,576]{1,0:T(4,128)S(1)}, f32[4,576]{1,0:T(4,128)S(1)}, u32[]{:S(2)}, u32[]{:S(2)}) %collective-permute-start.2) | collective-permute-done | bytes 9248 | tf_op jit(solution)/shard_map/ppermute | solution.py:163
  16.7 1.6 %collective-permute-start.4 = (bf16[64,1664]{1,0:T(8,128)(2,1)S(1)}, bf16[64,1664]{1,0:T(8,128)(2,1)S(1)}, u32[]{:S(2)}, u32[]{:S(2)}) collective-permute-start(bf16[64,1664]{1,0:T(8,128)(2,1)S(1)} %packed.1.refs_0_.after_ref), channel_id=1, source_target_pairs={{0,8},{8,0},{16,24},{24,16},{1,9},{9,1},{17,25},{25,17},{2,10},{10... | collective-permute-start | bytes 638984 | tf_op jit(solution)/shard_map/ppermute | solution.py:163
  18.3 1.5 %collective-permute-start.5 = (bf16[64,1664]{1,0:T(8,128)(2,1)S(1)}, bf16[64,1664]{1,0:T(8,128)(2,1)S(1)}, u32[]{:S(2)}, u32[]{:S(2)}) collective-permute-start(bf16[64,1664]{1,0:T(8,128)(2,1)S(1)} %packed.1.refs_0_.after_ref), channel_id=1, source_target_pairs={{0,16},{8,24},{16,0},{24,8},{1,17},{9,25},{17,1},{25,9},{2,18},{10... | collective-permute-start | bytes 638984 | tf_op jit(solution)/shard_map/ppermute | solution.py:163
  20.2 3.0 %staged.1.refs_8_.refs_1_ = bf16[3,1536,768]{2,1,0:T(8,128)(2,1)S(1)} custom-call(bf16[3,1536,768]{2,1,0:T(8,128)(2,1)} %bitcast.25, bf16[64,1664]{1,0:T(8,128)(2,1)S(1)} %packed.1.refs_0_.after_ref), custom_call_target="tpu_custom_call" | custom-call | bytes 7077888 | tf_op jit(solution)/shard_map/staged/pallas_call | solution.py:431
  23.2 1.6 %collective-permute-start.11 = (bf16[64,1536]{1,0:T(8,128)(2,1)S(1)}, bf16[64,1536]{1,0:T(8,128)(2,1)S(1)}, u32[]{:S(2)}, u32[]{:S(2)}) collective-permute-start(bf16[64,1536]{1,0:T(8,128)(2,1)S(1)} %collective-permute-done.3.refs_2_.refs_0_), channel_id=1, source_target_pairs={{0,8},{8,0},{16,24},{24,16},{1,9},{9,1},{17,25},{25,17},{2,10},{10... | collective-permute-start | bytes 589832 | tf_op jit(solution)/shard_map/ppermute | solution.py:163
  24.8 1.5 %collective-permute-start.12 = (bf16[64,1536]{1,0:T(8,128)(2,1)S(1)}, bf16[64,1536]{1,0:T(8,128)(2,1)S(1)}, u32[]{:S(2)}, u32[]{:S(2)}) collective-permute-start(bf16[64,1536]{1,0:T(8,128)(2,1)S(1)} %collective-permute-done.3.refs_2_.refs_0_), channel_id=1, source_target_pairs={{0,16},{8,24},{16,0},{24,8},{1,17},{9,25},{17,1},{25,9},{2,18},{10... | collective-permute-start | bytes 589832 | tf_op jit(solution)/shard_map/ppermute | solution.py:163
  26.4 1.0 collective-permute-start.13
  27.4 0.6 collective-permute-done.5.refs_2_
  28.0 2.5 %collective-permute-done.6.refs_3_ = bf16[64,1664]{1,0:T(8,128)(2,1)S(1)} collective-permute-done((bf16[64,1664]{1,0:T(8,128)(2,1)S(1)}, bf16[64,1664]{1,0:T(8,128)(2,1)S(1)}, u32[]{:S(2)}, u32[]{:S(2)}) %collective-permute-start.6) | collective-permute-done | bytes 213024 | tf_op jit(solution)/shard_map/ppermute | solution.py:163
  31.1 1.1 collective-permute-done.7.refs_5_
  32.2 2.8 %projected.4 = (bf16[256,384]{1,0:T(8,128)(2,1)S(1)}, bf16[256,384]{1,0:T(8,128)(2,1)S(1)}, bf16[256,384]{1,0:T(8,128)(2,1)S(1)}, bf16[256,1536]{1,0:T(8,128)(2,1)S(1)}) custom-call(bf16[64,1664]{1,0:T(8,128)(2,1)S(1)} %packed.1.refs_0_.after_ref, bf16[64,1664]{1,0:T(8,128)(2,1)S(1)} %collective-permute-done.4.refs_1_, ...), custom_call_target="tpu_custom_call" | custom-call | tf_op jit(solution)/shard_map/projected/pallas_call | solution.py:405
  35.7 2.2 %projected.5 = (bf16[256,384]{1,0:T(8,128)(2,1)S(1)}, bf16[256,384]{1,0:T(8,128)(2,1)S(1)}, bf16[256,384]{1,0:T(8,128)(2,1)S(1)}) custom-call(bf16[256,1536]{1,0:T(8,128)(2,1)S(1)} %get-tuple-element.27.refs_0_, bf16[3,1536,768]{2,1,0:T(8,128)(2,1)S(1)} %staged.1.refs_8_.refs_1_), custom_call_target="tpu_custom_call" | custom-call | tf_op jit(solution)/shard_map/projected/pallas_call | solution.py:405
  38.3 2.0 %collective-permute-start.14 = (bf16[256,768]{1,0:T(8,128)(2,1)S(1)}, bf16[256,768]{1,0:T(8,128)(2,1)S(1)}, u32[]{:S(2)}, u32[]{:S(2)}) collective-permute-start(bf16[256,768]{1,0:T(8,128)(2,1)S(1)} %get-tuple-element.35.refs_9_.refs_1_), channel_id=1, source_target_pairs={{0,2},{2,0},{4,6},{6,4},{1,3},{3,1},{5,7},{7,5},{8,10},{10,8},{12,... | collective-permute-start | bytes 1179656 | tf_op jit(solution)/shard_map/ppermute | solution.py:163
  40.8 1.3 %collective-permute-done.15.refs_5_ = f32[256,128]{1,0:T(8,128)S(1)} collective-permute-done((f32[256,128]{1,0:T(8,128)S(1)}, f32[256,128]{1,0:T(8,128)S(1)}, u32[]{:S(2)}, u32[]{:S(2)}) %collective-permute-start.15) | collective-permute-done | bytes 131104 | tf_op jit(solution)/shard_map/ppermute | solution.py:163
  42.0 1.9 %projected.6 = (bf16[256,384]{1,0:T(8,128)(2,1)S(1)}, bf16[256,384]{1,0:T(8,128)(2,1)S(1)}, bf16[256,1536]{1,0:T(8,128)(2,1)S(1)}) custom-call(bf16[64,1536]{1,0:T(8,128)(2,1)S(1)} %collective-permute-done.3.refs_2_.refs_0_, bf16[64,1536]{1,0:T(8,128)(2,1)S(1)} %collective-permute-done.11.refs_8_.refs_1_, ...), custom_call_target="tpu_custom_call" | custom-call | tf_op jit(solution)/shard_map/projected/pallas_call | solution.py:405
  44.5 1.5 %projected.7 = (bf16[256,384]{1,0:T(8,128)(2,1)S(1)}, bf16[256,384]{1,0:T(8,128)(2,1)S(1)}) custom-call(bf16[256,1536]{1,0:T(8,128)(2,1)S(1)} %get-tuple-element.36.refs_0_, bf16[3,1536,768]{2,1,0:T(8,128)(2,1)S(1)} %staged.1.refs_8_.refs_1_), custom_call_target="tpu_custom_call" | custom-call | tf_op jit(solution)/shard_map/projected/pallas_call | solution.py:405
  46.5 3.8 %collective-permute-done.14.values_ref.after_ref = bf16[256,768]{1,0:T(8,128)(2,1)S(1)} collective-permute-done((bf16[256,768]{1,0:T(8,128)(2,1)S(1)}, bf16[256,768]{1,0:T(8,128)(2,1)S(1)}, u32[]{:S(2)}, u32[]{:S(2)}) %collective-permute-start.14) | collective-permute-done | bytes 393248 | tf_op jit(solution)/shard_map/ppermute | solution.py:163
  50.4 8.0 %collective-permute-done.18.refs_4_ = bf16[256,768]{1,0:T(8,128)(2,1)S(1)} collective-permute-done((bf16[256,768]{1,0:T(8,128)(2,1)S(1)}, bf16[256,768]{1,0:T(8,128)(2,1)S(1)}, u32[]{:S(2)}, u32[]{:S(2)}) %collective-permute-start.18) | collective-permute-done | bytes 393248 | tf_op jit(solution)/shard_map/ppermute | solution.py:163
  58.4 1.6 %attention.1.own_ref = bf16[256,384]{1,0:T(8,128)(2,1)S(1)} custom-call(bf16[256,384]{1,0:T(8,128)(2,1)S(1)} %get-tuple-element.34.refs_0_, bf16[256,768]{1,0:T(8,128)(2,1)S(1)} %get-tuple-element.35.refs_9_.refs_1_, bf16[256,768]{1,0:T(8,128)(2,1)S(1)} %copied.3.refs_2_, bf16[256,768]{1,0:T(8,128)(2,1)S(1)} %split_heads.3.refs_3_, ...), custom_call_target="tpu_custom_call" | custom-call | flops 402653184 | bytes 1572864 | tf_op jit(solution)/shard_map/attention/pallas_call | solution.py:524
  60.1 1.4 %collective-permute-done.19.arrived_ref = bf16[256,384]{1,0:T(8,128)(2,1)S(1)} collective-permute-done((bf16[256,384]{1,0:T(8,128)(2,1)S(1)}, bf16[256,384]{1,0:T(8,128)(2,1)S(1)}, u32[]{:S(2)}, u32[]{:S(2)}) %collective-permute-start.19) | collective-permute-done | bytes 196640 | tf_op jit(solution)/shard_map/ppermute | solution.py:163
  61.6 1.7 %out_projected.1 = (bf16[64,1536]{1,0:T(8,128)(2,1)S(1)}, bf16[64,1536]{1,0:T(8,128)(2,1)S(1)}, bf16[64,1536]{1,0:T(8,128)(2,1)S(1)}, bf16[64,1536]{1,0:T(8,128)(2,1)S(1)}) custom-call(bf16[256,384]{1,0:T(8,128)(2,1)S(1)} %attention.1.own_ref, bf16[256,384]{1,0:T(8,128)(2,1)S(1)} %collective-permute-done.19.arrived_ref, bf16[768,1536]{1,0:T(8,128)(2,1)S(1)} %copy-done.1, ...), custom_call_target="tpu_custom_call" | custom-call | tf_op jit(solution)/shard_map/out_projected/pallas_call | solution.py:556
  63.2 1.6 %collective-permute-start.20 = (bf16[64,1536]{1,0:T(8,128)(2,1)S(1)}, bf16[64,1536]{1,0:T(8,128)(2,1)S(1)}, u32[]{:S(2)}, u32[]{:S(2)}) collective-permute-start(bf16[64,1536]{1,0:T(8,128)(2,1)S(1)} %get-tuple-element.42), channel_id=1, source_target_pairs={{0,8},{8,0},{16,24},{24,16},{1,9},{9,1},{17,25},{25,17},{2,10},{10... | collective-permute-start | bytes 589832 | tf_op jit(solution)/shard_map/ppermute | solution.py:163
  65.3 1.5 %collective-permute-start.22 = (bf16[64,1536]{1,0:T(8,128)(2,1)S(1)}, bf16[64,1536]{1,0:T(8,128)(2,1)S(1)}, u32[]{:S(2)}, u32[]{:S(2)}) collective-permute-start(bf16[64,1536]{1,0:T(8,128)(2,1)S(1)} %get-tuple-element.44), channel_id=1, source_target_pairs={{0,24},{8,16},{16,8},{24,0},{1,25},{9,17},{17,9},{25,1},{2,26},{10... | collective-permute-start | bytes 589832 | tf_op jit(solution)/shard_map/ppermute | solution.py:163
  66.8 4.3 %collective-permute-done.20 = bf16[64,1536]{1,0:T(8,128)(2,1)S(1)} collective-permute-done((bf16[64,1536]{1,0:T(8,128)(2,1)S(1)}, bf16[64,1536]{1,0:T(8,128)(2,1)S(1)}, u32[]{:S(2)}, u32[]{:S(2)}) %collective-permute-start.20) | collective-permute-done | bytes 196640 | tf_op jit(solution)/shard_map/ppermute | solution.py:163
  71.1 4.6 %collective-permute-done.21 = bf16[64,1536]{1,0:T(8,128)(2,1)S(1)} collective-permute-done((bf16[64,1536]{1,0:T(8,128)(2,1)S(1)}, bf16[64,1536]{1,0:T(8,128)(2,1)S(1)}, u32[]{:S(2)}, u32[]{:S(2)}) %collective-permute-start.21) | collective-permute-done | bytes 196640 | tf_op jit(solution)/shard_map/ppermute | solution.py:163
  76.1 1.1 %collective-permute-done.23 = f32[2,64]{1,0:T(2,128)S(1)} collective-permute-done((f32[2,64]{1,0:T(2,128)S(1)}, f32[2,64]{1,0:T(2,128)S(1)}, u32[]{:S(2)}, u32[]{:S(2)}) %collective-permute-start.23) | collective-permute-done | bytes 544 | tf_op jit(solution)/shard_map/ppermute | solution.py:163
  77.4 0.6 collective-permute-start.24
  77.9 1.2 %collective-permute-start.25 = (bf16[64,1536]{1,0:T(8,128)(2,1)S(1)}, bf16[64,1536]{1,0:T(8,128)(2,1)S(1)}, u32[]{:S(2)}, u32[]{:S(2)}) collective-permute-start(bf16[64,1536]{1,0:T(8,128)(2,1)S(1)} %add_convert_fusion.refs_0_), channel_id=1, source_target_pairs={{0,16},{8,24},{16,0},{24,8},{1,17},{9,25},{17,1},{25,9},{2,18},{10... | collective-permute-start | bytes 589832 | tf_op jit(solution)/shard_map/ppermute | solution.py:163
  79.2 1.8 %collective-permute-start.26 = (bf16[64,1536]{1,0:T(8,128)(2,1)S(1)}, bf16[64,1536]{1,0:T(8,128)(2,1)S(1)}, u32[]{:S(2)}, u32[]{:S(2)}) collective-permute-start(bf16[64,1536]{1,0:T(8,128)(2,1)S(1)} %add_convert_fusion.refs_0_), channel_id=1, source_target_pairs={{0,24},{8,16},{16,8},{24,0},{1,25},{9,17},{17,9},{25,1},{2,26},{10... | collective-permute-start | bytes 589832 | tf_op jit(solution)/shard_map/ppermute | solution.py:163
  80.9 4.3 %collective-permute-done.24.refs_1_ = bf16[64,1536]{1,0:T(8,128)(2,1)S(1)} collective-permute-done((bf16[64,1536]{1,0:T(8,128)(2,1)S(1)}, bf16[64,1536]{1,0:T(8,128)(2,1)S(1)}, u32[]{:S(2)}, u32[]{:S(2)}) %collective-permute-start.24) | collective-permute-done | bytes 196640 | tf_op jit(solution)/shard_map/ppermute | solution.py:163
  85.2 3.7 %collective-permute-done.25.refs_2_ = bf16[64,1536]{1,0:T(8,128)(2,1)S(1)} collective-permute-done((bf16[64,1536]{1,0:T(8,128)(2,1)S(1)}, bf16[64,1536]{1,0:T(8,128)(2,1)S(1)}, u32[]{:S(2)}, u32[]{:S(2)}) %collective-permute-start.25) | collective-permute-done | bytes 196640 | tf_op jit(solution)/shard_map/ppermute | solution.py:163
  88.9 2.2 %up_projected.3.refs_0_ = bf16[256,1536]{1,0:T(8,128)(2,1)S(1)} custom-call(bf16[64,1536]{1,0:T(8,128)(2,1)S(1)} %add_convert_fusion.refs_0_, bf16[64,1536]{1,0:T(8,128)(2,1)S(1)} %collective-permute-done.24.refs_1_, bf16[64,1536]{1,0:T(8,128)(2,1)S(1)} %collective-permute-done.25.refs_2_, bf16[64,1536]{1,0:T(8,128)(2,1)S(1)} %collective-permute-done.26.refs_3_, ...), custom_call_target="tpu_custom_call" | custom-call | flops 1207959552 | bytes 4718592 | tf_op jit(solution)/shard_map/up_projected/pallas_call | solution.py:593
  91.2 2.2 %up_projected.2.refs_0_ = bf16[256,1536]{1,0:T(8,128)(2,1)S(1)} custom-call(bf16[64,1536]{1,0:T(8,128)(2,1)S(1)} %add_convert_fusion.refs_0_, bf16[64,1536]{1,0:T(8,128)(2,1)S(1)} %collective-permute-done.24.refs_1_, bf16[64,1536]{1,0:T(8,128)(2,1)S(1)} %collective-permute-done.25.refs_2_, bf16[64,1536]{1,0:T(8,128)(2,1)S(1)} %collective-permute-done.26.refs_3_, ...), custom_call_target="tpu_custom_call" | custom-call | flops 1207959552 | bytes 4718592 | tf_op jit(solution)/shard_map/up_projected/pallas_call | solution.py:593
  94.0 2.5 %down_projected.2.refs_3_ = f32[256,1536]{1,0:T(8,128)S(1)} custom-call(bf16[256,1536]{1,0:T(8,128)(2,1)S(1)} %up_projected.3.refs_0_, bf16[256,1536]{1,0:T(8,128)(2,1)S(1)} %collective-permute-done.28.refs_1_, bf16[3072,1536]{1,0:T(8,128)(2,1)S(1)} %bitcast.20), custom_call_target="tpu_custom_call" | custom-call | flops 1207959552 | bytes 4718592 | tf_op jit(solution)/shard_map/down_projected/pallas_call | solution.py:651
  96.5 2.7 %down_projected.3 = (bf16[64,1536]{1,0:T(8,128)(2,1)S(1)}, bf16[64,1536]{1,0:T(8,128)(2,1)S(1)}, bf16[64,1536]{1,0:T(8,128)(2,1)S(1)}, bf16[64,1536]{1,0:T(8,128)(2,1)S(1)}) custom-call(bf16[256,1536]{1,0:T(8,128)(2,1)S(1)} %up_projected.2.refs_0_, bf16[256,1536]{1,0:T(8,128)(2,1)S(1)} %collective-permute-done.27.refs_1_, bf16[3072,1536]{1,0:T(8,128)(2,1)S(1)} %bitcast.20, ...), custom_call_target="tpu_custom_call" | custom-call | flops 1207959552 | bytes 4718592 | tf_op jit(solution)/shard_map/down_projected/pallas_call | solution.py:651
  99.2 1.6 %collective-permute-start.29 = (bf16[64,1536]{1,0:T(8,128)(2,1)S(1)}, bf16[64,1536]{1,0:T(8,128)(2,1)S(1)}, u32[]{:S(2)}, u32[]{:S(2)}) collective-permute-start(bf16[64,1536]{1,0:T(8,128)(2,1)S(1)} %get-tuple-element.46), channel_id=1, source_target_pairs={{0,8},{8,0},{16,24},{24,16},{1,9},{9,1},{17,25},{25,17},{2,10},{10... | collective-permute-start | bytes 589832 | tf_op jit(solution)/shard_map/ppermute | solution.py:163
  101.3 1.5 %collective-permute-start.31 = (bf16[64,1536]{1,0:T(8,128)(2,1)S(1)}, bf16[64,1536]{1,0:T(8,128)(2,1)S(1)}, u32[]{:S(2)}, u32[]{:S(2)}) collective-permute-start(bf16[64,1536]{1,0:T(8,128)(2,1)S(1)} %get-tuple-element.48), channel_id=1, source_target_pairs={{0,24},{8,16},{16,8},{24,0},{1,25},{9,17},{17,9},{25,1},{2,26},{10... | collective-permute-start | bytes 589832 | tf_op jit(solution)/shard_map/ppermute | solution.py:163
  102.7 4.3 %collective-permute-done.29 = bf16[64,1536]{1,0:T(8,128)(2,1)S(1)} collective-permute-done((bf16[64,1536]{1,0:T(8,128)(2,1)S(1)}, bf16[64,1536]{1,0:T(8,128)(2,1)S(1)}, u32[]{:S(2)}, u32[]{:S(2)}) %collective-permute-start.29) | collective-permute-done | bytes 196640 | tf_op jit(solution)/shard_map/ppermute | solution.py:163
  107.0 4.5 %collective-permute-done.30 = bf16[64,1536]{1,0:T(8,128)(2,1)S(1)} collective-permute-done((bf16[64,1536]{1,0:T(8,128)(2,1)S(1)}, bf16[64,1536]{1,0:T(8,128)(2,1)S(1)}, u32[]{:S(2)}, u32[]{:S(2)}) %collective-permute-start.30) | collective-permute-done | bytes 196640 | tf_op jit(solution)/shard_map/ppermute | solution.py:163
  111.5 0.9 multiply_add_fusion
  (73 shorter events, 5.9 us)
Async XLA Ops:
  0.0 2.0 %copy-start = (bf16[3072,576]{0,1:T(8,128)(2,1)S(1)}, bf16[3072,576]{0,1:T(8,128)(2,1)}, u32[]{:S(2)}) copy-start(bf16[3072,576]{0,1:T(8,128)(2,1)} %param.11) | copy-start | bytes 10616836
  0.0 3.0 %copy-start.2 = (bf16[64,1536]{1,0:T(8,128)(2,1)S(1)}, bf16[64,1536]{1,0:T(8,128)(2,1)}, u32[]{:S(2)}) copy-start(bf16[64,1536]{1,0:T(8,128)(2,1)} %values_ref.3) | copy-start | bytes 589828
  3.1 13.5 %collective-permute-start.3 = (bf16[64,1536]{1,0:T(8,128)(2,1)S(1)}, bf16[64,1536]{1,0:T(8,128)(2,1)S(1)}, u32[]{:S(2)}, u32[]{:S(2)}) collective-permute-start(bf16[64,1536]{1,0:T(8,128)(2,1)S(1)} %copied.2), channel_id=1, source_target_pairs={{0,4},{2,6},{4,0},{6,2},{1,5},{3,7},{5,1},{7,3},{8,12},{10,14},{12... | collective-permute-start | bytes 589832 | tf_op jit(solution)/shard_map/ppermute | solution.py:163
  7.2 1.2 %collective-permute-start = (f32[1,576]{1,0:T(1,128)S(1)}, f32[1,576]{1,0:T(1,128)S(1)}, u32[]{:S(2)}, u32[]{:S(2)}) collective-permute-start(f32[1,576]{1,0:T(1,128)S(1)} %fusion.9.refs_0_.after_ref), channel_id=1, source_target_pairs={{0,1},{1,0},{2,3},{3,2},{4,5},{5,4},{6,7},{7,6},{8,9},{9,8},{10,11... | collective-permute-start | bytes 6920 | tf_op jit(solution)/shard_map/ppermute | solution.py:163
  8.3 3.6 %collective-permute-start.1 = (f32[2,576]{1,0:T(2,128)S(1)}, f32[2,576]{1,0:T(2,128)S(1)}, u32[]{:S(2)}, u32[]{:S(2)}) collective-permute-start(f32[2,576]{1,0:T(2,128)S(1)} %merged.3.refs_0_), channel_id=1, source_target_pairs={{0,2},{2,0},{4,6},{6,4},{1,3},{3,1},{5,7},{7,5},{8,10},{10,8},{12,... | collective-permute-start | bytes 13832 | tf_op jit(solution)/shard_map/ppermute | solution.py:163
  12.0 4.6 %collective-permute-start.2 = (f32[4,576]{1,0:T(4,128)S(1)}, f32[4,576]{1,0:T(4,128)S(1)}, u32[]{:S(2)}, u32[]{:S(2)}) collective-permute-start(f32[4,576]{1,0:T(4,128)S(1)} %merged.4.refs_0_), channel_id=1, source_target_pairs={{0,4},{2,6},{4,0},{6,2},{1,5},{3,7},{5,1},{7,3},{8,12},{10,14},{12... | collective-permute-start | bytes 27656 | tf_op jit(solution)/shard_map/ppermute | solution.py:163
  16.7 9.7 %collective-permute-start.4 = (bf16[64,1664]{1,0:T(8,128)(2,1)S(1)}, bf16[64,1664]{1,0:T(8,128)(2,1)S(1)}, u32[]{:S(2)}, u32[]{:S(2)}) collective-permute-start(bf16[64,1664]{1,0:T(8,128)(2,1)S(1)} %packed.1.refs_0_.after_ref), channel_id=1, source_target_pairs={{0,8},{8,0},{16,24},{24,16},{1,9},{9,1},{17,25},{25,17},{2,10},{10... | collective-permute-start | bytes 638984 | tf_op jit(solution)/shard_map/ppermute | solution.py:163
  18.3 9.7 %collective-permute-start.5 = (bf16[64,1664]{1,0:T(8,128)(2,1)S(1)}, bf16[64,1664]{1,0:T(8,128)(2,1)S(1)}, u32[]{:S(2)}, u32[]{:S(2)}) collective-permute-start(bf16[64,1664]{1,0:T(8,128)(2,1)S(1)} %packed.1.refs_0_.after_ref), channel_id=1, source_target_pairs={{0,16},{8,24},{16,0},{24,8},{1,17},{9,25},{17,1},{25,9},{2,18},{10... | collective-permute-start | bytes 638984 | tf_op jit(solution)/shard_map/ppermute | solution.py:163
  19.8 10.7 %collective-permute-start.6 = (bf16[64,1664]{1,0:T(8,128)(2,1)S(1)}, bf16[64,1664]{1,0:T(8,128)(2,1)S(1)}, u32[]{:S(2)}, u32[]{:S(2)}) collective-permute-start(bf16[64,1664]{1,0:T(8,128)(2,1)S(1)} %packed.1.refs_0_.after_ref), channel_id=1, source_target_pairs={{0,24},{8,16},{16,8},{24,0},{1,25},{9,17},{17,9},{25,1},{2,26},{10... | collective-permute-start | bytes 638984 | tf_op jit(solution)/shard_map/ppermute | solution.py:163
  23.2 12.3 %collective-permute-start.11 = (bf16[64,1536]{1,0:T(8,128)(2,1)S(1)}, bf16[64,1536]{1,0:T(8,128)(2,1)S(1)}, u32[]{:S(2)}, u32[]{:S(2)}) collective-permute-start(bf16[64,1536]{1,0:T(8,128)(2,1)S(1)} %collective-permute-done.3.refs_2_.refs_0_), channel_id=1, source_target_pairs={{0,8},{8,0},{16,24},{24,16},{1,9},{9,1},{17,25},{25,17},{2,10},{10... | collective-permute-start | bytes 589832 | tf_op jit(solution)/shard_map/ppermute | solution.py:163
  24.8 13.1 %collective-permute-start.12 = (bf16[64,1536]{1,0:T(8,128)(2,1)S(1)}, bf16[64,1536]{1,0:T(8,128)(2,1)S(1)}, u32[]{:S(2)}, u32[]{:S(2)}) collective-permute-start(bf16[64,1536]{1,0:T(8,128)(2,1)S(1)} %collective-permute-done.3.refs_2_.refs_0_), channel_id=1, source_target_pairs={{0,16},{8,24},{16,0},{24,8},{1,17},{9,25},{17,1},{25,9},{2,18},{10... | collective-permute-start | bytes 589832 | tf_op jit(solution)/shard_map/ppermute | solution.py:163
  26.4 11.6 %collective-permute-start.13 = (bf16[64,1536]{1,0:T(8,128)(2,1)S(1)}, bf16[64,1536]{1,0:T(8,128)(2,1)S(1)}, u32[]{:S(2)}, u32[]{:S(2)}) collective-permute-start(bf16[64,1536]{1,0:T(8,128)(2,1)S(1)} %collective-permute-done.3.refs_2_.refs_0_), channel_id=1, source_target_pairs={{0,24},{8,16},{16,8},{24,0},{1,25},{9,17},{17,9},{25,1},{2,26},{10... | collective-permute-start | bytes 589832 | tf_op jit(solution)/shard_map/ppermute | solution.py:163
  30.8 1.4 %collective-permute-start.7 = (f32[256,128]{1,0:T(8,128)S(1)}, f32[256,128]{1,0:T(8,128)S(1)}, u32[]{:S(2)}, u32[]{:S(2)}) collective-permute-start(f32[256,128]{1,0:T(8,128)S(1)} %row_sums.2.refs_4_), channel_id=1, source_target_pairs={{0,1},{1,0},{2,3},{3,2},{4,5},{5,4},{6,7},{7,6},{8,9},{9,8},{10,11... | collective-permute-start | bytes 393224 | tf_op jit(solution)/shard_map/ppermute | solution.py:163
  35.0 3.0 %collective-permute-start.10 = (bf16[256,384]{1,0:T(8,128)(2,1)S(1)}, bf16[256,384]{1,0:T(8,128)(2,1)S(1)}, u32[]{:S(2)}, u32[]{:S(2)}) collective-permute-start(bf16[256,384]{1,0:T(8,128)(2,1)S(1)} %get-tuple-element.33), channel_id=1, source_target_pairs={{0,1},{1,0},{2,3},{3,2},{4,5},{5,4},{6,7},{7,6},{8,9},{9,8},{10,11... | collective-permute-start | bytes 589832 | tf_op jit(solution)/shard_map/ppermute | solution.py:163
  35.2 2.8 %collective-permute-start.8 = (bf16[256,384]{1,0:T(8,128)(2,1)S(1)}, bf16[256,384]{1,0:T(8,128)(2,1)S(1)}, u32[]{:S(2)}, u32[]{:S(2)}) collective-permute-start(bf16[256,384]{1,0:T(8,128)(2,1)S(1)} %get-tuple-element.31), channel_id=1, source_target_pairs={{0,1},{1,0},{2,3},{3,2},{4,5},{5,4},{6,7},{7,6},{8,9},{9,8},{10,11... | collective-permute-start | bytes 589832 | tf_op jit(solution)/shard_map/ppermute | solution.py:163
  35.5 2.4 %collective-permute-start.9 = (bf16[256,384]{1,0:T(8,128)(2,1)S(1)}, bf16[256,384]{1,0:T(8,128)(2,1)S(1)}, u32[]{:S(2)}, u32[]{:S(2)}) collective-permute-start(bf16[256,384]{1,0:T(8,128)(2,1)S(1)} %get-tuple-element.32), channel_id=1, source_target_pairs={{0,1},{1,0},{2,3},{3,2},{4,5},{5,4},{6,7},{7,6},{8,9},{9,8},{10,11... | collective-permute-start | bytes 589832 | tf_op jit(solution)/shard_map/ppermute | solution.py:163
  35.7 2.3 %copy-start.3 = (f32[128]{0:T(128)S(1)}, f32[128]{0:T(128)}, u32[]{:S(2)}) copy-start(f32[128]{0:T(128)} %param.13) | copy-start | bytes 1540
  35.7 2.3 %copy-start.4 = (f32[128]{0:T(128)S(1)}, f32[128]{0:T(128)}, u32[]{:S(2)}) copy-start(f32[128]{0:T(128)} %param.14) | copy-start | bytes 1540
  38.3 12.0 %collective-permute-start.14 = (bf16[256,768]{1,0:T(8,128)(2,1)S(1)}, bf16[256,768]{1,0:T(8,128)(2,1)S(1)}, u32[]{:S(2)}, u32[]{:S(2)}) collective-permute-start(bf16[256,768]{1,0:T(8,128)(2,1)S(1)} %get-tuple-element.35.refs_9_.refs_1_), channel_id=1, source_target_pairs={{0,2},{2,0},{4,6},{6,4},{1,3},{3,1},{5,7},{7,5},{8,10},{10,8},{12,... | collective-permute-start | bytes 1179656 | tf_op jit(solution)/shard_map/ppermute | solution.py:163
  40.6 1.4 %collective-permute-start.15 = (f32[256,128]{1,0:T(8,128)S(1)}, f32[256,128]{1,0:T(8,128)S(1)}, u32[]{:S(2)}, u32[]{:S(2)}) collective-permute-start(f32[256,128]{1,0:T(8,128)S(1)} %row_sums.3.refs_4_), channel_id=1, source_target_pairs={{0,1},{1,0},{2,3},{3,2},{4,5},{5,4},{6,7},{7,6},{8,9},{9,8},{10,11... | collective-permute-start | bytes 393224 | tf_op jit(solution)/shard_map/ppermute | solution.py:163
  44.0 2.1 %collective-permute-start.16 = (bf16[256,384]{1,0:T(8,128)(2,1)S(1)}, bf16[256,384]{1,0:T(8,128)(2,1)S(1)}, u32[]{:S(2)}, u32[]{:S(2)}) collective-permute-start(bf16[256,384]{1,0:T(8,128)(2,1)S(1)} %get-tuple-element.39), channel_id=1, source_target_pairs={{0,1},{1,0},{2,3},{3,2},{4,5},{5,4},{6,7},{7,6},{8,9},{9,8},{10,11... | collective-permute-start | bytes 589832 | tf_op jit(solution)/shard_map/ppermute | solution.py:163
  44.2 1.9 %collective-permute-start.17 = (bf16[256,384]{1,0:T(8,128)(2,1)S(1)}, bf16[256,384]{1,0:T(8,128)(2,1)S(1)}, u32[]{:S(2)}, u32[]{:S(2)}) collective-permute-start(bf16[256,384]{1,0:T(8,128)(2,1)S(1)} %get-tuple-element.40), channel_id=1, source_target_pairs={{0,1},{1,0},{2,3},{3,2},{4,5},{5,4},{6,7},{7,6},{8,9},{9,8},{10,11... | collective-permute-start | bytes 589832 | tf_op jit(solution)/shard_map/ppermute | solution.py:163
  46.0 42.8 %slice-start = ((s8[9437184]{0:T(1024)(128)(4,1)}), s8[4194304]{0:T(1024)(128)(4,1)S(1)}, s32[]{:S(2)}) async-start(s8[9437184]{0:T(1024)(128)(4,1)} %bitcast.17), calls=%async_computation | async-start | bytes 8388608
  46.3 42.6 %slice-start.1 = ((s8[9437184]{0:T(1024)(128)(4,1)}), s8[4194304]{0:T(1024)(128)(4,1)S(1)}, s32[]{:S(2)}) async-start(s8[9437184]{0:T(1024)(128)(4,1)} %bitcast.17), calls=%async_computation.1 | async-start | bytes 8388608
  46.3 42.6 %slice-start.2 = ((s8[9437184]{0:T(1024)(128)(4,1)}), s8[1048576]{0:T(1024)(128)(4,1)S(1)}, s32[]{:S(2)}) async-start(s8[9437184]{0:T(1024)(128)(4,1)} %bitcast.17), calls=%async_computation.2 | async-start | bytes 2097152
  46.3 12.1 %collective-permute-start.18 = (bf16[256,768]{1,0:T(8,128)(2,1)S(1)}, bf16[256,768]{1,0:T(8,128)(2,1)S(1)}, u32[]{:S(2)}, u32[]{:S(2)}) collective-permute-start(bf16[256,768]{1,0:T(8,128)(2,1)S(1)} %split_heads.3.refs_3_), channel_id=1, source_target_pairs={{0,2},{2,0},{4,6},{6,4},{1,3},{3,1},{5,7},{7,5},{8,10},{10,8},{12,... | collective-permute-start | bytes 1179656 | tf_op jit(solution)/shard_map/ppermute | solution.py:163
  50.3 11.2 %copy-start.1 = (bf16[768,1536]{1,0:T(8,128)(2,1)S(1)}, bf16[768,1536]{1,0:T(8,128)(2,1)}, u32[]{:S(2)}) copy-start(bf16[768,1536]{1,0:T(8,128)(2,1)} %other_weight_ref.1) | copy-start | bytes 7077892
  60.1 1.5 %collective-permute-start.19 = (bf16[256,384]{1,0:T(8,128)(2,1)S(1)}, bf16[256,384]{1,0:T(8,128)(2,1)S(1)}, u32[]{:S(2)}, u32[]{:S(2)}) collective-permute-start(bf16[256,384]{1,0:T(8,128)(2,1)S(1)} %attention.1.own_ref), channel_id=1, source_target_pairs={{0,1},{1,0},{2,3},{3,2},{4,5},{5,4},{6,7},{7,6},{8,9},{9,8},{10,11... | collective-permute-start | bytes 589832 | tf_op jit(solution)/shard_map/ppermute | solution.py:163
  63.2 7.8 %collective-permute-start.20 = (bf16[64,1536]{1,0:T(8,128)(2,1)S(1)}, bf16[64,1536]{1,0:T(8,128)(2,1)S(1)}, u32[]{:S(2)}, u32[]{:S(2)}) collective-permute-start(bf16[64,1536]{1,0:T(8,128)(2,1)S(1)} %get-tuple-element.42), channel_id=1, source_target_pairs={{0,8},{8,0},{16,24},{24,16},{1,9},{9,1},{17,25},{25,17},{2,10},{10... | collective-permute-start | bytes 589832 | tf_op jit(solution)/shard_map/ppermute | solution.py:163
  64.8 10.9 %collective-permute-start.21 = (bf16[64,1536]{1,0:T(8,128)(2,1)S(1)}, bf16[64,1536]{1,0:T(8,128)(2,1)S(1)}, u32[]{:S(2)}, u32[]{:S(2)}) collective-permute-start(bf16[64,1536]{1,0:T(8,128)(2,1)S(1)} %get-tuple-element.43), channel_id=1, source_target_pairs={{0,16},{8,24},{16,0},{24,8},{1,17},{9,25},{17,1},{25,9},{2,18},{10... | collective-permute-start | bytes 589832 | tf_op jit(solution)/shard_map/ppermute | solution.py:163
  65.3 10.4 %collective-permute-start.22 = (bf16[64,1536]{1,0:T(8,128)(2,1)S(1)}, bf16[64,1536]{1,0:T(8,128)(2,1)S(1)}, u32[]{:S(2)}, u32[]{:S(2)}) collective-permute-start(bf16[64,1536]{1,0:T(8,128)(2,1)S(1)} %get-tuple-element.44), channel_id=1, source_target_pairs={{0,24},{8,16},{16,8},{24,0},{1,25},{9,17},{17,9},{25,1},{2,26},{10... | collective-permute-start | bytes 589832 | tf_op jit(solution)/shard_map/ppermute | solution.py:163
  76.0 1.2 %collective-permute-start.23 = (f32[2,64]{1,0:T(2,128)S(1)}, f32[2,64]{1,0:T(2,128)S(1)}, u32[]{:S(2)}, u32[]{:S(2)}) collective-permute-start(f32[2,64]{1,0:T(2,128)S(1)} %pad_maximum_fusion), channel_id=1, source_target_pairs={{0,1},{1,0},{2,3},{3,2},{4,5},{5,4},{6,7},{7,6},{8,9},{9,8},{10,11... | collective-permute-start | bytes 1544 | tf_op jit(solution)/shard_map/ppermute | solution.py:163
  77.4 7.8 %collective-permute-start.24 = (bf16[64,1536]{1,0:T(8,128)(2,1)S(1)}, bf16[64,1536]{1,0:T(8,128)(2,1)S(1)}, u32[]{:S(2)}, u32[]{:S(2)}) collective-permute-start(bf16[64,1536]{1,0:T(8,128)(2,1)S(1)} %add_convert_fusion.refs_0_), channel_id=1, source_target_pairs={{0,8},{8,0},{16,24},{24,16},{1,9},{9,1},{17,25},{25,17},{2,10},{10... | collective-permute-start | bytes 589832 | tf_op jit(solution)/shard_map/ppermute | solution.py:163
  77.9 10.9 %collective-permute-start.25 = (bf16[64,1536]{1,0:T(8,128)(2,1)S(1)}, bf16[64,1536]{1,0:T(8,128)(2,1)S(1)}, u32[]{:S(2)}, u32[]{:S(2)}) collective-permute-start(bf16[64,1536]{1,0:T(8,128)(2,1)S(1)} %add_convert_fusion.refs_0_), channel_id=1, source_target_pairs={{0,16},{8,24},{16,0},{24,8},{1,17},{9,25},{17,1},{25,9},{2,18},{10... | collective-permute-start | bytes 589832 | tf_op jit(solution)/shard_map/ppermute | solution.py:163
  79.2 9.7 %collective-permute-start.26 = (bf16[64,1536]{1,0:T(8,128)(2,1)S(1)}, bf16[64,1536]{1,0:T(8,128)(2,1)S(1)}, u32[]{:S(2)}, u32[]{:S(2)}) collective-permute-start(bf16[64,1536]{1,0:T(8,128)(2,1)S(1)} %add_convert_fusion.refs_0_), channel_id=1, source_target_pairs={{0,24},{8,16},{16,8},{24,0},{1,25},{9,17},{17,9},{25,1},{2,26},{10... | collective-permute-start | bytes 589832 | tf_op jit(solution)/shard_map/ppermute | solution.py:163
  88.9 5.0 %slice-start.3 = ((s8[9437184]{0:T(1024)(128)(4,1)}), s8[4194304]{0:T(1024)(128)(4,1)S(1)}, s32[]{:S(2)}) async-start(s8[9437184]{0:T(1024)(128)(4,1)} %bitcast.19), calls=%async_computation.3 | async-start | bytes 8388608
  88.9 5.0 %slice-start.4 = ((s8[9437184]{0:T(1024)(128)(4,1)}), s8[4194304]{0:T(1024)(128)(4,1)S(1)}, s32[]{:S(2)}) async-start(s8[9437184]{0:T(1024)(128)(4,1)} %bitcast.19), calls=%async_computation.4 | async-start | bytes 8388608
  91.1 2.8 %slice-start.5 = ((s8[9437184]{0:T(1024)(128)(4,1)}), s8[1048576]{0:T(1024)(128)(4,1)S(1)}, s32[]{:S(2)}) async-start(s8[9437184]{0:T(1024)(128)(4,1)} %bitcast.19), calls=%async_computation.5 | async-start | bytes 2097152
  91.1 2.8 %collective-permute-start.28 = (bf16[256,1536]{1,0:T(8,128)(2,1)S(1)}, bf16[256,1536]{1,0:T(8,128)(2,1)S(1)}, u32[]{:S(2)}, u32[]{:S(2)}) collective-permute-start(bf16[256,1536]{1,0:T(8,128)(2,1)S(1)} %up_projected.3.refs_0_), channel_id=1, source_target_pairs={{0,1},{1,0},{2,3},{3,2},{4,5},{5,4},{6,7},{7,6},{8,9},{9,8},{10,11... | collective-permute-start | bytes 2359304 | tf_op jit(solution)/shard_map/ppermute | solution.py:163
  93.4 3.1 %collective-permute-start.27 = (bf16[256,1536]{1,0:T(8,128)(2,1)S(1)}, bf16[256,1536]{1,0:T(8,128)(2,1)S(1)}, u32[]{:S(2)}, u32[]{:S(2)}) collective-permute-start(bf16[256,1536]{1,0:T(8,128)(2,1)S(1)} %up_projected.2.refs_0_), channel_id=1, source_target_pairs={{0,1},{1,0},{2,3},{3,2},{4,5},{5,4},{6,7},{7,6},{8,9},{9,8},{10,11... | collective-permute-start | bytes 2359304 | tf_op jit(solution)/shard_map/ppermute | solution.py:163
  99.2 7.8 %collective-permute-start.29 = (bf16[64,1536]{1,0:T(8,128)(2,1)S(1)}, bf16[64,1536]{1,0:T(8,128)(2,1)S(1)}, u32[]{:S(2)}, u32[]{:S(2)}) collective-permute-start(bf16[64,1536]{1,0:T(8,128)(2,1)S(1)} %get-tuple-element.46), channel_id=1, source_target_pairs={{0,8},{8,0},{16,24},{24,16},{1,9},{9,1},{17,25},{25,17},{2,10},{10... | collective-permute-start | bytes 589832 | tf_op jit(solution)/shard_map/ppermute | solution.py:163
  100.8 10.8 %collective-permute-start.30 = (bf16[64,1536]{1,0:T(8,128)(2,1)S(1)}, bf16[64,1536]{1,0:T(8,128)(2,1)S(1)}, u32[]{:S(2)}, u32[]{:S(2)}) collective-permute-start(bf16[64,1536]{1,0:T(8,128)(2,1)S(1)} %get-tuple-element.47), channel_id=1, source_target_pairs={{0,16},{8,24},{16,0},{24,8},{1,17},{9,25},{17,1},{25,9},{2,18},{10... | collective-permute-start | bytes 589832 | tf_op jit(solution)/shard_map/ppermute | solution.py:163
  101.3 10.3 %collective-permute-start.31 = (bf16[64,1536]{1,0:T(8,128)(2,1)S(1)}, bf16[64,1536]{1,0:T(8,128)(2,1)S(1)}, u32[]{:S(2)}, u32[]{:S(2)}) collective-permute-start(bf16[64,1536]{1,0:T(8,128)(2,1)S(1)} %get-tuple-element.48), channel_id=1, source_target_pairs={{0,24},{8,16},{16,8},{24,0},{1,25},{9,17},{17,9},{25,1},{2,26},{10... | collective-permute-start | bytes 589832 | tf_op jit(solution)/shard_map/ppermute | solution.py:163

commit v5 on v4

--- a/solution.py
+++ b/solution.py
@@ -154,6 +154,7 @@
 
 VMEM_BYTES = 1024 * 1024
 COPY_AT = 1
+SHORT = pl.CostEstimate(flops=10000000000, bytes_accessed=0, transcendentals=0)
 LONG = pl.CostEstimate(flops=10**10, bytes_accessed=0, transcendentals=0)
 NO_COST = pl.CostEstimate(flops=0, bytes_accessed=0, transcendentals=0)
 
@@ -289,32 +290,69 @@
     )(*blocks)
 
 
-def row_sums_kernel(count, *refs):
-    block_refs, out_ref = refs[:count], refs[-1]
+def row_sums_kernel(values_ref, out_ref, copy_ref):
+    values = values_ref[...].astype(jnp.float32)
+    lane = lax.broadcasted_iota(jnp.int32, out_ref.shape, 1)
+    out_ref[...] = jnp.where(
+        lane < out_ref.shape[1] // 2,
+        jnp.sum(values, axis=-1, keepdims=True),
+        jnp.sum(values * values, axis=-1, keepdims=True),
+    )
+    copy_ref[...] = values_ref[...]
+
+
+def row_sums(values):
+    return pl.pallas_call(
+        row_sums_kernel,
+        out_shape=[
+            jax.ShapeDtypeStruct((values.shape[0], 128), jnp.float32),
+            jax.ShapeDtypeStruct(values.shape, values.dtype),
+        ],
+        compiler_params=pltpu.CompilerParams(vmem_limit_bytes=VMEM_BYTES * 2),
+        cost_estimate=NO_COST,
+        name="row_sums",
+    )(values)
+
+
+def standardize_kernel(features, values_ref, own_ref, arrived_ref, *refs):
+    total = own_ref[...] + arrived_ref[...]
+    average = total[:, :1] / features
+    variance = total[:, total.shape[1] // 2 :][:, :1] / features - average * average
+    values = values_ref[...].astype(jnp.float32)
+    refs[-1][...] = ((values - average) * lax.rsqrt(variance + 1e-06)).astype(jnp.bfloat16)
+
+
+def standardized(values, features, after):
+    own, values = row_sums(values)
+    whole = lambda array: pl.BlockSpec(array.shape, lambda j: (0, 0))
+    return pl.pallas_call(
+        lambda *refs: standardize_kernel(features, *refs),
+        grid=(1,),
+        in_specs=[whole(values), whole(own), whole(own)] + after_specs(after),
+        out_specs=whole(values),
+        out_shape=jax.ShapeDtypeStruct(values.shape, jnp.bfloat16),
+        compiler_params=pltpu.CompilerParams(vmem_limit_bytes=VMEM_BYTES * 2),
+        cost_estimate=NO_COST,
+        name="standardized",
+    )(values, own, permuted(own, "tensor", 1), *after)
+
+
+def stack_kernel(*refs):
+    *block_refs, out_ref = refs
     rows = block_refs[0].shape[0]
     for k, block_ref in enumerate(block_refs):
-        values = block_ref[...].astype(jnp.float32)
-        lane = lax.broadcasted_iota(jnp.int32, (rows, out_ref.shape[1]), 1)
-        out_ref[k * rows : (k + 1) * rows, :] = jnp.where(
-            lane < out_ref.shape[1] // 2,
-            jnp.sum(values, axis=-1, keepdims=True),
-            jnp.sum(values * values, axis=-1, keepdims=True),
-        )
-
-
-def row_sums(blocks, width, after):
-    rows = blocks[0].shape[0]
-    whole = lambda *shape: pl.BlockSpec(shape, lambda j: (0, 0))
-    return pl.pallas_call(
-        lambda *refs: row_sums_kernel(len(blocks), *refs),
-        grid=(1,),
-        in_specs=[whole(rows, width)] * len(blocks) + after_specs(after),
-        out_specs=whole(rows * len(blocks), 128),
-        out_shape=jax.ShapeDtypeStruct((rows * len(blocks), 128), jnp.float32),
-        compiler_params=pltpu.CompilerParams(vmem_limit_bytes=VMEM_BYTES * 4),
+        out_ref[k * rows : (k + 1) * rows, :] = block_ref[...]
+
+
+def stacked(blocks):
+    rows, width = blocks[0].shape
+    return pl.pallas_call(
+        stack_kernel,
+        out_shape=jax.ShapeDtypeStruct((rows * len(blocks), width), blocks[0].dtype),
+        compiler_params=pltpu.CompilerParams(vmem_limit_bytes=VMEM_BYTES * 2),
         cost_estimate=NO_COST,
-        name="row_sums",
-    )(*blocks, *after)
+        name="stacked",
+    )(*blocks)
 
 
 def copied_kernel(values_ref, after_ref, out_ref):
@@ -335,12 +373,6 @@
     )(values, after)
 
 
-def centered(values, total, features):
-    average = total[:, :1] / features
-    variance = total[:, total.shape[1] // 2 :][:, :1] / features - average * average
-    return (values - average) * lax.rsqrt(variance + 1e-06)
-
-
 def normalized(values, features):
     sums = jnp.stack([jnp.sum(values, axis=-1), jnp.sum(values * values, axis=-1)])
     sums = sums + permuted(sums, "tensor", 1)
@@ -360,86 +392,105 @@
     return total
 
 
-def project_kernel(count, features, parts, *refs):
+def project_kernel(count, parts, other, *refs):
     block_refs = refs[:count]
-    own_ref, arrived_ref, shift_ref, scale_ref, weight_ref = refs[count : count + 5]
+    shift_ref, scale_ref = refs[count : count + 2]
+    weight_refs = refs[count + 2 : count + 2 + parts]
     normed_ref = refs[-1]
-
-    @pl.when(pl.program_id(0) == 0)
-    def _():
-        rows = block_refs[0].shape[0]
-        for k, block_ref in enumerate(block_refs):
-            here = slice(k * rows, (k + 1) * rows)
-            total = own_ref[here, :] + arrived_ref[here, :]
-            values = centered(block_ref[...].astype(jnp.float32), total, features)
-            values = values * (1.0 + scale_ref[...]) + shift_ref[...]
-            normed_ref[here, :] = values.astype(jnp.bfloat16)
-
-    project_part(normed_ref, weight_ref, refs[-1 - parts : -1])
-
-
-def project_part(normed_ref, weight_ref, out_refs):
-    product = jnp.dot(normed_ref[...], weight_ref[0], preferred_element_type=jnp.float32)
-    for k, out_ref in enumerate(out_refs):
-
-        @pl.when(pl.program_id(0) == k)
-        def _(out_ref=out_ref):
-            out_ref[...] = product.astype(jnp.bfloat16)
-
-
-def project_again_kernel(parts, normed_ref, weight_ref, *refs):
-    project_part(normed_ref, weight_ref, refs[-parts:])
-
-
-def projected(blocks, small, weights, first, half, other, after=()):
-    rows, width = blocks[0].shape[0], weights.shape[1]
+    rows = block_refs[0].shape[0]
+    for k, block_ref in enumerate(block_refs):
+        values = block_ref[...].astype(jnp.float32)
+        values = values * (1.0 + scale_ref[...]) + shift_ref[...]
+        normed_ref[k * rows : (k + 1) * rows, :] = values.astype(jnp.bfloat16)
+    project_parts(normed_ref, weight_refs, refs[-1 - parts : -1], other)
+
+
+def project_parts(normed_ref, weight_refs, out_refs, other):
+    half = out_refs[0].shape[1]
+    position = lax.axis_index("tensor")
+    low = pl.multiple_of((1 - position if other else position) * half, 128)
+    for weight_ref, out_ref in zip(weight_refs, out_refs):
+        out_ref[...] = jnp.dot(
+            normed_ref[...], weight_ref[:, pl.ds(low, half)], preferred_element_type=jnp.float32
+        ).astype(jnp.bfloat16)
+
+
+def project_again_kernel(parts, other, normed_ref, *refs):
+    project_parts(normed_ref, refs[:parts], refs[-parts:], other)
+
+
+def projected(blocks, small, weights, half, other, after=()):
+    rows, width = blocks[0].shape[0], weights[0].shape[0]
     all_rows = rows * len(blocks)
-    count = weights.shape[0] - first
-
-    def columns(j):
-        position = lax.axis_index("tensor")
-        return (j + first, 0, 1 - position if other else position)
-
+    count = len(weights)
     whole = lambda shape: pl.BlockSpec(shape, lambda j: (0, 0))
     shapes = [(all_rows, half)] * count + [(all_rows, width)] * bool(small)
     return pl.pallas_call(
-        (lambda *refs: project_kernel(len(blocks), 2 * width, count, *refs))
+        (lambda *refs: project_kernel(len(blocks), count, other, *refs))
         if small
-        else (lambda *refs: project_again_kernel(count, *refs)),
-        grid=(count,),
+        else (lambda *refs: project_again_kernel(count, other, *refs)),
+        grid=(1,),
         in_specs=[whole((rows, width)) for _ in blocks]
         + [whole(array.shape) for array in small]
-        + [pl.BlockSpec((1, width, half), columns)]
+        + [pl.BlockSpec(memory_space=pltpu.VMEM) for _ in weights]
         + after_specs(after),
         out_specs=[whole(shape) for shape in shapes],
         out_shape=[jax.ShapeDtypeStruct(shape, jnp.bfloat16) for shape in shapes],
-        compiler_params=pltpu.CompilerParams(vmem_limit_bytes=VMEM_BYTES * 9),
+        compiler_params=pltpu.CompilerParams(vmem_limit_bytes=VMEM_BYTES * 20),
         cost_estimate=NO_COST,
         name="projected",
-    )(*blocks, *small, weights, *after)
-
-
-def staged(weights, after):
-    block = pl.BlockSpec(memory_space=pl.ANY)
-    count, width, columns = weights.shape
-
-    def kernel(weight_ref, after_ref, out_ref, sem):
-        copy = pltpu.make_async_copy(weight_ref, out_ref, sem)
-        copy.start()
-        copy.wait()
+    )(*blocks, *small, *weights, *after)
+
+
+def staged(weights, after, part=None):
+    width, columns = weights.shape[-2:]
+    pieces = 4 if width % 64 == 0 else 1
+    rows = width // pieces
+    anywhere = pl.BlockSpec(memory_space=pl.ANY)
+
+    def kernel(weight_ref, after_ref, out_ref, sems):
+        source_ref = weight_ref if part is None else weight_ref.at[part]
+        copies = [
+            pltpu.make_async_copy(
+                source_ref.at[pl.ds(k * rows, rows)], out_ref.at[pl.ds(k * rows, rows)], sems.at[k]
+            )
+            for k in range(pieces)
+        ]
+        for copy in copies:
+            copy.start()
+        for copy in copies:
+            copy.wait()
 
     return pl.pallas_call(
         kernel,
-        in_specs=[block, pl.BlockSpec(memory_space=pltpu.VMEM)],
+        grid=(1,),
+        in_specs=[anywhere] + after_specs([after]),
         out_specs=pl.BlockSpec(memory_space=pltpu.VMEM),
-        out_shape=pltpu.VMEM(weights.shape, weights.dtype),
-        scratch_shapes=[pltpu.SemaphoreType.DMA],
-        compiler_params=pltpu.CompilerParams(vmem_limit_bytes=VMEM_BYTES * 9),
+        out_shape=pltpu.VMEM((width, columns), weights.dtype),
+        scratch_shapes=[pltpu.SemaphoreType.DMA((pieces,))],
+        compiler_params=pltpu.CompilerParams(vmem_limit_bytes=VMEM_BYTES),
         cost_estimate=pl.CostEstimate(
-            flops=0, bytes_accessed=2 * weights.size, transcendentals=0
+            flops=0, bytes_accessed=2 * width * columns, transcendentals=0
         ),
         name="staged",
     )(weights, after)
+
+
+def mark_kernel(*refs):
+    refs[-1][...] = jnp.zeros(refs[-1].shape, jnp.float32)
+
+
+def mark(after, cost):
+    return pl.pallas_call(
+        mark_kernel,
+        grid=(1,),
+        in_specs=after_specs(after),
+        out_specs=pl.BlockSpec((8, 128), lambda j: (0, 0)),
+        out_shape=jax.ShapeDtypeStruct((8, 128), jnp.float32),
+        compiler_params=pltpu.CompilerParams(vmem_limit_bytes=VMEM_BYTES),
+        cost_estimate=cost,
+        name="mark",
+    )(*after)
 
 
 def heads_kernel(count, head_size, *refs):
@@ -487,8 +538,8 @@
     )(*own, *arrived, q_gain[None, :], k_gain[None, :], *after)
 
 
-def attention_kernel(head_size, query_ref, *refs):
-    *kv_refs, out_ref = refs
+def attention_kernel(head_size, count, query_ref, *refs):
+    kv_refs, out_ref = refs[:count], refs[-1]
     half = query_ref.shape[1]
     score_scale = 1.0 / math.sqrt(head_size)
     for lo in range(0, half, head_size):
@@ -518,11 +569,15 @@
         out_ref[:, lo : lo + head_size] = (summed / denominator).astype(jnp.bfloat16)
 
 
-def attention(queries, kv_parts, head_size):
+def attention(queries, kv_parts, head_size, after):
     rows, half = queries.shape
     keys = sum(part.shape[0] for part in kv_parts)
     return pl.pallas_call(
-        lambda *refs: attention_kernel(head_size, *refs),
+        lambda *refs: attention_kernel(head_size, len(kv_parts), *refs),
+        grid=(1,),
+        in_specs=[pl.BlockSpec(array.shape, lambda j: (0, 0)) for array in [queries, *kv_parts]]
+        + after_specs(after),
+        out_specs=pl.BlockSpec((rows, half), lambda j: (0, 0)),
         out_shape=jax.ShapeDtypeStruct((rows, half), jnp.bfloat16),
         compiler_params=pltpu.CompilerParams(vmem_limit_bytes=VMEM_BYTES * 12),
         cost_estimate=pl.CostEstimate(
@@ -531,114 +586,102 @@
             transcendentals=rows * keys * half // head_size,
         ),
         name="attention",
-    )(queries, *kv_parts)
-
-
-def row_blocks(values, out_refs):
+    )(queries, *kv_parts, *after)
+
+
+def column_tiles(columns):
+    size = columns // 3 if columns % 384 == 0 else columns
+    return [slice(low, low + size) for low in range(0, columns, size)]
+
+
+def out_kernel(own_ref, arrived_ref, weight_ref, *out_refs):
+    half = own_ref.shape[1]
+    position = lax.axis_index("tensor")
+    rows = [pl.ds(pl.multiple_of(at * half, 16), half) for at in (position, 1 - position)]
+    for here in column_tiles(weight_ref.shape[1]):
+        total = jnp.dot(
+            own_ref[...], weight_ref[rows[0], here], preferred_element_type=jnp.float32
+        ) + jnp.dot(arrived_ref[...], weight_ref[rows[1], here], preferred_element_type=jnp.float32)
+        row_blocks(total, here, out_refs)
+
+
+def row_blocks(values, columns, out_refs):
     rows = out_refs[0].shape[0]
     for k, out_ref in enumerate(out_refs):
-        out_ref[...] = values[k * rows : (k + 1) * rows].astype(jnp.bfloat16)
-
-
-def out_kernel(own_ref, arrived_ref, own_weight_ref, other_weight_ref, *out_refs):
-    total = jnp.dot(own_ref[...], own_weight_ref[...], preferred_element_type=jnp.float32)
-    total = total + jnp.dot(
-        arrived_ref[...], other_weight_ref[...], preferred_element_type=jnp.float32
-    )
-    row_blocks(total, out_refs)
+        out_ref[:, columns] = values[k * rows : (k + 1) * rows].astype(jnp.bfloat16)
 
 
 def out_projected(own, arrived, weight, rows):
     all_rows, half = own.shape
     width = weight.shape[1]
-    tile = width // 3 if width % 384 == 0 else width
     whole = pl.BlockSpec((all_rows, half), lambda j: (0, 0))
     return pl.pallas_call(
         out_kernel,
-        grid=(width // tile,),
-        in_specs=[
-            whole,
-            whole,
-            pl.BlockSpec((half, tile), lambda j: (lax.axis_index("tensor"), j)),
-            pl.BlockSpec((half, tile), lambda j: (1 - lax.axis_index("tensor"), j)),
-        ],
-        out_specs=[pl.BlockSpec((rows, tile), lambda j: (0, j))] * (all_rows // rows),
+        grid=(1,),
+        in_specs=[whole, whole, pl.BlockSpec(memory_space=pltpu.VMEM)],
+        out_specs=[pl.BlockSpec((rows, width), lambda j: (0, 0))] * (all_rows // rows),
         out_shape=[jax.ShapeDtypeStruct((rows, width), jnp.bfloat16)] * (all_rows // rows),
         compiler_params=pltpu.CompilerParams(vmem_limit_bytes=VMEM_BYTES * 8),
         cost_estimate=NO_COST,
         name="out_projected",
-    )(own, arrived, weight, weight)
-
-
-def up_kernel(*refs):
-    *block_refs, weight_ref, out_ref, joined_ref = refs
-
-    @pl.when(pl.program_id(0) == 0)
-    def _():
-        rows = block_refs[0].shape[0]
-        for k, block_ref in enumerate(block_refs):
-            joined_ref[k * rows : (k + 1) * rows, :] = block_ref[...]
-
-    out_ref[...] = jnp.dot(
-        joined_ref[...], weight_ref[...], preferred_element_type=jnp.float32
-    ).astype(jnp.bfloat16)
-
-
-def up_projected(blocks, weight, part, parts):
+    )(own, arrived, weight)
+
+
+def up_kernel(first, count, *refs):
+    block_refs, weight_ref, (out_ref, joined_ref) = refs[:count], refs[count], refs[-2:]
+    rows = block_refs[0].shape[0]
+    for k, block_ref in enumerate(block_refs):
+        joined_ref[k * rows : (k + 1) * rows, :] = block_ref[...]
+    for here in column_tiles(out_ref.shape[1]):
+        out_ref[:, here] = jnp.dot(
+            joined_ref[...],
+            weight_ref[:, first + here.start : first + here.stop],
+            preferred_element_type=jnp.float32,
+        ).astype(jnp.bfloat16)
+
+
+def up_projected(blocks, weight, part, parts, after=()):
     rows, width = blocks[0].shape
     all_rows = rows * len(blocks)
     columns = weight.shape[1] // parts
-    tile = columns // 3 if columns % 384 == 0 else columns
-    first = part * columns // tile
-    return pl.pallas_call(
-        up_kernel,
-        grid=(columns // tile,),
+    return pl.pallas_call(
+        lambda *refs: up_kernel(part * columns, len(blocks), *refs),
+        grid=(1,),
         in_specs=[pl.BlockSpec((rows, width), lambda j: (0, 0)) for _ in blocks]
-        + [pl.BlockSpec((width, tile), lambda j: (0, j + first))],
-        out_specs=pl.BlockSpec((all_rows, tile), lambda j: (0, j)),
+        + [pl.BlockSpec(memory_space=pltpu.VMEM)]
+        + after_specs(after),
+        out_specs=pl.BlockSpec((all_rows, columns), lambda j: (0, 0)),
         out_shape=jax.ShapeDtypeStruct((all_rows, columns), jnp.bfloat16),
         scratch_shapes=[pltpu.VMEM((all_rows, width), jnp.bfloat16)],
         compiler_params=pltpu.CompilerParams(vmem_limit_bytes=VMEM_BYTES * 8),
         cost_estimate=pl.CostEstimate(
-            flops=2 * all_rows * width * columns,
-            bytes_accessed=2 * width * columns,
-            transcendentals=0,
+            flops=2 * all_rows * width * columns, bytes_accessed=0, transcendentals=0
         ),
         name="up_projected",
-    )(*blocks, weight)
-
-
-def down_kernel(last, own_ref, arrived_ref, weight_ref, *refs):
-    step = pl.program_id(0)
-    out_refs, total_ref = refs[:-1], refs[-1]
-    hidden = own_ref[...].astype(jnp.float32) + arrived_ref[...].astype(jnp.float32)
-    activ = jax.nn.gelu(hidden, approximate=True).astype(jnp.bfloat16)
-    partial = jnp.dot(activ, weight_ref[...], preferred_element_type=jnp.float32)
-    if last:
-        before_ref, *out_refs = out_refs
-    else:
-        total_ref = out_refs[0]
-
-    @pl.when(step == 0)
-    def _():
-        total_ref[...] = partial + before_ref[...] if last else partial
-
-    @pl.when(step > 0)
-    def _():
-        total_ref[...] += partial
-
-    if last:
-
-        @pl.when(step == pl.num_programs(0) - 1)
-        def _():
-            row_blocks(total_ref[...], out_refs)
-
-
-def down_projected(own, arrived, weight, part, parts, before, rows):
-    all_rows, columns = own.shape
+    )(*blocks, weight, *after)
+
+
+def down_kernel(first, last, own_ref, arrived_ref, weight_ref, *refs):
+    *out_refs, activ_ref = refs
+    depth = own_ref.shape[1]
+    for here in column_tiles(depth):
+        hidden = own_ref[:, here].astype(jnp.float32) + arrived_ref[:, here].astype(jnp.float32)
+        activ_ref[:, here] = jax.nn.gelu(hidden, approximate=True).astype(jnp.bfloat16)
+    for here in column_tiles(weight_ref.shape[1]):
+        total = jnp.dot(
+            activ_ref[...],
+            weight_ref[first : first + depth, here],
+            preferred_element_type=jnp.float32,
+        )
+        if last:
+            row_blocks(total + out_refs[0][:, here], here, out_refs[1:])
+        else:
+            out_refs[0][:, here] = total
+
+
+def down_projected(own, arrived, weight, part, before, rows):
+    all_rows, depth = own.shape
     width = weight.shape[1]
-    tile = columns // 3 if columns % 384 == 0 else columns
-    first = part * columns // tile
     last = before is not None
     whole = pl.BlockSpec((all_rows, width), lambda j: (0, 0))
     if last:
@@ -647,24 +690,20 @@
     else:
         shapes = [jax.ShapeDtypeStruct((all_rows, width), jnp.float32)]
         out_specs = [whole]
-    scratch = pltpu.VMEM((all_rows, width) if last else (8, 128), jnp.float32)
-    return pl.pallas_call(
-        lambda *refs: down_kernel(last, *refs),
-        grid=(columns // tile,),
-        in_specs=[
-            pl.BlockSpec((all_rows, tile), lambda j: (0, j)),
-            pl.BlockSpec((all_rows, tile), lambda j: (0, j)),
-            pl.BlockSpec((tile, width), lambda j: (j + first, 0)),
-        ]
+    return pl.pallas_call(
+        lambda *refs: down_kernel(part * depth, last, *refs),
+        grid=(1,),
+        in_specs=[pl.BlockSpec((all_rows, depth), lambda j: (0, 0))] * 2
+        + [pl.BlockSpec(memory_space=pltpu.VMEM)]
         + [whole] * last,
         out_specs=out_specs,
         out_shape=shapes,
-        scratch_shapes=[scratch],
+        scratch_shapes=[pltpu.VMEM((all_rows, depth), jnp.bfloat16)],
         compiler_params=pltpu.CompilerParams(vmem_limit_bytes=VMEM_BYTES * 12),
         cost_estimate=pl.CostEstimate(
-            flops=2 * all_rows * width * columns,
-            bytes_accessed=2 * width * columns,
-            transcendentals=all_rows * columns,
+            flops=2 * all_rows * width * depth,
+            bytes_accessed=0,
+            transcendentals=all_rows * depth,
         ),
         name="down_projected",
     )(own, arrived, weight, *([before] * last))
@@ -686,51 +725,60 @@
 
     activated = jax.nn.silu(cond.astype(jnp.float32)).astype(jnp.bfloat16)
     pieces = jnp.dot(activated[None, :], mod_weight, preferred_element_type=jnp.float32)
-    weights = jnp.moveaxis(qkv_weight, 1, 0)
+    weights, out_weight, up_weight, down_weight = [
+        pltpu.with_memory_space_constraint(weight, pltpu.HBM)
+        for weight in (jnp.moveaxis(qkv_weight, 1, 0), out_weight, up_weight, down_weight)
+    ]
     start = copied(tokens, pieces, NO_COST)
     remote = [permuted(start, "blk", k) for k in range(2, blocks_z, 2)]
+    normal = standardized(tokens, features, [])
+    parts = []
     for stage in stages:
-        after = remote if stage == ("blk", 2) else []
+        after = []
+        if stage[0] == "blk":
+            take = [0] if stage[1] == 1 else range(len(parts), weights.shape[0])
+            parts += [staged(weights, pieces, part) for part in take]
+            after = parts + (remote if stage[1] == 2 else [normal])
         pieces = doubled_once(pieces, *stage, after)
-    own = packed(tokens, pieces)
-    weights = staged(pltpu.with_memory_space_constraint(weights, pltpu.HBM), own)
+    own = packed(normal, pieces)
     chunks = [from_all(own, "ulysses")]
-    chunks += [from_all(block, "ulysses") for block in remote]
+    if remote:
+        far = stacked(remote + [permuted(block, "blk", 1) for block in remote])
+        far = standardized(far, features, [])
+        chunks.append(from_all(far, "ulysses"))
     own_mod = assembled(chunks[0], "ulysses", *pieces.shape, width)
     mod_rows = [own_mod[0:1], own_mod[1:2]]
 
-    far = [block for blocks in chunks[1:] for block in blocks[1:]]
     kv_parts = []
     for index, blocks in enumerate(chunks):
-        first = min(index, 1)
-        after = [[], [], far]
-        if index:
-            after = [[own[0]], [kv_parts[0]], []]
-        sums = row_sums(blocks, width, after[0])
-        small = [sums, permuted(sums, "tensor", 1), *mod_rows]
-        *partial, normed = projected(blocks, small, weights, first, half, True, after[1])
+        use = parts[min(index, 1) :]
+        after = [kv_parts[0], mark(blocks[1:], SHORT)] if index else [far] * bool(remote)
+        *partial, normed = projected(blocks, mod_rows, use, half, True, after)
         arrived = [permuted(part, "tensor", 1) for part in partial]
-        own = projected([normed], [], weights, first, half, False)
-        outs = split_heads(own, arrived, q_gain, k_gain, after[2])
+        own = projected([normed], [], use, half, False)
+        outs = split_heads(own, arrived, q_gain, k_gain)
         kv_parts.append(outs[0])
         if index == 0:
             queries = outs[1]
-        if blocks_z > 1:
-            arrived = permuted(outs[0], "blk", 1)
-            kv_parts.append(arrived if index else copied(arrived, arrived, LONG))
-
-    context = attention(queries, kv_parts, head_size)
+            if blocks_z > 1:
+                arrived = permuted(outs[0], "blk", 1)
+                kv_parts.append(copied(arrived, arrived, LONG))
+
+    out_weight = staged(out_weight, kv_parts[0])
+    up_weight = staged(up_weight, out_weight)
+    down_weight = staged(down_weight, up_weight)
+    context = attention(queries, kv_parts, head_size, [out_weight, up_weight])
     partial = out_projected(context, permuted(context, "tensor", 1), out_weight, rows)
     attended = added(to_all(partial, "ulysses"))
     mixed = tokens.astype(jnp.float32) + own_mod[2] * attended
     normed_two = normalized(mixed, features) * (1.0 + own_mod[4]) + own_mod[3]
     blocks = from_all(normed_two.astype(jnp.bfloat16), "ulysses")
-    first = up_projected(blocks, up_weight, 0, 2)
+    first = up_projected(blocks, up_weight, 0, 2, [down_weight])
     first_arrived = permuted(first, "tensor", 1)
     second = up_projected(blocks, up_weight, 1, 2)
     second_arrived = permuted(second, "tensor", 1)
-    before = down_projected(first, first_arrived, down_weight, 0, 2, None, rows)[0]
-    partial = down_projected(second, second_arrived, down_weight, 1, 2, before, rows)
+    before = down_projected(first, first_arrived, down_weight, 0, None, rows)[0]
+    partial = down_projected(second, second_arrived, down_weight, 1, before, rows)
     feedforward = added(to_all(partial, "ulysses"))
     return mixed + own_mod[5] * feedforward
 

time: 113 us -> 109 us (0.965)
  waiting for transfers between devices: 51.4 us -> 42 us
  Pallas kernels: 25.7 us -> 31.4 us
    ppermute x32, waiting for transfers between devices: 51.4 us -> 42 us  [permuted(): return lax.ppermute(values, axis, [(i, i ^ distance) for i in range(size)])]
    pallas_call x13 -> x22, Pallas kernels: 24.8 us -> 30.4 us  [the longest x6 14.1 us: staged(): pl.pallas_call(kernel, grid=(1,), in_specs=[anywhere] + after_specs([afte...]
  transfers between devices with their start and end apart: 32 -> 32, of which waited for: 17 -> 20; matrix products, arithmetic and copies ran while one was open for 0% -> 0% of each run, Pallas kernels for 15% -> 22%
where the time goes in v5:
time: 109 us
  waiting for transfers between devices  42 us (39%)
  Pallas kernels  31.4 us (29%)
  starting transfers between devices  30.5 us (28%)
  other arithmetic  2.24 us (2%)
  local copies, waits for them, and re-layouts  1.17 us (1%)
    ppermute x32, waiting for transfers between devices, permuted(): return lax.ppermute(values, axis, [(i, i ^ distance) for i in range(size)])  42 us
    ppermute x32, starting transfers between devices, permuted(): return lax.ppermute(values, axis, [(i, i ^ distance) for i in range(size)])  30.5 us
    pallas_call x6, Pallas kernels, staged(): pl.pallas_call(kernel, grid=(1,), in_specs=[anywhere] + after_specs([afte...  14.1 us
    pallas_call x4, Pallas kernels, projected(): pl.pallas_call((lambda *refs: project_kernel(len(blocks), count, other, *...  6.45 us
    pallas_call x2, Pallas kernels, down_projected(): pl.pallas_call(lambda *refs: down_kernel(part * depth, last, *refs), grid...  3.36 us
    pallas_call x2, Pallas kernels, up_projected(): pl.pallas_call(lambda *refs: up_kernel(part * columns, len(blocks), *refs...  3.08 us
  transfers between devices with their start and end apart: 32, of which 20 were waited for; matrix products, arithmetic and copies ran while one was open for 0% of the time, Pallas kernels for 22%

profile of v5, /device:TPU:0, one launch (start us, length us, event | category | flops | bytes accessed | tf_op | source)
XLA Modules:
  0.0 108.7 jit_solution(16260747264757118634)
XLA Ops:
  0.0 0.9 fusion.3
  0.9 1.1 %copy-done = bf16[3072,576]{0,1:T(8,128)(2,1)S(1)} copy-done((bf16[3072,576]{0,1:T(8,128)(2,1)S(1)}, bf16[3072,576]{0,1:T(8,128)(2,1)}, u32[]{:S(2)}) %copy-start) | copy-done | bytes 3538968
  2.0 1.0 fusion.9.refs_0_.after_ref
  3.1 4.1 %collective-permute-start.4 = (bf16[64,1536]{1,0:T(8,128)(2,1)S(1)}, bf16[64,1536]{1,0:T(8,128)(2,1)S(1)}, u32[]{:S(2)}, u32[]{:S(2)}) collective-permute-start(bf16[64,1536]{1,0:T(8,128)(2,1)S(1)} %copied.2), channel_id=1, source_target_pairs={{0,4},{2,6},{4,0},{6,2},{1,5},{3,7},{5,1},{7,3},{8,12},{10,14},{12... | collective-permute-start | bytes 589832 | tf_op jit(solution)/shard_map/ppermute | solution.py:164
  7.9 0.8 collective-permute-done.1.refs_1_
  8.7 1.6 %collective-permute-start.2 = (f32[2,576]{1,0:T(2,128)S(1)}, f32[2,576]{1,0:T(2,128)S(1)}, u32[]{:S(2)}, u32[]{:S(2)}) collective-permute-start(f32[2,576]{1,0:T(2,128)S(1)} %merged.3.after_ref.refs_0_), channel_id=1, source_target_pairs={{0,2},{2,0},{4,6},{6,4},{1,3},{3,1},{5,7},{7,5},{8,10},{10,8},{12,... | collective-permute-start | bytes 13832 | tf_op jit(solution)/shard_map/ppermute | solution.py:164
  10.3 1.6 %staged.6.refs_2_.refs_6_.refs_1_ = bf16[1536,768]{1,0:T(8,128)(2,1)S(1)} custom-call(bf16[3,1536,768]{2,1,0:T(8,128)(2,1)} %bitcast.21, f32[2,576]{1,0:T(2,128)S(1)} %merged.3.after_ref.refs_0_), custom_call_target="tpu_custom_call" | custom-call | bytes 2359296 | tf_op jit(solution)/shard_map/staged/pallas_call | solution.py:464
  12.3 1.6 %collective-permute-start.3 = (f32[4,576]{1,0:T(4,128)S(1)}, f32[4,576]{1,0:T(4,128)S(1)}, u32[]{:S(2)}, u32[]{:S(2)}) collective-permute-start(f32[4,576]{1,0:T(4,128)S(1)} %merged.4.after_ref.refs_0_), channel_id=1, source_target_pairs={{0,4},{2,6},{4,0},{6,2},{1,5},{3,7},{5,1},{7,3},{8,12},{10,14},{12... | collective-permute-start | bytes 27656 | tf_op jit(solution)/shard_map/ppermute | solution.py:164
  13.9 1.6 %staged.8.refs_4_.refs_8_.refs_3_.refs_7_.refs_2_ = bf16[1536,768]{1,0:T(8,128)(2,1)S(1)} custom-call(bf16[3,1536,768]{2,1,0:T(8,128)(2,1)} %bitcast.22, f32[4,576]{1,0:T(4,128)S(1)} %merged.4.after_ref.refs_0_), custom_call_target="tpu_custom_call" | custom-call | bytes 2359296 | tf_op jit(solution)/shard_map/staged/pallas_call | solution.py:464
  15.6 1.6 %staged.7.refs_3_.refs_7_.refs_2_.refs_6_.refs_1_ = bf16[1536,768]{1,0:T(8,128)(2,1)S(1)} custom-call(bf16[3,1536,768]{2,1,0:T(8,128)(2,1)} %bitcast.23, f32[4,576]{1,0:T(4,128)S(1)} %merged.4.after_ref.refs_0_), custom_call_target="tpu_custom_call" | custom-call | bytes 2359296 | tf_op jit(solution)/shard_map/staged/pallas_call | solution.py:464
  17.3 2.5 %collective-permute-start.7 = (bf16[64,1664]{1,0:T(8,128)(2,1)S(1)}, bf16[64,1664]{1,0:T(8,128)(2,1)S(1)}, u32[]{:S(2)}, u32[]{:S(2)}) collective-permute-start(bf16[64,1664]{1,0:T(8,128)(2,1)S(1)} %packed.1.refs_0_), channel_id=1, source_target_pairs={{0,24},{8,16},{16,8},{24,0},{1,25},{9,17},{17,9},{25,1},{2,26},{10... | collective-permute-start | bytes 638984 | tf_op jit(solution)/shard_map/ppermute | solution.py:164
  20.9 1.4 %collective-permute-start.8 = (bf16[64,1536]{1,0:T(8,128)(2,1)S(1)}, bf16[64,1536]{1,0:T(8,128)(2,1)S(1)}, u32[]{:S(2)}, u32[]{:S(2)}) collective-permute-start(bf16[64,1536]{1,0:T(8,128)(2,1)S(1)} %collective-permute-done.4.refs_5_.refs_0_), channel_id=1, source_target_pairs={{0,2},{2,0},{4,6},{6,4},{1,3},{3,1},{5,7},{7,5},{8,10},{10,8},{12,... | collective-permute-start | bytes 589832 | tf_op jit(solution)/shard_map/ppermute | solution.py:164
  22.2 4.3 %collective-permute-done.8.refs_1_ = bf16[64,1536]{1,0:T(8,128)(2,1)S(1)} collective-permute-done((bf16[64,1536]{1,0:T(8,128)(2,1)S(1)}, bf16[64,1536]{1,0:T(8,128)(2,1)S(1)}, u32[]{:S(2)}, u32[]{:S(2)}) %collective-permute-start.8) | collective-permute-done | bytes 196640 | tf_op jit(solution)/shard_map/ppermute | solution.py:164
  26.8 2.1 %collective-permute-done.6.refs_2_ = bf16[64,1664]{1,0:T(8,128)(2,1)S(1)} collective-permute-done((bf16[64,1664]{1,0:T(8,128)(2,1)S(1)}, bf16[64,1664]{1,0:T(8,128)(2,1)S(1)}, u32[]{:S(2)}, u32[]{:S(2)}) %collective-permute-start.6) | collective-permute-done | bytes 213024 | tf_op jit(solution)/shard_map/ppermute | solution.py:164
  29.5 1.4 %projected.4 = (bf16[256,384]{1,0:T(8,128)(2,1)S(1)}, bf16[256,384]{1,0:T(8,128)(2,1)S(1)}, bf16[256,384]{1,0:T(8,128)(2,1)S(1)}, bf16[256,1536]{1,0:T(8,128)(2,1)S(1)}) custom-call(bf16[64,1664]{1,0:T(8,128)(2,1)S(1)} %packed.1.refs_0_, bf16[64,1664]{1,0:T(8,128)(2,1)S(1)} %collective-permute-done.5.refs_1_, ...), custom_call_target="tpu_custom_call" | custom-call | tf_op jit(solution)/shard_map/projected/pallas_call | solution.py:428
  31.0 1.7 %collective-permute-start.16 = (bf16[128,1536]{1,0:T(8,128)(2,1)S(1)}, bf16[128,1536]{1,0:T(8,128)(2,1)S(1)}, u32[]{:S(2)}, u32[]{:S(2)}) collective-permute-start(bf16[128,1536]{1,0:T(8,128)(2,1)S(1)} %standardized.3.refs_9_.refs_0_), channel_id=1, source_target_pairs={{0,24},{8,16},{16,8},{24,0},{1,25},{9,17},{17,9},{25,1},{2,26},{10... | collective-permute-start | bytes 1179656 | tf_op jit(solution)/shard_map/ppermute | solution.py:164
  32.7 1.3 %collective-permute-start.15 = (bf16[128,1536]{1,0:T(8,128)(2,1)S(1)}, bf16[128,1536]{1,0:T(8,128)(2,1)S(1)}, u32[]{:S(2)}, u32[]{:S(2)}) collective-permute-start(bf16[128,1536]{1,0:T(8,128)(2,1)S(1)} %standardized.3.refs_9_.refs_0_), channel_id=1, source_target_pairs={{0,16},{8,24},{16,0},{24,8},{1,17},{9,25},{17,1},{25,9},{2,18},{10... | collective-permute-start | bytes 1179656 | tf_op jit(solution)/shard_map/ppermute | solution.py:164
  35.1 1.4 %projected.5 = (bf16[256,384]{1,0:T(8,128)(2,1)S(1)}, bf16[256,384]{1,0:T(8,128)(2,1)S(1)}, bf16[256,384]{1,0:T(8,128)(2,1)S(1)}) custom-call(bf16[256,1536]{1,0:T(8,128)(2,1)S(1)} %get-tuple-element.35.refs_0_, bf16[1536,768]{1,0:T(8,128)(2,1)S(1)} %staged.6.refs_2_.refs_6_.refs_1_, bf16[1536,768]{1,0:T(8,128)(2,1)S(1)} %staged.7.refs_3_.refs_7_.refs_2_.refs_6_.refs_1_, ...), custom_call_target="tpu_custom_call" | custom-call | tf_op jit(solution)/shard_map/projected/pallas_call | solution.py:428
  36.8 1.4 %collective-permute-start.13 = (bf16[256,768]{1,0:T(8,128)(2,1)S(1)}, bf16[256,768]{1,0:T(8,128)(2,1)S(1)}, u32[]{:S(2)}, u32[]{:S(2)}) collective-permute-start(bf16[256,768]{1,0:T(8,128)(2,1)S(1)} %get-tuple-element.43.refs_8_.after_ref.refs_1_), channel_id=1, source_target_pairs={{0,2},{2,0},{4,6},{6,4},{1,3},{3,1},{5,7},{7,5},{8,10},{10,8},{12,... | collective-permute-start | bytes 1179656 | tf_op jit(solution)/shard_map/ppermute | solution.py:164
  38.2 1.6 %staged.9.after_ref.refs_4_.weight_ref = bf16[768,1536]{1,0:T(8,128)(2,1)S(1)} custom-call(bf16[768,1536]{1,0:T(8,128)(2,1)} %weight_ref.3, bf16[256,768]{1,0:T(8,128)(2,1)S(1)} %get-tuple-element.43.refs_8_.after_ref.refs_1_), custom_call_target="tpu_custom_call" | custom-call | bytes 2359296 | tf_op jit(solution)/shard_map/staged/pallas_call | solution.py:464
  39.9 3.8 %staged.10.refs_5_.refs_4_.after_ref = bf16[1536,3072]{1,0:T(8,128)(2,1)S(1)} custom-call(bf16[1536,3072]{1,0:T(8,128)(2,1)} %weight_ref.4, bf16[768,1536]{1,0:T(8,128)(2,1)S(1)} %staged.9.after_ref.refs_4_.weight_ref), custom_call_target="tpu_custom_call" | custom-call | bytes 9437184 | tf_op jit(solution)/shard_map/staged/pallas_call | solution.py:464
  43.9 7.9 %collective-permute-done.15.refs_1_.refs_2_ = bf16[128,1536]{1,0:T(8,128)(2,1)S(1)} collective-permute-done((bf16[128,1536]{1,0:T(8,128)(2,1)S(1)}, bf16[128,1536]{1,0:T(8,128)(2,1)S(1)}, u32[]{:S(2)}, u32[]{:S(2)}) %collective-permute-start.15) | collective-permute-done | bytes 393248 | tf_op jit(solution)/shard_map/ppermute | solution.py:164
  51.9 1.8 %projected.6 = (bf16[512,384]{1,0:T(8,128)(2,1)S(1)}, bf16[512,384]{1,0:T(8,128)(2,1)S(1)}, bf16[512,1536]{1,0:T(8,128)(2,1)S(1)}) custom-call(bf16[128,1536]{1,0:T(8,128)(2,1)S(1)} %standardized.3.refs_9_.refs_0_, bf16[128,1536]{1,0:T(8,128)(2,1)S(1)} %collective-permute-done.14.refs_0_.refs_1_, ...), custom_call_target="tpu_custom_call" | custom-call | tf_op jit(solution)/shard_map/projected/pallas_call | solution.py:428
  53.7 1.8 %projected.7 = (bf16[512,384]{1,0:T(8,128)(2,1)S(1)}, bf16[512,384]{1,0:T(8,128)(2,1)S(1)}) custom-call(bf16[512,1536]{1,0:T(8,128)(2,1)S(1)} %get-tuple-element.44.refs_0_, bf16[1536,768]{1,0:T(8,128)(2,1)S(1)} %staged.7.refs_3_.refs_7_.refs_2_.refs_6_.refs_1_, bf16[1536,768]{1,0:T(8,128)(2,1)S(1)} %staged.8.refs_4_.refs_8_.refs_3_.refs_7_.refs_2_), custom_call_target="tpu_custom_call" | custom-call | tf_op jit(solution)/shard_map/projected/pallas_call | solution.py:428
  56.1 1.2 %collective-permute-done.17.refs_2_ = bf16[512,384]{1,0:T(8,128)(2,1)S(1)} collective-permute-done((bf16[512,384]{1,0:T(8,128)(2,1)S(1)}, bf16[512,384]{1,0:T(8,128)(2,1)S(1)}, u32[]{:S(2)}, u32[]{:S(2)}) %collective-permute-start.17) | collective-permute-done | bytes 393248 | tf_op jit(solution)/shard_map/ppermute | solution.py:164
  58.3 1.7 %attention.1.own_ref = bf16[256,384]{1,0:T(8,128)(2,1)S(1)} custom-call(bf16[256,384]{1,0:T(8,128)(2,1)S(1)} %get-tuple-element.42.refs_0_, bf16[256,768]{1,0:T(8,128)(2,1)S(1)} %get-tuple-element.43.refs_8_.after_ref.refs_1_, bf16[256,768]{1,0:T(8,128)(2,1)S(1)} %copied.3.refs_2_, bf16[512,768]{1,0:T(8,128)(2,1)S(1)} %split_heads.3.refs_3_, ...), custom_call_target="tpu_custom_call" | custom-call | flops 402653184 | bytes 1572864 | tf_op jit(solution)/shard_map/attention/pallas_call | solution.py:575
  60.2 1.3 %collective-permute-done.19.arrived_ref = bf16[256,384]{1,0:T(8,128)(2,1)S(1)} collective-permute-done((bf16[256,384]{1,0:T(8,128)(2,1)S(1)}, bf16[256,384]{1,0:T(8,128)(2,1)S(1)}, u32[]{:S(2)}, u32[]{:S(2)}) %collective-permute-start.19) | collective-permute-done | bytes 196640 | tf_op jit(solution)/shard_map/ppermute | solution.py:164
  61.5 1.0 out_projected.1
  62.5 1.6 %collective-permute-start.20 = (bf16[64,1536]{1,0:T(8,128)(2,1)S(1)}, bf16[64,1536]{1,0:T(8,128)(2,1)S(1)}, u32[]{:S(2)}, u32[]{:S(2)}) collective-permute-start(bf16[64,1536]{1,0:T(8,128)(2,1)S(1)} %get-tuple-element.50), channel_id=1, source_target_pairs={{0,8},{8,0},{16,24},{24,16},{1,9},{9,1},{17,25},{25,17},{2,10},{10... | collective-permute-start | bytes 589832 | tf_op jit(solution)/shard_map/ppermute | solution.py:164
  64.0 0.7 collective-permute-start.21
  64.7 1.3 %collective-permute-start.22 = (bf16[64,1536]{1,0:T(8,128)(2,1)S(1)}, bf16[64,1536]{1,0:T(8,128)(2,1)S(1)}, u32[]{:S(2)}, u32[]{:S(2)}) collective-permute-start(bf16[64,1536]{1,0:T(8,128)(2,1)S(1)} %get-tuple-element.52), channel_id=1, source_target_pairs={{0,24},{8,16},{16,8},{24,0},{1,25},{9,17},{17,9},{25,1},{2,26},{10... | collective-permute-start | bytes 589832 | tf_op jit(solution)/shard_map/ppermute | solution.py:164
  66.0 4.3 %collective-permute-done.20 = bf16[64,1536]{1,0:T(8,128)(2,1)S(1)} collective-permute-done((bf16[64,1536]{1,0:T(8,128)(2,1)S(1)}, bf16[64,1536]{1,0:T(8,128)(2,1)S(1)}, u32[]{:S(2)}, u32[]{:S(2)}) %collective-permute-start.20) | collective-permute-done | bytes 196640 | tf_op jit(solution)/shard_map/ppermute | solution.py:164
  70.3 4.6 %collective-permute-done.21 = bf16[64,1536]{1,0:T(8,128)(2,1)S(1)} collective-permute-done((bf16[64,1536]{1,0:T(8,128)(2,1)S(1)}, bf16[64,1536]{1,0:T(8,128)(2,1)S(1)}, u32[]{:S(2)}, u32[]{:S(2)}) %collective-permute-start.21) | collective-permute-done | bytes 196640 | tf_op jit(solution)/shard_map/ppermute | solution.py:164
  75.3 1.1 %collective-permute-done.23 = f32[2,64]{1,0:T(2,128)S(1)} collective-permute-done((f32[2,64]{1,0:T(2,128)S(1)}, f32[2,64]{1,0:T(2,128)S(1)}, u32[]{:S(2)}, u32[]{:S(2)}) %collective-permute-start.23) | collective-permute-done | bytes 544 | tf_op jit(solution)/shard_map/ppermute | solution.py:164
  76.6 1.5 %collective-permute-start.26 = (bf16[64,1536]{1,0:T(8,128)(2,1)S(1)}, bf16[64,1536]{1,0:T(8,128)(2,1)S(1)}, u32[]{:S(2)}, u32[]{:S(2)}) collective-permute-start(bf16[64,1536]{1,0:T(8,128)(2,1)S(1)} %add_convert_fusion.refs_0_), channel_id=1, source_target_pairs={{0,24},{8,16},{16,8},{24,0},{1,25},{9,17},{17,9},{25,1},{2,26},{10... | collective-permute-start | bytes 589832 | tf_op jit(solution)/shard_map/ppermute | solution.py:164
  78.6 1.5 %collective-permute-start.24 = (bf16[64,1536]{1,0:T(8,128)(2,1)S(1)}, bf16[64,1536]{1,0:T(8,128)(2,1)S(1)}, u32[]{:S(2)}, u32[]{:S(2)}) collective-permute-start(bf16[64,1536]{1,0:T(8,128)(2,1)S(1)} %add_convert_fusion.refs_0_), channel_id=1, source_target_pairs={{0,8},{8,0},{16,24},{24,16},{1,9},{9,1},{17,25},{25,17},{2,10},{10... | collective-permute-start | bytes 589832 | tf_op jit(solution)/shard_map/ppermute | solution.py:164
  80.1 3.8 %staged.11.refs_5_.refs_2_ = bf16[3072,1536]{1,0:T(8,128)(2,1)S(1)} custom-call(bf16[3072,1536]{1,0:T(8,128)(2,1)} %weight_ref.5, bf16[1536,3072]{1,0:T(8,128)(2,1)S(1)} %staged.10.refs_5_.refs_4_.after_ref), custom_call_target="tpu_custom_call" | custom-call | bytes 9437184 | tf_op jit(solution)/shard_map/staged/pallas_call | solution.py:464
  83.9 1.4 %collective-permute-done.26.refs_3_ = bf16[64,1536]{1,0:T(8,128)(2,1)S(1)} collective-permute-done((bf16[64,1536]{1,0:T(8,128)(2,1)S(1)}, bf16[64,1536]{1,0:T(8,128)(2,1)S(1)}, u32[]{:S(2)}, u32[]{:S(2)}) %collective-permute-start.26) | collective-permute-done | bytes 196640 | tf_op jit(solution)/shard_map/ppermute | solution.py:164
  85.3 3.4 %collective-permute-done.25.refs_2_ = bf16[64,1536]{1,0:T(8,128)(2,1)S(1)} collective-permute-done((bf16[64,1536]{1,0:T(8,128)(2,1)S(1)}, bf16[64,1536]{1,0:T(8,128)(2,1)S(1)}, u32[]{:S(2)}, u32[]{:S(2)}) %collective-permute-start.25) | collective-permute-done | bytes 196640 | tf_op jit(solution)/shard_map/ppermute | solution.py:164
  88.7 1.4 %up_projected.3.refs_0_ = bf16[256,1536]{1,0:T(8,128)(2,1)S(1)} custom-call(bf16[64,1536]{1,0:T(8,128)(2,1)S(1)} %add_convert_fusion.refs_0_, bf16[64,1536]{1,0:T(8,128)(2,1)S(1)} %collective-permute-done.24.refs_1_, bf16[64,1536]{1,0:T(8,128)(2,1)S(1)} %collective-permute-done.25.refs_2_, bf16[64,1536]{1,0:T(8,128)(2,1)S(1)} %collective-permute-done.26.refs_3_, ...), custom_call_target="tpu_custom_call" | custom-call | flops 1207959552 | tf_op jit(solution)/shard_map/up_projected/pallas_call | solution.py:647
  90.3 1.6 %up_projected.2.refs_0_ = bf16[256,1536]{1,0:T(8,128)(2,1)S(1)} custom-call(bf16[64,1536]{1,0:T(8,128)(2,1)S(1)} %add_convert_fusion.refs_0_, bf16[64,1536]{1,0:T(8,128)(2,1)S(1)} %collective-permute-done.24.refs_1_, bf16[64,1536]{1,0:T(8,128)(2,1)S(1)} %collective-permute-done.25.refs_2_, bf16[64,1536]{1,0:T(8,128)(2,1)S(1)} %collective-permute-done.26.refs_3_, ...), custom_call_target="tpu_custom_call" | custom-call | flops 1207959552 | tf_op jit(solution)/shard_map/up_projected/pallas_call | solution.py:647
  92.5 1.7 %down_projected.2.refs_3_ = f32[256,1536]{1,0:T(8,128)S(1)} custom-call(bf16[256,1536]{1,0:T(8,128)(2,1)S(1)} %up_projected.3.refs_0_, bf16[256,1536]{1,0:T(8,128)(2,1)S(1)} %collective-permute-done.28.refs_1_, bf16[3072,1536]{1,0:T(8,128)(2,1)S(1)} %staged.11.refs_5_.refs_2_), custom_call_target="tpu_custom_call" | custom-call | flops 1207959552 | tf_op jit(solution)/shard_map/down_projected/pallas_call | solution.py:693
  94.4 1.7 %down_projected.3 = (bf16[64,1536]{1,0:T(8,128)(2,1)S(1)}, bf16[64,1536]{1,0:T(8,128)(2,1)S(1)}, bf16[64,1536]{1,0:T(8,128)(2,1)S(1)}, bf16[64,1536]{1,0:T(8,128)(2,1)S(1)}) custom-call(bf16[256,1536]{1,0:T(8,128)(2,1)S(1)} %up_projected.2.refs_0_, bf16[256,1536]{1,0:T(8,128)(2,1)S(1)} %collective-permute-done.27.refs_1_, ...), custom_call_target="tpu_custom_call" | custom-call | flops 1207959552 | tf_op jit(solution)/shard_map/down_projected/pallas_call | solution.py:693
  96.7 1.4 %collective-permute-start.30 = (bf16[64,1536]{1,0:T(8,128)(2,1)S(1)}, bf16[64,1536]{1,0:T(8,128)(2,1)S(1)}, u32[]{:S(2)}, u32[]{:S(2)}) collective-permute-start(bf16[64,1536]{1,0:T(8,128)(2,1)S(1)} %get-tuple-element.55), channel_id=1, source_target_pairs={{0,16},{8,24},{16,0},{24,8},{1,17},{9,25},{17,1},{25,9},{2,18},{10... | collective-permute-start | bytes 589832 | tf_op jit(solution)/shard_map/ppermute | solution.py:164
  98.1 1.5 %collective-permute-start.31 = (bf16[64,1536]{1,0:T(8,128)(2,1)S(1)}, bf16[64,1536]{1,0:T(8,128)(2,1)S(1)}, u32[]{:S(2)}, u32[]{:S(2)}) collective-permute-start(bf16[64,1536]{1,0:T(8,128)(2,1)S(1)} %get-tuple-element.56), channel_id=1, source_target_pairs={{0,24},{8,16},{16,8},{24,0},{1,25},{9,17},{17,9},{25,1},{2,26},{10... | collective-permute-start | bytes 589832 | tf_op jit(solution)/shard_map/ppermute | solution.py:164
  99.7 4.2 %collective-permute-done.29 = bf16[64,1536]{1,0:T(8,128)(2,1)S(1)} collective-permute-done((bf16[64,1536]{1,0:T(8,128)(2,1)S(1)}, bf16[64,1536]{1,0:T(8,128)(2,1)S(1)}, u32[]{:S(2)}, u32[]{:S(2)}) %collective-permute-start.29) | collective-permute-done | bytes 196640 | tf_op jit(solution)/shard_map/ppermute | solution.py:164
  104.2 3.7 %collective-permute-done.31 = bf16[64,1536]{1,0:T(8,128)(2,1)S(1)} collective-permute-done((bf16[64,1536]{1,0:T(8,128)(2,1)S(1)}, bf16[64,1536]{1,0:T(8,128)(2,1)S(1)}, u32[]{:S(2)}, u32[]{:S(2)}) %collective-permute-start.31) | collective-permute-done | bytes 196640 | tf_op jit(solution)/shard_map/ppermute | solution.py:164
  107.8 0.9 multiply_add_fusion
  (68 shorter events, 9.5 us)
Async XLA Ops:
  0.0 2.0 %copy-start = (bf16[3072,576]{0,1:T(8,128)(2,1)S(1)}, bf16[3072,576]{0,1:T(8,128)(2,1)}, u32[]{:S(2)}) copy-start(bf16[3072,576]{0,1:T(8,128)(2,1)} %param.11) | copy-start | bytes 10616836
  0.0 3.0 %copy-start.2 = (bf16[64,1536]{1,0:T(8,128)(2,1)S(1)}, bf16[64,1536]{1,0:T(8,128)(2,1)}, u32[]{:S(2)}) copy-start(bf16[64,1536]{1,0:T(8,128)(2,1)} %values_ref.3) | copy-start | bytes 589828
  3.1 14.2 %collective-permute-start.4 = (bf16[64,1536]{1,0:T(8,128)(2,1)S(1)}, bf16[64,1536]{1,0:T(8,128)(2,1)S(1)}, u32[]{:S(2)}, u32[]{:S(2)}) collective-permute-start(bf16[64,1536]{1,0:T(8,128)(2,1)S(1)} %copied.2), channel_id=1, source_target_pairs={{0,4},{2,6},{4,0},{6,2},{1,5},{3,7},{5,1},{7,3},{8,12},{10,14},{12... | collective-permute-start | bytes 589832 | tf_op jit(solution)/shard_map/ppermute | solution.py:164
  7.3 4.6 %collective-permute-start = (f32[64,128]{1,0:T(8,128)S(1)}, f32[64,128]{1,0:T(8,128)S(1)}, u32[]{:S(2)}, u32[]{:S(2)}) collective-permute-start(f32[64,128]{1,0:T(8,128)S(1)} %get-tuple-element.32.refs_1_), channel_id=1, source_target_pairs={{0,1},{1,0},{2,3},{3,2},{4,5},{5,4},{6,7},{7,6},{8,9},{9,8},{10,11... | collective-permute-start | bytes 98312 | tf_op jit(solution)/shard_map/ppermute | solution.py:164
  7.4 1.3 %collective-permute-start.1 = (f32[1,576]{1,0:T(1,128)S(1)}, f32[1,576]{1,0:T(1,128)S(1)}, u32[]{:S(2)}, u32[]{:S(2)}) collective-permute-start(f32[1,576]{1,0:T(1,128)S(1)} %fusion.9.refs_0_.after_ref), channel_id=1, source_target_pairs={{0,1},{1,0},{2,3},{3,2},{4,5},{5,4},{6,7},{7,6},{8,9},{9,8},{10,11... | collective-permute-start | bytes 6920 | tf_op jit(solution)/shard_map/ppermute | solution.py:164
  8.7 3.6 %collective-permute-start.2 = (f32[2,576]{1,0:T(2,128)S(1)}, f32[2,576]{1,0:T(2,128)S(1)}, u32[]{:S(2)}, u32[]{:S(2)}) collective-permute-start(f32[2,576]{1,0:T(2,128)S(1)} %merged.3.after_ref.refs_0_), channel_id=1, source_target_pairs={{0,2},{2,0},{4,6},{6,4},{1,3},{3,1},{5,7},{7,5},{8,10},{10,8},{12,... | collective-permute-start | bytes 13832 | tf_op jit(solution)/shard_map/ppermute | solution.py:164
  12.3 4.9 %collective-permute-start.3 = (f32[4,576]{1,0:T(4,128)S(1)}, f32[4,576]{1,0:T(4,128)S(1)}, u32[]{:S(2)}, u32[]{:S(2)}) collective-permute-start(f32[4,576]{1,0:T(4,128)S(1)} %merged.4.after_ref.refs_0_), channel_id=1, source_target_pairs={{0,4},{2,6},{4,0},{6,2},{1,5},{3,7},{5,1},{7,3},{8,12},{10,14},{12... | collective-permute-start | bytes 27656 | tf_op jit(solution)/shard_map/ppermute | solution.py:164
  17.3 9.5 %collective-permute-start.7 = (bf16[64,1664]{1,0:T(8,128)(2,1)S(1)}, bf16[64,1664]{1,0:T(8,128)(2,1)S(1)}, u32[]{:S(2)}, u32[]{:S(2)}) collective-permute-start(bf16[64,1664]{1,0:T(8,128)(2,1)S(1)} %packed.1.refs_0_), channel_id=1, source_target_pairs={{0,24},{8,16},{16,8},{24,0},{1,25},{9,17},{17,9},{25,1},{2,26},{10... | collective-permute-start | bytes 638984 | tf_op jit(solution)/shard_map/ppermute | solution.py:164
  19.8 9.1 %collective-permute-start.6 = (bf16[64,1664]{1,0:T(8,128)(2,1)S(1)}, bf16[64,1664]{1,0:T(8,128)(2,1)S(1)}, u32[]{:S(2)}, u32[]{:S(2)}) collective-permute-start(bf16[64,1664]{1,0:T(8,128)(2,1)S(1)} %packed.1.refs_0_), channel_id=1, source_target_pairs={{0,16},{8,24},{16,0},{24,8},{1,17},{9,25},{17,1},{25,9},{2,18},{10... | collective-permute-start | bytes 638984 | tf_op jit(solution)/shard_map/ppermute | solution.py:164
  20.3 8.7 %collective-permute-start.5 = (bf16[64,1664]{1,0:T(8,128)(2,1)S(1)}, bf16[64,1664]{1,0:T(8,128)(2,1)S(1)}, u32[]{:S(2)}, u32[]{:S(2)}) collective-permute-start(bf16[64,1664]{1,0:T(8,128)(2,1)S(1)} %packed.1.refs_0_), channel_id=1, source_target_pairs={{0,8},{8,0},{16,24},{24,16},{1,9},{9,1},{17,25},{25,17},{2,10},{10... | collective-permute-start | bytes 638984 | tf_op jit(solution)/shard_map/ppermute | solution.py:164
  20.9 5.7 %collective-permute-start.8 = (bf16[64,1536]{1,0:T(8,128)(2,1)S(1)}, bf16[64,1536]{1,0:T(8,128)(2,1)S(1)}, u32[]{:S(2)}, u32[]{:S(2)}) collective-permute-start(bf16[64,1536]{1,0:T(8,128)(2,1)S(1)} %collective-permute-done.4.refs_5_.refs_0_), channel_id=1, source_target_pairs={{0,2},{2,0},{4,6},{6,4},{1,3},{3,1},{5,7},{7,5},{8,10},{10,8},{12,... | collective-permute-start | bytes 589832 | tf_op jit(solution)/shard_map/ppermute | solution.py:164
  26.7 2.5 %collective-permute-start.9 = (f32[128,128]{1,0:T(8,128)S(1)}, f32[128,128]{1,0:T(8,128)S(1)}, u32[]{:S(2)}, u32[]{:S(2)}) collective-permute-start(f32[128,128]{1,0:T(8,128)S(1)} %get-tuple-element.34.refs_1_), channel_id=1, source_target_pairs={{0,1},{1,0},{2,3},{3,2},{4,5},{5,4},{6,7},{7,6},{8,9},{9,8},{10,11... | collective-permute-start | bytes 196616 | tf_op jit(solution)/shard_map/ppermute | solution.py:164
  30.9 3.6 %collective-permute-start.10 = (bf16[256,384]{1,0:T(8,128)(2,1)S(1)}, bf16[256,384]{1,0:T(8,128)(2,1)S(1)}, u32[]{:S(2)}, u32[]{:S(2)}) collective-permute-start(bf16[256,384]{1,0:T(8,128)(2,1)S(1)} %get-tuple-element.39), channel_id=1, source_target_pairs={{0,1},{1,0},{2,3},{3,2},{4,5},{5,4},{6,7},{7,6},{8,9},{9,8},{10,11... | collective-permute-start | bytes 589832 | tf_op jit(solution)/shard_map/ppermute | solution.py:164
  31.0 12.9 %collective-permute-start.16 = (bf16[128,1536]{1,0:T(8,128)(2,1)S(1)}, bf16[128,1536]{1,0:T(8,128)(2,1)S(1)}, u32[]{:S(2)}, u32[]{:S(2)}) collective-permute-start(bf16[128,1536]{1,0:T(8,128)(2,1)S(1)} %standardized.3.refs_9_.refs_0_), channel_id=1, source_target_pairs={{0,24},{8,16},{16,8},{24,0},{1,25},{9,17},{17,9},{25,1},{2,26},{10... | collective-permute-start | bytes 1179656 | tf_op jit(solution)/shard_map/ppermute | solution.py:164
  32.7 19.1 %collective-permute-start.15 = (bf16[128,1536]{1,0:T(8,128)(2,1)S(1)}, bf16[128,1536]{1,0:T(8,128)(2,1)S(1)}, u32[]{:S(2)}, u32[]{:S(2)}) collective-permute-start(bf16[128,1536]{1,0:T(8,128)(2,1)S(1)} %standardized.3.refs_9_.refs_0_), channel_id=1, source_target_pairs={{0,16},{8,24},{16,0},{24,8},{1,17},{9,25},{17,1},{25,9},{2,18},{10... | collective-permute-start | bytes 1179656 | tf_op jit(solution)/shard_map/ppermute | solution.py:164
  34.0 17.8 %collective-permute-start.14 = (bf16[128,1536]{1,0:T(8,128)(2,1)S(1)}, bf16[128,1536]{1,0:T(8,128)(2,1)S(1)}, u32[]{:S(2)}, u32[]{:S(2)}) collective-permute-start(bf16[128,1536]{1,0:T(8,128)(2,1)S(1)} %standardized.3.refs_9_.refs_0_), channel_id=1, source_target_pairs={{0,8},{8,0},{16,24},{24,16},{1,9},{9,1},{17,25},{25,17},{2,10},{10... | collective-permute-start | bytes 1179656 | tf_op jit(solution)/shard_map/ppermute | solution.py:164
  34.5 1.9 %collective-permute-start.11 = (bf16[256,384]{1,0:T(8,128)(2,1)S(1)}, bf16[256,384]{1,0:T(8,128)(2,1)S(1)}, u32[]{:S(2)}, u32[]{:S(2)}) collective-permute-start(bf16[256,384]{1,0:T(8,128)(2,1)S(1)} %get-tuple-element.40), channel_id=1, source_target_pairs={{0,1},{1,0},{2,3},{3,2},{4,5},{5,4},{6,7},{7,6},{8,9},{9,8},{10,11... | collective-permute-start | bytes 589832 | tf_op jit(solution)/shard_map/ppermute | solution.py:164
  34.6 1.9 %collective-permute-start.12 = (bf16[256,384]{1,0:T(8,128)(2,1)S(1)}, bf16[256,384]{1,0:T(8,128)(2,1)S(1)}, u32[]{:S(2)}, u32[]{:S(2)}) collective-permute-start(bf16[256,384]{1,0:T(8,128)(2,1)S(1)} %get-tuple-element.41), channel_id=1, source_target_pairs={{0,1},{1,0},{2,3},{3,2},{4,5},{5,4},{6,7},{7,6},{8,9},{9,8},{10,11... | collective-permute-start | bytes 589832 | tf_op jit(solution)/shard_map/ppermute | solution.py:164
  35.1 1.4 %copy-start.3 = (f32[128]{0:T(128)S(1)}, f32[128]{0:T(128)}, u32[]{:S(2)}) copy-start(f32[128]{0:T(128)} %param.13) | copy-start | bytes 1540
  35.1 1.4 %copy-start.4 = (f32[128]{0:T(128)S(1)}, f32[128]{0:T(128)}, u32[]{:S(2)}) copy-start(f32[128]{0:T(128)} %param.14) | copy-start | bytes 1540
  36.8 19.2 %collective-permute-start.13 = (bf16[256,768]{1,0:T(8,128)(2,1)S(1)}, bf16[256,768]{1,0:T(8,128)(2,1)S(1)}, u32[]{:S(2)}, u32[]{:S(2)}) collective-permute-start(bf16[256,768]{1,0:T(8,128)(2,1)S(1)} %get-tuple-element.43.refs_8_.after_ref.refs_1_), channel_id=1, source_target_pairs={{0,2},{2,0},{4,6},{6,4},{1,3},{3,1},{5,7},{7,5},{8,10},{10,8},{12,... | collective-permute-start | bytes 1179656 | tf_op jit(solution)/shard_map/ppermute | solution.py:164
  55.5 1.8 %collective-permute-start.17 = (bf16[512,384]{1,0:T(8,128)(2,1)S(1)}, bf16[512,384]{1,0:T(8,128)(2,1)S(1)}, u32[]{:S(2)}, u32[]{:S(2)}) collective-permute-start(bf16[512,384]{1,0:T(8,128)(2,1)S(1)} %get-tuple-element.47), channel_id=1, source_target_pairs={{0,1},{1,0},{2,3},{3,2},{4,5},{5,4},{6,7},{7,6},{8,9},{9,8},{10,11... | collective-permute-start | bytes 1179656 | tf_op jit(solution)/shard_map/ppermute | solution.py:164
  55.6 2.3 %collective-permute-start.18 = (bf16[512,384]{1,0:T(8,128)(2,1)S(1)}, bf16[512,384]{1,0:T(8,128)(2,1)S(1)}, u32[]{:S(2)}, u32[]{:S(2)}) collective-permute-start(bf16[512,384]{1,0:T(8,128)(2,1)S(1)} %get-tuple-element.48), channel_id=1, source_target_pairs={{0,1},{1,0},{2,3},{3,2},{4,5},{5,4},{6,7},{7,6},{8,9},{9,8},{10,11... | collective-permute-start | bytes 1179656 | tf_op jit(solution)/shard_map/ppermute | solution.py:164
  60.0 1.5 %collective-permute-start.19 = (bf16[256,384]{1,0:T(8,128)(2,1)S(1)}, bf16[256,384]{1,0:T(8,128)(2,1)S(1)}, u32[]{:S(2)}, u32[]{:S(2)}) collective-permute-start(bf16[256,384]{1,0:T(8,128)(2,1)S(1)} %attention.1.own_ref), channel_id=1, source_target_pairs={{0,1},{1,0},{2,3},{3,2},{4,5},{5,4},{6,7},{7,6},{8,9},{9,8},{10,11... | collective-permute-start | bytes 589832 | tf_op jit(solution)/shard_map/ppermute | solution.py:164
  62.5 7.8 %collective-permute-start.20 = (bf16[64,1536]{1,0:T(8,128)(2,1)S(1)}, bf16[64,1536]{1,0:T(8,128)(2,1)S(1)}, u32[]{:S(2)}, u32[]{:S(2)}) collective-permute-start(bf16[64,1536]{1,0:T(8,128)(2,1)S(1)} %get-tuple-element.50), channel_id=1, source_target_pairs={{0,8},{8,0},{16,24},{24,16},{1,9},{9,1},{17,25},{25,17},{2,10},{10... | collective-permute-start | bytes 589832 | tf_op jit(solution)/shard_map/ppermute | solution.py:164
  64.0 10.9 %collective-permute-start.21 = (bf16[64,1536]{1,0:T(8,128)(2,1)S(1)}, bf16[64,1536]{1,0:T(8,128)(2,1)S(1)}, u32[]{:S(2)}, u32[]{:S(2)}) collective-permute-start(bf16[64,1536]{1,0:T(8,128)(2,1)S(1)} %get-tuple-element.51), channel_id=1, source_target_pairs={{0,16},{8,24},{16,0},{24,8},{1,17},{9,25},{17,1},{25,9},{2,18},{10... | collective-permute-start | bytes 589832 | tf_op jit(solution)/shard_map/ppermute | solution.py:164
  64.7 10.2 %collective-permute-start.22 = (bf16[64,1536]{1,0:T(8,128)(2,1)S(1)}, bf16[64,1536]{1,0:T(8,128)(2,1)S(1)}, u32[]{:S(2)}, u32[]{:S(2)}) collective-permute-start(bf16[64,1536]{1,0:T(8,128)(2,1)S(1)} %get-tuple-element.52), channel_id=1, source_target_pairs={{0,24},{8,16},{16,8},{24,0},{1,25},{9,17},{17,9},{25,1},{2,26},{10... | collective-permute-start | bytes 589832 | tf_op jit(solution)/shard_map/ppermute | solution.py:164
  75.2 1.2 %collective-permute-start.23 = (f32[2,64]{1,0:T(2,128)S(1)}, f32[2,64]{1,0:T(2,128)S(1)}, u32[]{:S(2)}, u32[]{:S(2)}) collective-permute-start(f32[2,64]{1,0:T(2,128)S(1)} %pad_maximum_fusion), channel_id=1, source_target_pairs={{0,1},{1,0},{2,3},{3,2},{4,5},{5,4},{6,7},{7,6},{8,9},{9,8},{10,11... | collective-permute-start | bytes 1544 | tf_op jit(solution)/shard_map/ppermute | solution.py:164
  76.6 8.8 %collective-permute-start.26 = (bf16[64,1536]{1,0:T(8,128)(2,1)S(1)}, bf16[64,1536]{1,0:T(8,128)(2,1)S(1)}, u32[]{:S(2)}, u32[]{:S(2)}) collective-permute-start(bf16[64,1536]{1,0:T(8,128)(2,1)S(1)} %add_convert_fusion.refs_0_), channel_id=1, source_target_pairs={{0,24},{8,16},{16,8},{24,0},{1,25},{9,17},{17,9},{25,1},{2,26},{10... | collective-permute-start | bytes 589832 | tf_op jit(solution)/shard_map/ppermute | solution.py:164
  78.0 10.7 %collective-permute-start.25 = (bf16[64,1536]{1,0:T(8,128)(2,1)S(1)}, bf16[64,1536]{1,0:T(8,128)(2,1)S(1)}, u32[]{:S(2)}, u32[]{:S(2)}) collective-permute-start(bf16[64,1536]{1,0:T(8,128)(2,1)S(1)} %add_convert_fusion.refs_0_), channel_id=1, source_target_pairs={{0,16},{8,24},{16,0},{24,8},{1,17},{9,25},{17,1},{25,9},{2,18},{10... | collective-permute-start | bytes 589832 | tf_op jit(solution)/shard_map/ppermute | solution.py:164
  78.6 10.1 %collective-permute-start.24 = (bf16[64,1536]{1,0:T(8,128)(2,1)S(1)}, bf16[64,1536]{1,0:T(8,128)(2,1)S(1)}, u32[]{:S(2)}, u32[]{:S(2)}) collective-permute-start(bf16[64,1536]{1,0:T(8,128)(2,1)S(1)} %add_convert_fusion.refs_0_), channel_id=1, source_target_pairs={{0,8},{8,0},{16,24},{24,16},{1,9},{9,1},{17,25},{25,17},{2,10},{10... | collective-permute-start | bytes 589832 | tf_op jit(solution)/shard_map/ppermute | solution.py:164
  90.2 2.4 %collective-permute-start.28 = (bf16[256,1536]{1,0:T(8,128)(2,1)S(1)}, bf16[256,1536]{1,0:T(8,128)(2,1)S(1)}, u32[]{:S(2)}, u32[]{:S(2)}) collective-permute-start(bf16[256,1536]{1,0:T(8,128)(2,1)S(1)} %up_projected.3.refs_0_), channel_id=1, source_target_pairs={{0,1},{1,0},{2,3},{3,2},{4,5},{5,4},{6,7},{7,6},{8,9},{9,8},{10,11... | collective-permute-start | bytes 2359304 | tf_op jit(solution)/shard_map/ppermute | solution.py:164
  91.9 2.5 %collective-permute-start.27 = (bf16[256,1536]{1,0:T(8,128)(2,1)S(1)}, bf16[256,1536]{1,0:T(8,128)(2,1)S(1)}, u32[]{:S(2)}, u32[]{:S(2)}) collective-permute-start(bf16[256,1536]{1,0:T(8,128)(2,1)S(1)} %up_projected.2.refs_0_), channel_id=1, source_target_pairs={{0,1},{1,0},{2,3},{3,2},{4,5},{5,4},{6,7},{7,6},{8,9},{9,8},{10,11... | collective-permute-start | bytes 2359304 | tf_op jit(solution)/shard_map/ppermute | solution.py:164
  94.4 14.3 %copy-start.1 = (bf16[3072,576]{0,1:T(8,128)(2,1)S(1)}, bf16[3072,576]{0,1:T(8,128)(2,1)}, u32[]{:S(2)}) copy-start(bf16[3072,576]{0,1:T(8,128)(2,1)} %param.11) | copy-start | bytes 10616836
  96.1 7.8 %collective-permute-start.29 = (bf16[64,1536]{1,0:T(8,128)(2,1)S(1)}, bf16[64,1536]{1,0:T(8,128)(2,1)S(1)}, u32[]{:S(2)}, u32[]{:S(2)}) collective-permute-start(bf16[64,1536]{1,0:T(8,128)(2,1)S(1)} %get-tuple-element.54), channel_id=1, source_target_pairs={{0,8},{8,0},{16,24},{24,16},{1,9},{9,1},{17,25},{25,17},{2,10},{10... | collective-permute-start | bytes 589832 | tf_op jit(solution)/shard_map/ppermute | solution.py:164
  96.7 7.4 %collective-permute-start.30 = (bf16[64,1536]{1,0:T(8,128)(2,1)S(1)}, bf16[64,1536]{1,0:T(8,128)(2,1)S(1)}, u32[]{:S(2)}, u32[]{:S(2)}) collective-permute-start(bf16[64,1536]{1,0:T(8,128)(2,1)S(1)} %get-tuple-element.55), channel_id=1, source_target_pairs={{0,16},{8,24},{16,0},{24,8},{1,17},{9,25},{17,1},{25,9},{2,18},{10... | collective-permute-start | bytes 589832 | tf_op jit(solution)/shard_map/ppermute | solution.py:164
  98.1 9.7 %collective-permute-start.31 = (bf16[64,1536]{1,0:T(8,128)(2,1)S(1)}, bf16[64,1536]{1,0:T(8,128)(2,1)S(1)}, u32[]{:S(2)}, u32[]{:S(2)}) collective-permute-start(bf16[64,1536]{1,0:T(8,128)(2,1)S(1)} %get-tuple-element.56), channel_id=1, source_target_pairs={{0,24},{8,16},{16,8},{24,0},{1,25},{9,17},{17,9},{25,1},{2,26},{10... | collective-permute-start | bytes 589832 | tf_op jit(solution)/shard_map/ppermute | solution.py:164

commit v6 on v5

--- a/solution.py
+++ b/solution.py
@@ -154,7 +154,7 @@
 
 VMEM_BYTES = 1024 * 1024
 COPY_AT = 1
-SHORT = pl.CostEstimate(flops=10000000000, bytes_accessed=0, transcendentals=0)
+SHORT = pl.CostEstimate(flops=10**10, bytes_accessed=0, transcendentals=0)
 LONG = pl.CostEstimate(flops=10**10, bytes_accessed=0, transcendentals=0)
 NO_COST = pl.CostEstimate(flops=0, bytes_accessed=0, transcendentals=0)
 
@@ -344,13 +344,13 @@
         out_ref[k * rows : (k + 1) * rows, :] = block_ref[...]
 
 
-def stacked(blocks):
+def stacked(blocks, cost):
     rows, width = blocks[0].shape
     return pl.pallas_call(
         stack_kernel,
         out_shape=jax.ShapeDtypeStruct((rows * len(blocks), width), blocks[0].dtype),
         compiler_params=pltpu.CompilerParams(vmem_limit_bytes=VMEM_BYTES * 2),
-        cost_estimate=NO_COST,
+        cost_estimate=cost,
         name="stacked",
     )(*blocks)
 
@@ -371,18 +371,6 @@
         cost_estimate=cost,
         name="copied",
     )(values, after)
-
-
-def normalized(values, features):
-    sums = jnp.stack([jnp.sum(values, axis=-1), jnp.sum(values * values, axis=-1)])
-    sums = sums + permuted(sums, "tensor", 1)
-    average = sums[0][:, None] / features
-    variance = sums[1][:, None] / features - average * average
-    return (values - average) * lax.rsqrt(variance + 1e-06)
-
-
-def product(left, right):
-    return jnp.dot(left, right, preferred_element_type=jnp.float32).astype(jnp.bfloat16)
 
 
 def added(blocks):
@@ -493,6 +481,11 @@
     )(*after)
 
 
+def head_normal(values, gain_ref):
+    spread = jnp.mean(values * values, axis=-1, keepdims=True) + 1e-06
+    return (values * lax.rsqrt(spread) * gain_ref[...]).astype(jnp.bfloat16)
+
+
 def heads_kernel(count, head_size, *refs):
     own_refs, arrived_refs = refs[:count], refs[count : 2 * count]
     q_gain_ref, k_gain_ref = refs[2 * count : 2 * count + 2]
@@ -504,15 +497,11 @@
             jnp.float32
         )
 
-    def normal(values, gain_ref):
-        spread = jnp.mean(values * values, axis=-1, keepdims=True) + 1e-06
-        return (values * lax.rsqrt(spread) * gain_ref[...]).astype(jnp.bfloat16)
-
     for low in range(0, half, head_size):
         here = slice(low, low + head_size)
         if count == 3:
-            out_refs[1][:, here] = normal(total(0, here), q_gain_ref)
-        out_refs[0][:, here] = normal(total(count - 2, here), k_gain_ref)
+            out_refs[1][:, here] = head_normal(total(0, here), q_gain_ref)
+        out_refs[0][:, here] = head_normal(total(count - 2, here), k_gain_ref)
         out_refs[0][:, half + low : half + low + head_size] = total(count - 1, here).astype(
             jnp.bfloat16
         )
@@ -538,55 +527,99 @@
     )(*own, *arrived, q_gain[None, :], k_gain[None, :], *after)
 
 
-def attention_kernel(head_size, count, query_ref, *refs):
-    kv_refs, out_ref = refs[:count], refs[-1]
+def head_scores(query, key, head_size):
+    product = lax.dot_general(
+        query, key, (((1,), (1,)), ((), ())), preferred_element_type=jnp.float32
+    )
+    return product * (1.0 / math.sqrt(head_size))
+
+
+def weighted(scores, values, top):
+    total, summed = 0.0, 0.0
+    for part, value in zip(scores, values):
+        weights = jnp.exp(part - top)
+        total = total + jnp.sum(weights, axis=-1, keepdims=True)
+        summed = summed + jnp.dot(
+            weights.astype(jnp.bfloat16), value, preferred_element_type=jnp.float32
+        )
+    return total, summed
+
+
+def highest(scores, top=None):
+    for part in scores:
+        part_top = jnp.max(part, axis=-1, keepdims=True)
+        top = part_top if top is None else jnp.maximum(top, part_top)
+    return top
+
+
+def attend_kernel(head_size, count, query_ref, *refs):
+    kv_refs, (top_ref, total_ref, summed_ref) = refs[:count], refs[-3:]
     half = query_ref.shape[1]
-    score_scale = 1.0 / math.sqrt(head_size)
-    for lo in range(0, half, head_size):
-        query = query_ref[:, lo : lo + head_size]
-        scores = [
-            lax.dot_general(
-                query,
-                kv_ref[:, lo : lo + head_size],
-                (((1,), (1,)), ((), ())),
-                preferred_element_type=jnp.float32,
+    for low in range(0, half, head_size):
+        here = slice(low, low + head_size)
+        scores = [head_scores(query_ref[:, here], ref[:, here], head_size) for ref in kv_refs]
+        values = [ref[:, half + low : half + low + head_size] for ref in kv_refs]
+        top = highest(scores)
+        total, summed = weighted(scores, values, top)
+        top_ref[:, here] = jnp.broadcast_to(top, summed.shape)
+        total_ref[:, here] = jnp.broadcast_to(total, summed.shape)
+        summed_ref[:, here] = summed
+
+
+def attend(queries, kv_parts, head_size, after):
+    whole = lambda array: pl.BlockSpec(array.shape, lambda j: (0, 0))
+    state = jax.ShapeDtypeStruct(queries.shape, jnp.float32)
+    return pl.pallas_call(
+        lambda *refs: attend_kernel(head_size, len(kv_parts), *refs),
+        grid=(1,),
+        in_specs=[whole(array) for array in [queries, *kv_parts]] + after_specs(after),
+        out_specs=[whole(queries)] * 3,
+        out_shape=[state] * 3,
+        compiler_params=pltpu.CompilerParams(vmem_limit_bytes=VMEM_BYTES * 12),
+        cost_estimate=NO_COST,
+        name="attend",
+    )(queries, *kv_parts, *after)
+
+
+def finish_kernel(head_size, query_ref, top_ref, total_ref, summed_ref, *refs):
+    *refs, out_ref = refs
+    half = query_ref.shape[1]
+    for low in range(0, half, head_size):
+        here = slice(low, low + head_size)
+        top, total, summed = top_ref[:, here], total_ref[:, here], summed_ref[:, here]
+        if refs:
+            own_key, own_value, other_key, other_value, k_gain_ref = refs
+            key = head_normal(
+                own_key[:, here].astype(jnp.float32) + other_key[:, here].astype(jnp.float32),
+                k_gain_ref,
             )
-            * score_scale
-            for kv_ref in kv_refs
-        ]
-        top = jnp.max(scores[0], axis=-1, keepdims=True)
-        for part in scores[1:]:
-            top = jnp.maximum(top, jnp.max(part, axis=-1, keepdims=True))
-        denominator, summed = 0.0, 0.0
-        for part, kv_ref in zip(scores, kv_refs):
-            weights = jnp.exp(part - top)
-            denominator = denominator + jnp.sum(weights, axis=-1, keepdims=True)
-            summed = summed + jnp.dot(
-                weights.astype(jnp.bfloat16),
-                kv_ref[:, half + lo : half + lo + head_size],
-                preferred_element_type=jnp.float32,
+            value = own_value[:, here].astype(jnp.float32) + other_value[:, here].astype(
+                jnp.float32
             )
-        out_ref[:, lo : lo + head_size] = (summed / denominator).astype(jnp.bfloat16)
-
-
-def attention(queries, kv_parts, head_size, after):
-    rows, half = queries.shape
-    keys = sum(part.shape[0] for part in kv_parts)
-    return pl.pallas_call(
-        lambda *refs: attention_kernel(head_size, len(kv_parts), *refs),
-        grid=(1,),
-        in_specs=[pl.BlockSpec(array.shape, lambda j: (0, 0)) for array in [queries, *kv_parts]]
-        + after_specs(after),
-        out_specs=pl.BlockSpec((rows, half), lambda j: (0, 0)),
-        out_shape=jax.ShapeDtypeStruct((rows, half), jnp.bfloat16),
+            scores = [head_scores(query_ref[:, here], key, head_size)]
+            new_top = jnp.maximum(top, highest(scores))
+            more_total, more_summed = weighted(
+                scores, [value.astype(jnp.bfloat16)], new_top[:, :1]
+            )
+            decay = jnp.exp(top - new_top)
+            total = total * decay + more_total
+            summed = summed * decay + more_summed
+        out_ref[:, here] = (summed / total).astype(jnp.bfloat16)
+
+
+def finished(queries, state, parts, head_size):
+    whole = lambda array: pl.BlockSpec(array.shape, lambda j: (0, 0))
+    arrays = [queries, *state, *parts]
+    return pl.pallas_call(
+        lambda *refs: finish_kernel(head_size, *refs),
+        grid=(1,),
+        in_specs=[whole(array) for array in arrays],
+        out_specs=whole(queries),
+        out_shape=jax.ShapeDtypeStruct(queries.shape, jnp.bfloat16),
         compiler_params=pltpu.CompilerParams(vmem_limit_bytes=VMEM_BYTES * 12),
-        cost_estimate=pl.CostEstimate(
-            flops=4 * rows * keys * half,
-            bytes_accessed=4 * keys * half,
-            transcendentals=rows * keys * half // head_size,
-        ),
-        name="attention",
-    )(queries, *kv_parts, *after)
+        cost_estimate=NO_COST,
+        name="finished",
+    )(*arrays)
 
 
 def column_tiles(columns):
@@ -661,7 +694,7 @@
     )(*blocks, weight, *after)
 
 
-def down_kernel(first, last, own_ref, arrived_ref, weight_ref, *refs):
+def down_kernel(first, count, more, own_ref, arrived_ref, weight_ref, *refs):
     *out_refs, activ_ref = refs
     depth = own_ref.shape[1]
     for here in column_tiles(depth):
@@ -673,40 +706,86 @@
             weight_ref[first : first + depth, here],
             preferred_element_type=jnp.float32,
         )
-        if last:
-            row_blocks(total + out_refs[0][:, here], here, out_refs[1:])
+        if more:
+            total = total + out_refs[0][:, here]
+        if count:
+            row_blocks(total, here, out_refs[-count:])
         else:
             out_refs[0][:, here] = total
 
 
-def down_projected(own, arrived, weight, part, before, rows):
+def down_projected(own, arrived, weight, first, before, count):
     all_rows, depth = own.shape
     width = weight.shape[1]
-    last = before is not None
-    whole = pl.BlockSpec((all_rows, width), lambda j: (0, 0))
-    if last:
-        shapes = [jax.ShapeDtypeStruct((rows, width), jnp.bfloat16)] * (all_rows // rows)
-        out_specs = [pl.BlockSpec((rows, width), lambda j: (0, 0))] * (all_rows // rows)
-    else:
-        shapes = [jax.ShapeDtypeStruct((all_rows, width), jnp.float32)]
-        out_specs = [whole]
-    return pl.pallas_call(
-        lambda *refs: down_kernel(part * depth, last, *refs),
-        grid=(1,),
-        in_specs=[pl.BlockSpec((all_rows, depth), lambda j: (0, 0))] * 2
+    whole = lambda *shape: pl.BlockSpec(shape, lambda j: (0, 0))
+    shape, kind = (all_rows // max(count, 1), width), jnp.bfloat16 if count else jnp.float32
+    return pl.pallas_call(
+        lambda *refs: down_kernel(first, count, len(before), *refs),
+        grid=(1,),
+        in_specs=[whole(all_rows, depth)] * 2
         + [pl.BlockSpec(memory_space=pltpu.VMEM)]
-        + [whole] * last,
-        out_specs=out_specs,
-        out_shape=shapes,
+        + [whole(all_rows, width)] * len(before),
+        out_specs=[whole(*shape)] * max(count, 1),
+        out_shape=[jax.ShapeDtypeStruct(shape, kind)] * max(count, 1),
         scratch_shapes=[pltpu.VMEM((all_rows, depth), jnp.bfloat16)],
         compiler_params=pltpu.CompilerParams(vmem_limit_bytes=VMEM_BYTES * 12),
-        cost_estimate=pl.CostEstimate(
-            flops=2 * all_rows * width * depth,
-            bytes_accessed=0,
-            transcendentals=all_rows * depth,
-        ),
+        cost_estimate=NO_COST,
         name="down_projected",
-    )(own, arrived, weight, *([before] * last))
+    )(own, arrived, weight, *before)
+
+
+def mix_kernel(count, *refs):
+    block_refs, token_ref, gate_ref = refs[:count], refs[count], refs[count + 1]
+    mixed_ref, sums_ref = refs[-2:]
+    total = block_refs[0][...].astype(jnp.float32)
+    for block_ref in block_refs[1:]:
+        total = total + block_ref[...].astype(jnp.float32)
+    mixed = token_ref[...].astype(jnp.float32) + gate_ref[...] * total
+    mixed_ref[...] = mixed
+    lane = lax.broadcasted_iota(jnp.int32, sums_ref.shape, 1)
+    sums_ref[...] = jnp.where(
+        lane < sums_ref.shape[1] // 2,
+        jnp.sum(mixed, axis=-1, keepdims=True),
+        jnp.sum(mixed * mixed, axis=-1, keepdims=True),
+    )
+
+
+def mixed_rows(blocks, tokens, gate_row, after):
+    rows, width = tokens.shape
+    whole = lambda *shape: pl.BlockSpec(shape, lambda j: (0, 0))
+    return pl.pallas_call(
+        lambda *refs: mix_kernel(len(blocks), *refs),
+        grid=(1,),
+        in_specs=[whole(rows, width)] * (len(blocks) + 1)
+        + [whole(1, width)]
+        + after_specs(after),
+        out_specs=[whole(rows, width), whole(rows, 128)],
+        out_shape=[
+            jax.ShapeDtypeStruct((rows, width), jnp.float32),
+            jax.ShapeDtypeStruct((rows, 128), jnp.float32),
+        ],
+        compiler_params=pltpu.CompilerParams(vmem_limit_bytes=VMEM_BYTES * 4),
+        cost_estimate=NO_COST,
+        name="mixed_rows",
+    )(*blocks, tokens, gate_row, *after)
+
+
+def norm_kernel(features, mixed_ref, own_ref, arrived_ref, shift_ref, scale_ref, out_ref):
+    total = own_ref[...] + arrived_ref[...]
+    average = total[:, :1] / features
+    variance = total[:, total.shape[1] // 2 :][:, :1] / features - average * average
+    values = (mixed_ref[...] - average) * lax.rsqrt(variance + 1e-06)
+    out_ref[...] = (values * (1.0 + scale_ref[...]) + shift_ref[...]).astype(jnp.bfloat16)
+
+
+def normed_rows(mixed, sums, shift_row, scale_row, features):
+    return pl.pallas_call(
+        lambda *refs: norm_kernel(features, *refs),
+        out_shape=jax.ShapeDtypeStruct(mixed.shape, jnp.bfloat16),
+        compiler_params=pltpu.CompilerParams(vmem_limit_bytes=VMEM_BYTES * 2),
+        cost_estimate=NO_COST,
+        name="normed_rows",
+    )(mixed, sums, permuted(sums, "tensor", 1), shift_row, scale_row)
 
 
 def on_pair(
@@ -725,10 +804,7 @@
 
     activated = jax.nn.silu(cond.astype(jnp.float32)).astype(jnp.bfloat16)
     pieces = jnp.dot(activated[None, :], mod_weight, preferred_element_type=jnp.float32)
-    weights, out_weight, up_weight, down_weight = [
-        pltpu.with_memory_space_constraint(weight, pltpu.HBM)
-        for weight in (jnp.moveaxis(qkv_weight, 1, 0), out_weight, up_weight, down_weight)
-    ]
+    weights = pltpu.with_memory_space_constraint(jnp.moveaxis(qkv_weight, 1, 0), pltpu.HBM)
     start = copied(tokens, pieces, NO_COST)
     remote = [permuted(start, "blk", k) for k in range(2, blocks_z, 2)]
     normal = standardized(tokens, features, [])
@@ -736,51 +812,78 @@
     for stage in stages:
         after = []
         if stage[0] == "blk":
-            take = [0] if stage[1] == 1 else range(len(parts), weights.shape[0])
+            take = [1] if stage[1] == 1 else [2]
             parts += [staged(weights, pieces, part) for part in take]
             after = parts + (remote if stage[1] == 2 else [normal])
         pieces = doubled_once(pieces, *stage, after)
     own = packed(normal, pieces)
+    parts = [staged(weights, own, 0)] + parts
     chunks = [from_all(own, "ulysses")]
     if remote:
-        far = stacked(remote + [permuted(block, "blk", 1) for block in remote])
+        far = stacked(remote + [permuted(block, "blk", 1) for block in remote], NO_COST)
         far = standardized(far, features, [])
         chunks.append(from_all(far, "ulysses"))
     own_mod = assembled(chunks[0], "ulysses", *pieces.shape, width)
-    mod_rows = [own_mod[0:1], own_mod[1:2]]
-
-    kv_parts = []
-    for index, blocks in enumerate(chunks):
-        use = parts[min(index, 1) :]
-        after = [kv_parts[0], mark(blocks[1:], SHORT)] if index else [far] * bool(remote)
-        *partial, normed = projected(blocks, mod_rows, use, half, True, after)
+    row = lambda k: own_mod[k : k + 1]
+    out_weight, up_weight, down_weight = [
+        pltpu.with_memory_space_constraint(weight, pltpu.HBM)
+        for weight in (out_weight, up_weight, down_weight)
+    ]
+
+    def project(blocks, use, after):
+        *partial, normed = projected(blocks, [row(0), row(1)], use, half, True, after)
         arrived = [permuted(part, "tensor", 1) for part in partial]
-        own = projected([normed], [], use, half, False)
-        outs = split_heads(own, arrived, q_gain, k_gain)
-        kv_parts.append(outs[0])
-        if index == 0:
-            queries = outs[1]
-            if blocks_z > 1:
-                arrived = permuted(outs[0], "blk", 1)
-                kv_parts.append(copied(arrived, arrived, LONG))
-
-    out_weight = staged(out_weight, kv_parts[0])
+        return projected([normed], [], use, half, False), arrived
+
+    own, arrived = project(chunks[0], parts, [far] * bool(remote))
+    own_kv, queries = split_heads(own, arrived, q_gain, k_gain)
+    kv_parts = [own_kv]
+    if blocks_z > 1:
+        arrived = permuted(own_kv, "blk", 1)
+        kv_parts.append(copied(arrived, arrived, LONG))
+    out_weight = staged(out_weight, own_kv)
     up_weight = staged(up_weight, out_weight)
-    down_weight = staged(down_weight, up_weight)
-    context = attention(queries, kv_parts, head_size, [out_weight, up_weight])
+    last = []
+    first_blocks, last_blocks = halves(chunks[-1])
+    if remote:
+        own, arrived = project(first_blocks, parts[1:], [own_kv])
+        kv_parts += split_heads(own, arrived, q_gain, k_gain)
+    state = attend(queries, kv_parts, head_size, [out_weight, up_weight])
+    if remote and last_blocks:
+        tie = mark([*chunks[-1][1:], state[0]], SHORT)
+        own, arrived = project(last_blocks, parts[1:], [state[0], tie])
+        last = [*own, *arrived, k_gain[None, :]]
+    context = finished(queries, state, last, head_size)
+
     partial = out_projected(context, permuted(context, "tensor", 1), out_weight, rows)
-    attended = added(to_all(partial, "ulysses"))
-    mixed = tokens.astype(jnp.float32) + own_mod[2] * attended
-    normed_two = normalized(mixed, features) * (1.0 + own_mod[4]) + own_mod[3]
-    blocks = from_all(normed_two.astype(jnp.bfloat16), "ulysses")
-    first = up_projected(blocks, up_weight, 0, 2, [down_weight])
-    first_arrived = permuted(first, "tensor", 1)
-    second = up_projected(blocks, up_weight, 1, 2)
-    second_arrived = permuted(second, "tensor", 1)
-    before = down_projected(first, first_arrived, down_weight, 0, None, rows)[0]
-    partial = down_projected(second, second_arrived, down_weight, 1, before, rows)
-    feedforward = added(to_all(partial, "ulysses"))
+    down_weight = staged(down_weight, partial[0])
+    mixed, sums = mixed_rows(to_all(partial, "ulysses"), tokens, row(2), [down_weight])
+    normed_two = normed_rows(mixed, sums, row(3), row(4), features)
+    blocks = from_all(normed_two, "ulysses")
+    order = halves(list(range(len(blocks))))
+    outs = {}
+    for part, places in enumerate(order):
+        if not places:
+            continue
+        here = [blocks[k] for k in places]
+        here = [stacked(here, LONG)] if part else here
+        pieces = 2
+        after = [outs[order[0][0]]] if part else []
+        ups = [up_projected(here, up_weight, k, pieces, after) for k in range(pieces)]
+        arrived = [permuted(piece, "tensor", 1) for piece in ups]
+        before = []
+        for k, (own, other) in enumerate(zip(ups, arrived)):
+            count = len(places) if k == pieces - 1 else 0
+            before = down_projected(own, other, down_weight, k * own.shape[1], before, count)
+        outs.update(zip(places, before))
+    feedforward = added(to_all([outs[k] for k in range(len(blocks))], "ulysses"))
     return mixed + own_mod[5] * feedforward
+
+
+def halves(items):
+    order = items[:1] + items[:0:-1]
+    middle = (len(order) + 1) // 2
+    return order[:middle], order[middle:]
 
 
 def solution(mesh):

time: 109 us -> 103 us (0.945)
  waiting for transfers between devices: 42 us -> 32.2 us
  Pallas kernels: 31.4 us -> 33.6 us
  starting transfers between devices: 30.5 us -> 32.3 us
    ppermute x32 -> x36, waiting for transfers between devices: 42 us -> 32.2 us  [permuted(): return lax.ppermute(values, axis, [(i, i ^ distance) for i in range(size)])]
    ppermute x32 -> x36, starting transfers between devices: 30.5 us -> 32.3 us  [permuted(): return lax.ppermute(values, axis, [(i, i ^ distance) for i in range(size)])]
    pallas_call x3 -> x8, Pallas kernels: 5.04 us -> 6.73 us  [the longest x4 3.74 us: down_projected(): pl.pallas_call(lambda *refs: down_kernel(first, count, len(before), *refs...]
    pallas_call x4 -> x6, Pallas kernels: 6.45 us -> 6.8 us  [projected(): pl.pallas_call((lambda *refs: project_kernel(len(blocks), count, other, *...]
    pallas_call x2 -> x4, Pallas kernels: 3.08 us -> 3.33 us  [up_projected(): pl.pallas_call(lambda *refs: up_kernel(part * columns, len(blocks), *refs...]
  transfers between devices with their start and end apart: 32 -> 36, of which waited for: 20 -> 21; matrix products, arithmetic and copies ran while one was open for 0% -> 0% of each run, Pallas kernels for 22% -> 26%
where the time goes in v6:
time: 103 us; the launch traced here: 102 us
  Pallas kernels  33.6 us (33%)
  starting transfers between devices  32.3 us (31%)
  waiting for transfers between devices  32.2 us (31%)
  other arithmetic  1.74 us (2%)
  local copies, waits for them, and re-layouts  1.21 us (1%)
    ppermute x36, starting transfers between devices, permuted(): return lax.ppermute(values, axis, [(i, i ^ distance) for i in range(size)])  32.3 us
    ppermute x36, waiting for transfers between devices, permuted(): return lax.ppermute(values, axis, [(i, i ^ distance) for i in range(size)])  32.2 us
    pallas_call x6, Pallas kernels, staged(): pl.pallas_call(kernel, grid=(1,), in_specs=[anywhere] + after_specs([afte...  14.1 us
    pallas_call x6, Pallas kernels, projected(): pl.pallas_call((lambda *refs: project_kernel(len(blocks), count, other, *...  6.8 us
    pallas_call x4, Pallas kernels, down_projected(): pl.pallas_call(lambda *refs: down_kernel(first, count, len(before), *refs...  3.74 us
    pallas_call x4, Pallas kernels, up_projected(): pl.pallas_call(lambda *refs: up_kernel(part * columns, len(blocks), *refs...  3.33 us
  transfers between devices with their start and end apart: 36, of which 21 were waited for; matrix products, arithmetic and copies ran while one was open for 0% of the time, Pallas kernels for 26%

profile of v6, /device:TPU:0, one launch (start us, length us, event | category | flops | bytes accessed | tf_op | source)
XLA Modules:
  0.0 102.4 jit_solution(17472309465850172187)
XLA Ops:
  0.9 1.1 %copy-done = bf16[3072,576]{0,1:T(8,128)(2,1)S(1)} copy-done((bf16[3072,576]{0,1:T(8,128)(2,1)S(1)}, bf16[3072,576]{0,1:T(8,128)(2,1)}, u32[]{:S(2)}) %copy-start) | copy-done | bytes 3538968
  2.0 1.0 fusion.4.refs_0_.after_ref
  3.1 4.1 %collective-permute-start.4 = (bf16[64,1536]{1,0:T(8,128)(2,1)S(1)}, bf16[64,1536]{1,0:T(8,128)(2,1)S(1)}, u32[]{:S(2)}, u32[]{:S(2)}) collective-permute-start(bf16[64,1536]{1,0:T(8,128)(2,1)S(1)} %copied.2), channel_id=1, source_target_pairs={{0,4},{2,6},{4,0},{6,2},{1,5},{3,7},{5,1},{7,3},{8,12},{10,14},{12... | collective-permute-start | bytes 589832 | tf_op jit(solution)/shard_map/ppermute | solution.py:164
  8.7 1.6 %collective-permute-start.2 = (f32[2,576]{1,0:T(2,128)S(1)}, f32[2,576]{1,0:T(2,128)S(1)}, u32[]{:S(2)}, u32[]{:S(2)}) collective-permute-start(f32[2,576]{1,0:T(2,128)S(1)} %merged.3.after_ref.refs_0_), channel_id=1, source_target_pairs={{0,2},{2,0},{4,6},{6,4},{1,3},{3,1},{5,7},{7,5},{8,10},{10,8},{12,... | collective-permute-start | bytes 13832 | tf_op jit(solution)/shard_map/ppermute | solution.py:164
  10.3 1.6 %staged.6.refs_2_.refs_7_.refs_4_.refs_1_ = bf16[1536,768]{1,0:T(8,128)(2,1)S(1)} custom-call(bf16[3,1536,768]{2,1,0:T(8,128)(2,1)} %bitcast.10, f32[2,576]{1,0:T(2,128)S(1)} %merged.3.after_ref.refs_0_), custom_call_target="tpu_custom_call" | custom-call | bytes 2359296 | tf_op jit(solution)/shard_map/staged/pallas_call | solution.py:452
  12.3 1.6 %collective-permute-start.3 = (f32[4,576]{1,0:T(4,128)S(1)}, f32[4,576]{1,0:T(4,128)S(1)}, u32[]{:S(2)}, u32[]{:S(2)}) collective-permute-start(f32[4,576]{1,0:T(4,128)S(1)} %merged.4.after_ref.refs_0_), channel_id=1, source_target_pairs={{0,4},{2,6},{4,0},{6,2},{1,5},{3,7},{5,1},{7,3},{8,12},{10,14},{12... | collective-permute-start | bytes 27656 | tf_op jit(solution)/shard_map/ppermute | solution.py:164
  13.9 1.6 %staged.7.refs_3_.refs_8_.refs_5_.refs_2_ = bf16[1536,768]{1,0:T(8,128)(2,1)S(1)} custom-call(bf16[3,1536,768]{2,1,0:T(8,128)(2,1)} %bitcast.11, f32[4,576]{1,0:T(4,128)S(1)} %merged.4.after_ref.refs_0_), custom_call_target="tpu_custom_call" | custom-call | bytes 2359296 | tf_op jit(solution)/shard_map/staged/pallas_call | solution.py:452
  15.6 1.4 %collective-permute-done.3.refs_1_ = f32[4,576]{1,0:T(4,128)S(1)} collective-permute-done((f32[4,576]{1,0:T(4,128)S(1)}, f32[4,576]{1,0:T(4,128)S(1)}, u32[]{:S(2)}, u32[]{:S(2)}) %collective-permute-start.3) | collective-permute-done | bytes 9248 | tf_op jit(solution)/shard_map/ppermute | solution.py:164
  17.0 1.6 %collective-permute-start.5 = (bf16[64,1664]{1,0:T(8,128)(2,1)S(1)}, bf16[64,1664]{1,0:T(8,128)(2,1)S(1)}, u32[]{:S(2)}, u32[]{:S(2)}) collective-permute-start(bf16[64,1664]{1,0:T(8,128)(2,1)S(1)} %packed.1.refs_0_.after_ref), channel_id=1, source_target_pairs={{0,8},{8,0},{16,24},{24,16},{1,9},{9,1},{17,25},{25,17},{2,10},{10... | collective-permute-start | bytes 638984 | tf_op jit(solution)/shard_map/ppermute | solution.py:164
  18.6 1.5 %collective-permute-start.6 = (bf16[64,1664]{1,0:T(8,128)(2,1)S(1)}, bf16[64,1664]{1,0:T(8,128)(2,1)S(1)}, u32[]{:S(2)}, u32[]{:S(2)}) collective-permute-start(bf16[64,1664]{1,0:T(8,128)(2,1)S(1)} %packed.1.refs_0_.after_ref), channel_id=1, source_target_pairs={{0,16},{8,24},{16,0},{24,8},{1,17},{9,25},{17,1},{25,9},{2,18},{10... | collective-permute-start | bytes 638984 | tf_op jit(solution)/shard_map/ppermute | solution.py:164
  20.6 1.6 %collective-permute-start.8 = (bf16[64,1536]{1,0:T(8,128)(2,1)S(1)}, bf16[64,1536]{1,0:T(8,128)(2,1)S(1)}, u32[]{:S(2)}, u32[]{:S(2)}) collective-permute-start(bf16[64,1536]{1,0:T(8,128)(2,1)S(1)} %collective-permute-done.4.refs_4_.refs_0_), channel_id=1, source_target_pairs={{0,2},{2,0},{4,6},{6,4},{1,3},{3,1},{5,7},{7,5},{8,10},{10,8},{12,... | collective-permute-start | bytes 589832 | tf_op jit(solution)/shard_map/ppermute | solution.py:164
  22.2 1.6 %staged.8.refs_6_.refs_1_ = bf16[1536,768]{1,0:T(8,128)(2,1)S(1)} custom-call(bf16[3,1536,768]{2,1,0:T(8,128)(2,1)} %bitcast.12, bf16[64,1664]{1,0:T(8,128)(2,1)S(1)} %packed.1.refs_0_.after_ref), custom_call_target="tpu_custom_call" | custom-call | bytes 2359296 | tf_op jit(solution)/shard_map/staged/pallas_call | solution.py:452
  23.9 2.4 %collective-permute-done.8.refs_1_ = bf16[64,1536]{1,0:T(8,128)(2,1)S(1)} collective-permute-done((bf16[64,1536]{1,0:T(8,128)(2,1)S(1)}, bf16[64,1536]{1,0:T(8,128)(2,1)S(1)}, u32[]{:S(2)}, u32[]{:S(2)}) %collective-permute-start.8) | collective-permute-done | bytes 196640 | tf_op jit(solution)/shard_map/ppermute | solution.py:164
  26.5 2.7 %collective-permute-done.6.refs_2_ = bf16[64,1664]{1,0:T(8,128)(2,1)S(1)} collective-permute-done((bf16[64,1664]{1,0:T(8,128)(2,1)S(1)}, bf16[64,1664]{1,0:T(8,128)(2,1)S(1)}, u32[]{:S(2)}, u32[]{:S(2)}) %collective-permute-start.6) | collective-permute-done | bytes 213024 | tf_op jit(solution)/shard_map/ppermute | solution.py:164
  29.7 1.4 %projected.6 = (bf16[256,384]{1,0:T(8,128)(2,1)S(1)}, bf16[256,384]{1,0:T(8,128)(2,1)S(1)}, bf16[256,384]{1,0:T(8,128)(2,1)S(1)}, bf16[256,1536]{1,0:T(8,128)(2,1)S(1)}) custom-call(bf16[64,1664]{1,0:T(8,128)(2,1)S(1)} %packed.1.refs_0_.after_ref, bf16[64,1664]{1,0:T(8,128)(2,1)S(1)} %collective-permute-done.5.refs_1_, ...), custom_call_target="tpu_custom_call" | custom-call | tf_op jit(solution)/shard_map/projected/pallas_call | solution.py:416
  31.7 1.5 %collective-permute-start.14 = (bf16[128,1536]{1,0:T(8,128)(2,1)S(1)}, bf16[128,1536]{1,0:T(8,128)(2,1)S(1)}, u32[]{:S(2)}, u32[]{:S(2)}) collective-permute-start(bf16[128,1536]{1,0:T(8,128)(2,1)S(1)} %standardized.3.refs_9_.refs_0_), channel_id=1, source_target_pairs={{0,24},{8,16},{16,8},{24,0},{1,25},{9,17},{17,9},{25,1},{2,26},{10... | collective-permute-start | bytes 1179656 | tf_op jit(solution)/shard_map/ppermute | solution.py:164
  33.2 1.4 %projected.7 = (bf16[256,384]{1,0:T(8,128)(2,1)S(1)}, bf16[256,384]{1,0:T(8,128)(2,1)S(1)}, bf16[256,384]{1,0:T(8,128)(2,1)S(1)}) custom-call(bf16[256,1536]{1,0:T(8,128)(2,1)S(1)} %get-tuple-element.45.refs_0_, bf16[1536,768]{1,0:T(8,128)(2,1)S(1)} %staged.8.refs_6_.refs_1_, bf16[1536,768]{1,0:T(8,128)(2,1)S(1)} %staged.6.refs_2_.refs_7_.refs_4_.refs_1_, ...), custom_call_target="tpu_custom_call" | custom-call | tf_op jit(solution)/shard_map/projected/pallas_call | solution.py:416
  35.0 1.4 %collective-permute-start.13 = (bf16[256,768]{1,0:T(8,128)(2,1)S(1)}, bf16[256,768]{1,0:T(8,128)(2,1)S(1)}, u32[]{:S(2)}, u32[]{:S(2)}) collective-permute-start(bf16[256,768]{1,0:T(8,128)(2,1)S(1)} %get-tuple-element.53.refs_6_.after_ref.refs_1_), channel_id=1, source_target_pairs={{0,2},{2,0},{4,6},{6,4},{1,3},{3,1},{5,7},{7,5},{8,10},{10,8},{12,... | collective-permute-start | bytes 1179656 | tf_op jit(solution)/shard_map/ppermute | solution.py:164
  36.4 1.2 %collective-permute-start.17 = (bf16[128,1536]{1,0:T(8,128)(2,1)S(1)}, bf16[128,1536]{1,0:T(8,128)(2,1)S(1)}, u32[]{:S(2)}, u32[]{:S(2)}) collective-permute-start(bf16[128,1536]{1,0:T(8,128)(2,1)S(1)} %standardized.3.refs_9_.refs_0_), channel_id=1, source_target_pairs={{0,16},{8,24},{16,0},{24,8},{1,17},{9,25},{17,1},{25,9},{2,18},{10... | collective-permute-start | bytes 1179656 | tf_op jit(solution)/shard_map/ppermute | solution.py:164
  38.4 1.6 %staged.9.after_ref.refs_4_.weight_ref = bf16[768,1536]{1,0:T(8,128)(2,1)S(1)} custom-call(bf16[768,1536]{1,0:T(8,128)(2,1)} %weight_ref.3, bf16[256,768]{1,0:T(8,128)(2,1)S(1)} %get-tuple-element.53.refs_6_.after_ref.refs_1_), custom_call_target="tpu_custom_call" | custom-call | bytes 2359296 | tf_op jit(solution)/shard_map/staged/pallas_call | solution.py:452
  40.1 3.8 %staged.10.refs_5_.refs_2_.refs_1_ = bf16[1536,3072]{1,0:T(8,128)(2,1)S(1)} custom-call(bf16[1536,3072]{1,0:T(8,128)(2,1)} %weight_ref.4, bf16[768,1536]{1,0:T(8,128)(2,1)S(1)} %staged.9.after_ref.refs_4_.weight_ref), custom_call_target="tpu_custom_call" | custom-call | bytes 9437184 | tf_op jit(solution)/shard_map/staged/pallas_call | solution.py:452
  44.6 1.0 projected.8
  45.6 1.0 projected.9
  47.2 0.9 collective-permute-done.15.refs_2_
  48.6 1.4 %attend.1 = (f32[256,384]{1,0:T(8,128)S(1)}, f32[256,384]{1,0:T(8,128)S(1)}, f32[256,384]{1,0:T(8,128)S(1)}) custom-call(bf16[256,384]{1,0:T(8,128)(2,1)S(1)} %get-tuple-element.52.refs_0_, bf16[256,768]{1,0:T(8,128)(2,1)S(1)} %get-tuple-element.53.refs_6_.after_ref.refs_1_, bf16[256,768]{1,0:T(8,128)(2,1)S(1)} %copied.3.refs_2_, ...), custom_call_target="tpu_custom_call" | custom-call | tf_op jit(solution)/shard_map/attend/pallas_call | solution.py:572
  50.1 2.5 %collective-permute-done.17.refs_1_.refs_0_ = bf16[128,1536]{1,0:T(8,128)(2,1)S(1)} collective-permute-done((bf16[128,1536]{1,0:T(8,128)(2,1)S(1)}, bf16[128,1536]{1,0:T(8,128)(2,1)S(1)}, u32[]{:S(2)}, u32[]{:S(2)}) %collective-permute-start.17) | collective-permute-done | bytes 393248 | tf_op jit(solution)/shard_map/ppermute | solution.py:164
  52.6 1.0 projected.10
  54.2 1.0 projected.11
  55.4 1.1 %finished.1.own_ref = bf16[256,384]{1,0:T(8,128)(2,1)S(1)} custom-call(bf16[256,384]{1,0:T(8,128)(2,1)S(1)} %get-tuple-element.52.refs_0_, f32[256,384]{1,0:T(8,128)S(1)} %get-tuple-element.59.refs_3_.refs_6_.refs_1_, f32[256,384]{1,0:T(8,128)S(1)} %get-tuple-element.60.refs_2_, f32[256,384]{1,0:T(8,128)S(1)} %get-tuple-element.61.refs_3_, ...), custom_call_target="tpu_custom_call" | custom-call | tf_op jit(solution)/shard_map/finished/pallas_call | solution.py:613
  56.9 1.2 %collective-permute-done.21.arrived_ref = bf16[256,384]{1,0:T(8,128)(2,1)S(1)} collective-permute-done((bf16[256,384]{1,0:T(8,128)(2,1)S(1)}, bf16[256,384]{1,0:T(8,128)(2,1)S(1)}, u32[]{:S(2)}, u32[]{:S(2)}) %collective-permute-start.21) | collective-permute-done | bytes 196640 | tf_op jit(solution)/shard_map/ppermute | solution.py:164
  58.1 1.0 out_projected.1
  59.1 1.2 %collective-permute-start.22 = (bf16[64,1536]{1,0:T(8,128)(2,1)S(1)}, bf16[64,1536]{1,0:T(8,128)(2,1)S(1)}, u32[]{:S(2)}, u32[]{:S(2)}) collective-permute-start(bf16[64,1536]{1,0:T(8,128)(2,1)S(1)} %get-tuple-element.68), channel_id=1, source_target_pairs={{0,8},{8,0},{16,24},{24,16},{1,9},{9,1},{17,25},{25,17},{2,10},{10... | collective-permute-start | bytes 589832 | tf_op jit(solution)/shard_map/ppermute | solution.py:164
  61.1 1.5 %collective-permute-start.24 = (bf16[64,1536]{1,0:T(8,128)(2,1)S(1)}, bf16[64,1536]{1,0:T(8,128)(2,1)S(1)}, u32[]{:S(2)}, u32[]{:S(2)}) collective-permute-start(bf16[64,1536]{1,0:T(8,128)(2,1)S(1)} %get-tuple-element.70), channel_id=1, source_target_pairs={{0,24},{8,16},{16,8},{24,0},{1,25},{9,17},{17,9},{25,1},{2,26},{10... | collective-permute-start | bytes 589832 | tf_op jit(solution)/shard_map/ppermute | solution.py:164
  62.6 3.8 %staged.11.refs_6_.refs_2_ = bf16[3072,1536]{1,0:T(8,128)(2,1)S(1)} custom-call(bf16[3072,1536]{1,0:T(8,128)(2,1)} %weight_ref.5, bf16[64,1536]{1,0:T(8,128)(2,1)S(1)} %get-tuple-element.67.after_ref.refs_0_), custom_call_target="tpu_custom_call" | custom-call | bytes 9437184 | tf_op jit(solution)/shard_map/staged/pallas_call | solution.py:452
  67.7 3.5 %collective-permute-done.24.refs_3_ = bf16[64,1536]{1,0:T(8,128)(2,1)S(1)} collective-permute-done((bf16[64,1536]{1,0:T(8,128)(2,1)S(1)}, bf16[64,1536]{1,0:T(8,128)(2,1)S(1)}, u32[]{:S(2)}, u32[]{:S(2)}) %collective-permute-start.24) | collective-permute-done | bytes 196640 | tf_op jit(solution)/shard_map/ppermute | solution.py:164
  71.6 1.2 %collective-permute-done.25.refs_2_ = f32[64,128]{1,0:T(8,128)S(1)} collective-permute-done((f32[64,128]{1,0:T(8,128)S(1)}, f32[64,128]{1,0:T(8,128)S(1)}, u32[]{:S(2)}, u32[]{:S(2)}) %collective-permute-start.25) | collective-permute-done | bytes 32800 | tf_op jit(solution)/shard_map/ppermute | solution.py:164
  73.0 2.0 %collective-permute-start.26 = (bf16[64,1536]{1,0:T(8,128)(2,1)S(1)}, bf16[64,1536]{1,0:T(8,128)(2,1)S(1)}, u32[]{:S(2)}, u32[]{:S(2)}) collective-permute-start(bf16[64,1536]{1,0:T(8,128)(2,1)S(1)} %normed_rows.1.refs_0_), channel_id=1, source_target_pairs={{0,24},{8,16},{16,8},{24,0},{1,25},{9,17},{17,9},{25,1},{2,26},{10... | collective-permute-start | bytes 589832 | tf_op jit(solution)/shard_map/ppermute | solution.py:164
  75.6 1.1 %collective-permute-start.30 = (bf16[64,1536]{1,0:T(8,128)(2,1)S(1)}, bf16[64,1536]{1,0:T(8,128)(2,1)S(1)}, u32[]{:S(2)}, u32[]{:S(2)}) collective-permute-start(bf16[64,1536]{1,0:T(8,128)(2,1)S(1)} %normed_rows.1.refs_0_), channel_id=1, source_target_pairs={{0,8},{8,0},{16,24},{24,16},{1,9},{9,1},{17,25},{25,17},{2,10},{10... | collective-permute-start | bytes 589832 | tf_op jit(solution)/shard_map/ppermute | solution.py:164
  76.7 5.2 %collective-permute-done.26.refs_1_ = bf16[64,1536]{1,0:T(8,128)(2,1)S(1)} collective-permute-done((bf16[64,1536]{1,0:T(8,128)(2,1)S(1)}, bf16[64,1536]{1,0:T(8,128)(2,1)S(1)}, u32[]{:S(2)}, u32[]{:S(2)}) %collective-permute-start.26) | collective-permute-done | bytes 196640 | tf_op jit(solution)/shard_map/ppermute | solution.py:164
  84.3 1.0 %collective-permute-done.29.refs_0_ = bf16[64,1536]{1,0:T(8,128)(2,1)S(1)} collective-permute-done((bf16[64,1536]{1,0:T(8,128)(2,1)S(1)}, bf16[64,1536]{1,0:T(8,128)(2,1)S(1)}, u32[]{:S(2)}, u32[]{:S(2)}) %collective-permute-start.29) | collective-permute-done | bytes 196640 | tf_op jit(solution)/shard_map/ppermute | solution.py:164
  85.4 0.9 down_projected.4.refs_3_
  86.3 0.9 down_projected.5
  89.5 1.7 %collective-permute-start.35 = (bf16[64,1536]{1,0:T(8,128)(2,1)S(1)}, bf16[64,1536]{1,0:T(8,128)(2,1)S(1)}, u32[]{:S(2)}, u32[]{:S(2)}) collective-permute-start(bf16[64,1536]{1,0:T(8,128)(2,1)S(1)} %get-tuple-element.76), channel_id=1, source_target_pairs={{0,24},{8,16},{16,8},{24,0},{1,25},{9,17},{17,9},{25,1},{2,26},{10... | collective-permute-start | bytes 589832 | tf_op jit(solution)/shard_map/ppermute | solution.py:164
  91.3 0.9 down_projected.6.refs_3_
  92.2 0.9 down_projected.7
  93.8 1.2 %collective-permute-start.34 = (bf16[64,1536]{1,0:T(8,128)(2,1)S(1)}, bf16[64,1536]{1,0:T(8,128)(2,1)S(1)}, u32[]{:S(2)}, u32[]{:S(2)}) collective-permute-start(bf16[64,1536]{1,0:T(8,128)(2,1)S(1)} %get-tuple-element.75), channel_id=1, source_target_pairs={{0,16},{8,24},{16,0},{24,8},{1,17},{9,25},{17,1},{25,9},{2,18},{10... | collective-permute-start | bytes 589832 | tf_op jit(solution)/shard_map/ppermute | solution.py:164
  95.0 3.2 %collective-permute-done.35 = bf16[64,1536]{1,0:T(8,128)(2,1)S(1)} collective-permute-done((bf16[64,1536]{1,0:T(8,128)(2,1)S(1)}, bf16[64,1536]{1,0:T(8,128)(2,1)S(1)}, u32[]{:S(2)}, u32[]{:S(2)}) %collective-permute-start.35) | collective-permute-done | bytes 196640 | tf_op jit(solution)/shard_map/ppermute | solution.py:164
  98.2 2.7 %collective-permute-done.33 = bf16[64,1536]{1,0:T(8,128)(2,1)S(1)} collective-permute-done((bf16[64,1536]{1,0:T(8,128)(2,1)S(1)}, bf16[64,1536]{1,0:T(8,128)(2,1)S(1)}, u32[]{:S(2)}, u32[]{:S(2)}) %collective-permute-start.33) | collective-permute-done | bytes 196640 | tf_op jit(solution)/shard_map/ppermute | solution.py:164
  (80 shorter events, 18.9 us)
Async XLA Ops:
  0.0 2.0 %copy-start = (bf16[3072,576]{0,1:T(8,128)(2,1)S(1)}, bf16[3072,576]{0,1:T(8,128)(2,1)}, u32[]{:S(2)}) copy-start(bf16[3072,576]{0,1:T(8,128)(2,1)} %param.11) | copy-start | bytes 10616836
  0.0 3.0 %copy-start.2 = (bf16[64,1536]{1,0:T(8,128)(2,1)S(1)}, bf16[64,1536]{1,0:T(8,128)(2,1)}, u32[]{:S(2)}) copy-start(bf16[64,1536]{1,0:T(8,128)(2,1)} %refs_4_.1) | copy-start | bytes 589828
  3.1 13.9 %collective-permute-start.4 = (bf16[64,1536]{1,0:T(8,128)(2,1)S(1)}, bf16[64,1536]{1,0:T(8,128)(2,1)S(1)}, u32[]{:S(2)}, u32[]{:S(2)}) collective-permute-start(bf16[64,1536]{1,0:T(8,128)(2,1)S(1)} %copied.2), channel_id=1, source_target_pairs={{0,4},{2,6},{4,0},{6,2},{1,5},{3,7},{5,1},{7,3},{8,12},{10,14},{12... | collective-permute-start | bytes 589832 | tf_op jit(solution)/shard_map/ppermute | solution.py:164
  7.3 4.6 %collective-permute-start = (f32[64,128]{1,0:T(8,128)S(1)}, f32[64,128]{1,0:T(8,128)S(1)}, u32[]{:S(2)}, u32[]{:S(2)}) collective-permute-start(f32[64,128]{1,0:T(8,128)S(1)} %get-tuple-element.42.refs_1_), channel_id=1, source_target_pairs={{0,1},{1,0},{2,3},{3,2},{4,5},{5,4},{6,7},{7,6},{8,9},{9,8},{10,11... | collective-permute-start | bytes 98312 | tf_op jit(solution)/shard_map/ppermute | solution.py:164
  7.4 1.3 %collective-permute-start.1 = (f32[1,576]{1,0:T(1,128)S(1)}, f32[1,576]{1,0:T(1,128)S(1)}, u32[]{:S(2)}, u32[]{:S(2)}) collective-permute-start(f32[1,576]{1,0:T(1,128)S(1)} %fusion.4.refs_0_.after_ref), channel_id=1, source_target_pairs={{0,1},{1,0},{2,3},{3,2},{4,5},{5,4},{6,7},{7,6},{8,9},{9,8},{10,11... | collective-permute-start | bytes 6920 | tf_op jit(solution)/shard_map/ppermute | solution.py:164
  8.7 3.6 %collective-permute-start.2 = (f32[2,576]{1,0:T(2,128)S(1)}, f32[2,576]{1,0:T(2,128)S(1)}, u32[]{:S(2)}, u32[]{:S(2)}) collective-permute-start(f32[2,576]{1,0:T(2,128)S(1)} %merged.3.after_ref.refs_0_), channel_id=1, source_target_pairs={{0,2},{2,0},{4,6},{6,4},{1,3},{3,1},{5,7},{7,5},{8,10},{10,8},{12,... | collective-permute-start | bytes 13832 | tf_op jit(solution)/shard_map/ppermute | solution.py:164
  12.3 4.6 %collective-permute-start.3 = (f32[4,576]{1,0:T(4,128)S(1)}, f32[4,576]{1,0:T(4,128)S(1)}, u32[]{:S(2)}, u32[]{:S(2)}) collective-permute-start(f32[4,576]{1,0:T(4,128)S(1)} %merged.4.after_ref.refs_0_), channel_id=1, source_target_pairs={{0,4},{2,6},{4,0},{6,2},{1,5},{3,7},{5,1},{7,3},{8,12},{10,14},{12... | collective-permute-start | bytes 27656 | tf_op jit(solution)/shard_map/ppermute | solution.py:164
  17.0 9.5 %collective-permute-start.5 = (bf16[64,1664]{1,0:T(8,128)(2,1)S(1)}, bf16[64,1664]{1,0:T(8,128)(2,1)S(1)}, u32[]{:S(2)}, u32[]{:S(2)}) collective-permute-start(bf16[64,1664]{1,0:T(8,128)(2,1)S(1)} %packed.1.refs_0_.after_ref), channel_id=1, source_target_pairs={{0,8},{8,0},{16,24},{24,16},{1,9},{9,1},{17,25},{25,17},{2,10},{10... | collective-permute-start | bytes 638984 | tf_op jit(solution)/shard_map/ppermute | solution.py:164
  18.6 10.6 %collective-permute-start.6 = (bf16[64,1664]{1,0:T(8,128)(2,1)S(1)}, bf16[64,1664]{1,0:T(8,128)(2,1)S(1)}, u32[]{:S(2)}, u32[]{:S(2)}) collective-permute-start(bf16[64,1664]{1,0:T(8,128)(2,1)S(1)} %packed.1.refs_0_.after_ref), channel_id=1, source_target_pairs={{0,16},{8,24},{16,0},{24,8},{1,17},{9,25},{17,1},{25,9},{2,18},{10... | collective-permute-start | bytes 638984 | tf_op jit(solution)/shard_map/ppermute | solution.py:164
  20.1 9.1 %collective-permute-start.7 = (bf16[64,1664]{1,0:T(8,128)(2,1)S(1)}, bf16[64,1664]{1,0:T(8,128)(2,1)S(1)}, u32[]{:S(2)}, u32[]{:S(2)}) collective-permute-start(bf16[64,1664]{1,0:T(8,128)(2,1)S(1)} %packed.1.refs_0_.after_ref), channel_id=1, source_target_pairs={{0,24},{8,16},{16,8},{24,0},{1,25},{9,17},{17,9},{25,1},{2,26},{10... | collective-permute-start | bytes 638984 | tf_op jit(solution)/shard_map/ppermute | solution.py:164
  20.6 5.7 %collective-permute-start.8 = (bf16[64,1536]{1,0:T(8,128)(2,1)S(1)}, bf16[64,1536]{1,0:T(8,128)(2,1)S(1)}, u32[]{:S(2)}, u32[]{:S(2)}) collective-permute-start(bf16[64,1536]{1,0:T(8,128)(2,1)S(1)} %collective-permute-done.4.refs_4_.refs_0_), channel_id=1, source_target_pairs={{0,2},{2,0},{4,6},{6,4},{1,3},{3,1},{5,7},{7,5},{8,10},{10,8},{12,... | collective-permute-start | bytes 589832 | tf_op jit(solution)/shard_map/ppermute | solution.py:164
  26.4 3.0 %collective-permute-start.9 = (f32[128,128]{1,0:T(8,128)S(1)}, f32[128,128]{1,0:T(8,128)S(1)}, u32[]{:S(2)}, u32[]{:S(2)}) collective-permute-start(f32[128,128]{1,0:T(8,128)S(1)} %get-tuple-element.44.refs_1_), channel_id=1, source_target_pairs={{0,1},{1,0},{2,3},{3,2},{4,5},{5,4},{6,7},{7,6},{8,9},{9,8},{10,11... | collective-permute-start | bytes 196616 | tf_op jit(solution)/shard_map/ppermute | solution.py:164
  31.1 3.5 %collective-permute-start.10 = (bf16[256,384]{1,0:T(8,128)(2,1)S(1)}, bf16[256,384]{1,0:T(8,128)(2,1)S(1)}, u32[]{:S(2)}, u32[]{:S(2)}) collective-permute-start(bf16[256,384]{1,0:T(8,128)(2,1)S(1)} %get-tuple-element.49), channel_id=1, source_target_pairs={{0,1},{1,0},{2,3},{3,2},{4,5},{5,4},{6,7},{7,6},{8,9},{9,8},{10,11... | collective-permute-start | bytes 589832 | tf_op jit(solution)/shard_map/ppermute | solution.py:164
  31.2 3.5 %collective-permute-start.11 = (bf16[256,384]{1,0:T(8,128)(2,1)S(1)}, bf16[256,384]{1,0:T(8,128)(2,1)S(1)}, u32[]{:S(2)}, u32[]{:S(2)}) collective-permute-start(bf16[256,384]{1,0:T(8,128)(2,1)S(1)} %get-tuple-element.50), channel_id=1, source_target_pairs={{0,1},{1,0},{2,3},{3,2},{4,5},{5,4},{6,7},{7,6},{8,9},{9,8},{10,11... | collective-permute-start | bytes 589832 | tf_op jit(solution)/shard_map/ppermute | solution.py:164
  31.7 3.0 %collective-permute-start.12 = (bf16[256,384]{1,0:T(8,128)(2,1)S(1)}, bf16[256,384]{1,0:T(8,128)(2,1)S(1)}, u32[]{:S(2)}, u32[]{:S(2)}) collective-permute-start(bf16[256,384]{1,0:T(8,128)(2,1)S(1)} %get-tuple-element.51), channel_id=1, source_target_pairs={{0,1},{1,0},{2,3},{3,2},{4,5},{5,4},{6,7},{7,6},{8,9},{9,8},{10,11... | collective-permute-start | bytes 589832 | tf_op jit(solution)/shard_map/ppermute | solution.py:164
  31.7 12.9 %collective-permute-start.14 = (bf16[128,1536]{1,0:T(8,128)(2,1)S(1)}, bf16[128,1536]{1,0:T(8,128)(2,1)S(1)}, u32[]{:S(2)}, u32[]{:S(2)}) collective-permute-start(bf16[128,1536]{1,0:T(8,128)(2,1)S(1)} %standardized.3.refs_9_.refs_0_), channel_id=1, source_target_pairs={{0,24},{8,16},{16,8},{24,0},{1,25},{9,17},{17,9},{25,1},{2,26},{10... | collective-permute-start | bytes 1179656 | tf_op jit(solution)/shard_map/ppermute | solution.py:164
  33.2 1.4 %copy-start.3 = (f32[128]{0:T(128)S(1)}, f32[128]{0:T(128)}, u32[]{:S(2)}) copy-start(f32[128]{0:T(128)} %param.14) | copy-start | bytes 1540
  33.2 1.4 %copy-start.4 = (f32[128]{0:T(128)S(1)}, f32[128]{0:T(128)}, u32[]{:S(2)}) copy-start(f32[128]{0:T(128)} %param.13) | copy-start | bytes 1540
  35.0 12.1 %collective-permute-start.13 = (bf16[256,768]{1,0:T(8,128)(2,1)S(1)}, bf16[256,768]{1,0:T(8,128)(2,1)S(1)}, u32[]{:S(2)}, u32[]{:S(2)}) collective-permute-start(bf16[256,768]{1,0:T(8,128)(2,1)S(1)} %get-tuple-element.53.refs_6_.after_ref.refs_1_), channel_id=1, source_target_pairs={{0,2},{2,0},{4,6},{6,4},{1,3},{3,1},{5,7},{7,5},{8,10},{10,8},{12,... | collective-permute-start | bytes 1179656 | tf_op jit(solution)/shard_map/ppermute | solution.py:164
  36.4 16.1 %collective-permute-start.17 = (bf16[128,1536]{1,0:T(8,128)(2,1)S(1)}, bf16[128,1536]{1,0:T(8,128)(2,1)S(1)}, u32[]{:S(2)}, u32[]{:S(2)}) collective-permute-start(bf16[128,1536]{1,0:T(8,128)(2,1)S(1)} %standardized.3.refs_9_.refs_0_), channel_id=1, source_target_pairs={{0,16},{8,24},{16,0},{24,8},{1,17},{9,25},{17,1},{25,9},{2,18},{10... | collective-permute-start | bytes 1179656 | tf_op jit(solution)/shard_map/ppermute | solution.py:164
  37.6 15.0 %collective-permute-start.18 = (bf16[128,1536]{1,0:T(8,128)(2,1)S(1)}, bf16[128,1536]{1,0:T(8,128)(2,1)S(1)}, u32[]{:S(2)}, u32[]{:S(2)}) collective-permute-start(bf16[128,1536]{1,0:T(8,128)(2,1)S(1)} %standardized.3.refs_9_.refs_0_), channel_id=1, source_target_pairs={{0,8},{8,0},{16,24},{24,16},{1,9},{9,1},{17,25},{25,17},{2,10},{10... | collective-permute-start | bytes 1179656 | tf_op jit(solution)/shard_map/ppermute | solution.py:164
  46.6 1.5 %collective-permute-start.15 = (bf16[256,384]{1,0:T(8,128)(2,1)S(1)}, bf16[256,384]{1,0:T(8,128)(2,1)S(1)}, u32[]{:S(2)}, u32[]{:S(2)}) collective-permute-start(bf16[256,384]{1,0:T(8,128)(2,1)S(1)} %get-tuple-element.57), channel_id=1, source_target_pairs={{0,1},{1,0},{2,3},{3,2},{4,5},{5,4},{6,7},{7,6},{8,9},{9,8},{10,11... | collective-permute-start | bytes 589832 | tf_op jit(solution)/shard_map/ppermute | solution.py:164
  46.7 1.7 %collective-permute-start.16 = (bf16[256,384]{1,0:T(8,128)(2,1)S(1)}, bf16[256,384]{1,0:T(8,128)(2,1)S(1)}, u32[]{:S(2)}, u32[]{:S(2)}) collective-permute-start(bf16[256,384]{1,0:T(8,128)(2,1)S(1)} %get-tuple-element.58), channel_id=1, source_target_pairs={{0,1},{1,0},{2,3},{3,2},{4,5},{5,4},{6,7},{7,6},{8,9},{9,8},{10,11... | collective-permute-start | bytes 589832 | tf_op jit(solution)/shard_map/ppermute | solution.py:164
  53.7 1.6 %collective-permute-start.19 = (bf16[256,384]{1,0:T(8,128)(2,1)S(1)}, bf16[256,384]{1,0:T(8,128)(2,1)S(1)}, u32[]{:S(2)}, u32[]{:S(2)}) collective-permute-start(bf16[256,384]{1,0:T(8,128)(2,1)S(1)} %get-tuple-element.65), channel_id=1, source_target_pairs={{0,1},{1,0},{2,3},{3,2},{4,5},{5,4},{6,7},{7,6},{8,9},{9,8},{10,11... | collective-permute-start | bytes 589832 | tf_op jit(solution)/shard_map/ppermute | solution.py:164
  53.7 1.7 %collective-permute-start.20 = (bf16[256,384]{1,0:T(8,128)(2,1)S(1)}, bf16[256,384]{1,0:T(8,128)(2,1)S(1)}, u32[]{:S(2)}, u32[]{:S(2)}) collective-permute-start(bf16[256,384]{1,0:T(8,128)(2,1)S(1)} %get-tuple-element.66), channel_id=1, source_target_pairs={{0,1},{1,0},{2,3},{3,2},{4,5},{5,4},{6,7},{7,6},{8,9},{9,8},{10,11... | collective-permute-start | bytes 589832 | tf_op jit(solution)/shard_map/ppermute | solution.py:164
  56.6 1.5 %collective-permute-start.21 = (bf16[256,384]{1,0:T(8,128)(2,1)S(1)}, bf16[256,384]{1,0:T(8,128)(2,1)S(1)}, u32[]{:S(2)}, u32[]{:S(2)}) collective-permute-start(bf16[256,384]{1,0:T(8,128)(2,1)S(1)} %finished.1.own_ref), channel_id=1, source_target_pairs={{0,1},{1,0},{2,3},{3,2},{4,5},{5,4},{6,7},{7,6},{8,9},{9,8},{10,11... | collective-permute-start | bytes 589832 | tf_op jit(solution)/shard_map/ppermute | solution.py:164
  59.1 7.8 %collective-permute-start.22 = (bf16[64,1536]{1,0:T(8,128)(2,1)S(1)}, bf16[64,1536]{1,0:T(8,128)(2,1)S(1)}, u32[]{:S(2)}, u32[]{:S(2)}) collective-permute-start(bf16[64,1536]{1,0:T(8,128)(2,1)S(1)} %get-tuple-element.68), channel_id=1, source_target_pairs={{0,8},{8,0},{16,24},{24,16},{1,9},{9,1},{17,25},{25,17},{2,10},{10... | collective-permute-start | bytes 589832 | tf_op jit(solution)/shard_map/ppermute | solution.py:164
  60.3 7.5 %collective-permute-start.23 = (bf16[64,1536]{1,0:T(8,128)(2,1)S(1)}, bf16[64,1536]{1,0:T(8,128)(2,1)S(1)}, u32[]{:S(2)}, u32[]{:S(2)}) collective-permute-start(bf16[64,1536]{1,0:T(8,128)(2,1)S(1)} %get-tuple-element.69), channel_id=1, source_target_pairs={{0,16},{8,24},{16,0},{24,8},{1,17},{9,25},{17,1},{25,9},{2,18},{10... | collective-permute-start | bytes 589832 | tf_op jit(solution)/shard_map/ppermute | solution.py:164
  61.1 10.2 %collective-permute-start.24 = (bf16[64,1536]{1,0:T(8,128)(2,1)S(1)}, bf16[64,1536]{1,0:T(8,128)(2,1)S(1)}, u32[]{:S(2)}, u32[]{:S(2)}) collective-permute-start(bf16[64,1536]{1,0:T(8,128)(2,1)S(1)} %get-tuple-element.70), channel_id=1, source_target_pairs={{0,24},{8,16},{16,8},{24,0},{1,25},{9,17},{17,9},{25,1},{2,26},{10... | collective-permute-start | bytes 589832 | tf_op jit(solution)/shard_map/ppermute | solution.py:164
  71.5 1.3 %collective-permute-start.25 = (f32[64,128]{1,0:T(8,128)S(1)}, f32[64,128]{1,0:T(8,128)S(1)}, u32[]{:S(2)}, u32[]{:S(2)}) collective-permute-start(f32[64,128]{1,0:T(8,128)S(1)} %get-tuple-element.72.refs_1_), channel_id=1, source_target_pairs={{0,1},{1,0},{2,3},{3,2},{4,5},{5,4},{6,7},{7,6},{8,9},{9,8},{10,11... | collective-permute-start | bytes 98312 | tf_op jit(solution)/shard_map/ppermute | solution.py:164
  73.0 8.9 %collective-permute-start.26 = (bf16[64,1536]{1,0:T(8,128)(2,1)S(1)}, bf16[64,1536]{1,0:T(8,128)(2,1)S(1)}, u32[]{:S(2)}, u32[]{:S(2)}) collective-permute-start(bf16[64,1536]{1,0:T(8,128)(2,1)S(1)} %normed_rows.1.refs_0_), channel_id=1, source_target_pairs={{0,24},{8,16},{16,8},{24,0},{1,25},{9,17},{17,9},{25,1},{2,26},{10... | collective-permute-start | bytes 589832 | tf_op jit(solution)/shard_map/ppermute | solution.py:164
  75.0 10.3 %collective-permute-start.29 = (bf16[64,1536]{1,0:T(8,128)(2,1)S(1)}, bf16[64,1536]{1,0:T(8,128)(2,1)S(1)}, u32[]{:S(2)}, u32[]{:S(2)}) collective-permute-start(bf16[64,1536]{1,0:T(8,128)(2,1)S(1)} %normed_rows.1.refs_0_), channel_id=1, source_target_pairs={{0,16},{8,24},{16,0},{24,8},{1,17},{9,25},{17,1},{25,9},{2,18},{10... | collective-permute-start | bytes 589832 | tf_op jit(solution)/shard_map/ppermute | solution.py:164
  75.6 9.7 %collective-permute-start.30 = (bf16[64,1536]{1,0:T(8,128)(2,1)S(1)}, bf16[64,1536]{1,0:T(8,128)(2,1)S(1)}, u32[]{:S(2)}, u32[]{:S(2)}) collective-permute-start(bf16[64,1536]{1,0:T(8,128)(2,1)S(1)} %normed_rows.1.refs_0_), channel_id=1, source_target_pairs={{0,8},{8,0},{16,24},{24,16},{1,9},{9,1},{17,25},{25,17},{2,10},{10... | collective-permute-start | bytes 589832 | tf_op jit(solution)/shard_map/ppermute | solution.py:164
  82.8 2.6 %collective-permute-start.28 = (bf16[128,1536]{1,0:T(8,128)(2,1)S(1)}, bf16[128,1536]{1,0:T(8,128)(2,1)S(1)}, u32[]{:S(2)}, u32[]{:S(2)}) collective-permute-start(bf16[128,1536]{1,0:T(8,128)(2,1)S(1)} %up_projected.5.refs_0_), channel_id=1, source_target_pairs={{0,1},{1,0},{2,3},{3,2},{4,5},{5,4},{6,7},{7,6},{8,9},{9,8},{10,11... | collective-permute-start | bytes 1179656 | tf_op jit(solution)/shard_map/ppermute | solution.py:164
  83.7 2.6 %collective-permute-start.27 = (bf16[128,1536]{1,0:T(8,128)(2,1)S(1)}, bf16[128,1536]{1,0:T(8,128)(2,1)S(1)}, u32[]{:S(2)}, u32[]{:S(2)}) collective-permute-start(bf16[128,1536]{1,0:T(8,128)(2,1)S(1)} %up_projected.4.refs_0_), channel_id=1, source_target_pairs={{0,1},{1,0},{2,3},{3,2},{4,5},{5,4},{6,7},{7,6},{8,9},{9,8},{10,11... | collective-permute-start | bytes 1179656 | tf_op jit(solution)/shard_map/ppermute | solution.py:164
  88.1 3.2 %collective-permute-start.32 = (bf16[128,1536]{1,0:T(8,128)(2,1)S(1)}, bf16[128,1536]{1,0:T(8,128)(2,1)S(1)}, u32[]{:S(2)}, u32[]{:S(2)}) collective-permute-start(bf16[128,1536]{1,0:T(8,128)(2,1)S(1)} %up_projected.7.refs_0_), channel_id=1, source_target_pairs={{0,1},{1,0},{2,3},{3,2},{4,5},{5,4},{6,7},{7,6},{8,9},{9,8},{10,11... | collective-permute-start | bytes 1179656 | tf_op jit(solution)/shard_map/ppermute | solution.py:164
  89.0 3.2 %collective-permute-start.31 = (bf16[128,1536]{1,0:T(8,128)(2,1)S(1)}, bf16[128,1536]{1,0:T(8,128)(2,1)S(1)}, u32[]{:S(2)}, u32[]{:S(2)}) collective-permute-start(bf16[128,1536]{1,0:T(8,128)(2,1)S(1)} %up_projected.6.refs_0_), channel_id=1, source_target_pairs={{0,1},{1,0},{2,3},{3,2},{4,5},{5,4},{6,7},{7,6},{8,9},{9,8},{10,11... | collective-permute-start | bytes 1179656 | tf_op jit(solution)/shard_map/ppermute | solution.py:164
  89.5 8.7 %collective-permute-start.35 = (bf16[64,1536]{1,0:T(8,128)(2,1)S(1)}, bf16[64,1536]{1,0:T(8,128)(2,1)S(1)}, u32[]{:S(2)}, u32[]{:S(2)}) collective-permute-start(bf16[64,1536]{1,0:T(8,128)(2,1)S(1)} %get-tuple-element.76), channel_id=1, source_target_pairs={{0,24},{8,16},{16,8},{24,0},{1,25},{9,17},{17,9},{25,1},{2,26},{10... | collective-permute-start | bytes 589832 | tf_op jit(solution)/shard_map/ppermute | solution.py:164
  92.2 10.2 %copy-start.1 = (bf16[3072,576]{0,1:T(8,128)(2,1)S(1)}, bf16[3072,576]{0,1:T(8,128)(2,1)}, u32[]{:S(2)}) copy-start(bf16[3072,576]{0,1:T(8,128)(2,1)} %param.11) | copy-start | bytes 10616836
  93.2 7.7 %collective-permute-start.33 = (bf16[64,1536]{1,0:T(8,128)(2,1)S(1)}, bf16[64,1536]{1,0:T(8,128)(2,1)S(1)}, u32[]{:S(2)}, u32[]{:S(2)}) collective-permute-start(bf16[64,1536]{1,0:T(8,128)(2,1)S(1)} %get-tuple-element.74), channel_id=1, source_target_pairs={{0,8},{8,0},{16,24},{24,16},{1,9},{9,1},{17,25},{25,17},{2,10},{10... | collective-permute-start | bytes 589832 | tf_op jit(solution)/shard_map/ppermute | solution.py:164
  93.8 7.7 %collective-permute-start.34 = (bf16[64,1536]{1,0:T(8,128)(2,1)S(1)}, bf16[64,1536]{1,0:T(8,128)(2,1)S(1)}, u32[]{:S(2)}, u32[]{:S(2)}) collective-permute-start(bf16[64,1536]{1,0:T(8,128)(2,1)S(1)} %get-tuple-element.75), channel_id=1, source_target_pairs={{0,16},{8,24},{16,0},{24,8},{1,17},{9,25},{17,1},{25,9},{2,18},{10... | collective-permute-start | bytes 589832 | tf_op jit(solution)/shard_map/ppermute | solution.py:164

commit v7 on v6

--- a/solution.py
+++ b/solution.py
@@ -555,12 +555,15 @@
 def attend_kernel(head_size, count, query_ref, *refs):
     kv_refs, (top_ref, total_ref, summed_ref) = refs[:count], refs[-3:]
     half = query_ref.shape[1]
-    for low in range(0, half, head_size):
-        here = slice(low, low + head_size)
-        scores = [head_scores(query_ref[:, here], ref[:, here], head_size) for ref in kv_refs]
-        values = [ref[:, half + low : half + low + head_size] for ref in kv_refs]
-        top = highest(scores)
-        total, summed = weighted(scores, values, top)
+    places = [slice(low, low + head_size) for low in range(0, half, head_size)]
+    scores = [
+        [head_scores(query_ref[:, here], ref[:, here], head_size) for ref in kv_refs]
+        for here in places
+    ]
+    tops = [highest(parts) for parts in scores]
+    for here, parts, top in zip(places, scores, tops):
+        values = [ref[:, half + here.start : half + here.stop] for ref in kv_refs]
+        total, summed = weighted(parts, values, top)
         top_ref[:, here] = jnp.broadcast_to(top, summed.shape)
         total_ref[:, here] = jnp.broadcast_to(total, summed.shape)
         summed_ref[:, here] = summed
@@ -581,45 +584,48 @@
     )(queries, *kv_parts, *after)
 
 
-def finish_kernel(head_size, query_ref, top_ref, total_ref, summed_ref, *refs):
-    *refs, out_ref = refs
+def finish_kernel(head_size, count, query_ref, top_ref, total_ref, summed_ref, *refs):
+    kv_refs, out_ref = refs[:count], refs[-1]
     half = query_ref.shape[1]
-    for low in range(0, half, head_size):
-        here = slice(low, low + head_size)
-        top, total, summed = top_ref[:, here], total_ref[:, here], summed_ref[:, here]
-        if refs:
-            own_key, own_value, other_key, other_value, k_gain_ref = refs
-            key = head_normal(
-                own_key[:, here].astype(jnp.float32) + other_key[:, here].astype(jnp.float32),
-                k_gain_ref,
-            )
-            value = own_value[:, here].astype(jnp.float32) + other_value[:, here].astype(
-                jnp.float32
-            )
-            scores = [head_scores(query_ref[:, here], key, head_size)]
-            new_top = jnp.maximum(top, highest(scores))
-            more_total, more_summed = weighted(
-                scores, [value.astype(jnp.bfloat16)], new_top[:, :1]
-            )
-            decay = jnp.exp(top - new_top)
-            total = total * decay + more_total
-            summed = summed * decay + more_summed
-        out_ref[:, here] = (summed / total).astype(jnp.bfloat16)
-
-
-def finished(queries, state, parts, head_size):
+    places = [slice(low, low + head_size) for low in range(0, half, head_size)]
+    tops = [top_ref[:, here] for here in places]
+    totals = [total_ref[:, here] for here in places]
+    sums = [summed_ref[:, here] for here in places]
+    if kv_refs:
+        keys = [kv_refs[0][:, here] for here in places]
+        values = [kv_refs[0][:, half + here.start : half + here.stop] for here in places]
+        scores = [
+            head_scores(query_ref[:, here], key, head_size) for here, key in zip(places, keys)
+        ]
+        new_tops = [jnp.maximum(top, highest([part])) for top, part in zip(tops, scores)]
+        decays = [jnp.exp(top - new_top) for top, new_top in zip(tops, new_tops)]
+        weights = [jnp.exp(part - new_top[:, :1]) for part, new_top in zip(scores, new_tops)]
+        products = [
+            jnp.dot(part.astype(jnp.bfloat16), value, preferred_element_type=jnp.float32)
+            for part, value in zip(weights, values)
+        ]
+        totals = [
+            total * decay + jnp.sum(part, axis=-1, keepdims=True)
+            for total, decay, part in zip(totals, decays, weights)
+        ]
+        sums = [part * decay + more for part, decay, more in zip(sums, decays, products)]
+    for here, total, part in zip(places, totals, sums):
+        out_ref[:, here] = (part / total).astype(jnp.bfloat16)
+
+
+def finished(queries, state, parts, head_size, first, count, after=()):
     whole = lambda array: pl.BlockSpec(array.shape, lambda j: (0, 0))
-    arrays = [queries, *state, *parts]
-    return pl.pallas_call(
-        lambda *refs: finish_kernel(head_size, *refs),
-        grid=(1,),
-        in_specs=[whole(array) for array in arrays],
-        out_specs=whole(queries),
-        out_shape=jax.ShapeDtypeStruct(queries.shape, jnp.bfloat16),
+    some = pl.BlockSpec((count, queries.shape[1]), lambda j: (first // count, 0))
+    return pl.pallas_call(
+        lambda *refs: finish_kernel(head_size, len(parts), *refs),
+        grid=(1,),
+        in_specs=[some] * 4 + [whole(array) for array in parts] + after_specs(after),
+        out_specs=pl.BlockSpec((count, queries.shape[1]), lambda j: (0, 0)),
+        out_shape=jax.ShapeDtypeStruct((count, queries.shape[1]), jnp.bfloat16),
         compiler_params=pltpu.CompilerParams(vmem_limit_bytes=VMEM_BYTES * 12),
         cost_estimate=NO_COST,
         name="finished",
-    )(*arrays)
+    )(queries, *state, *parts, *after)
 
 
 def column_tiles(columns):
@@ -627,7 +633,8 @@
     return [slice(low, low + size) for low in range(0, columns, size)]
 
 
-def out_kernel(own_ref, arrived_ref, weight_ref, *out_refs):
+def out_kernel(count, own_ref, arrived_ref, weight_ref, *refs):
+    out_refs = refs[-count:]
     half = own_ref.shape[1]
     position = lax.axis_index("tensor")
     rows = [pl.ds(pl.multiple_of(at * half, 16), half) for at in (position, 1 - position)]
@@ -644,20 +651,20 @@
         out_ref[:, columns] = values[k * rows : (k + 1) * rows].astype(jnp.bfloat16)
 
 
-def out_projected(own, arrived, weight, rows):
+def out_projected(own, arrived, weight, rows, after):
     all_rows, half = own.shape
     width = weight.shape[1]
     whole = pl.BlockSpec((all_rows, half), lambda j: (0, 0))
     return pl.pallas_call(
-        out_kernel,
-        grid=(1,),
-        in_specs=[whole, whole, pl.BlockSpec(memory_space=pltpu.VMEM)],
+        lambda *refs: out_kernel(all_rows // rows, *refs),
+        grid=(1,),
+        in_specs=[whole, whole, pl.BlockSpec(memory_space=pltpu.VMEM)] + after_specs(after),
         out_specs=[pl.BlockSpec((rows, width), lambda j: (0, 0))] * (all_rows // rows),
         out_shape=[jax.ShapeDtypeStruct((rows, width), jnp.bfloat16)] * (all_rows // rows),
         compiler_params=pltpu.CompilerParams(vmem_limit_bytes=VMEM_BYTES * 8),
         cost_estimate=NO_COST,
         name="out_projected",
-    )(own, arrived, weight)
+    )(own, arrived, weight, *after)
 
 
 def up_kernel(first, count, *refs):
@@ -734,30 +741,64 @@
     )(own, arrived, weight, *before)
 
 
-def mix_kernel(count, *refs):
-    block_refs, token_ref, gate_ref = refs[:count], refs[count], refs[count + 1]
+def add_kernel(first_ref, second_ref, out_ref):
+    total = first_ref[...].astype(jnp.float32) + second_ref[...].astype(jnp.float32)
+    out_ref[...] = total.astype(jnp.bfloat16)
+
+
+def rounded_sum(first, second):
+    return pl.pallas_call(
+        add_kernel,
+        out_shape=jax.ShapeDtypeStruct(first.shape, first.dtype),
+        compiler_params=pltpu.CompilerParams(vmem_limit_bytes=VMEM_BYTES * 2),
+        cost_estimate=NO_COST,
+        name="rounded_sum",
+    )(first, second)
+
+
+def row_groups(blocks, axis):
+    groups = len(blocks) // lax.axis_size(axis)
+    pieces = [blocks[k : k + groups] for k in range(0, len(blocks), groups)]
+    if groups != 2 or len(pieces) != 4:
+        return [to_all([piece[k] for piece in pieces], axis) for k in range(groups)]
+    own, first, second, far = pieces
+    low, high = permuted(far[0], axis, 1), permuted(far[1], axis, 2)
+    first_low, second_high = permuted(first[0], axis, 1), permuted(second[1], axis, 2)
+    second_low = permuted(rounded_sum(second[0], low), axis, 2)
+    first_high = permuted(rounded_sum(first[1], high), axis, 1)
+    return [[own[0], first_low, second_low], [own[1], first_high, second_high]]
+
+
+def mix_kernel(counts, *refs):
+    token_ref, gate_ref = refs[sum(counts)], refs[sum(counts) + 1]
     mixed_ref, sums_ref = refs[-2:]
-    total = block_refs[0][...].astype(jnp.float32)
-    for block_ref in block_refs[1:]:
-        total = total + block_ref[...].astype(jnp.float32)
-    mixed = token_ref[...].astype(jnp.float32) + gate_ref[...] * total
-    mixed_ref[...] = mixed
-    lane = lax.broadcasted_iota(jnp.int32, sums_ref.shape, 1)
-    sums_ref[...] = jnp.where(
-        lane < sums_ref.shape[1] // 2,
-        jnp.sum(mixed, axis=-1, keepdims=True),
-        jnp.sum(mixed * mixed, axis=-1, keepdims=True),
-    )
-
-
-def mixed_rows(blocks, tokens, gate_row, after):
+    rows = refs[0].shape[0]
+    lane = lax.broadcasted_iota(jnp.int32, (rows, sums_ref.shape[1]), 1)
+    at = 0
+    for group, count in enumerate(counts):
+        here = slice(group * rows, (group + 1) * rows)
+        total = refs[at][...].astype(jnp.float32)
+        for block_ref in refs[at + 1 : at + count]:
+            total = total + block_ref[...].astype(jnp.float32)
+        at += count
+        mixed = token_ref[here, :].astype(jnp.float32) + gate_ref[...] * total
+        mixed_ref[here, :] = mixed
+        sums_ref[here, :] = jnp.where(
+            lane < sums_ref.shape[1] // 2,
+            jnp.sum(mixed, axis=-1, keepdims=True),
+            jnp.sum(mixed * mixed, axis=-1, keepdims=True),
+        )
+
+
+def mixed_rows(groups, tokens, gate_row, after):
     rows, width = tokens.shape
     whole = lambda *shape: pl.BlockSpec(shape, lambda j: (0, 0))
-    return pl.pallas_call(
-        lambda *refs: mix_kernel(len(blocks), *refs),
-        grid=(1,),
-        in_specs=[whole(rows, width)] * (len(blocks) + 1)
-        + [whole(1, width)]
+    blocks = [block for group in groups for block in group]
+    return pl.pallas_call(
+        lambda *refs: mix_kernel([len(group) for group in groups], *refs),
+        grid=(1,),
+        in_specs=[whole(*block.shape) for block in blocks]
+        + [whole(rows, width), whole(1, width)]
         + after_specs(after),
         out_specs=[whole(rows, width), whole(rows, 128)],
         out_shape=[
@@ -852,14 +893,25 @@
     if remote and last_blocks:
         tie = mark([*chunks[-1][1:], state[0]], SHORT)
         own, arrived = project(last_blocks, parts[1:], [state[0], tie])
-        last = [*own, *arrived, k_gain[None, :]]
-    context = finished(queries, state, last, head_size)
-
-    partial = out_projected(context, permuted(context, "tensor", 1), out_weight, rows)
-    down_weight = staged(down_weight, partial[0])
-    mixed, sums = mixed_rows(to_all(partial, "ulysses"), tokens, row(2), [down_weight])
+        last = split_heads(own, arrived, q_gain, k_gain)
+    all_rows = queries.shape[0]
+    last_rows = rows if all_rows > rows else 0
+    partial, arrived = [], []
+    if last_rows:
+        context = finished(queries, state, last, head_size, all_rows - rows, rows)
+        arrived.append((context, permuted(context, "tensor", 1)))
+    after = [own for own, _ in arrived]
+    context = finished(queries, state, last, head_size, 0, all_rows - last_rows, after)
+    other = permuted(context, "tensor", 1)
+    arrived.append((context, other))
+    for own, other in arrived:
+        after = [] if own is context else [context]
+        partial = list(out_projected(own, other, out_weight, rows // 2, after)) + partial
+    summed = row_groups(partial, "ulysses")
+    mixed, sums = mixed_rows(summed, tokens, row(2), [])
     normed_two = normed_rows(mixed, sums, row(3), row(4), features)
     blocks = from_all(normed_two, "ulysses")
+    down_weight = staged(down_weight, normed_two)
     order = halves(list(range(len(blocks))))
     outs = {}
     for part, places in enumerate(order):
@@ -868,7 +920,7 @@
         here = [blocks[k] for k in places]
         here = [stacked(here, LONG)] if part else here
         pieces = 2
-        after = [outs[order[0][0]]] if part else []
+        after = [outs[order[0][0]]] if part else [down_weight]
         ups = [up_projected(here, up_weight, k, pieces, after) for k in range(pieces)]
         arrived = [permuted(piece, "tensor", 1) for piece in ups]
         before = []

time: 103 us -> 102 us (level)
  waiting for transfers between devices: 32.2 us -> 29.1 us
  starting transfers between devices: 32.3 us -> 34.3 us
    ppermute x36 -> x40, waiting for transfers between devices: 32.2 us -> 29.1 us  [permuted(): return lax.ppermute(values, axis, [(i, i ^ distance) for i in range(size)])]
    ppermute x36 -> x40, starting transfers between devices: 32.3 us -> 34.3 us  [permuted(): return lax.ppermute(values, axis, [(i, i ^ distance) for i in range(size)])]
    pallas_call x3 -> x7, Pallas kernels: 2.35 us -> 2.91 us  [the longest x2 1.29 us: out_projected(): pl.pallas_call(lambda *refs: out_kernel(all_rows // rows, *refs), grid=(1...]
  transfers between devices with their start and end apart: 36 -> 40, of which waited for: 21 -> 24; matrix products, arithmetic and copies ran while one was open for 0% -> 0% of each run, Pallas kernels for 26% -> 27%
where the time goes in v7:
time: 102 us
  starting transfers between devices  34.3 us (34%)
  Pallas kernels  33.7 us (33%)
  waiting for transfers between devices  29.1 us (29%)
  other arithmetic  1.72 us (2%)
  local copies, waits for them, and re-layouts  1.21 us (1%)
    ppermute x40, starting transfers between devices, permuted(): return lax.ppermute(values, axis, [(i, i ^ distance) for i in range(size)])  34.3 us
    ppermute x40, waiting for transfers between devices, permuted(): return lax.ppermute(values, axis, [(i, i ^ distance) for i in range(size)])  29.1 us
    pallas_call x6, Pallas kernels, staged(): pl.pallas_call(kernel, grid=(1,), in_specs=[anywhere] + after_specs([afte...  14.1 us
    pallas_call x6, Pallas kernels, projected(): pl.pallas_call((lambda *refs: project_kernel(len(blocks), count, other, *...  6.8 us
    pallas_call x4, Pallas kernels, down_projected(): pl.pallas_call(lambda *refs: down_kernel(first, count, len(before), *refs...  3.56 us
    pallas_call x4, Pallas kernels, up_projected(): pl.pallas_call(lambda *refs: up_kernel(part * columns, len(blocks), *refs...  3.13 us
  transfers between devices with their start and end apart: 40, of which 24 were waited for; matrix products, arithmetic and copies ran while one was open for 0% of the time, Pallas kernels for 27%

profile of v7, /device:TPU:0, one launch (start us, length us, event | category | flops | bytes accessed | tf_op | source)
XLA Modules:
  0.0 101.5 jit_solution(3922541245531771842)
XLA Ops:
  0.9 1.1 %copy-done = bf16[3072,576]{0,1:T(8,128)(2,1)S(1)} copy-done((bf16[3072,576]{0,1:T(8,128)(2,1)S(1)}, bf16[3072,576]{0,1:T(8,128)(2,1)}, u32[]{:S(2)}) %copy-start) | copy-done | bytes 3538968
  2.0 1.0 fusion.4.refs_0_.after_ref
  3.1 4.1 %collective-permute-start.4 = (bf16[64,1536]{1,0:T(8,128)(2,1)S(1)}, bf16[64,1536]{1,0:T(8,128)(2,1)S(1)}, u32[]{:S(2)}, u32[]{:S(2)}) collective-permute-start(bf16[64,1536]{1,0:T(8,128)(2,1)S(1)} %copied.2), channel_id=1, source_target_pairs={{0,4},{2,6},{4,0},{6,2},{1,5},{3,7},{5,1},{7,3},{8,12},{10,14},{12... | collective-permute-start | bytes 589832 | tf_op jit(solution)/shard_map/ppermute | solution.py:164
  8.7 1.6 %collective-permute-start.2 = (f32[2,576]{1,0:T(2,128)S(1)}, f32[2,576]{1,0:T(2,128)S(1)}, u32[]{:S(2)}, u32[]{:S(2)}) collective-permute-start(f32[2,576]{1,0:T(2,128)S(1)} %merged.3.after_ref.refs_0_), channel_id=1, source_target_pairs={{0,2},{2,0},{4,6},{6,4},{1,3},{3,1},{5,7},{7,5},{8,10},{10,8},{12,... | collective-permute-start | bytes 13832 | tf_op jit(solution)/shard_map/ppermute | solution.py:164
  10.3 1.6 %staged.6.refs_2_.refs_7_.refs_4_.refs_1_ = bf16[1536,768]{1,0:T(8,128)(2,1)S(1)} custom-call(bf16[3,1536,768]{2,1,0:T(8,128)(2,1)} %bitcast.11, f32[2,576]{1,0:T(2,128)S(1)} %merged.3.after_ref.refs_0_), custom_call_target="tpu_custom_call" | custom-call | bytes 2359296 | tf_op jit(solution)/shard_map/staged/pallas_call | solution.py:452
  12.3 1.6 %collective-permute-start.3 = (f32[4,576]{1,0:T(4,128)S(1)}, f32[4,576]{1,0:T(4,128)S(1)}, u32[]{:S(2)}, u32[]{:S(2)}) collective-permute-start(f32[4,576]{1,0:T(4,128)S(1)} %merged.4.after_ref.refs_0_), channel_id=1, source_target_pairs={{0,4},{2,6},{4,0},{6,2},{1,5},{3,7},{5,1},{7,3},{8,12},{10,14},{12... | collective-permute-start | bytes 27656 | tf_op jit(solution)/shard_map/ppermute | solution.py:164
  13.9 1.6 %staged.7.refs_3_.refs_8_.refs_5_.refs_2_ = bf16[1536,768]{1,0:T(8,128)(2,1)S(1)} custom-call(bf16[3,1536,768]{2,1,0:T(8,128)(2,1)} %bitcast.12, f32[4,576]{1,0:T(4,128)S(1)} %merged.4.after_ref.refs_0_), custom_call_target="tpu_custom_call" | custom-call | bytes 2359296 | tf_op jit(solution)/shard_map/staged/pallas_call | solution.py:452
  15.6 1.4 %collective-permute-done.3.refs_1_ = f32[4,576]{1,0:T(4,128)S(1)} collective-permute-done((f32[4,576]{1,0:T(4,128)S(1)}, f32[4,576]{1,0:T(4,128)S(1)}, u32[]{:S(2)}, u32[]{:S(2)}) %collective-permute-start.3) | collective-permute-done | bytes 9248 | tf_op jit(solution)/shard_map/ppermute | solution.py:164
  17.0 1.6 %collective-permute-start.5 = (bf16[64,1664]{1,0:T(8,128)(2,1)S(1)}, bf16[64,1664]{1,0:T(8,128)(2,1)S(1)}, u32[]{:S(2)}, u32[]{:S(2)}) collective-permute-start(bf16[64,1664]{1,0:T(8,128)(2,1)S(1)} %packed.1.refs_0_.after_ref), channel_id=1, source_target_pairs={{0,8},{8,0},{16,24},{24,16},{1,9},{9,1},{17,25},{25,17},{2,10},{10... | collective-permute-start | bytes 638984 | tf_op jit(solution)/shard_map/ppermute | solution.py:164
  18.6 1.5 %collective-permute-start.6 = (bf16[64,1664]{1,0:T(8,128)(2,1)S(1)}, bf16[64,1664]{1,0:T(8,128)(2,1)S(1)}, u32[]{:S(2)}, u32[]{:S(2)}) collective-permute-start(bf16[64,1664]{1,0:T(8,128)(2,1)S(1)} %packed.1.refs_0_.after_ref), channel_id=1, source_target_pairs={{0,16},{8,24},{16,0},{24,8},{1,17},{9,25},{17,1},{25,9},{2,18},{10... | collective-permute-start | bytes 638984 | tf_op jit(solution)/shard_map/ppermute | solution.py:164
  20.6 1.6 %collective-permute-start.8 = (bf16[64,1536]{1,0:T(8,128)(2,1)S(1)}, bf16[64,1536]{1,0:T(8,128)(2,1)S(1)}, u32[]{:S(2)}, u32[]{:S(2)}) collective-permute-start(bf16[64,1536]{1,0:T(8,128)(2,1)S(1)} %collective-permute-done.4.refs_4_.refs_0_), channel_id=1, source_target_pairs={{0,2},{2,0},{4,6},{6,4},{1,3},{3,1},{5,7},{7,5},{8,10},{10,8},{12,... | collective-permute-start | bytes 589832 | tf_op jit(solution)/shard_map/ppermute | solution.py:164
  22.2 1.6 %staged.8.refs_6_.refs_1_ = bf16[1536,768]{1,0:T(8,128)(2,1)S(1)} custom-call(bf16[3,1536,768]{2,1,0:T(8,128)(2,1)} %bitcast.13, bf16[64,1664]{1,0:T(8,128)(2,1)S(1)} %packed.1.refs_0_.after_ref), custom_call_target="tpu_custom_call" | custom-call | bytes 2359296 | tf_op jit(solution)/shard_map/staged/pallas_call | solution.py:452
  23.9 2.4 %collective-permute-done.8.refs_1_ = bf16[64,1536]{1,0:T(8,128)(2,1)S(1)} collective-permute-done((bf16[64,1536]{1,0:T(8,128)(2,1)S(1)}, bf16[64,1536]{1,0:T(8,128)(2,1)S(1)}, u32[]{:S(2)}, u32[]{:S(2)}) %collective-permute-start.8) | collective-permute-done | bytes 196640 | tf_op jit(solution)/shard_map/ppermute | solution.py:164
  26.5 2.7 %collective-permute-done.6.refs_2_ = bf16[64,1664]{1,0:T(8,128)(2,1)S(1)} collective-permute-done((bf16[64,1664]{1,0:T(8,128)(2,1)S(1)}, bf16[64,1664]{1,0:T(8,128)(2,1)S(1)}, u32[]{:S(2)}, u32[]{:S(2)}) %collective-permute-start.6) | collective-permute-done | bytes 213024 | tf_op jit(solution)/shard_map/ppermute | solution.py:164
  29.7 1.4 %projected.6 = (bf16[256,384]{1,0:T(8,128)(2,1)S(1)}, bf16[256,384]{1,0:T(8,128)(2,1)S(1)}, bf16[256,384]{1,0:T(8,128)(2,1)S(1)}, bf16[256,1536]{1,0:T(8,128)(2,1)S(1)}) custom-call(bf16[64,1664]{1,0:T(8,128)(2,1)S(1)} %packed.1.refs_0_.after_ref, bf16[64,1664]{1,0:T(8,128)(2,1)S(1)} %collective-permute-done.5.refs_1_, ...), custom_call_target="tpu_custom_call" | custom-call | tf_op jit(solution)/shard_map/projected/pallas_call | solution.py:416
  31.7 1.5 %collective-permute-start.14 = (bf16[128,1536]{1,0:T(8,128)(2,1)S(1)}, bf16[128,1536]{1,0:T(8,128)(2,1)S(1)}, u32[]{:S(2)}, u32[]{:S(2)}) collective-permute-start(bf16[128,1536]{1,0:T(8,128)(2,1)S(1)} %standardized.3.refs_9_.refs_0_), channel_id=1, source_target_pairs={{0,24},{8,16},{16,8},{24,0},{1,25},{9,17},{17,9},{25,1},{2,26},{10... | collective-permute-start | bytes 1179656 | tf_op jit(solution)/shard_map/ppermute | solution.py:164
  33.2 1.4 %projected.7 = (bf16[256,384]{1,0:T(8,128)(2,1)S(1)}, bf16[256,384]{1,0:T(8,128)(2,1)S(1)}, bf16[256,384]{1,0:T(8,128)(2,1)S(1)}) custom-call(bf16[256,1536]{1,0:T(8,128)(2,1)S(1)} %get-tuple-element.49.refs_0_, bf16[1536,768]{1,0:T(8,128)(2,1)S(1)} %staged.8.refs_6_.refs_1_, bf16[1536,768]{1,0:T(8,128)(2,1)S(1)} %staged.6.refs_2_.refs_7_.refs_4_.refs_1_, ...), custom_call_target="tpu_custom_call" | custom-call | tf_op jit(solution)/shard_map/projected/pallas_call | solution.py:416
  35.0 1.4 %collective-permute-start.13 = (bf16[256,768]{1,0:T(8,128)(2,1)S(1)}, bf16[256,768]{1,0:T(8,128)(2,1)S(1)}, u32[]{:S(2)}, u32[]{:S(2)}) collective-permute-start(bf16[256,768]{1,0:T(8,128)(2,1)S(1)} %get-tuple-element.57.refs_6_.after_ref.refs_1_), channel_id=1, source_target_pairs={{0,2},{2,0},{4,6},{6,4},{1,3},{3,1},{5,7},{7,5},{8,10},{10,8},{12,... | collective-permute-start | bytes 1179656 | tf_op jit(solution)/shard_map/ppermute | solution.py:164
  36.4 1.2 %collective-permute-start.17 = (bf16[128,1536]{1,0:T(8,128)(2,1)S(1)}, bf16[128,1536]{1,0:T(8,128)(2,1)S(1)}, u32[]{:S(2)}, u32[]{:S(2)}) collective-permute-start(bf16[128,1536]{1,0:T(8,128)(2,1)S(1)} %standardized.3.refs_9_.refs_0_), channel_id=1, source_target_pairs={{0,16},{8,24},{16,0},{24,8},{1,17},{9,25},{17,1},{25,9},{2,18},{10... | collective-permute-start | bytes 1179656 | tf_op jit(solution)/shard_map/ppermute | solution.py:164
  38.4 1.6 %staged.9.after_ref.refs_4_.refs_2_ = bf16[768,1536]{1,0:T(8,128)(2,1)S(1)} custom-call(bf16[768,1536]{1,0:T(8,128)(2,1)} %weight_ref.3, bf16[256,768]{1,0:T(8,128)(2,1)S(1)} %get-tuple-element.57.refs_6_.after_ref.refs_1_), custom_call_target="tpu_custom_call" | custom-call | bytes 2359296 | tf_op jit(solution)/shard_map/staged/pallas_call | solution.py:452
  40.1 3.8 %staged.10.refs_5_.refs_2_.refs_1_ = bf16[1536,3072]{1,0:T(8,128)(2,1)S(1)} custom-call(bf16[1536,3072]{1,0:T(8,128)(2,1)} %weight_ref.4, bf16[768,1536]{1,0:T(8,128)(2,1)S(1)} %staged.9.after_ref.refs_4_.refs_2_), custom_call_target="tpu_custom_call" | custom-call | bytes 9437184 | tf_op jit(solution)/shard_map/staged/pallas_call | solution.py:452
  44.6 1.0 projected.8
  45.6 1.0 projected.9
  47.2 0.9 collective-permute-done.15.refs_2_
  48.6 1.1 %attend.1 = (f32[256,384]{1,0:T(8,128)S(1)}, f32[256,384]{1,0:T(8,128)S(1)}, f32[256,384]{1,0:T(8,128)S(1)}) custom-call(bf16[256,384]{1,0:T(8,128)(2,1)S(1)} %get-tuple-element.56.refs_0_, bf16[256,768]{1,0:T(8,128)(2,1)S(1)} %get-tuple-element.57.refs_6_.after_ref.refs_1_, bf16[256,768]{1,0:T(8,128)(2,1)S(1)} %copied.3.refs_2_, ...), custom_call_target="tpu_custom_call" | custom-call | tf_op jit(solution)/shard_map/attend/pallas_call | solution.py:575
  49.8 2.8 %collective-permute-done.17.refs_1_.refs_0_ = bf16[128,1536]{1,0:T(8,128)(2,1)S(1)} collective-permute-done((bf16[128,1536]{1,0:T(8,128)(2,1)S(1)}, bf16[128,1536]{1,0:T(8,128)(2,1)S(1)}, u32[]{:S(2)}, u32[]{:S(2)}) %collective-permute-start.17) | collective-permute-done | bytes 393248 | tf_op jit(solution)/shard_map/ppermute | solution.py:164
  52.6 1.0 projected.10
  54.2 1.0 projected.11
  57.5 1.0 collective-permute-done.23.refs_1_
  58.9 1.5 %collective-permute-start.26 = (bf16[32,1536]{1,0:T(8,128)(2,1)S(1)}, bf16[32,1536]{1,0:T(8,128)(2,1)S(1)}, u32[]{:S(2)}, u32[]{:S(2)}) collective-permute-start(bf16[32,1536]{1,0:T(8,128)(2,1)S(1)} %get-tuple-element.77), channel_id=1, source_target_pairs={{0,16},{8,24},{16,0},{24,8},{1,17},{9,25},{17,1},{25,9},{2,18},{10... | collective-permute-start | bytes 294920 | tf_op jit(solution)/shard_map/ppermute | solution.py:164
  61.7 1.6 %collective-permute-start.22 = (bf16[32,1536]{1,0:T(8,128)(2,1)S(1)}, bf16[32,1536]{1,0:T(8,128)(2,1)S(1)}, u32[]{:S(2)}, u32[]{:S(2)}) collective-permute-start(bf16[32,1536]{1,0:T(8,128)(2,1)S(1)} %get-tuple-element.72), channel_id=1, source_target_pairs={{0,8},{8,0},{16,24},{24,16},{1,9},{9,1},{17,25},{25,17},{2,10},{10... | collective-permute-start | bytes 294920 | tf_op jit(solution)/shard_map/ppermute | solution.py:164
  64.0 1.2 %collective-permute-start.27 = (bf16[32,1536]{1,0:T(8,128)(2,1)S(1)}, bf16[32,1536]{1,0:T(8,128)(2,1)S(1)}, u32[]{:S(2)}, u32[]{:S(2)}) collective-permute-start(bf16[32,1536]{1,0:T(8,128)(2,1)S(1)} %rounded_sum.3), channel_id=1, source_target_pairs={{0,8},{8,0},{16,24},{24,16},{1,9},{9,1},{17,25},{25,17},{2,10},{10... | collective-permute-start | bytes 294920 | tf_op jit(solution)/shard_map/ppermute | solution.py:164
  66.3 1.9 %collective-permute-done.22.refs_1_ = bf16[32,1536]{1,0:T(8,128)(2,1)S(1)} collective-permute-done((bf16[32,1536]{1,0:T(8,128)(2,1)S(1)}, bf16[32,1536]{1,0:T(8,128)(2,1)S(1)}, u32[]{:S(2)}, u32[]{:S(2)}) %collective-permute-start.22) | collective-permute-done | bytes 98336 | tf_op jit(solution)/shard_map/ppermute | solution.py:164
  69.4 1.5 %collective-permute-done.25.refs_2_ = bf16[32,1536]{1,0:T(8,128)(2,1)S(1)} collective-permute-done((bf16[32,1536]{1,0:T(8,128)(2,1)S(1)}, bf16[32,1536]{1,0:T(8,128)(2,1)S(1)}, u32[]{:S(2)}, u32[]{:S(2)}) %collective-permute-start.25) | collective-permute-done | bytes 98336 | tf_op jit(solution)/shard_map/ppermute | solution.py:164
  71.3 1.2 %collective-permute-done.29.refs_2_ = f32[64,128]{1,0:T(8,128)S(1)} collective-permute-done((f32[64,128]{1,0:T(8,128)S(1)}, f32[64,128]{1,0:T(8,128)S(1)}, u32[]{:S(2)}, u32[]{:S(2)}) %collective-permute-start.29) | collective-permute-done | bytes 32800 | tf_op jit(solution)/shard_map/ppermute | solution.py:164
  72.7 1.0 collective-permute-start.30
  74.2 2.0 %collective-permute-start.34 = (bf16[64,1536]{1,0:T(8,128)(2,1)S(1)}, bf16[64,1536]{1,0:T(8,128)(2,1)S(1)}, u32[]{:S(2)}, u32[]{:S(2)}) collective-permute-start(bf16[64,1536]{1,0:T(8,128)(2,1)S(1)} %normed_rows.1.after_ref.refs_0_), channel_id=1, source_target_pairs={{0,8},{8,0},{16,24},{24,16},{1,9},{9,1},{17,25},{25,17},{2,10},{10... | collective-permute-start | bytes 589832 | tf_op jit(solution)/shard_map/ppermute | solution.py:164
  76.2 3.8 %staged.11.refs_3_.refs_2_ = bf16[3072,1536]{1,0:T(8,128)(2,1)S(1)} custom-call(bf16[3072,1536]{1,0:T(8,128)(2,1)} %weight_ref.5, bf16[64,1536]{1,0:T(8,128)(2,1)S(1)} %normed_rows.1.after_ref.refs_0_), custom_call_target="tpu_custom_call" | custom-call | bytes 9437184 | tf_op jit(solution)/shard_map/staged/pallas_call | solution.py:452
  80.0 1.4 %collective-permute-done.30.refs_1_ = bf16[64,1536]{1,0:T(8,128)(2,1)S(1)} collective-permute-done((bf16[64,1536]{1,0:T(8,128)(2,1)S(1)}, bf16[64,1536]{1,0:T(8,128)(2,1)S(1)}, u32[]{:S(2)}, u32[]{:S(2)}) %collective-permute-start.30) | collective-permute-done | bytes 196640 | tf_op jit(solution)/shard_map/ppermute | solution.py:164
  83.7 0.9 collective-permute-done.33.refs_0_
  84.6 0.9 down_projected.4.refs_3_
  85.5 0.9 down_projected.5
  88.7 1.2 %collective-permute-start.39 = (bf16[64,1536]{1,0:T(8,128)(2,1)S(1)}, bf16[64,1536]{1,0:T(8,128)(2,1)S(1)}, u32[]{:S(2)}, u32[]{:S(2)}) collective-permute-start(bf16[64,1536]{1,0:T(8,128)(2,1)S(1)} %get-tuple-element.84), channel_id=1, source_target_pairs={{0,24},{8,16},{16,8},{24,0},{1,25},{9,17},{17,9},{25,1},{2,26},{10... | collective-permute-start | bytes 589832 | tf_op jit(solution)/shard_map/ppermute | solution.py:164
  90.8 0.9 down_projected.7
  91.7 1.2 %collective-permute-start.37 = (bf16[64,1536]{1,0:T(8,128)(2,1)S(1)}, bf16[64,1536]{1,0:T(8,128)(2,1)S(1)}, u32[]{:S(2)}, u32[]{:S(2)}) collective-permute-start(bf16[64,1536]{1,0:T(8,128)(2,1)S(1)} %get-tuple-element.82), channel_id=1, source_target_pairs={{0,8},{8,0},{16,24},{24,16},{1,9},{9,1},{17,25},{25,17},{2,10},{10... | collective-permute-start | bytes 589832 | tf_op jit(solution)/shard_map/ppermute | solution.py:164
  92.9 1.2 %collective-permute-start.38 = (bf16[64,1536]{1,0:T(8,128)(2,1)S(1)}, bf16[64,1536]{1,0:T(8,128)(2,1)S(1)}, u32[]{:S(2)}, u32[]{:S(2)}) collective-permute-start(bf16[64,1536]{1,0:T(8,128)(2,1)S(1)} %get-tuple-element.83), channel_id=1, source_target_pairs={{0,16},{8,24},{16,0},{24,8},{1,17},{9,25},{17,1},{25,9},{2,18},{10... | collective-permute-start | bytes 589832 | tf_op jit(solution)/shard_map/ppermute | solution.py:164
  94.1 3.3 %collective-permute-done.39 = bf16[64,1536]{1,0:T(8,128)(2,1)S(1)} collective-permute-done((bf16[64,1536]{1,0:T(8,128)(2,1)S(1)}, bf16[64,1536]{1,0:T(8,128)(2,1)S(1)}, u32[]{:S(2)}, u32[]{:S(2)}) %collective-permute-start.39) | collective-permute-done | bytes 196640 | tf_op jit(solution)/shard_map/ppermute | solution.py:164
  97.3 2.7 %collective-permute-done.37 = bf16[64,1536]{1,0:T(8,128)(2,1)S(1)} collective-permute-done((bf16[64,1536]{1,0:T(8,128)(2,1)S(1)}, bf16[64,1536]{1,0:T(8,128)(2,1)S(1)}, u32[]{:S(2)}, u32[]{:S(2)}) %collective-permute-start.37) | collective-permute-done | bytes 196640 | tf_op jit(solution)/shard_map/ppermute | solution.py:164
  (93 shorter events, 23.3 us)
Async XLA Ops:
  0.0 2.0 %copy-start = (bf16[3072,576]{0,1:T(8,128)(2,1)S(1)}, bf16[3072,576]{0,1:T(8,128)(2,1)}, u32[]{:S(2)}) copy-start(bf16[3072,576]{0,1:T(8,128)(2,1)} %param.11) | copy-start | bytes 10616836
  0.0 3.0 %copy-start.2 = (bf16[64,1536]{1,0:T(8,128)(2,1)S(1)}, bf16[64,1536]{1,0:T(8,128)(2,1)}, u32[]{:S(2)}) copy-start(bf16[64,1536]{1,0:T(8,128)(2,1)} %refs_6_.1) | copy-start | bytes 589828
  3.1 13.9 %collective-permute-start.4 = (bf16[64,1536]{1,0:T(8,128)(2,1)S(1)}, bf16[64,1536]{1,0:T(8,128)(2,1)S(1)}, u32[]{:S(2)}, u32[]{:S(2)}) collective-permute-start(bf16[64,1536]{1,0:T(8,128)(2,1)S(1)} %copied.2), channel_id=1, source_target_pairs={{0,4},{2,6},{4,0},{6,2},{1,5},{3,7},{5,1},{7,3},{8,12},{10,14},{12... | collective-permute-start | bytes 589832 | tf_op jit(solution)/shard_map/ppermute | solution.py:164
  7.3 4.6 %collective-permute-start = (f32[64,128]{1,0:T(8,128)S(1)}, f32[64,128]{1,0:T(8,128)S(1)}, u32[]{:S(2)}, u32[]{:S(2)}) collective-permute-start(f32[64,128]{1,0:T(8,128)S(1)} %get-tuple-element.46.refs_1_), channel_id=1, source_target_pairs={{0,1},{1,0},{2,3},{3,2},{4,5},{5,4},{6,7},{7,6},{8,9},{9,8},{10,11... | collective-permute-start | bytes 98312 | tf_op jit(solution)/shard_map/ppermute | solution.py:164
  7.4 1.3 %collective-permute-start.1 = (f32[1,576]{1,0:T(1,128)S(1)}, f32[1,576]{1,0:T(1,128)S(1)}, u32[]{:S(2)}, u32[]{:S(2)}) collective-permute-start(f32[1,576]{1,0:T(1,128)S(1)} %fusion.4.refs_0_.after_ref), channel_id=1, source_target_pairs={{0,1},{1,0},{2,3},{3,2},{4,5},{5,4},{6,7},{7,6},{8,9},{9,8},{10,11... | collective-permute-start | bytes 6920 | tf_op jit(solution)/shard_map/ppermute | solution.py:164
  8.7 3.6 %collective-permute-start.2 = (f32[2,576]{1,0:T(2,128)S(1)}, f32[2,576]{1,0:T(2,128)S(1)}, u32[]{:S(2)}, u32[]{:S(2)}) collective-permute-start(f32[2,576]{1,0:T(2,128)S(1)} %merged.3.after_ref.refs_0_), channel_id=1, source_target_pairs={{0,2},{2,0},{4,6},{6,4},{1,3},{3,1},{5,7},{7,5},{8,10},{10,8},{12,... | collective-permute-start | bytes 13832 | tf_op jit(solution)/shard_map/ppermute | solution.py:164
  12.3 4.6 %collective-permute-start.3 = (f32[4,576]{1,0:T(4,128)S(1)}, f32[4,576]{1,0:T(4,128)S(1)}, u32[]{:S(2)}, u32[]{:S(2)}) collective-permute-start(f32[4,576]{1,0:T(4,128)S(1)} %merged.4.after_ref.refs_0_), channel_id=1, source_target_pairs={{0,4},{2,6},{4,0},{6,2},{1,5},{3,7},{5,1},{7,3},{8,12},{10,14},{12... | collective-permute-start | bytes 27656 | tf_op jit(solution)/shard_map/ppermute | solution.py:164
  17.0 9.5 %collective-permute-start.5 = (bf16[64,1664]{1,0:T(8,128)(2,1)S(1)}, bf16[64,1664]{1,0:T(8,128)(2,1)S(1)}, u32[]{:S(2)}, u32[]{:S(2)}) collective-permute-start(bf16[64,1664]{1,0:T(8,128)(2,1)S(1)} %packed.1.refs_0_.after_ref), channel_id=1, source_target_pairs={{0,8},{8,0},{16,24},{24,16},{1,9},{9,1},{17,25},{25,17},{2,10},{10... | collective-permute-start | bytes 638984 | tf_op jit(solution)/shard_map/ppermute | solution.py:164
  18.6 10.6 %collective-permute-start.6 = (bf16[64,1664]{1,0:T(8,128)(2,1)S(1)}, bf16[64,1664]{1,0:T(8,128)(2,1)S(1)}, u32[]{:S(2)}, u32[]{:S(2)}) collective-permute-start(bf16[64,1664]{1,0:T(8,128)(2,1)S(1)} %packed.1.refs_0_.after_ref), channel_id=1, source_target_pairs={{0,16},{8,24},{16,0},{24,8},{1,17},{9,25},{17,1},{25,9},{2,18},{10... | collective-permute-start | bytes 638984 | tf_op jit(solution)/shard_map/ppermute | solution.py:164
  20.1 9.1 %collective-permute-start.7 = (bf16[64,1664]{1,0:T(8,128)(2,1)S(1)}, bf16[64,1664]{1,0:T(8,128)(2,1)S(1)}, u32[]{:S(2)}, u32[]{:S(2)}) collective-permute-start(bf16[64,1664]{1,0:T(8,128)(2,1)S(1)} %packed.1.refs_0_.after_ref), channel_id=1, source_target_pairs={{0,24},{8,16},{16,8},{24,0},{1,25},{9,17},{17,9},{25,1},{2,26},{10... | collective-permute-start | bytes 638984 | tf_op jit(solution)/shard_map/ppermute | solution.py:164
  20.6 5.7 %collective-permute-start.8 = (bf16[64,1536]{1,0:T(8,128)(2,1)S(1)}, bf16[64,1536]{1,0:T(8,128)(2,1)S(1)}, u32[]{:S(2)}, u32[]{:S(2)}) collective-permute-start(bf16[64,1536]{1,0:T(8,128)(2,1)S(1)} %collective-permute-done.4.refs_4_.refs_0_), channel_id=1, source_target_pairs={{0,2},{2,0},{4,6},{6,4},{1,3},{3,1},{5,7},{7,5},{8,10},{10,8},{12,... | collective-permute-start | bytes 589832 | tf_op jit(solution)/shard_map/ppermute | solution.py:164
  26.4 3.0 %collective-permute-start.9 = (f32[128,128]{1,0:T(8,128)S(1)}, f32[128,128]{1,0:T(8,128)S(1)}, u32[]{:S(2)}, u32[]{:S(2)}) collective-permute-start(f32[128,128]{1,0:T(8,128)S(1)} %get-tuple-element.48.refs_1_), channel_id=1, source_target_pairs={{0,1},{1,0},{2,3},{3,2},{4,5},{5,4},{6,7},{7,6},{8,9},{9,8},{10,11... | collective-permute-start | bytes 196616 | tf_op jit(solution)/shard_map/ppermute | solution.py:164
  31.1 3.5 %collective-permute-start.10 = (bf16[256,384]{1,0:T(8,128)(2,1)S(1)}, bf16[256,384]{1,0:T(8,128)(2,1)S(1)}, u32[]{:S(2)}, u32[]{:S(2)}) collective-permute-start(bf16[256,384]{1,0:T(8,128)(2,1)S(1)} %get-tuple-element.53), channel_id=1, source_target_pairs={{0,1},{1,0},{2,3},{3,2},{4,5},{5,4},{6,7},{7,6},{8,9},{9,8},{10,11... | collective-permute-start | bytes 589832 | tf_op jit(solution)/shard_map/ppermute | solution.py:164
  31.2 3.5 %collective-permute-start.11 = (bf16[256,384]{1,0:T(8,128)(2,1)S(1)}, bf16[256,384]{1,0:T(8,128)(2,1)S(1)}, u32[]{:S(2)}, u32[]{:S(2)}) collective-permute-start(bf16[256,384]{1,0:T(8,128)(2,1)S(1)} %get-tuple-element.54), channel_id=1, source_target_pairs={{0,1},{1,0},{2,3},{3,2},{4,5},{5,4},{6,7},{7,6},{8,9},{9,8},{10,11... | collective-permute-start | bytes 589832 | tf_op jit(solution)/shard_map/ppermute | solution.py:164
  31.7 3.0 %collective-permute-start.12 = (bf16[256,384]{1,0:T(8,128)(2,1)S(1)}, bf16[256,384]{1,0:T(8,128)(2,1)S(1)}, u32[]{:S(2)}, u32[]{:S(2)}) collective-permute-start(bf16[256,384]{1,0:T(8,128)(2,1)S(1)} %get-tuple-element.55), channel_id=1, source_target_pairs={{0,1},{1,0},{2,3},{3,2},{4,5},{5,4},{6,7},{7,6},{8,9},{9,8},{10,11... | collective-permute-start | bytes 589832 | tf_op jit(solution)/shard_map/ppermute | solution.py:164
  31.7 12.9 %collective-permute-start.14 = (bf16[128,1536]{1,0:T(8,128)(2,1)S(1)}, bf16[128,1536]{1,0:T(8,128)(2,1)S(1)}, u32[]{:S(2)}, u32[]{:S(2)}) collective-permute-start(bf16[128,1536]{1,0:T(8,128)(2,1)S(1)} %standardized.3.refs_9_.refs_0_), channel_id=1, source_target_pairs={{0,24},{8,16},{16,8},{24,0},{1,25},{9,17},{17,9},{25,1},{2,26},{10... | collective-permute-start | bytes 1179656 | tf_op jit(solution)/shard_map/ppermute | solution.py:164
  33.2 1.4 %copy-start.3 = (f32[128]{0:T(128)S(1)}, f32[128]{0:T(128)}, u32[]{:S(2)}) copy-start(f32[128]{0:T(128)} %param.13) | copy-start | bytes 1540
  33.2 1.4 %copy-start.4 = (f32[128]{0:T(128)S(1)}, f32[128]{0:T(128)}, u32[]{:S(2)}) copy-start(f32[128]{0:T(128)} %param.14) | copy-start | bytes 1540
  35.0 12.2 %collective-permute-start.13 = (bf16[256,768]{1,0:T(8,128)(2,1)S(1)}, bf16[256,768]{1,0:T(8,128)(2,1)S(1)}, u32[]{:S(2)}, u32[]{:S(2)}) collective-permute-start(bf16[256,768]{1,0:T(8,128)(2,1)S(1)} %get-tuple-element.57.refs_6_.after_ref.refs_1_), channel_id=1, source_target_pairs={{0,2},{2,0},{4,6},{6,4},{1,3},{3,1},{5,7},{7,5},{8,10},{10,8},{12,... | collective-permute-start | bytes 1179656 | tf_op jit(solution)/shard_map/ppermute | solution.py:164
  36.4 16.1 %collective-permute-start.17 = (bf16[128,1536]{1,0:T(8,128)(2,1)S(1)}, bf16[128,1536]{1,0:T(8,128)(2,1)S(1)}, u32[]{:S(2)}, u32[]{:S(2)}) collective-permute-start(bf16[128,1536]{1,0:T(8,128)(2,1)S(1)} %standardized.3.refs_9_.refs_0_), channel_id=1, source_target_pairs={{0,16},{8,24},{16,0},{24,8},{1,17},{9,25},{17,1},{25,9},{2,18},{10... | collective-permute-start | bytes 1179656 | tf_op jit(solution)/shard_map/ppermute | solution.py:164
  37.6 15.0 %collective-permute-start.18 = (bf16[128,1536]{1,0:T(8,128)(2,1)S(1)}, bf16[128,1536]{1,0:T(8,128)(2,1)S(1)}, u32[]{:S(2)}, u32[]{:S(2)}) collective-permute-start(bf16[128,1536]{1,0:T(8,128)(2,1)S(1)} %standardized.3.refs_9_.refs_0_), channel_id=1, source_target_pairs={{0,8},{8,0},{16,24},{24,16},{1,9},{9,1},{17,25},{25,17},{2,10},{10... | collective-permute-start | bytes 1179656 | tf_op jit(solution)/shard_map/ppermute | solution.py:164
  46.6 1.5 %collective-permute-start.15 = (bf16[256,384]{1,0:T(8,128)(2,1)S(1)}, bf16[256,384]{1,0:T(8,128)(2,1)S(1)}, u32[]{:S(2)}, u32[]{:S(2)}) collective-permute-start(bf16[256,384]{1,0:T(8,128)(2,1)S(1)} %get-tuple-element.61), channel_id=1, source_target_pairs={{0,1},{1,0},{2,3},{3,2},{4,5},{5,4},{6,7},{7,6},{8,9},{9,8},{10,11... | collective-permute-start | bytes 589832 | tf_op jit(solution)/shard_map/ppermute | solution.py:164
  46.7 1.7 %collective-permute-start.16 = (bf16[256,384]{1,0:T(8,128)(2,1)S(1)}, bf16[256,384]{1,0:T(8,128)(2,1)S(1)}, u32[]{:S(2)}, u32[]{:S(2)}) collective-permute-start(bf16[256,384]{1,0:T(8,128)(2,1)S(1)} %get-tuple-element.62), channel_id=1, source_target_pairs={{0,1},{1,0},{2,3},{3,2},{4,5},{5,4},{6,7},{7,6},{8,9},{9,8},{10,11... | collective-permute-start | bytes 589832 | tf_op jit(solution)/shard_map/ppermute | solution.py:164
  53.7 1.6 %collective-permute-start.19 = (bf16[256,384]{1,0:T(8,128)(2,1)S(1)}, bf16[256,384]{1,0:T(8,128)(2,1)S(1)}, u32[]{:S(2)}, u32[]{:S(2)}) collective-permute-start(bf16[256,384]{1,0:T(8,128)(2,1)S(1)} %get-tuple-element.69), channel_id=1, source_target_pairs={{0,1},{1,0},{2,3},{3,2},{4,5},{5,4},{6,7},{7,6},{8,9},{9,8},{10,11... | collective-permute-start | bytes 589832 | tf_op jit(solution)/shard_map/ppermute | solution.py:164
  53.7 1.7 %collective-permute-start.20 = (bf16[256,384]{1,0:T(8,128)(2,1)S(1)}, bf16[256,384]{1,0:T(8,128)(2,1)S(1)}, u32[]{:S(2)}, u32[]{:S(2)}) collective-permute-start(bf16[256,384]{1,0:T(8,128)(2,1)S(1)} %get-tuple-element.70), channel_id=1, source_target_pairs={{0,1},{1,0},{2,3},{3,2},{4,5},{5,4},{6,7},{7,6},{8,9},{9,8},{10,11... | collective-permute-start | bytes 589832 | tf_op jit(solution)/shard_map/ppermute | solution.py:164
  56.9 4.1 %collective-permute-start.21 = (bf16[192,384]{1,0:T(8,128)(2,1)S(1)}, bf16[192,384]{1,0:T(8,128)(2,1)S(1)}, u32[]{:S(2)}, u32[]{:S(2)}) collective-permute-start(bf16[192,384]{1,0:T(8,128)(2,1)S(1)} %finished.3.refs_0_.refs_3_), channel_id=1, source_target_pairs={{0,1},{1,0},{2,3},{3,2},{4,5},{5,4},{6,7},{7,6},{8,9},{9,8},{10,11... | collective-permute-start | bytes 442376 | tf_op jit(solution)/shard_map/ppermute | solution.py:164
  57.2 1.2 %collective-permute-start.23 = (bf16[64,384]{1,0:T(8,128)(2,1)S(1)}, bf16[64,384]{1,0:T(8,128)(2,1)S(1)}, u32[]{:S(2)}, u32[]{:S(2)}) collective-permute-start(bf16[64,384]{1,0:T(8,128)(2,1)S(1)} %finished.2.refs_5_.refs_0_), channel_id=1, source_target_pairs={{0,1},{1,0},{2,3},{3,2},{4,5},{5,4},{6,7},{7,6},{8,9},{9,8},{10,11... | collective-permute-start | bytes 147464 | tf_op jit(solution)/shard_map/ppermute | solution.py:164
  58.9 5.0 %collective-permute-start.26 = (bf16[32,1536]{1,0:T(8,128)(2,1)S(1)}, bf16[32,1536]{1,0:T(8,128)(2,1)S(1)}, u32[]{:S(2)}, u32[]{:S(2)}) collective-permute-start(bf16[32,1536]{1,0:T(8,128)(2,1)S(1)} %get-tuple-element.77), channel_id=1, source_target_pairs={{0,16},{8,24},{16,0},{24,8},{1,17},{9,25},{17,1},{25,9},{2,18},{10... | collective-permute-start | bytes 294920 | tf_op jit(solution)/shard_map/ppermute | solution.py:164
  60.4 5.7 %collective-permute-start.24 = (bf16[32,1536]{1,0:T(8,128)(2,1)S(1)}, bf16[32,1536]{1,0:T(8,128)(2,1)S(1)}, u32[]{:S(2)}, u32[]{:S(2)}) collective-permute-start(bf16[32,1536]{1,0:T(8,128)(2,1)S(1)} %get-tuple-element.74), channel_id=1, source_target_pairs={{0,8},{8,0},{16,24},{24,16},{1,9},{9,1},{17,25},{25,17},{2,10},{10... | collective-permute-start | bytes 294920 | tf_op jit(solution)/shard_map/ppermute | solution.py:164
  61.7 6.5 %collective-permute-start.22 = (bf16[32,1536]{1,0:T(8,128)(2,1)S(1)}, bf16[32,1536]{1,0:T(8,128)(2,1)S(1)}, u32[]{:S(2)}, u32[]{:S(2)}) collective-permute-start(bf16[32,1536]{1,0:T(8,128)(2,1)S(1)} %get-tuple-element.72), channel_id=1, source_target_pairs={{0,8},{8,0},{16,24},{24,16},{1,9},{9,1},{17,25},{25,17},{2,10},{10... | collective-permute-start | bytes 294920 | tf_op jit(solution)/shard_map/ppermute | solution.py:164
  63.3 5.4 %collective-permute-start.28 = (bf16[32,1536]{1,0:T(8,128)(2,1)S(1)}, bf16[32,1536]{1,0:T(8,128)(2,1)S(1)}, u32[]{:S(2)}, u32[]{:S(2)}) collective-permute-start(bf16[32,1536]{1,0:T(8,128)(2,1)S(1)} %get-tuple-element.78), channel_id=1, source_target_pairs={{0,16},{8,24},{16,0},{24,8},{1,17},{9,25},{17,1},{25,9},{2,18},{10... | collective-permute-start | bytes 294920 | tf_op jit(solution)/shard_map/ppermute | solution.py:164
  64.0 5.3 %collective-permute-start.27 = (bf16[32,1536]{1,0:T(8,128)(2,1)S(1)}, bf16[32,1536]{1,0:T(8,128)(2,1)S(1)}, u32[]{:S(2)}, u32[]{:S(2)}) collective-permute-start(bf16[32,1536]{1,0:T(8,128)(2,1)S(1)} %rounded_sum.3), channel_id=1, source_target_pairs={{0,8},{8,0},{16,24},{24,16},{1,9},{9,1},{17,25},{25,17},{2,10},{10... | collective-permute-start | bytes 294920 | tf_op jit(solution)/shard_map/ppermute | solution.py:164
  66.1 4.7 %collective-permute-start.25 = (bf16[32,1536]{1,0:T(8,128)(2,1)S(1)}, bf16[32,1536]{1,0:T(8,128)(2,1)S(1)}, u32[]{:S(2)}, u32[]{:S(2)}) collective-permute-start(bf16[32,1536]{1,0:T(8,128)(2,1)S(1)} %rounded_sum.2), channel_id=1, source_target_pairs={{0,16},{8,24},{16,0},{24,8},{1,17},{9,25},{17,1},{25,9},{2,18},{10... | collective-permute-start | bytes 294920 | tf_op jit(solution)/shard_map/ppermute | solution.py:164
  71.2 1.3 %collective-permute-start.29 = (f32[64,128]{1,0:T(8,128)S(1)}, f32[64,128]{1,0:T(8,128)S(1)}, u32[]{:S(2)}, u32[]{:S(2)}) collective-permute-start(f32[64,128]{1,0:T(8,128)S(1)} %get-tuple-element.80.refs_1_), channel_id=1, source_target_pairs={{0,1},{1,0},{2,3},{3,2},{4,5},{5,4},{6,7},{7,6},{8,9},{9,8},{10,11... | collective-permute-start | bytes 98312 | tf_op jit(solution)/shard_map/ppermute | solution.py:164
  72.7 8.8 %collective-permute-start.30 = (bf16[64,1536]{1,0:T(8,128)(2,1)S(1)}, bf16[64,1536]{1,0:T(8,128)(2,1)S(1)}, u32[]{:S(2)}, u32[]{:S(2)}) collective-permute-start(bf16[64,1536]{1,0:T(8,128)(2,1)S(1)} %normed_rows.1.after_ref.refs_0_), channel_id=1, source_target_pairs={{0,24},{8,16},{16,8},{24,0},{1,25},{9,17},{17,9},{25,1},{2,26},{10... | collective-permute-start | bytes 589832 | tf_op jit(solution)/shard_map/ppermute | solution.py:164
  73.7 10.9 %collective-permute-start.33 = (bf16[64,1536]{1,0:T(8,128)(2,1)S(1)}, bf16[64,1536]{1,0:T(8,128)(2,1)S(1)}, u32[]{:S(2)}, u32[]{:S(2)}) collective-permute-start(bf16[64,1536]{1,0:T(8,128)(2,1)S(1)} %normed_rows.1.after_ref.refs_0_), channel_id=1, source_target_pairs={{0,16},{8,24},{16,0},{24,8},{1,17},{9,25},{17,1},{25,9},{2,18},{10... | collective-permute-start | bytes 589832 | tf_op jit(solution)/shard_map/ppermute | solution.py:164
  74.2 10.4 %collective-permute-start.34 = (bf16[64,1536]{1,0:T(8,128)(2,1)S(1)}, bf16[64,1536]{1,0:T(8,128)(2,1)S(1)}, u32[]{:S(2)}, u32[]{:S(2)}) collective-permute-start(bf16[64,1536]{1,0:T(8,128)(2,1)S(1)} %normed_rows.1.after_ref.refs_0_), channel_id=1, source_target_pairs={{0,8},{8,0},{16,24},{24,16},{1,9},{9,1},{17,25},{25,17},{2,10},{10... | collective-permute-start | bytes 589832 | tf_op jit(solution)/shard_map/ppermute | solution.py:164
  82.2 2.4 %collective-permute-start.32 = (bf16[128,1536]{1,0:T(8,128)(2,1)S(1)}, bf16[128,1536]{1,0:T(8,128)(2,1)S(1)}, u32[]{:S(2)}, u32[]{:S(2)}) collective-permute-start(bf16[128,1536]{1,0:T(8,128)(2,1)S(1)} %up_projected.5.refs_0_), channel_id=1, source_target_pairs={{0,1},{1,0},{2,3},{3,2},{4,5},{5,4},{6,7},{7,6},{8,9},{9,8},{10,11... | collective-permute-start | bytes 1179656 | tf_op jit(solution)/shard_map/ppermute | solution.py:164
  83.1 2.4 %collective-permute-start.31 = (bf16[128,1536]{1,0:T(8,128)(2,1)S(1)}, bf16[128,1536]{1,0:T(8,128)(2,1)S(1)}, u32[]{:S(2)}, u32[]{:S(2)}) collective-permute-start(bf16[128,1536]{1,0:T(8,128)(2,1)S(1)} %up_projected.4.refs_0_), channel_id=1, source_target_pairs={{0,1},{1,0},{2,3},{3,2},{4,5},{5,4},{6,7},{7,6},{8,9},{9,8},{10,11... | collective-permute-start | bytes 1179656 | tf_op jit(solution)/shard_map/ppermute | solution.py:164
  87.2 2.6 %collective-permute-start.36 = (bf16[128,1536]{1,0:T(8,128)(2,1)S(1)}, bf16[128,1536]{1,0:T(8,128)(2,1)S(1)}, u32[]{:S(2)}, u32[]{:S(2)}) collective-permute-start(bf16[128,1536]{1,0:T(8,128)(2,1)S(1)} %up_projected.7.refs_0_), channel_id=1, source_target_pairs={{0,1},{1,0},{2,3},{3,2},{4,5},{5,4},{6,7},{7,6},{8,9},{9,8},{10,11... | collective-permute-start | bytes 1179656 | tf_op jit(solution)/shard_map/ppermute | solution.py:164
  88.1 2.6 %collective-permute-start.35 = (bf16[128,1536]{1,0:T(8,128)(2,1)S(1)}, bf16[128,1536]{1,0:T(8,128)(2,1)S(1)}, u32[]{:S(2)}, u32[]{:S(2)}) collective-permute-start(bf16[128,1536]{1,0:T(8,128)(2,1)S(1)} %up_projected.6.refs_0_), channel_id=1, source_target_pairs={{0,1},{1,0},{2,3},{3,2},{4,5},{5,4},{6,7},{7,6},{8,9},{9,8},{10,11... | collective-permute-start | bytes 1179656 | tf_op jit(solution)/shard_map/ppermute | solution.py:164
  88.7 8.7 %collective-permute-start.39 = (bf16[64,1536]{1,0:T(8,128)(2,1)S(1)}, bf16[64,1536]{1,0:T(8,128)(2,1)S(1)}, u32[]{:S(2)}, u32[]{:S(2)}) collective-permute-start(bf16[64,1536]{1,0:T(8,128)(2,1)S(1)} %get-tuple-element.84), channel_id=1, source_target_pairs={{0,24},{8,16},{16,8},{24,0},{1,25},{9,17},{17,9},{25,1},{2,26},{10... | collective-permute-start | bytes 589832 | tf_op jit(solution)/shard_map/ppermute | solution.py:164
  90.8 10.8 %copy-start.1 = (bf16[3072,576]{0,1:T(8,128)(2,1)S(1)}, bf16[3072,576]{0,1:T(8,128)(2,1)}, u32[]{:S(2)}) copy-start(bf16[3072,576]{0,1:T(8,128)(2,1)} %param.11) | copy-start | bytes 10616836
  91.7 8.4 %collective-permute-start.37 = (bf16[64,1536]{1,0:T(8,128)(2,1)S(1)}, bf16[64,1536]{1,0:T(8,128)(2,1)S(1)}, u32[]{:S(2)}, u32[]{:S(2)}) collective-permute-start(bf16[64,1536]{1,0:T(8,128)(2,1)S(1)} %get-tuple-element.82), channel_id=1, source_target_pairs={{0,8},{8,0},{16,24},{24,16},{1,9},{9,1},{17,25},{25,17},{2,10},{10... | collective-permute-start | bytes 589832 | tf_op jit(solution)/shard_map/ppermute | solution.py:164
  92.9 7.8 %collective-permute-start.38 = (bf16[64,1536]{1,0:T(8,128)(2,1)S(1)}, bf16[64,1536]{1,0:T(8,128)(2,1)S(1)}, u32[]{:S(2)}, u32[]{:S(2)}) collective-permute-start(bf16[64,1536]{1,0:T(8,128)(2,1)S(1)} %get-tuple-element.83), channel_id=1, source_target_pairs={{0,16},{8,24},{16,0},{24,8},{1,17},{9,25},{17,1},{25,9},{2,18},{10... | collective-permute-start | bytes 589832 | tf_op jit(solution)/shard_map/ppermute | solution.py:164

commit v8 on v7

--- a/solution.py
+++ b/solution.py
@@ -290,14 +290,23 @@
     )(*blocks)
 
 
+def moments(values, shape):
+    average = jnp.mean(values, axis=-1, keepdims=True)
+    away = values - average
+    lane = lax.broadcasted_iota(jnp.int32, shape, 1)
+    return jnp.where(lane < shape[1] // 2, average, jnp.sum(away * away, axis=-1, keepdims=True))
+
+
+def combined(own, arrived, features):
+    middle = own.shape[1] // 2
+    first, second = own[:, :1], arrived[:, :1]
+    squares = own[:, middle:][:, :1] + arrived[:, middle:][:, :1]
+    apart = first - second
+    return (first + second) * 0.5, squares / features + apart * apart * 0.25
+
+
 def row_sums_kernel(values_ref, out_ref, copy_ref):
-    values = values_ref[...].astype(jnp.float32)
-    lane = lax.broadcasted_iota(jnp.int32, out_ref.shape, 1)
-    out_ref[...] = jnp.where(
-        lane < out_ref.shape[1] // 2,
-        jnp.sum(values, axis=-1, keepdims=True),
-        jnp.sum(values * values, axis=-1, keepdims=True),
-    )
+    out_ref[...] = moments(values_ref[...].astype(jnp.float32), out_ref.shape)
     copy_ref[...] = values_ref[...]
 
 
@@ -315,9 +324,7 @@
 
 
 def standardize_kernel(features, values_ref, own_ref, arrived_ref, *refs):
-    total = own_ref[...] + arrived_ref[...]
-    average = total[:, :1] / features
-    variance = total[:, total.shape[1] // 2 :][:, :1] / features - average * average
+    average, variance = combined(own_ref[...], arrived_ref[...], features)
     values = values_ref[...].astype(jnp.float32)
     refs[-1][...] = ((values - average) * lax.rsqrt(variance + 1e-06)).astype(jnp.bfloat16)
 
@@ -773,7 +780,6 @@
     token_ref, gate_ref = refs[sum(counts)], refs[sum(counts) + 1]
     mixed_ref, sums_ref = refs[-2:]
     rows = refs[0].shape[0]
-    lane = lax.broadcasted_iota(jnp.int32, (rows, sums_ref.shape[1]), 1)
     at = 0
     for group, count in enumerate(counts):
         here = slice(group * rows, (group + 1) * rows)
@@ -783,11 +789,7 @@
         at += count
         mixed = token_ref[here, :].astype(jnp.float32) + gate_ref[...] * total
         mixed_ref[here, :] = mixed
-        sums_ref[here, :] = jnp.where(
-            lane < sums_ref.shape[1] // 2,
-            jnp.sum(mixed, axis=-1, keepdims=True),
-            jnp.sum(mixed * mixed, axis=-1, keepdims=True),
-        )
+        sums_ref[here, :] = moments(mixed, (rows, sums_ref.shape[1]))
 
 
 def mixed_rows(groups, tokens, gate_row, after):
@@ -812,9 +814,7 @@
 
 
 def norm_kernel(features, mixed_ref, own_ref, arrived_ref, shift_ref, scale_ref, out_ref):
-    total = own_ref[...] + arrived_ref[...]
-    average = total[:, :1] / features
-    variance = total[:, total.shape[1] // 2 :][:, :1] / features - average * average
+    average, variance = combined(own_ref[...], arrived_ref[...], features)
     values = (mixed_ref[...] - average) * lax.rsqrt(variance + 1e-06)
     out_ref[...] = (values * (1.0 + scale_ref[...]) + shift_ref[...]).astype(jnp.bfloat16)
 

time: 102 us -> 102 us (level)
  no operation moved by 1% of the time
where the time goes in v8:
time: 102 us
  Pallas kernels  34.2 us (34%)
  starting transfers between devices  34 us (33%)
  waiting for transfers between devices  29.3 us (29%)
  other arithmetic  1.72 us (2%)
  local copies, waits for them, and re-layouts  1.21 us (1%)
    ppermute x40, starting transfers between devices, permuted(): return lax.ppermute(values, axis, [(i, i ^ distance) for i in range(size)])  34 us
    ppermute x40, waiting for transfers between devices, permuted(): return lax.ppermute(values, axis, [(i, i ^ distance) for i in range(size)])  29.3 us
    pallas_call x6, Pallas kernels, staged(): pl.pallas_call(kernel, grid=(1,), in_specs=[anywhere] + after_specs([afte...  14.1 us
    pallas_call x6, Pallas kernels, projected(): pl.pallas_call((lambda *refs: project_kernel(len(blocks), count, other, *...  6.8 us
    pallas_call x4, Pallas kernels, down_projected(): pl.pallas_call(lambda *refs: down_kernel(first, count, len(before), *refs...  3.56 us
    pallas_call x4, Pallas kernels, up_projected(): pl.pallas_call(lambda *refs: up_kernel(part * columns, len(blocks), *refs...  3.12 us
  transfers between devices with their start and end apart: 40, of which 24 were waited for; matrix products, arithmetic and copies ran while one was open for 0% of the time, Pallas kernels for 27%

profile of v8, /device:TPU:0, one launch (start us, length us, event | category | flops | bytes accessed | tf_op | source)
XLA Modules:
  0.0 101.9 jit_solution(9956244993471021871)
XLA Ops:
  0.9 1.1 %copy-done = bf16[3072,576]{0,1:T(8,128)(2,1)S(1)} copy-done((bf16[3072,576]{0,1:T(8,128)(2,1)S(1)}, bf16[3072,576]{0,1:T(8,128)(2,1)}, u32[]{:S(2)}) %copy-start) | copy-done | bytes 3538968
  2.0 1.0 fusion.4.refs_0_.after_ref
  3.1 4.1 %collective-permute-start.4 = (bf16[64,1536]{1,0:T(8,128)(2,1)S(1)}, bf16[64,1536]{1,0:T(8,128)(2,1)S(1)}, u32[]{:S(2)}, u32[]{:S(2)}) collective-permute-start(bf16[64,1536]{1,0:T(8,128)(2,1)S(1)} %copied.2), channel_id=1, source_target_pairs={{0,4},{2,6},{4,0},{6,2},{1,5},{3,7},{5,1},{7,3},{8,12},{10,14},{12... | collective-permute-start | bytes 589832 | tf_op jit(solution)/shard_map/ppermute | solution.py:164
  8.8 1.6 %collective-permute-start.2 = (f32[2,576]{1,0:T(2,128)S(1)}, f32[2,576]{1,0:T(2,128)S(1)}, u32[]{:S(2)}, u32[]{:S(2)}) collective-permute-start(f32[2,576]{1,0:T(2,128)S(1)} %merged.3.after_ref.refs_0_), channel_id=1, source_target_pairs={{0,2},{2,0},{4,6},{6,4},{1,3},{3,1},{5,7},{7,5},{8,10},{10,8},{12,... | collective-permute-start | bytes 13832 | tf_op jit(solution)/shard_map/ppermute | solution.py:164
  10.3 1.6 %staged.6.refs_2_.refs_7_.refs_4_.refs_1_ = bf16[1536,768]{1,0:T(8,128)(2,1)S(1)} custom-call(bf16[3,1536,768]{2,1,0:T(8,128)(2,1)} %bitcast.11, f32[2,576]{1,0:T(2,128)S(1)} %merged.3.after_ref.refs_0_), custom_call_target="tpu_custom_call" | custom-call | bytes 2359296 | tf_op jit(solution)/shard_map/staged/pallas_call | solution.py:459
  12.4 1.5 %collective-permute-start.3 = (f32[4,576]{1,0:T(4,128)S(1)}, f32[4,576]{1,0:T(4,128)S(1)}, u32[]{:S(2)}, u32[]{:S(2)}) collective-permute-start(f32[4,576]{1,0:T(4,128)S(1)} %merged.4.after_ref.refs_0_), channel_id=1, source_target_pairs={{0,4},{2,6},{4,0},{6,2},{1,5},{3,7},{5,1},{7,3},{8,12},{10,14},{12... | collective-permute-start | bytes 27656 | tf_op jit(solution)/shard_map/ppermute | solution.py:164
  13.9 1.6 %staged.7.refs_3_.refs_8_.refs_5_.refs_2_ = bf16[1536,768]{1,0:T(8,128)(2,1)S(1)} custom-call(bf16[3,1536,768]{2,1,0:T(8,128)(2,1)} %bitcast.12, f32[4,576]{1,0:T(4,128)S(1)} %merged.4.after_ref.refs_0_), custom_call_target="tpu_custom_call" | custom-call | bytes 2359296 | tf_op jit(solution)/shard_map/staged/pallas_call | solution.py:459
  15.6 1.5 %collective-permute-done.3.refs_1_ = f32[4,576]{1,0:T(4,128)S(1)} collective-permute-done((f32[4,576]{1,0:T(4,128)S(1)}, f32[4,576]{1,0:T(4,128)S(1)}, u32[]{:S(2)}, u32[]{:S(2)}) %collective-permute-start.3) | collective-permute-done | bytes 9248 | tf_op jit(solution)/shard_map/ppermute | solution.py:164
  17.1 1.6 %collective-permute-start.5 = (bf16[64,1664]{1,0:T(8,128)(2,1)S(1)}, bf16[64,1664]{1,0:T(8,128)(2,1)S(1)}, u32[]{:S(2)}, u32[]{:S(2)}) collective-permute-start(bf16[64,1664]{1,0:T(8,128)(2,1)S(1)} %packed.1.refs_0_.after_ref), channel_id=1, source_target_pairs={{0,8},{8,0},{16,24},{24,16},{1,9},{9,1},{17,25},{25,17},{2,10},{10... | collective-permute-start | bytes 638984 | tf_op jit(solution)/shard_map/ppermute | solution.py:164
  18.6 1.5 %collective-permute-start.6 = (bf16[64,1664]{1,0:T(8,128)(2,1)S(1)}, bf16[64,1664]{1,0:T(8,128)(2,1)S(1)}, u32[]{:S(2)}, u32[]{:S(2)}) collective-permute-start(bf16[64,1664]{1,0:T(8,128)(2,1)S(1)} %packed.1.refs_0_.after_ref), channel_id=1, source_target_pairs={{0,16},{8,24},{16,0},{24,8},{1,17},{9,25},{17,1},{25,9},{2,18},{10... | collective-permute-start | bytes 638984 | tf_op jit(solution)/shard_map/ppermute | solution.py:164
  20.6 1.6 %collective-permute-start.8 = (bf16[64,1536]{1,0:T(8,128)(2,1)S(1)}, bf16[64,1536]{1,0:T(8,128)(2,1)S(1)}, u32[]{:S(2)}, u32[]{:S(2)}) collective-permute-start(bf16[64,1536]{1,0:T(8,128)(2,1)S(1)} %collective-permute-done.4.refs_4_.refs_0_), channel_id=1, source_target_pairs={{0,2},{2,0},{4,6},{6,4},{1,3},{3,1},{5,7},{7,5},{8,10},{10,8},{12,... | collective-permute-start | bytes 589832 | tf_op jit(solution)/shard_map/ppermute | solution.py:164
  22.2 1.6 %staged.8.refs_6_.refs_1_ = bf16[1536,768]{1,0:T(8,128)(2,1)S(1)} custom-call(bf16[3,1536,768]{2,1,0:T(8,128)(2,1)} %bitcast.13, bf16[64,1664]{1,0:T(8,128)(2,1)S(1)} %packed.1.refs_0_.after_ref), custom_call_target="tpu_custom_call" | custom-call | bytes 2359296 | tf_op jit(solution)/shard_map/staged/pallas_call | solution.py:459
  23.9 2.5 %collective-permute-done.8.refs_1_ = bf16[64,1536]{1,0:T(8,128)(2,1)S(1)} collective-permute-done((bf16[64,1536]{1,0:T(8,128)(2,1)S(1)}, bf16[64,1536]{1,0:T(8,128)(2,1)S(1)}, u32[]{:S(2)}, u32[]{:S(2)}) %collective-permute-start.8) | collective-permute-done | bytes 196640 | tf_op jit(solution)/shard_map/ppermute | solution.py:164
  26.7 2.6 %collective-permute-done.6.refs_2_ = bf16[64,1664]{1,0:T(8,128)(2,1)S(1)} collective-permute-done((bf16[64,1664]{1,0:T(8,128)(2,1)S(1)}, bf16[64,1664]{1,0:T(8,128)(2,1)S(1)}, u32[]{:S(2)}, u32[]{:S(2)}) %collective-permute-start.6) | collective-permute-done | bytes 213024 | tf_op jit(solution)/shard_map/ppermute | solution.py:164
  29.9 1.4 %projected.6 = (bf16[256,384]{1,0:T(8,128)(2,1)S(1)}, bf16[256,384]{1,0:T(8,128)(2,1)S(1)}, bf16[256,384]{1,0:T(8,128)(2,1)S(1)}, bf16[256,1536]{1,0:T(8,128)(2,1)S(1)}) custom-call(bf16[64,1664]{1,0:T(8,128)(2,1)S(1)} %packed.1.refs_0_.after_ref, bf16[64,1664]{1,0:T(8,128)(2,1)S(1)} %collective-permute-done.5.refs_1_, ...), custom_call_target="tpu_custom_call" | custom-call | tf_op jit(solution)/shard_map/projected/pallas_call | solution.py:423
  32.0 1.5 %collective-permute-start.14 = (bf16[128,1536]{1,0:T(8,128)(2,1)S(1)}, bf16[128,1536]{1,0:T(8,128)(2,1)S(1)}, u32[]{:S(2)}, u32[]{:S(2)}) collective-permute-start(bf16[128,1536]{1,0:T(8,128)(2,1)S(1)} %standardized.3.refs_9_.refs_0_), channel_id=1, source_target_pairs={{0,24},{8,16},{16,8},{24,0},{1,25},{9,17},{17,9},{25,1},{2,26},{10... | collective-permute-start | bytes 1179656 | tf_op jit(solution)/shard_map/ppermute | solution.py:164
  33.5 1.4 %projected.7 = (bf16[256,384]{1,0:T(8,128)(2,1)S(1)}, bf16[256,384]{1,0:T(8,128)(2,1)S(1)}, bf16[256,384]{1,0:T(8,128)(2,1)S(1)}) custom-call(bf16[256,1536]{1,0:T(8,128)(2,1)S(1)} %get-tuple-element.49.refs_0_, bf16[1536,768]{1,0:T(8,128)(2,1)S(1)} %staged.8.refs_6_.refs_1_, bf16[1536,768]{1,0:T(8,128)(2,1)S(1)} %staged.6.refs_2_.refs_7_.refs_4_.refs_1_, ...), custom_call_target="tpu_custom_call" | custom-call | tf_op jit(solution)/shard_map/projected/pallas_call | solution.py:423
  35.3 1.3 %collective-permute-start.13 = (bf16[256,768]{1,0:T(8,128)(2,1)S(1)}, bf16[256,768]{1,0:T(8,128)(2,1)S(1)}, u32[]{:S(2)}, u32[]{:S(2)}) collective-permute-start(bf16[256,768]{1,0:T(8,128)(2,1)S(1)} %get-tuple-element.57.refs_6_.after_ref.refs_1_), channel_id=1, source_target_pairs={{0,2},{2,0},{4,6},{6,4},{1,3},{3,1},{5,7},{7,5},{8,10},{10,8},{12,... | collective-permute-start | bytes 1179656 | tf_op jit(solution)/shard_map/ppermute | solution.py:164
  36.6 1.2 %collective-permute-start.17 = (bf16[128,1536]{1,0:T(8,128)(2,1)S(1)}, bf16[128,1536]{1,0:T(8,128)(2,1)S(1)}, u32[]{:S(2)}, u32[]{:S(2)}) collective-permute-start(bf16[128,1536]{1,0:T(8,128)(2,1)S(1)} %standardized.3.refs_9_.refs_0_), channel_id=1, source_target_pairs={{0,16},{8,24},{16,0},{24,8},{1,17},{9,25},{17,1},{25,9},{2,18},{10... | collective-permute-start | bytes 1179656 | tf_op jit(solution)/shard_map/ppermute | solution.py:164
  38.6 1.6 %staged.9.after_ref.refs_4_.refs_2_ = bf16[768,1536]{1,0:T(8,128)(2,1)S(1)} custom-call(bf16[768,1536]{1,0:T(8,128)(2,1)} %weight_ref.3, bf16[256,768]{1,0:T(8,128)(2,1)S(1)} %get-tuple-element.57.refs_6_.after_ref.refs_1_), custom_call_target="tpu_custom_call" | custom-call | bytes 2359296 | tf_op jit(solution)/shard_map/staged/pallas_call | solution.py:459
  40.2 3.8 %staged.10.refs_5_.refs_2_.refs_1_ = bf16[1536,3072]{1,0:T(8,128)(2,1)S(1)} custom-call(bf16[1536,3072]{1,0:T(8,128)(2,1)} %weight_ref.4, bf16[768,1536]{1,0:T(8,128)(2,1)S(1)} %staged.9.after_ref.refs_4_.refs_2_), custom_call_target="tpu_custom_call" | custom-call | bytes 9437184 | tf_op jit(solution)/shard_map/staged/pallas_call | solution.py:459
  44.9 1.0 projected.8
  45.9 1.0 projected.9
  47.5 0.9 collective-permute-done.15.refs_2_
  48.9 1.1 %attend.1 = (f32[256,384]{1,0:T(8,128)S(1)}, f32[256,384]{1,0:T(8,128)S(1)}, f32[256,384]{1,0:T(8,128)S(1)}) custom-call(bf16[256,384]{1,0:T(8,128)(2,1)S(1)} %get-tuple-element.56.refs_0_, bf16[256,768]{1,0:T(8,128)(2,1)S(1)} %get-tuple-element.57.refs_6_.after_ref.refs_1_, bf16[256,768]{1,0:T(8,128)(2,1)S(1)} %copied.3.refs_2_, ...), custom_call_target="tpu_custom_call" | custom-call | tf_op jit(solution)/shard_map/attend/pallas_call | solution.py:582
  50.0 2.8 %collective-permute-done.17.refs_1_.refs_0_ = bf16[128,1536]{1,0:T(8,128)(2,1)S(1)} collective-permute-done((bf16[128,1536]{1,0:T(8,128)(2,1)S(1)}, bf16[128,1536]{1,0:T(8,128)(2,1)S(1)}, u32[]{:S(2)}, u32[]{:S(2)}) %collective-permute-start.17) | collective-permute-done | bytes 393248 | tf_op jit(solution)/shard_map/ppermute | solution.py:164
  52.9 1.0 projected.10
  54.5 1.0 projected.11
  57.7 1.0 collective-permute-done.23.refs_1_
  59.2 1.5 %collective-permute-start.26 = (bf16[32,1536]{1,0:T(8,128)(2,1)S(1)}, bf16[32,1536]{1,0:T(8,128)(2,1)S(1)}, u32[]{:S(2)}, u32[]{:S(2)}) collective-permute-start(bf16[32,1536]{1,0:T(8,128)(2,1)S(1)} %get-tuple-element.77), channel_id=1, source_target_pairs={{0,16},{8,24},{16,0},{24,8},{1,17},{9,25},{17,1},{25,9},{2,18},{10... | collective-permute-start | bytes 294920 | tf_op jit(solution)/shard_map/ppermute | solution.py:164
  62.0 1.5 %collective-permute-start.22 = (bf16[32,1536]{1,0:T(8,128)(2,1)S(1)}, bf16[32,1536]{1,0:T(8,128)(2,1)S(1)}, u32[]{:S(2)}, u32[]{:S(2)}) collective-permute-start(bf16[32,1536]{1,0:T(8,128)(2,1)S(1)} %get-tuple-element.72), channel_id=1, source_target_pairs={{0,8},{8,0},{16,24},{24,16},{1,9},{9,1},{17,25},{25,17},{2,10},{10... | collective-permute-start | bytes 294920 | tf_op jit(solution)/shard_map/ppermute | solution.py:164
  64.3 1.2 %collective-permute-start.27 = (bf16[32,1536]{1,0:T(8,128)(2,1)S(1)}, bf16[32,1536]{1,0:T(8,128)(2,1)S(1)}, u32[]{:S(2)}, u32[]{:S(2)}) collective-permute-start(bf16[32,1536]{1,0:T(8,128)(2,1)S(1)} %rounded_sum.3), channel_id=1, source_target_pairs={{0,8},{8,0},{16,24},{24,16},{1,9},{9,1},{17,25},{25,17},{2,10},{10... | collective-permute-start | bytes 294920 | tf_op jit(solution)/shard_map/ppermute | solution.py:164
  66.5 1.9 %collective-permute-done.22.refs_1_ = bf16[32,1536]{1,0:T(8,128)(2,1)S(1)} collective-permute-done((bf16[32,1536]{1,0:T(8,128)(2,1)S(1)}, bf16[32,1536]{1,0:T(8,128)(2,1)S(1)}, u32[]{:S(2)}, u32[]{:S(2)}) %collective-permute-start.22) | collective-permute-done | bytes 98336 | tf_op jit(solution)/shard_map/ppermute | solution.py:164
  69.6 1.5 %collective-permute-done.25.refs_2_ = bf16[32,1536]{1,0:T(8,128)(2,1)S(1)} collective-permute-done((bf16[32,1536]{1,0:T(8,128)(2,1)S(1)}, bf16[32,1536]{1,0:T(8,128)(2,1)S(1)}, u32[]{:S(2)}, u32[]{:S(2)}) %collective-permute-start.25) | collective-permute-done | bytes 98336 | tf_op jit(solution)/shard_map/ppermute | solution.py:164
  71.6 1.2 %collective-permute-done.29.refs_2_ = f32[64,128]{1,0:T(8,128)S(1)} collective-permute-done((f32[64,128]{1,0:T(8,128)S(1)}, f32[64,128]{1,0:T(8,128)S(1)}, u32[]{:S(2)}, u32[]{:S(2)}) %collective-permute-start.29) | collective-permute-done | bytes 32800 | tf_op jit(solution)/shard_map/ppermute | solution.py:164
  73.0 1.0 collective-permute-start.30
  74.6 2.0 %collective-permute-start.34 = (bf16[64,1536]{1,0:T(8,128)(2,1)S(1)}, bf16[64,1536]{1,0:T(8,128)(2,1)S(1)}, u32[]{:S(2)}, u32[]{:S(2)}) collective-permute-start(bf16[64,1536]{1,0:T(8,128)(2,1)S(1)} %normed_rows.1.after_ref.refs_0_), channel_id=1, source_target_pairs={{0,8},{8,0},{16,24},{24,16},{1,9},{9,1},{17,25},{25,17},{2,10},{10... | collective-permute-start | bytes 589832 | tf_op jit(solution)/shard_map/ppermute | solution.py:164
  76.6 3.8 %staged.11.refs_3_.refs_2_ = bf16[3072,1536]{1,0:T(8,128)(2,1)S(1)} custom-call(bf16[3072,1536]{1,0:T(8,128)(2,1)} %weight_ref.5, bf16[64,1536]{1,0:T(8,128)(2,1)S(1)} %normed_rows.1.after_ref.refs_0_), custom_call_target="tpu_custom_call" | custom-call | bytes 9437184 | tf_op jit(solution)/shard_map/staged/pallas_call | solution.py:459
  80.4 1.4 %collective-permute-done.30.refs_1_ = bf16[64,1536]{1,0:T(8,128)(2,1)S(1)} collective-permute-done((bf16[64,1536]{1,0:T(8,128)(2,1)S(1)}, bf16[64,1536]{1,0:T(8,128)(2,1)S(1)}, u32[]{:S(2)}, u32[]{:S(2)}) %collective-permute-start.30) | collective-permute-done | bytes 196640 | tf_op jit(solution)/shard_map/ppermute | solution.py:164
  84.0 0.9 collective-permute-done.33.refs_0_
  85.0 0.9 down_projected.4.refs_3_
  85.9 0.9 down_projected.5
  89.0 1.2 %collective-permute-start.39 = (bf16[64,1536]{1,0:T(8,128)(2,1)S(1)}, bf16[64,1536]{1,0:T(8,128)(2,1)S(1)}, u32[]{:S(2)}, u32[]{:S(2)}) collective-permute-start(bf16[64,1536]{1,0:T(8,128)(2,1)S(1)} %get-tuple-element.84), channel_id=1, source_target_pairs={{0,24},{8,16},{16,8},{24,0},{1,25},{9,17},{17,9},{25,1},{2,26},{10... | collective-permute-start | bytes 589832 | tf_op jit(solution)/shard_map/ppermute | solution.py:164
  91.1 0.9 down_projected.7
  92.0 1.2 %collective-permute-start.37 = (bf16[64,1536]{1,0:T(8,128)(2,1)S(1)}, bf16[64,1536]{1,0:T(8,128)(2,1)S(1)}, u32[]{:S(2)}, u32[]{:S(2)}) collective-permute-start(bf16[64,1536]{1,0:T(8,128)(2,1)S(1)} %get-tuple-element.82), channel_id=1, source_target_pairs={{0,8},{8,0},{16,24},{24,16},{1,9},{9,1},{17,25},{25,17},{2,10},{10... | collective-permute-start | bytes 589832 | tf_op jit(solution)/shard_map/ppermute | solution.py:164
  93.2 1.2 %collective-permute-start.38 = (bf16[64,1536]{1,0:T(8,128)(2,1)S(1)}, bf16[64,1536]{1,0:T(8,128)(2,1)S(1)}, u32[]{:S(2)}, u32[]{:S(2)}) collective-permute-start(bf16[64,1536]{1,0:T(8,128)(2,1)S(1)} %get-tuple-element.83), channel_id=1, source_target_pairs={{0,16},{8,24},{16,0},{24,8},{1,17},{9,25},{17,1},{25,9},{2,18},{10... | collective-permute-start | bytes 589832 | tf_op jit(solution)/shard_map/ppermute | solution.py:164
  94.4 3.3 %collective-permute-done.39 = bf16[64,1536]{1,0:T(8,128)(2,1)S(1)} collective-permute-done((bf16[64,1536]{1,0:T(8,128)(2,1)S(1)}, bf16[64,1536]{1,0:T(8,128)(2,1)S(1)}, u32[]{:S(2)}, u32[]{:S(2)}) %collective-permute-start.39) | collective-permute-done | bytes 196640 | tf_op jit(solution)/shard_map/ppermute | solution.py:164
  97.7 2.7 %collective-permute-done.37 = bf16[64,1536]{1,0:T(8,128)(2,1)S(1)} collective-permute-done((bf16[64,1536]{1,0:T(8,128)(2,1)S(1)}, bf16[64,1536]{1,0:T(8,128)(2,1)S(1)}, u32[]{:S(2)}, u32[]{:S(2)}) %collective-permute-start.37) | collective-permute-done | bytes 196640 | tf_op jit(solution)/shard_map/ppermute | solution.py:164
  (93 shorter events, 23.8 us)
Async XLA Ops:
  0.0 2.0 %copy-start = (bf16[3072,576]{0,1:T(8,128)(2,1)S(1)}, bf16[3072,576]{0,1:T(8,128)(2,1)}, u32[]{:S(2)}) copy-start(bf16[3072,576]{0,1:T(8,128)(2,1)} %param.11) | copy-start | bytes 10616836
  0.0 3.0 %copy-start.2 = (bf16[64,1536]{1,0:T(8,128)(2,1)S(1)}, bf16[64,1536]{1,0:T(8,128)(2,1)}, u32[]{:S(2)}) copy-start(bf16[64,1536]{1,0:T(8,128)(2,1)} %refs_6_.1) | copy-start | bytes 589828
  3.1 14.0 %collective-permute-start.4 = (bf16[64,1536]{1,0:T(8,128)(2,1)S(1)}, bf16[64,1536]{1,0:T(8,128)(2,1)S(1)}, u32[]{:S(2)}, u32[]{:S(2)}) collective-permute-start(bf16[64,1536]{1,0:T(8,128)(2,1)S(1)} %copied.2), channel_id=1, source_target_pairs={{0,4},{2,6},{4,0},{6,2},{1,5},{3,7},{5,1},{7,3},{8,12},{10,14},{12... | collective-permute-start | bytes 589832 | tf_op jit(solution)/shard_map/ppermute | solution.py:164
  7.4 4.6 %collective-permute-start = (f32[64,128]{1,0:T(8,128)S(1)}, f32[64,128]{1,0:T(8,128)S(1)}, u32[]{:S(2)}, u32[]{:S(2)}) collective-permute-start(f32[64,128]{1,0:T(8,128)S(1)} %get-tuple-element.46.refs_1_), channel_id=1, source_target_pairs={{0,1},{1,0},{2,3},{3,2},{4,5},{5,4},{6,7},{7,6},{8,9},{9,8},{10,11... | collective-permute-start | bytes 98312 | tf_op jit(solution)/shard_map/ppermute | solution.py:164
  7.4 1.3 %collective-permute-start.1 = (f32[1,576]{1,0:T(1,128)S(1)}, f32[1,576]{1,0:T(1,128)S(1)}, u32[]{:S(2)}, u32[]{:S(2)}) collective-permute-start(f32[1,576]{1,0:T(1,128)S(1)} %fusion.4.refs_0_.after_ref), channel_id=1, source_target_pairs={{0,1},{1,0},{2,3},{3,2},{4,5},{5,4},{6,7},{7,6},{8,9},{9,8},{10,11... | collective-permute-start | bytes 6920 | tf_op jit(solution)/shard_map/ppermute | solution.py:164
  8.8 3.6 %collective-permute-start.2 = (f32[2,576]{1,0:T(2,128)S(1)}, f32[2,576]{1,0:T(2,128)S(1)}, u32[]{:S(2)}, u32[]{:S(2)}) collective-permute-start(f32[2,576]{1,0:T(2,128)S(1)} %merged.3.after_ref.refs_0_), channel_id=1, source_target_pairs={{0,2},{2,0},{4,6},{6,4},{1,3},{3,1},{5,7},{7,5},{8,10},{10,8},{12,... | collective-permute-start | bytes 13832 | tf_op jit(solution)/shard_map/ppermute | solution.py:164
  12.4 4.6 %collective-permute-start.3 = (f32[4,576]{1,0:T(4,128)S(1)}, f32[4,576]{1,0:T(4,128)S(1)}, u32[]{:S(2)}, u32[]{:S(2)}) collective-permute-start(f32[4,576]{1,0:T(4,128)S(1)} %merged.4.after_ref.refs_0_), channel_id=1, source_target_pairs={{0,4},{2,6},{4,0},{6,2},{1,5},{3,7},{5,1},{7,3},{8,12},{10,14},{12... | collective-permute-start | bytes 27656 | tf_op jit(solution)/shard_map/ppermute | solution.py:164
  17.1 9.6 %collective-permute-start.5 = (bf16[64,1664]{1,0:T(8,128)(2,1)S(1)}, bf16[64,1664]{1,0:T(8,128)(2,1)S(1)}, u32[]{:S(2)}, u32[]{:S(2)}) collective-permute-start(bf16[64,1664]{1,0:T(8,128)(2,1)S(1)} %packed.1.refs_0_.after_ref), channel_id=1, source_target_pairs={{0,8},{8,0},{16,24},{24,16},{1,9},{9,1},{17,25},{25,17},{2,10},{10... | collective-permute-start | bytes 638984 | tf_op jit(solution)/shard_map/ppermute | solution.py:164
  18.6 10.6 %collective-permute-start.6 = (bf16[64,1664]{1,0:T(8,128)(2,1)S(1)}, bf16[64,1664]{1,0:T(8,128)(2,1)S(1)}, u32[]{:S(2)}, u32[]{:S(2)}) collective-permute-start(bf16[64,1664]{1,0:T(8,128)(2,1)S(1)} %packed.1.refs_0_.after_ref), channel_id=1, source_target_pairs={{0,16},{8,24},{16,0},{24,8},{1,17},{9,25},{17,1},{25,9},{2,18},{10... | collective-permute-start | bytes 638984 | tf_op jit(solution)/shard_map/ppermute | solution.py:164
  20.2 9.1 %collective-permute-start.7 = (bf16[64,1664]{1,0:T(8,128)(2,1)S(1)}, bf16[64,1664]{1,0:T(8,128)(2,1)S(1)}, u32[]{:S(2)}, u32[]{:S(2)}) collective-permute-start(bf16[64,1664]{1,0:T(8,128)(2,1)S(1)} %packed.1.refs_0_.after_ref), channel_id=1, source_target_pairs={{0,24},{8,16},{16,8},{24,0},{1,25},{9,17},{17,9},{25,1},{2,26},{10... | collective-permute-start | bytes 638984 | tf_op jit(solution)/shard_map/ppermute | solution.py:164
  20.6 5.7 %collective-permute-start.8 = (bf16[64,1536]{1,0:T(8,128)(2,1)S(1)}, bf16[64,1536]{1,0:T(8,128)(2,1)S(1)}, u32[]{:S(2)}, u32[]{:S(2)}) collective-permute-start(bf16[64,1536]{1,0:T(8,128)(2,1)S(1)} %collective-permute-done.4.refs_4_.refs_0_), channel_id=1, source_target_pairs={{0,2},{2,0},{4,6},{6,4},{1,3},{3,1},{5,7},{7,5},{8,10},{10,8},{12,... | collective-permute-start | bytes 589832 | tf_op jit(solution)/shard_map/ppermute | solution.py:164
  26.6 3.1 %collective-permute-start.9 = (f32[128,128]{1,0:T(8,128)S(1)}, f32[128,128]{1,0:T(8,128)S(1)}, u32[]{:S(2)}, u32[]{:S(2)}) collective-permute-start(f32[128,128]{1,0:T(8,128)S(1)} %get-tuple-element.48.refs_1_), channel_id=1, source_target_pairs={{0,1},{1,0},{2,3},{3,2},{4,5},{5,4},{6,7},{7,6},{8,9},{9,8},{10,11... | collective-permute-start | bytes 196616 | tf_op jit(solution)/shard_map/ppermute | solution.py:164
  31.3 3.5 %collective-permute-start.10 = (bf16[256,384]{1,0:T(8,128)(2,1)S(1)}, bf16[256,384]{1,0:T(8,128)(2,1)S(1)}, u32[]{:S(2)}, u32[]{:S(2)}) collective-permute-start(bf16[256,384]{1,0:T(8,128)(2,1)S(1)} %get-tuple-element.53), channel_id=1, source_target_pairs={{0,1},{1,0},{2,3},{3,2},{4,5},{5,4},{6,7},{7,6},{8,9},{9,8},{10,11... | collective-permute-start | bytes 589832 | tf_op jit(solution)/shard_map/ppermute | solution.py:164
  31.4 3.5 %collective-permute-start.11 = (bf16[256,384]{1,0:T(8,128)(2,1)S(1)}, bf16[256,384]{1,0:T(8,128)(2,1)S(1)}, u32[]{:S(2)}, u32[]{:S(2)}) collective-permute-start(bf16[256,384]{1,0:T(8,128)(2,1)S(1)} %get-tuple-element.54), channel_id=1, source_target_pairs={{0,1},{1,0},{2,3},{3,2},{4,5},{5,4},{6,7},{7,6},{8,9},{9,8},{10,11... | collective-permute-start | bytes 589832 | tf_op jit(solution)/shard_map/ppermute | solution.py:164
  31.9 3.0 %collective-permute-start.12 = (bf16[256,384]{1,0:T(8,128)(2,1)S(1)}, bf16[256,384]{1,0:T(8,128)(2,1)S(1)}, u32[]{:S(2)}, u32[]{:S(2)}) collective-permute-start(bf16[256,384]{1,0:T(8,128)(2,1)S(1)} %get-tuple-element.55), channel_id=1, source_target_pairs={{0,1},{1,0},{2,3},{3,2},{4,5},{5,4},{6,7},{7,6},{8,9},{9,8},{10,11... | collective-permute-start | bytes 589832 | tf_op jit(solution)/shard_map/ppermute | solution.py:164
  32.0 12.9 %collective-permute-start.14 = (bf16[128,1536]{1,0:T(8,128)(2,1)S(1)}, bf16[128,1536]{1,0:T(8,128)(2,1)S(1)}, u32[]{:S(2)}, u32[]{:S(2)}) collective-permute-start(bf16[128,1536]{1,0:T(8,128)(2,1)S(1)} %standardized.3.refs_9_.refs_0_), channel_id=1, source_target_pairs={{0,24},{8,16},{16,8},{24,0},{1,25},{9,17},{17,9},{25,1},{2,26},{10... | collective-permute-start | bytes 1179656 | tf_op jit(solution)/shard_map/ppermute | solution.py:164
  33.5 1.4 %copy-start.3 = (f32[128]{0:T(128)S(1)}, f32[128]{0:T(128)}, u32[]{:S(2)}) copy-start(f32[128]{0:T(128)} %param.13) | copy-start | bytes 1540
  33.5 1.4 %copy-start.4 = (f32[128]{0:T(128)S(1)}, f32[128]{0:T(128)}, u32[]{:S(2)}) copy-start(f32[128]{0:T(128)} %param.14) | copy-start | bytes 1540
  35.3 12.2 %collective-permute-start.13 = (bf16[256,768]{1,0:T(8,128)(2,1)S(1)}, bf16[256,768]{1,0:T(8,128)(2,1)S(1)}, u32[]{:S(2)}, u32[]{:S(2)}) collective-permute-start(bf16[256,768]{1,0:T(8,128)(2,1)S(1)} %get-tuple-element.57.refs_6_.after_ref.refs_1_), channel_id=1, source_target_pairs={{0,2},{2,0},{4,6},{6,4},{1,3},{3,1},{5,7},{7,5},{8,10},{10,8},{12,... | collective-permute-start | bytes 1179656 | tf_op jit(solution)/shard_map/ppermute | solution.py:164
  36.6 16.2 %collective-permute-start.17 = (bf16[128,1536]{1,0:T(8,128)(2,1)S(1)}, bf16[128,1536]{1,0:T(8,128)(2,1)S(1)}, u32[]{:S(2)}, u32[]{:S(2)}) collective-permute-start(bf16[128,1536]{1,0:T(8,128)(2,1)S(1)} %standardized.3.refs_9_.refs_0_), channel_id=1, source_target_pairs={{0,16},{8,24},{16,0},{24,8},{1,17},{9,25},{17,1},{25,9},{2,18},{10... | collective-permute-start | bytes 1179656 | tf_op jit(solution)/shard_map/ppermute | solution.py:164
  37.8 15.1 %collective-permute-start.18 = (bf16[128,1536]{1,0:T(8,128)(2,1)S(1)}, bf16[128,1536]{1,0:T(8,128)(2,1)S(1)}, u32[]{:S(2)}, u32[]{:S(2)}) collective-permute-start(bf16[128,1536]{1,0:T(8,128)(2,1)S(1)} %standardized.3.refs_9_.refs_0_), channel_id=1, source_target_pairs={{0,8},{8,0},{16,24},{24,16},{1,9},{9,1},{17,25},{25,17},{2,10},{10... | collective-permute-start | bytes 1179656 | tf_op jit(solution)/shard_map/ppermute | solution.py:164
  46.9 1.5 %collective-permute-start.15 = (bf16[256,384]{1,0:T(8,128)(2,1)S(1)}, bf16[256,384]{1,0:T(8,128)(2,1)S(1)}, u32[]{:S(2)}, u32[]{:S(2)}) collective-permute-start(bf16[256,384]{1,0:T(8,128)(2,1)S(1)} %get-tuple-element.61), channel_id=1, source_target_pairs={{0,1},{1,0},{2,3},{3,2},{4,5},{5,4},{6,7},{7,6},{8,9},{9,8},{10,11... | collective-permute-start | bytes 589832 | tf_op jit(solution)/shard_map/ppermute | solution.py:164
  46.9 1.7 %collective-permute-start.16 = (bf16[256,384]{1,0:T(8,128)(2,1)S(1)}, bf16[256,384]{1,0:T(8,128)(2,1)S(1)}, u32[]{:S(2)}, u32[]{:S(2)}) collective-permute-start(bf16[256,384]{1,0:T(8,128)(2,1)S(1)} %get-tuple-element.62), channel_id=1, source_target_pairs={{0,1},{1,0},{2,3},{3,2},{4,5},{5,4},{6,7},{7,6},{8,9},{9,8},{10,11... | collective-permute-start | bytes 589832 | tf_op jit(solution)/shard_map/ppermute | solution.py:164
  53.9 1.6 %collective-permute-start.19 = (bf16[256,384]{1,0:T(8,128)(2,1)S(1)}, bf16[256,384]{1,0:T(8,128)(2,1)S(1)}, u32[]{:S(2)}, u32[]{:S(2)}) collective-permute-start(bf16[256,384]{1,0:T(8,128)(2,1)S(1)} %get-tuple-element.69), channel_id=1, source_target_pairs={{0,1},{1,0},{2,3},{3,2},{4,5},{5,4},{6,7},{7,6},{8,9},{9,8},{10,11... | collective-permute-start | bytes 589832 | tf_op jit(solution)/shard_map/ppermute | solution.py:164
  54.0 1.7 %collective-permute-start.20 = (bf16[256,384]{1,0:T(8,128)(2,1)S(1)}, bf16[256,384]{1,0:T(8,128)(2,1)S(1)}, u32[]{:S(2)}, u32[]{:S(2)}) collective-permute-start(bf16[256,384]{1,0:T(8,128)(2,1)S(1)} %get-tuple-element.70), channel_id=1, source_target_pairs={{0,1},{1,0},{2,3},{3,2},{4,5},{5,4},{6,7},{7,6},{8,9},{9,8},{10,11... | collective-permute-start | bytes 589832 | tf_op jit(solution)/shard_map/ppermute | solution.py:164
  57.1 4.1 %collective-permute-start.21 = (bf16[192,384]{1,0:T(8,128)(2,1)S(1)}, bf16[192,384]{1,0:T(8,128)(2,1)S(1)}, u32[]{:S(2)}, u32[]{:S(2)}) collective-permute-start(bf16[192,384]{1,0:T(8,128)(2,1)S(1)} %finished.3.refs_0_.refs_3_), channel_id=1, source_target_pairs={{0,1},{1,0},{2,3},{3,2},{4,5},{5,4},{6,7},{7,6},{8,9},{9,8},{10,11... | collective-permute-start | bytes 442376 | tf_op jit(solution)/shard_map/ppermute | solution.py:164
  57.4 1.2 %collective-permute-start.23 = (bf16[64,384]{1,0:T(8,128)(2,1)S(1)}, bf16[64,384]{1,0:T(8,128)(2,1)S(1)}, u32[]{:S(2)}, u32[]{:S(2)}) collective-permute-start(bf16[64,384]{1,0:T(8,128)(2,1)S(1)} %finished.2.refs_5_.refs_0_), channel_id=1, source_target_pairs={{0,1},{1,0},{2,3},{3,2},{4,5},{5,4},{6,7},{7,6},{8,9},{9,8},{10,11... | collective-permute-start | bytes 147464 | tf_op jit(solution)/shard_map/ppermute | solution.py:164
  59.2 5.0 %collective-permute-start.26 = (bf16[32,1536]{1,0:T(8,128)(2,1)S(1)}, bf16[32,1536]{1,0:T(8,128)(2,1)S(1)}, u32[]{:S(2)}, u32[]{:S(2)}) collective-permute-start(bf16[32,1536]{1,0:T(8,128)(2,1)S(1)} %get-tuple-element.77), channel_id=1, source_target_pairs={{0,16},{8,24},{16,0},{24,8},{1,17},{9,25},{17,1},{25,9},{2,18},{10... | collective-permute-start | bytes 294920 | tf_op jit(solution)/shard_map/ppermute | solution.py:164
  60.7 5.7 %collective-permute-start.24 = (bf16[32,1536]{1,0:T(8,128)(2,1)S(1)}, bf16[32,1536]{1,0:T(8,128)(2,1)S(1)}, u32[]{:S(2)}, u32[]{:S(2)}) collective-permute-start(bf16[32,1536]{1,0:T(8,128)(2,1)S(1)} %get-tuple-element.74), channel_id=1, source_target_pairs={{0,8},{8,0},{16,24},{24,16},{1,9},{9,1},{17,25},{25,17},{2,10},{10... | collective-permute-start | bytes 294920 | tf_op jit(solution)/shard_map/ppermute | solution.py:164
  62.0 6.4 %collective-permute-start.22 = (bf16[32,1536]{1,0:T(8,128)(2,1)S(1)}, bf16[32,1536]{1,0:T(8,128)(2,1)S(1)}, u32[]{:S(2)}, u32[]{:S(2)}) collective-permute-start(bf16[32,1536]{1,0:T(8,128)(2,1)S(1)} %get-tuple-element.72), channel_id=1, source_target_pairs={{0,8},{8,0},{16,24},{24,16},{1,9},{9,1},{17,25},{25,17},{2,10},{10... | collective-permute-start | bytes 294920 | tf_op jit(solution)/shard_map/ppermute | solution.py:164
  63.6 5.4 %collective-permute-start.28 = (bf16[32,1536]{1,0:T(8,128)(2,1)S(1)}, bf16[32,1536]{1,0:T(8,128)(2,1)S(1)}, u32[]{:S(2)}, u32[]{:S(2)}) collective-permute-start(bf16[32,1536]{1,0:T(8,128)(2,1)S(1)} %get-tuple-element.78), channel_id=1, source_target_pairs={{0,16},{8,24},{16,0},{24,8},{1,17},{9,25},{17,1},{25,9},{2,18},{10... | collective-permute-start | bytes 294920 | tf_op jit(solution)/shard_map/ppermute | solution.py:164
  64.3 5.3 %collective-permute-start.27 = (bf16[32,1536]{1,0:T(8,128)(2,1)S(1)}, bf16[32,1536]{1,0:T(8,128)(2,1)S(1)}, u32[]{:S(2)}, u32[]{:S(2)}) collective-permute-start(bf16[32,1536]{1,0:T(8,128)(2,1)S(1)} %rounded_sum.3), channel_id=1, source_target_pairs={{0,8},{8,0},{16,24},{24,16},{1,9},{9,1},{17,25},{25,17},{2,10},{10... | collective-permute-start | bytes 294920 | tf_op jit(solution)/shard_map/ppermute | solution.py:164
  66.4 4.7 %collective-permute-start.25 = (bf16[32,1536]{1,0:T(8,128)(2,1)S(1)}, bf16[32,1536]{1,0:T(8,128)(2,1)S(1)}, u32[]{:S(2)}, u32[]{:S(2)}) collective-permute-start(bf16[32,1536]{1,0:T(8,128)(2,1)S(1)} %rounded_sum.2), channel_id=1, source_target_pairs={{0,16},{8,24},{16,0},{24,8},{1,17},{9,25},{17,1},{25,9},{2,18},{10... | collective-permute-start | bytes 294920 | tf_op jit(solution)/shard_map/ppermute | solution.py:164
  71.6 1.2 %collective-permute-start.29 = (f32[64,128]{1,0:T(8,128)S(1)}, f32[64,128]{1,0:T(8,128)S(1)}, u32[]{:S(2)}, u32[]{:S(2)}) collective-permute-start(f32[64,128]{1,0:T(8,128)S(1)} %get-tuple-element.80.refs_1_), channel_id=1, source_target_pairs={{0,1},{1,0},{2,3},{3,2},{4,5},{5,4},{6,7},{7,6},{8,9},{9,8},{10,11... | collective-permute-start | bytes 98312 | tf_op jit(solution)/shard_map/ppermute | solution.py:164
  73.0 8.8 %collective-permute-start.30 = (bf16[64,1536]{1,0:T(8,128)(2,1)S(1)}, bf16[64,1536]{1,0:T(8,128)(2,1)S(1)}, u32[]{:S(2)}, u32[]{:S(2)}) collective-permute-start(bf16[64,1536]{1,0:T(8,128)(2,1)S(1)} %normed_rows.1.after_ref.refs_0_), channel_id=1, source_target_pairs={{0,24},{8,16},{16,8},{24,0},{1,25},{9,17},{17,9},{25,1},{2,26},{10... | collective-permute-start | bytes 589832 | tf_op jit(solution)/shard_map/ppermute | solution.py:164
  74.0 10.9 %collective-permute-start.33 = (bf16[64,1536]{1,0:T(8,128)(2,1)S(1)}, bf16[64,1536]{1,0:T(8,128)(2,1)S(1)}, u32[]{:S(2)}, u32[]{:S(2)}) collective-permute-start(bf16[64,1536]{1,0:T(8,128)(2,1)S(1)} %normed_rows.1.after_ref.refs_0_), channel_id=1, source_target_pairs={{0,16},{8,24},{16,0},{24,8},{1,17},{9,25},{17,1},{25,9},{2,18},{10... | collective-permute-start | bytes 589832 | tf_op jit(solution)/shard_map/ppermute | solution.py:164
  74.6 10.4 %collective-permute-start.34 = (bf16[64,1536]{1,0:T(8,128)(2,1)S(1)}, bf16[64,1536]{1,0:T(8,128)(2,1)S(1)}, u32[]{:S(2)}, u32[]{:S(2)}) collective-permute-start(bf16[64,1536]{1,0:T(8,128)(2,1)S(1)} %normed_rows.1.after_ref.refs_0_), channel_id=1, source_target_pairs={{0,8},{8,0},{16,24},{24,16},{1,9},{9,1},{17,25},{25,17},{2,10},{10... | collective-permute-start | bytes 589832 | tf_op jit(solution)/shard_map/ppermute | solution.py:164
  82.6 2.4 %collective-permute-start.32 = (bf16[128,1536]{1,0:T(8,128)(2,1)S(1)}, bf16[128,1536]{1,0:T(8,128)(2,1)S(1)}, u32[]{:S(2)}, u32[]{:S(2)}) collective-permute-start(bf16[128,1536]{1,0:T(8,128)(2,1)S(1)} %up_projected.5.refs_0_), channel_id=1, source_target_pairs={{0,1},{1,0},{2,3},{3,2},{4,5},{5,4},{6,7},{7,6},{8,9},{9,8},{10,11... | collective-permute-start | bytes 1179656 | tf_op jit(solution)/shard_map/ppermute | solution.py:164
  83.4 2.4 %collective-permute-start.31 = (bf16[128,1536]{1,0:T(8,128)(2,1)S(1)}, bf16[128,1536]{1,0:T(8,128)(2,1)S(1)}, u32[]{:S(2)}, u32[]{:S(2)}) collective-permute-start(bf16[128,1536]{1,0:T(8,128)(2,1)S(1)} %up_projected.4.refs_0_), channel_id=1, source_target_pairs={{0,1},{1,0},{2,3},{3,2},{4,5},{5,4},{6,7},{7,6},{8,9},{9,8},{10,11... | collective-permute-start | bytes 1179656 | tf_op jit(solution)/shard_map/ppermute | solution.py:164
  87.6 2.6 %collective-permute-start.36 = (bf16[128,1536]{1,0:T(8,128)(2,1)S(1)}, bf16[128,1536]{1,0:T(8,128)(2,1)S(1)}, u32[]{:S(2)}, u32[]{:S(2)}) collective-permute-start(bf16[128,1536]{1,0:T(8,128)(2,1)S(1)} %up_projected.7.refs_0_), channel_id=1, source_target_pairs={{0,1},{1,0},{2,3},{3,2},{4,5},{5,4},{6,7},{7,6},{8,9},{9,8},{10,11... | collective-permute-start | bytes 1179656 | tf_op jit(solution)/shard_map/ppermute | solution.py:164
  88.4 2.6 %collective-permute-start.35 = (bf16[128,1536]{1,0:T(8,128)(2,1)S(1)}, bf16[128,1536]{1,0:T(8,128)(2,1)S(1)}, u32[]{:S(2)}, u32[]{:S(2)}) collective-permute-start(bf16[128,1536]{1,0:T(8,128)(2,1)S(1)} %up_projected.6.refs_0_), channel_id=1, source_target_pairs={{0,1},{1,0},{2,3},{3,2},{4,5},{5,4},{6,7},{7,6},{8,9},{9,8},{10,11... | collective-permute-start | bytes 1179656 | tf_op jit(solution)/shard_map/ppermute | solution.py:164
  89.0 8.7 %collective-permute-start.39 = (bf16[64,1536]{1,0:T(8,128)(2,1)S(1)}, bf16[64,1536]{1,0:T(8,128)(2,1)S(1)}, u32[]{:S(2)}, u32[]{:S(2)}) collective-permute-start(bf16[64,1536]{1,0:T(8,128)(2,1)S(1)} %get-tuple-element.84), channel_id=1, source_target_pairs={{0,24},{8,16},{16,8},{24,0},{1,25},{9,17},{17,9},{25,1},{2,26},{10... | collective-permute-start | bytes 589832 | tf_op jit(solution)/shard_map/ppermute | solution.py:164
  91.1 10.8 %copy-start.1 = (bf16[3072,576]{0,1:T(8,128)(2,1)S(1)}, bf16[3072,576]{0,1:T(8,128)(2,1)}, u32[]{:S(2)}) copy-start(bf16[3072,576]{0,1:T(8,128)(2,1)} %param.11) | copy-start | bytes 10616836
  92.0 8.4 %collective-permute-start.37 = (bf16[64,1536]{1,0:T(8,128)(2,1)S(1)}, bf16[64,1536]{1,0:T(8,128)(2,1)S(1)}, u32[]{:S(2)}, u32[]{:S(2)}) collective-permute-start(bf16[64,1536]{1,0:T(8,128)(2,1)S(1)} %get-tuple-element.82), channel_id=1, source_target_pairs={{0,8},{8,0},{16,24},{24,16},{1,9},{9,1},{17,25},{25,17},{2,10},{10... | collective-permute-start | bytes 589832 | tf_op jit(solution)/shard_map/ppermute | solution.py:164
  93.2 7.8 %collective-permute-start.38 = (bf16[64,1536]{1,0:T(8,128)(2,1)S(1)}, bf16[64,1536]{1,0:T(8,128)(2,1)S(1)}, u32[]{:S(2)}, u32[]{:S(2)}) collective-permute-start(bf16[64,1536]{1,0:T(8,128)(2,1)S(1)} %get-tuple-element.83), channel_id=1, source_target_pairs={{0,16},{8,24},{16,0},{24,8},{1,17},{9,25},{17,1},{25,9},{2,18},{10... | collective-permute-start | bytes 589832 | tf_op jit(solution)/shard_map/ppermute | solution.py:164

commit v9 on v8

--- a/solution.py
+++ b/solution.py
@@ -899,7 +899,8 @@
     partial, arrived = [], []
     if last_rows:
         context = finished(queries, state, last, head_size, all_rows - rows, rows)
-        arrived.append((context, permuted(context, "tensor", 1)))
+        other = permuted(context, "tensor", 1)
+        arrived.append((context, copied(other, other, LONG)))
     after = [own for own, _ in arrived]
     context = finished(queries, state, last, head_size, 0, all_rows - last_rows, after)
     other = permuted(context, "tensor", 1)

time: 102 us -> 101 us (level)
  transfers between devices with their start and end apart: 40 -> 40, of which waited for: 24 -> 22; matrix products, arithmetic and copies ran while one was open for 0% -> 0% of each run, Pallas kernels for 27% -> 28%
where the time goes in v9:
time: 101 us
  Pallas kernels  34.2 us (34%)
  starting transfers between devices  34 us (34%)
  waiting for transfers between devices  28.3 us (28%)
  other arithmetic  1.72 us (2%)
  local copies, waits for them, and re-layouts  1.21 us (1%)
  matrix products  1.01 us (1%)
    ppermute x40, starting transfers between devices, permuted(): return lax.ppermute(values, axis, [(i, i ^ distance) for i in range(size)])  34 us
    ppermute x40, waiting for transfers between devices, permuted(): return lax.ppermute(values, axis, [(i, i ^ distance) for i in range(size)])  28.3 us
    pallas_call x6, Pallas kernels, staged(): pl.pallas_call(kernel, grid=(1,), in_specs=[anywhere] + after_specs([afte...  14.1 us
    pallas_call x6, Pallas kernels, projected(): pl.pallas_call((lambda *refs: project_kernel(len(blocks), count, other, *...  6.8 us
    pallas_call x4, Pallas kernels, down_projected(): pl.pallas_call(lambda *refs: down_kernel(first, count, len(before), *refs...  3.56 us
    pallas_call x4, Pallas kernels, up_projected(): pl.pallas_call(lambda *refs: up_kernel(part * columns, len(blocks), *refs...  3.13 us
  transfers between devices with their start and end apart: 40, of which 22 were waited for; matrix products, arithmetic and copies ran while one was open for 0% of the time, Pallas kernels for 28%

profile of v9, /device:TPU:0, one launch (start us, length us, event | category | flops | bytes accessed | tf_op | source)
XLA Modules:
  0.0 100.9 jit_solution(488799694691286275)
XLA Ops:
  0.9 1.1 %copy-done = bf16[3072,576]{0,1:T(8,128)(2,1)S(1)} copy-done((bf16[3072,576]{0,1:T(8,128)(2,1)S(1)}, bf16[3072,576]{0,1:T(8,128)(2,1)}, u32[]{:S(2)}) %copy-start) | copy-done | bytes 3538968
  2.0 1.0 %fusion.4.refs_0_.after_ref = f32[1,576]{1,0:T(1,128)S(1)} fusion(bf16[3072,1]{0,1:T(2,128)(2,1)S(1)} %reshape.3, bf16[3072,576]{0,1:T(8,128)(2,1)S(1)} %copy-done), kind=kOutput, calls=%fused_computation.8 | convolution fusion | flops 3538944 | bytes 3547392 | tf_op jit(solution)/shard_map/dot_general | solution.py:847
  3.1 4.1 %collective-permute-start.4 = (bf16[64,1536]{1,0:T(8,128)(2,1)S(1)}, bf16[64,1536]{1,0:T(8,128)(2,1)S(1)}, u32[]{:S(2)}, u32[]{:S(2)}) collective-permute-start(bf16[64,1536]{1,0:T(8,128)(2,1)S(1)} %copied.3), channel_id=1, source_target_pairs={{0,4},{2,6},{4,0},{6,2},{1,5},{3,7},{5,1},{7,3},{8,12},{10,14},{12... | collective-permute-start | bytes 589832 | tf_op jit(solution)/shard_map/ppermute | solution.py:164
  8.8 1.6 %collective-permute-start.2 = (f32[2,576]{1,0:T(2,128)S(1)}, f32[2,576]{1,0:T(2,128)S(1)}, u32[]{:S(2)}, u32[]{:S(2)}) collective-permute-start(f32[2,576]{1,0:T(2,128)S(1)} %merged.3.after_ref.refs_0_), channel_id=1, source_target_pairs={{0,2},{2,0},{4,6},{6,4},{1,3},{3,1},{5,7},{7,5},{8,10},{10,8},{12,... | collective-permute-start | bytes 13832 | tf_op jit(solution)/shard_map/ppermute | solution.py:164
  10.3 1.6 %staged.6.refs_2_.refs_7_.refs_4_.refs_1_ = bf16[1536,768]{1,0:T(8,128)(2,1)S(1)} custom-call(bf16[3,1536,768]{2,1,0:T(8,128)(2,1)} %bitcast.11, f32[2,576]{1,0:T(2,128)S(1)} %merged.3.after_ref.refs_0_), custom_call_target="tpu_custom_call" | custom-call | bytes 2359296 | tf_op jit(solution)/shard_map/staged/pallas_call | solution.py:459
  12.4 1.5 %collective-permute-start.3 = (f32[4,576]{1,0:T(4,128)S(1)}, f32[4,576]{1,0:T(4,128)S(1)}, u32[]{:S(2)}, u32[]{:S(2)}) collective-permute-start(f32[4,576]{1,0:T(4,128)S(1)} %merged.4.after_ref.refs_0_), channel_id=1, source_target_pairs={{0,4},{2,6},{4,0},{6,2},{1,5},{3,7},{5,1},{7,3},{8,12},{10,14},{12... | collective-permute-start | bytes 27656 | tf_op jit(solution)/shard_map/ppermute | solution.py:164
  13.9 1.6 %staged.7.refs_3_.refs_8_.refs_5_.refs_2_ = bf16[1536,768]{1,0:T(8,128)(2,1)S(1)} custom-call(bf16[3,1536,768]{2,1,0:T(8,128)(2,1)} %bitcast.12, f32[4,576]{1,0:T(4,128)S(1)} %merged.4.after_ref.refs_0_), custom_call_target="tpu_custom_call" | custom-call | bytes 2359296 | tf_op jit(solution)/shard_map/staged/pallas_call | solution.py:459
  15.6 1.5 %collective-permute-done.3.refs_1_ = f32[4,576]{1,0:T(4,128)S(1)} collective-permute-done((f32[4,576]{1,0:T(4,128)S(1)}, f32[4,576]{1,0:T(4,128)S(1)}, u32[]{:S(2)}, u32[]{:S(2)}) %collective-permute-start.3) | collective-permute-done | bytes 9248 | tf_op jit(solution)/shard_map/ppermute | solution.py:164
  17.1 1.6 %collective-permute-start.5 = (bf16[64,1664]{1,0:T(8,128)(2,1)S(1)}, bf16[64,1664]{1,0:T(8,128)(2,1)S(1)}, u32[]{:S(2)}, u32[]{:S(2)}) collective-permute-start(bf16[64,1664]{1,0:T(8,128)(2,1)S(1)} %packed.1.refs_0_.after_ref), channel_id=1, source_target_pairs={{0,8},{8,0},{16,24},{24,16},{1,9},{9,1},{17,25},{25,17},{2,10},{10... | collective-permute-start | bytes 638984 | tf_op jit(solution)/shard_map/ppermute | solution.py:164
  18.6 1.5 %collective-permute-start.6 = (bf16[64,1664]{1,0:T(8,128)(2,1)S(1)}, bf16[64,1664]{1,0:T(8,128)(2,1)S(1)}, u32[]{:S(2)}, u32[]{:S(2)}) collective-permute-start(bf16[64,1664]{1,0:T(8,128)(2,1)S(1)} %packed.1.refs_0_.after_ref), channel_id=1, source_target_pairs={{0,16},{8,24},{16,0},{24,8},{1,17},{9,25},{17,1},{25,9},{2,18},{10... | collective-permute-start | bytes 638984 | tf_op jit(solution)/shard_map/ppermute | solution.py:164
  20.6 1.6 %collective-permute-start.8 = (bf16[64,1536]{1,0:T(8,128)(2,1)S(1)}, bf16[64,1536]{1,0:T(8,128)(2,1)S(1)}, u32[]{:S(2)}, u32[]{:S(2)}) collective-permute-start(bf16[64,1536]{1,0:T(8,128)(2,1)S(1)} %collective-permute-done.4.refs_4_.refs_0_), channel_id=1, source_target_pairs={{0,2},{2,0},{4,6},{6,4},{1,3},{3,1},{5,7},{7,5},{8,10},{10,8},{12,... | collective-permute-start | bytes 589832 | tf_op jit(solution)/shard_map/ppermute | solution.py:164
  22.2 1.6 %staged.8.refs_6_.refs_1_ = bf16[1536,768]{1,0:T(8,128)(2,1)S(1)} custom-call(bf16[3,1536,768]{2,1,0:T(8,128)(2,1)} %bitcast.13, bf16[64,1664]{1,0:T(8,128)(2,1)S(1)} %packed.1.refs_0_.after_ref), custom_call_target="tpu_custom_call" | custom-call | bytes 2359296 | tf_op jit(solution)/shard_map/staged/pallas_call | solution.py:459
  23.9 2.5 %collective-permute-done.8.refs_1_ = bf16[64,1536]{1,0:T(8,128)(2,1)S(1)} collective-permute-done((bf16[64,1536]{1,0:T(8,128)(2,1)S(1)}, bf16[64,1536]{1,0:T(8,128)(2,1)S(1)}, u32[]{:S(2)}, u32[]{:S(2)}) %collective-permute-start.8) | collective-permute-done | bytes 196640 | tf_op jit(solution)/shard_map/ppermute | solution.py:164
  26.7 2.6 %collective-permute-done.6.refs_2_ = bf16[64,1664]{1,0:T(8,128)(2,1)S(1)} collective-permute-done((bf16[64,1664]{1,0:T(8,128)(2,1)S(1)}, bf16[64,1664]{1,0:T(8,128)(2,1)S(1)}, u32[]{:S(2)}, u32[]{:S(2)}) %collective-permute-start.6) | collective-permute-done | bytes 213024 | tf_op jit(solution)/shard_map/ppermute | solution.py:164
  29.9 1.4 %projected.6 = (bf16[256,384]{1,0:T(8,128)(2,1)S(1)}, bf16[256,384]{1,0:T(8,128)(2,1)S(1)}, bf16[256,384]{1,0:T(8,128)(2,1)S(1)}, bf16[256,1536]{1,0:T(8,128)(2,1)S(1)}) custom-call(bf16[64,1664]{1,0:T(8,128)(2,1)S(1)} %packed.1.refs_0_.after_ref, bf16[64,1664]{1,0:T(8,128)(2,1)S(1)} %collective-permute-done.5.refs_1_, ...), custom_call_target="tpu_custom_call" | custom-call | tf_op jit(solution)/shard_map/projected/pallas_call | solution.py:423
  32.0 1.5 %collective-permute-start.14 = (bf16[128,1536]{1,0:T(8,128)(2,1)S(1)}, bf16[128,1536]{1,0:T(8,128)(2,1)S(1)}, u32[]{:S(2)}, u32[]{:S(2)}) collective-permute-start(bf16[128,1536]{1,0:T(8,128)(2,1)S(1)} %standardized.3.refs_9_.refs_0_), channel_id=1, source_target_pairs={{0,24},{8,16},{16,8},{24,0},{1,25},{9,17},{17,9},{25,1},{2,26},{10... | collective-permute-start | bytes 1179656 | tf_op jit(solution)/shard_map/ppermute | solution.py:164
  33.5 1.4 %projected.7 = (bf16[256,384]{1,0:T(8,128)(2,1)S(1)}, bf16[256,384]{1,0:T(8,128)(2,1)S(1)}, bf16[256,384]{1,0:T(8,128)(2,1)S(1)}) custom-call(bf16[256,1536]{1,0:T(8,128)(2,1)S(1)} %get-tuple-element.49.refs_0_, bf16[1536,768]{1,0:T(8,128)(2,1)S(1)} %staged.8.refs_6_.refs_1_, bf16[1536,768]{1,0:T(8,128)(2,1)S(1)} %staged.6.refs_2_.refs_7_.refs_4_.refs_1_, ...), custom_call_target="tpu_custom_call" | custom-call | tf_op jit(solution)/shard_map/projected/pallas_call | solution.py:423
  35.3 1.3 %collective-permute-start.13 = (bf16[256,768]{1,0:T(8,128)(2,1)S(1)}, bf16[256,768]{1,0:T(8,128)(2,1)S(1)}, u32[]{:S(2)}, u32[]{:S(2)}) collective-permute-start(bf16[256,768]{1,0:T(8,128)(2,1)S(1)} %get-tuple-element.57.refs_6_.after_ref.refs_1_), channel_id=1, source_target_pairs={{0,2},{2,0},{4,6},{6,4},{1,3},{3,1},{5,7},{7,5},{8,10},{10,8},{12,... | collective-permute-start | bytes 1179656 | tf_op jit(solution)/shard_map/ppermute | solution.py:164
  36.6 1.2 %collective-permute-start.17 = (bf16[128,1536]{1,0:T(8,128)(2,1)S(1)}, bf16[128,1536]{1,0:T(8,128)(2,1)S(1)}, u32[]{:S(2)}, u32[]{:S(2)}) collective-permute-start(bf16[128,1536]{1,0:T(8,128)(2,1)S(1)} %standardized.3.refs_9_.refs_0_), channel_id=1, source_target_pairs={{0,16},{8,24},{16,0},{24,8},{1,17},{9,25},{17,1},{25,9},{2,18},{10... | collective-permute-start | bytes 1179656 | tf_op jit(solution)/shard_map/ppermute | solution.py:164
  38.6 1.6 %staged.9.after_ref.refs_4_.refs_2_ = bf16[768,1536]{1,0:T(8,128)(2,1)S(1)} custom-call(bf16[768,1536]{1,0:T(8,128)(2,1)} %weight_ref.3, bf16[256,768]{1,0:T(8,128)(2,1)S(1)} %get-tuple-element.57.refs_6_.after_ref.refs_1_), custom_call_target="tpu_custom_call" | custom-call | bytes 2359296 | tf_op jit(solution)/shard_map/staged/pallas_call | solution.py:459
  40.2 3.8 %staged.10.refs_5_.refs_2_.refs_1_ = bf16[1536,3072]{1,0:T(8,128)(2,1)S(1)} custom-call(bf16[1536,3072]{1,0:T(8,128)(2,1)} %weight_ref.4, bf16[768,1536]{1,0:T(8,128)(2,1)S(1)} %staged.9.after_ref.refs_4_.refs_2_), custom_call_target="tpu_custom_call" | custom-call | bytes 9437184 | tf_op jit(solution)/shard_map/staged/pallas_call | solution.py:459
  44.9 1.0 projected.8
  45.9 1.0 projected.9
  47.5 0.9 collective-permute-done.15.refs_2_
  48.9 1.1 %attend.1 = (f32[256,384]{1,0:T(8,128)S(1)}, f32[256,384]{1,0:T(8,128)S(1)}, f32[256,384]{1,0:T(8,128)S(1)}) custom-call(bf16[256,384]{1,0:T(8,128)(2,1)S(1)} %get-tuple-element.56.refs_0_, bf16[256,768]{1,0:T(8,128)(2,1)S(1)} %get-tuple-element.57.refs_6_.after_ref.refs_1_, bf16[256,768]{1,0:T(8,128)(2,1)S(1)} %copied.4.refs_2_, ...), custom_call_target="tpu_custom_call" | custom-call | tf_op jit(solution)/shard_map/attend/pallas_call | solution.py:582
  50.0 2.8 %collective-permute-done.17.refs_1_.refs_0_ = bf16[128,1536]{1,0:T(8,128)(2,1)S(1)} collective-permute-done((bf16[128,1536]{1,0:T(8,128)(2,1)S(1)}, bf16[128,1536]{1,0:T(8,128)(2,1)S(1)}, u32[]{:S(2)}, u32[]{:S(2)}) %collective-permute-start.17) | collective-permute-done | bytes 393248 | tf_op jit(solution)/shard_map/ppermute | solution.py:164
  52.9 1.0 projected.10
  54.5 1.0 projected.11
  58.3 1.5 %collective-permute-start.26 = (bf16[32,1536]{1,0:T(8,128)(2,1)S(1)}, bf16[32,1536]{1,0:T(8,128)(2,1)S(1)}, u32[]{:S(2)}, u32[]{:S(2)}) collective-permute-start(bf16[32,1536]{1,0:T(8,128)(2,1)S(1)} %get-tuple-element.77), channel_id=1, source_target_pairs={{0,16},{8,24},{16,0},{24,8},{1,17},{9,25},{17,1},{25,9},{2,18},{10... | collective-permute-start | bytes 294920 | tf_op jit(solution)/shard_map/ppermute | solution.py:164
  61.2 1.6 %collective-permute-start.22 = (bf16[32,1536]{1,0:T(8,128)(2,1)S(1)}, bf16[32,1536]{1,0:T(8,128)(2,1)S(1)}, u32[]{:S(2)}, u32[]{:S(2)}) collective-permute-start(bf16[32,1536]{1,0:T(8,128)(2,1)S(1)} %get-tuple-element.72), channel_id=1, source_target_pairs={{0,8},{8,0},{16,24},{24,16},{1,9},{9,1},{17,25},{25,17},{2,10},{10... | collective-permute-start | bytes 294920 | tf_op jit(solution)/shard_map/ppermute | solution.py:164
  63.4 1.2 %collective-permute-start.27 = (bf16[32,1536]{1,0:T(8,128)(2,1)S(1)}, bf16[32,1536]{1,0:T(8,128)(2,1)S(1)}, u32[]{:S(2)}, u32[]{:S(2)}) collective-permute-start(bf16[32,1536]{1,0:T(8,128)(2,1)S(1)} %rounded_sum.3), channel_id=1, source_target_pairs={{0,8},{8,0},{16,24},{24,16},{1,9},{9,1},{17,25},{25,17},{2,10},{10... | collective-permute-start | bytes 294920 | tf_op jit(solution)/shard_map/ppermute | solution.py:164
  64.6 0.9 collective-permute-done.24.second_ref
  65.6 2.0 %collective-permute-done.22.refs_1_ = bf16[32,1536]{1,0:T(8,128)(2,1)S(1)} collective-permute-done((bf16[32,1536]{1,0:T(8,128)(2,1)S(1)}, bf16[32,1536]{1,0:T(8,128)(2,1)S(1)}, u32[]{:S(2)}, u32[]{:S(2)}) %collective-permute-start.22) | collective-permute-done | bytes 98336 | tf_op jit(solution)/shard_map/ppermute | solution.py:164
  68.7 1.5 %collective-permute-done.25.refs_2_ = bf16[32,1536]{1,0:T(8,128)(2,1)S(1)} collective-permute-done((bf16[32,1536]{1,0:T(8,128)(2,1)S(1)}, bf16[32,1536]{1,0:T(8,128)(2,1)S(1)}, u32[]{:S(2)}, u32[]{:S(2)}) %collective-permute-start.25) | collective-permute-done | bytes 98336 | tf_op jit(solution)/shard_map/ppermute | solution.py:164
  70.7 1.2 %collective-permute-done.29.refs_2_ = f32[64,128]{1,0:T(8,128)S(1)} collective-permute-done((f32[64,128]{1,0:T(8,128)S(1)}, f32[64,128]{1,0:T(8,128)S(1)}, u32[]{:S(2)}, u32[]{:S(2)}) %collective-permute-start.29) | collective-permute-done | bytes 32800 | tf_op jit(solution)/shard_map/ppermute | solution.py:164
  72.1 0.9 collective-permute-start.30
  73.6 2.1 %collective-permute-start.34 = (bf16[64,1536]{1,0:T(8,128)(2,1)S(1)}, bf16[64,1536]{1,0:T(8,128)(2,1)S(1)}, u32[]{:S(2)}, u32[]{:S(2)}) collective-permute-start(bf16[64,1536]{1,0:T(8,128)(2,1)S(1)} %normed_rows.1.after_ref.refs_0_), channel_id=1, source_target_pairs={{0,8},{8,0},{16,24},{24,16},{1,9},{9,1},{17,25},{25,17},{2,10},{10... | collective-permute-start | bytes 589832 | tf_op jit(solution)/shard_map/ppermute | solution.py:164
  75.7 3.8 %staged.11.refs_3_.refs_2_ = bf16[3072,1536]{1,0:T(8,128)(2,1)S(1)} custom-call(bf16[3072,1536]{1,0:T(8,128)(2,1)} %weight_ref.5, bf16[64,1536]{1,0:T(8,128)(2,1)S(1)} %normed_rows.1.after_ref.refs_0_), custom_call_target="tpu_custom_call" | custom-call | bytes 9437184 | tf_op jit(solution)/shard_map/staged/pallas_call | solution.py:459
  79.5 1.4 %collective-permute-done.30.refs_1_ = bf16[64,1536]{1,0:T(8,128)(2,1)S(1)} collective-permute-done((bf16[64,1536]{1,0:T(8,128)(2,1)S(1)}, bf16[64,1536]{1,0:T(8,128)(2,1)S(1)}, u32[]{:S(2)}, u32[]{:S(2)}) %collective-permute-start.30) | collective-permute-done | bytes 196640 | tf_op jit(solution)/shard_map/ppermute | solution.py:164
  84.0 0.9 down_projected.4.refs_3_
  84.9 0.9 down_projected.5
  88.1 1.2 %collective-permute-start.39 = (bf16[64,1536]{1,0:T(8,128)(2,1)S(1)}, bf16[64,1536]{1,0:T(8,128)(2,1)S(1)}, u32[]{:S(2)}, u32[]{:S(2)}) collective-permute-start(bf16[64,1536]{1,0:T(8,128)(2,1)S(1)} %get-tuple-element.84), channel_id=1, source_target_pairs={{0,24},{8,16},{16,8},{24,0},{1,25},{9,17},{17,9},{25,1},{2,26},{10... | collective-permute-start | bytes 589832 | tf_op jit(solution)/shard_map/ppermute | solution.py:164
  89.2 0.9 down_projected.6.refs_3_
  90.2 0.9 down_projected.7
  91.1 1.3 %collective-permute-start.37 = (bf16[64,1536]{1,0:T(8,128)(2,1)S(1)}, bf16[64,1536]{1,0:T(8,128)(2,1)S(1)}, u32[]{:S(2)}, u32[]{:S(2)}) collective-permute-start(bf16[64,1536]{1,0:T(8,128)(2,1)S(1)} %get-tuple-element.82), channel_id=1, source_target_pairs={{0,8},{8,0},{16,24},{24,16},{1,9},{9,1},{17,25},{25,17},{2,10},{10... | collective-permute-start | bytes 589832 | tf_op jit(solution)/shard_map/ppermute | solution.py:164
  92.3 1.1 %collective-permute-start.38 = (bf16[64,1536]{1,0:T(8,128)(2,1)S(1)}, bf16[64,1536]{1,0:T(8,128)(2,1)S(1)}, u32[]{:S(2)}, u32[]{:S(2)}) collective-permute-start(bf16[64,1536]{1,0:T(8,128)(2,1)S(1)} %get-tuple-element.83), channel_id=1, source_target_pairs={{0,16},{8,24},{16,0},{24,8},{1,17},{9,25},{17,1},{25,9},{2,18},{10... | collective-permute-start | bytes 589832 | tf_op jit(solution)/shard_map/ppermute | solution.py:164
  93.4 3.3 %collective-permute-done.39 = bf16[64,1536]{1,0:T(8,128)(2,1)S(1)} collective-permute-done((bf16[64,1536]{1,0:T(8,128)(2,1)S(1)}, bf16[64,1536]{1,0:T(8,128)(2,1)S(1)}, u32[]{:S(2)}, u32[]{:S(2)}) %collective-permute-start.39) | collective-permute-done | bytes 196640 | tf_op jit(solution)/shard_map/ppermute | solution.py:164
  96.7 2.8 %collective-permute-done.37 = bf16[64,1536]{1,0:T(8,128)(2,1)S(1)} collective-permute-done((bf16[64,1536]{1,0:T(8,128)(2,1)S(1)}, bf16[64,1536]{1,0:T(8,128)(2,1)S(1)}, u32[]{:S(2)}, u32[]{:S(2)}) %collective-permute-start.37) | collective-permute-done | bytes 196640 | tf_op jit(solution)/shard_map/ppermute | solution.py:164
  (94 shorter events, 22.8 us)
Async XLA Ops:
  0.0 2.0 %copy-start = (bf16[3072,576]{0,1:T(8,128)(2,1)S(1)}, bf16[3072,576]{0,1:T(8,128)(2,1)}, u32[]{:S(2)}) copy-start(bf16[3072,576]{0,1:T(8,128)(2,1)} %param.11) | copy-start | bytes 10616836
  0.0 3.0 %copy-start.2 = (bf16[64,1536]{1,0:T(8,128)(2,1)S(1)}, bf16[64,1536]{1,0:T(8,128)(2,1)}, u32[]{:S(2)}) copy-start(bf16[64,1536]{1,0:T(8,128)(2,1)} %refs_6_.1) | copy-start | bytes 589828
  3.1 14.0 %collective-permute-start.4 = (bf16[64,1536]{1,0:T(8,128)(2,1)S(1)}, bf16[64,1536]{1,0:T(8,128)(2,1)S(1)}, u32[]{:S(2)}, u32[]{:S(2)}) collective-permute-start(bf16[64,1536]{1,0:T(8,128)(2,1)S(1)} %copied.3), channel_id=1, source_target_pairs={{0,4},{2,6},{4,0},{6,2},{1,5},{3,7},{5,1},{7,3},{8,12},{10,14},{12... | collective-permute-start | bytes 589832 | tf_op jit(solution)/shard_map/ppermute | solution.py:164
  7.4 4.6 %collective-permute-start = (f32[64,128]{1,0:T(8,128)S(1)}, f32[64,128]{1,0:T(8,128)S(1)}, u32[]{:S(2)}, u32[]{:S(2)}) collective-permute-start(f32[64,128]{1,0:T(8,128)S(1)} %get-tuple-element.46.refs_1_), channel_id=1, source_target_pairs={{0,1},{1,0},{2,3},{3,2},{4,5},{5,4},{6,7},{7,6},{8,9},{9,8},{10,11... | collective-permute-start | bytes 98312 | tf_op jit(solution)/shard_map/ppermute | solution.py:164
  7.4 1.3 %collective-permute-start.1 = (f32[1,576]{1,0:T(1,128)S(1)}, f32[1,576]{1,0:T(1,128)S(1)}, u32[]{:S(2)}, u32[]{:S(2)}) collective-permute-start(f32[1,576]{1,0:T(1,128)S(1)} %fusion.4.refs_0_.after_ref), channel_id=1, source_target_pairs={{0,1},{1,0},{2,3},{3,2},{4,5},{5,4},{6,7},{7,6},{8,9},{9,8},{10,11... | collective-permute-start | bytes 6920 | tf_op jit(solution)/shard_map/ppermute | solution.py:164
  8.8 3.6 %collective-permute-start.2 = (f32[2,576]{1,0:T(2,128)S(1)}, f32[2,576]{1,0:T(2,128)S(1)}, u32[]{:S(2)}, u32[]{:S(2)}) collective-permute-start(f32[2,576]{1,0:T(2,128)S(1)} %merged.3.after_ref.refs_0_), channel_id=1, source_target_pairs={{0,2},{2,0},{4,6},{6,4},{1,3},{3,1},{5,7},{7,5},{8,10},{10,8},{12,... | collective-permute-start | bytes 13832 | tf_op jit(solution)/shard_map/ppermute | solution.py:164
  12.4 4.6 %collective-permute-start.3 = (f32[4,576]{1,0:T(4,128)S(1)}, f32[4,576]{1,0:T(4,128)S(1)}, u32[]{:S(2)}, u32[]{:S(2)}) collective-permute-start(f32[4,576]{1,0:T(4,128)S(1)} %merged.4.after_ref.refs_0_), channel_id=1, source_target_pairs={{0,4},{2,6},{4,0},{6,2},{1,5},{3,7},{5,1},{7,3},{8,12},{10,14},{12... | collective-permute-start | bytes 27656 | tf_op jit(solution)/shard_map/ppermute | solution.py:164
  17.1 9.6 %collective-permute-start.5 = (bf16[64,1664]{1,0:T(8,128)(2,1)S(1)}, bf16[64,1664]{1,0:T(8,128)(2,1)S(1)}, u32[]{:S(2)}, u32[]{:S(2)}) collective-permute-start(bf16[64,1664]{1,0:T(8,128)(2,1)S(1)} %packed.1.refs_0_.after_ref), channel_id=1, source_target_pairs={{0,8},{8,0},{16,24},{24,16},{1,9},{9,1},{17,25},{25,17},{2,10},{10... | collective-permute-start | bytes 638984 | tf_op jit(solution)/shard_map/ppermute | solution.py:164
  18.6 10.6 %collective-permute-start.6 = (bf16[64,1664]{1,0:T(8,128)(2,1)S(1)}, bf16[64,1664]{1,0:T(8,128)(2,1)S(1)}, u32[]{:S(2)}, u32[]{:S(2)}) collective-permute-start(bf16[64,1664]{1,0:T(8,128)(2,1)S(1)} %packed.1.refs_0_.after_ref), channel_id=1, source_target_pairs={{0,16},{8,24},{16,0},{24,8},{1,17},{9,25},{17,1},{25,9},{2,18},{10... | collective-permute-start | bytes 638984 | tf_op jit(solution)/shard_map/ppermute | solution.py:164
  20.2 9.1 %collective-permute-start.7 = (bf16[64,1664]{1,0:T(8,128)(2,1)S(1)}, bf16[64,1664]{1,0:T(8,128)(2,1)S(1)}, u32[]{:S(2)}, u32[]{:S(2)}) collective-permute-start(bf16[64,1664]{1,0:T(8,128)(2,1)S(1)} %packed.1.refs_0_.after_ref), channel_id=1, source_target_pairs={{0,24},{8,16},{16,8},{24,0},{1,25},{9,17},{17,9},{25,1},{2,26},{10... | collective-permute-start | bytes 638984 | tf_op jit(solution)/shard_map/ppermute | solution.py:164
  20.6 5.7 %collective-permute-start.8 = (bf16[64,1536]{1,0:T(8,128)(2,1)S(1)}, bf16[64,1536]{1,0:T(8,128)(2,1)S(1)}, u32[]{:S(2)}, u32[]{:S(2)}) collective-permute-start(bf16[64,1536]{1,0:T(8,128)(2,1)S(1)} %collective-permute-done.4.refs_4_.refs_0_), channel_id=1, source_target_pairs={{0,2},{2,0},{4,6},{6,4},{1,3},{3,1},{5,7},{7,5},{8,10},{10,8},{12,... | collective-permute-start | bytes 589832 | tf_op jit(solution)/shard_map/ppermute | solution.py:164
  26.6 3.1 %collective-permute-start.9 = (f32[128,128]{1,0:T(8,128)S(1)}, f32[128,128]{1,0:T(8,128)S(1)}, u32[]{:S(2)}, u32[]{:S(2)}) collective-permute-start(f32[128,128]{1,0:T(8,128)S(1)} %get-tuple-element.48.refs_1_), channel_id=1, source_target_pairs={{0,1},{1,0},{2,3},{3,2},{4,5},{5,4},{6,7},{7,6},{8,9},{9,8},{10,11... | collective-permute-start | bytes 196616 | tf_op jit(solution)/shard_map/ppermute | solution.py:164
  31.3 3.5 %collective-permute-start.10 = (bf16[256,384]{1,0:T(8,128)(2,1)S(1)}, bf16[256,384]{1,0:T(8,128)(2,1)S(1)}, u32[]{:S(2)}, u32[]{:S(2)}) collective-permute-start(bf16[256,384]{1,0:T(8,128)(2,1)S(1)} %get-tuple-element.53), channel_id=1, source_target_pairs={{0,1},{1,0},{2,3},{3,2},{4,5},{5,4},{6,7},{7,6},{8,9},{9,8},{10,11... | collective-permute-start | bytes 589832 | tf_op jit(solution)/shard_map/ppermute | solution.py:164
  31.4 3.5 %collective-permute-start.11 = (bf16[256,384]{1,0:T(8,128)(2,1)S(1)}, bf16[256,384]{1,0:T(8,128)(2,1)S(1)}, u32[]{:S(2)}, u32[]{:S(2)}) collective-permute-start(bf16[256,384]{1,0:T(8,128)(2,1)S(1)} %get-tuple-element.54), channel_id=1, source_target_pairs={{0,1},{1,0},{2,3},{3,2},{4,5},{5,4},{6,7},{7,6},{8,9},{9,8},{10,11... | collective-permute-start | bytes 589832 | tf_op jit(solution)/shard_map/ppermute | solution.py:164
  31.9 3.0 %collective-permute-start.12 = (bf16[256,384]{1,0:T(8,128)(2,1)S(1)}, bf16[256,384]{1,0:T(8,128)(2,1)S(1)}, u32[]{:S(2)}, u32[]{:S(2)}) collective-permute-start(bf16[256,384]{1,0:T(8,128)(2,1)S(1)} %get-tuple-element.55), channel_id=1, source_target_pairs={{0,1},{1,0},{2,3},{3,2},{4,5},{5,4},{6,7},{7,6},{8,9},{9,8},{10,11... | collective-permute-start | bytes 589832 | tf_op jit(solution)/shard_map/ppermute | solution.py:164
  32.0 12.9 %collective-permute-start.14 = (bf16[128,1536]{1,0:T(8,128)(2,1)S(1)}, bf16[128,1536]{1,0:T(8,128)(2,1)S(1)}, u32[]{:S(2)}, u32[]{:S(2)}) collective-permute-start(bf16[128,1536]{1,0:T(8,128)(2,1)S(1)} %standardized.3.refs_9_.refs_0_), channel_id=1, source_target_pairs={{0,24},{8,16},{16,8},{24,0},{1,25},{9,17},{17,9},{25,1},{2,26},{10... | collective-permute-start | bytes 1179656 | tf_op jit(solution)/shard_map/ppermute | solution.py:164
  33.5 1.4 %copy-start.3 = (f32[128]{0:T(128)S(1)}, f32[128]{0:T(128)}, u32[]{:S(2)}) copy-start(f32[128]{0:T(128)} %param.13) | copy-start | bytes 1540
  33.5 1.4 %copy-start.4 = (f32[128]{0:T(128)S(1)}, f32[128]{0:T(128)}, u32[]{:S(2)}) copy-start(f32[128]{0:T(128)} %param.14) | copy-start | bytes 1540
  35.3 12.2 %collective-permute-start.13 = (bf16[256,768]{1,0:T(8,128)(2,1)S(1)}, bf16[256,768]{1,0:T(8,128)(2,1)S(1)}, u32[]{:S(2)}, u32[]{:S(2)}) collective-permute-start(bf16[256,768]{1,0:T(8,128)(2,1)S(1)} %get-tuple-element.57.refs_6_.after_ref.refs_1_), channel_id=1, source_target_pairs={{0,2},{2,0},{4,6},{6,4},{1,3},{3,1},{5,7},{7,5},{8,10},{10,8},{12,... | collective-permute-start | bytes 1179656 | tf_op jit(solution)/shard_map/ppermute | solution.py:164
  36.6 16.2 %collective-permute-start.17 = (bf16[128,1536]{1,0:T(8,128)(2,1)S(1)}, bf16[128,1536]{1,0:T(8,128)(2,1)S(1)}, u32[]{:S(2)}, u32[]{:S(2)}) collective-permute-start(bf16[128,1536]{1,0:T(8,128)(2,1)S(1)} %standardized.3.refs_9_.refs_0_), channel_id=1, source_target_pairs={{0,16},{8,24},{16,0},{24,8},{1,17},{9,25},{17,1},{25,9},{2,18},{10... | collective-permute-start | bytes 1179656 | tf_op jit(solution)/shard_map/ppermute | solution.py:164
  37.8 15.1 %collective-permute-start.18 = (bf16[128,1536]{1,0:T(8,128)(2,1)S(1)}, bf16[128,1536]{1,0:T(8,128)(2,1)S(1)}, u32[]{:S(2)}, u32[]{:S(2)}) collective-permute-start(bf16[128,1536]{1,0:T(8,128)(2,1)S(1)} %standardized.3.refs_9_.refs_0_), channel_id=1, source_target_pairs={{0,8},{8,0},{16,24},{24,16},{1,9},{9,1},{17,25},{25,17},{2,10},{10... | collective-permute-start | bytes 1179656 | tf_op jit(solution)/shard_map/ppermute | solution.py:164
  46.9 1.5 %collective-permute-start.15 = (bf16[256,384]{1,0:T(8,128)(2,1)S(1)}, bf16[256,384]{1,0:T(8,128)(2,1)S(1)}, u32[]{:S(2)}, u32[]{:S(2)}) collective-permute-start(bf16[256,384]{1,0:T(8,128)(2,1)S(1)} %get-tuple-element.61), channel_id=1, source_target_pairs={{0,1},{1,0},{2,3},{3,2},{4,5},{5,4},{6,7},{7,6},{8,9},{9,8},{10,11... | collective-permute-start | bytes 589832 | tf_op jit(solution)/shard_map/ppermute | solution.py:164
  46.9 1.7 %collective-permute-start.16 = (bf16[256,384]{1,0:T(8,128)(2,1)S(1)}, bf16[256,384]{1,0:T(8,128)(2,1)S(1)}, u32[]{:S(2)}, u32[]{:S(2)}) collective-permute-start(bf16[256,384]{1,0:T(8,128)(2,1)S(1)} %get-tuple-element.62), channel_id=1, source_target_pairs={{0,1},{1,0},{2,3},{3,2},{4,5},{5,4},{6,7},{7,6},{8,9},{9,8},{10,11... | collective-permute-start | bytes 589832 | tf_op jit(solution)/shard_map/ppermute | solution.py:164
  53.9 1.6 %collective-permute-start.19 = (bf16[256,384]{1,0:T(8,128)(2,1)S(1)}, bf16[256,384]{1,0:T(8,128)(2,1)S(1)}, u32[]{:S(2)}, u32[]{:S(2)}) collective-permute-start(bf16[256,384]{1,0:T(8,128)(2,1)S(1)} %get-tuple-element.69), channel_id=1, source_target_pairs={{0,1},{1,0},{2,3},{3,2},{4,5},{5,4},{6,7},{7,6},{8,9},{9,8},{10,11... | collective-permute-start | bytes 589832 | tf_op jit(solution)/shard_map/ppermute | solution.py:164
  54.0 1.7 %collective-permute-start.20 = (bf16[256,384]{1,0:T(8,128)(2,1)S(1)}, bf16[256,384]{1,0:T(8,128)(2,1)S(1)}, u32[]{:S(2)}, u32[]{:S(2)}) collective-permute-start(bf16[256,384]{1,0:T(8,128)(2,1)S(1)} %get-tuple-element.70), channel_id=1, source_target_pairs={{0,1},{1,0},{2,3},{3,2},{4,5},{5,4},{6,7},{7,6},{8,9},{9,8},{10,11... | collective-permute-start | bytes 589832 | tf_op jit(solution)/shard_map/ppermute | solution.py:164
  56.4 1.4 %collective-permute-start.23 = (bf16[64,384]{1,0:T(8,128)(2,1)S(1)}, bf16[64,384]{1,0:T(8,128)(2,1)S(1)}, u32[]{:S(2)}, u32[]{:S(2)}) collective-permute-start(bf16[64,384]{1,0:T(8,128)(2,1)S(1)} %finished.2.refs_5_.refs_0_), channel_id=1, source_target_pairs={{0,1},{1,0},{2,3},{3,2},{4,5},{5,4},{6,7},{7,6},{8,9},{9,8},{10,11... | collective-permute-start | bytes 147464 | tf_op jit(solution)/shard_map/ppermute | solution.py:164
  57.4 2.9 %collective-permute-start.21 = (bf16[192,384]{1,0:T(8,128)(2,1)S(1)}, bf16[192,384]{1,0:T(8,128)(2,1)S(1)}, u32[]{:S(2)}, u32[]{:S(2)}) collective-permute-start(bf16[192,384]{1,0:T(8,128)(2,1)S(1)} %finished.3.refs_0_.refs_3_), channel_id=1, source_target_pairs={{0,1},{1,0},{2,3},{3,2},{4,5},{5,4},{6,7},{7,6},{8,9},{9,8},{10,11... | collective-permute-start | bytes 442376 | tf_op jit(solution)/shard_map/ppermute | solution.py:164
  58.3 5.0 %collective-permute-start.26 = (bf16[32,1536]{1,0:T(8,128)(2,1)S(1)}, bf16[32,1536]{1,0:T(8,128)(2,1)S(1)}, u32[]{:S(2)}, u32[]{:S(2)}) collective-permute-start(bf16[32,1536]{1,0:T(8,128)(2,1)S(1)} %get-tuple-element.77), channel_id=1, source_target_pairs={{0,16},{8,24},{16,0},{24,8},{1,17},{9,25},{17,1},{25,9},{2,18},{10... | collective-permute-start | bytes 294920 | tf_op jit(solution)/shard_map/ppermute | solution.py:164
  59.8 5.7 %collective-permute-start.24 = (bf16[32,1536]{1,0:T(8,128)(2,1)S(1)}, bf16[32,1536]{1,0:T(8,128)(2,1)S(1)}, u32[]{:S(2)}, u32[]{:S(2)}) collective-permute-start(bf16[32,1536]{1,0:T(8,128)(2,1)S(1)} %get-tuple-element.74), channel_id=1, source_target_pairs={{0,8},{8,0},{16,24},{24,16},{1,9},{9,1},{17,25},{25,17},{2,10},{10... | collective-permute-start | bytes 294920 | tf_op jit(solution)/shard_map/ppermute | solution.py:164
  61.2 6.4 %collective-permute-start.22 = (bf16[32,1536]{1,0:T(8,128)(2,1)S(1)}, bf16[32,1536]{1,0:T(8,128)(2,1)S(1)}, u32[]{:S(2)}, u32[]{:S(2)}) collective-permute-start(bf16[32,1536]{1,0:T(8,128)(2,1)S(1)} %get-tuple-element.72), channel_id=1, source_target_pairs={{0,8},{8,0},{16,24},{24,16},{1,9},{9,1},{17,25},{25,17},{2,10},{10... | collective-permute-start | bytes 294920 | tf_op jit(solution)/shard_map/ppermute | solution.py:164
  62.7 5.6 %collective-permute-start.28 = (bf16[32,1536]{1,0:T(8,128)(2,1)S(1)}, bf16[32,1536]{1,0:T(8,128)(2,1)S(1)}, u32[]{:S(2)}, u32[]{:S(2)}) collective-permute-start(bf16[32,1536]{1,0:T(8,128)(2,1)S(1)} %get-tuple-element.78), channel_id=1, source_target_pairs={{0,16},{8,24},{16,0},{24,8},{1,17},{9,25},{17,1},{25,9},{2,18},{10... | collective-permute-start | bytes 294920 | tf_op jit(solution)/shard_map/ppermute | solution.py:164
  63.4 5.3 %collective-permute-start.27 = (bf16[32,1536]{1,0:T(8,128)(2,1)S(1)}, bf16[32,1536]{1,0:T(8,128)(2,1)S(1)}, u32[]{:S(2)}, u32[]{:S(2)}) collective-permute-start(bf16[32,1536]{1,0:T(8,128)(2,1)S(1)} %rounded_sum.3), channel_id=1, source_target_pairs={{0,8},{8,0},{16,24},{24,16},{1,9},{9,1},{17,25},{25,17},{2,10},{10... | collective-permute-start | bytes 294920 | tf_op jit(solution)/shard_map/ppermute | solution.py:164
  65.5 4.7 %collective-permute-start.25 = (bf16[32,1536]{1,0:T(8,128)(2,1)S(1)}, bf16[32,1536]{1,0:T(8,128)(2,1)S(1)}, u32[]{:S(2)}, u32[]{:S(2)}) collective-permute-start(bf16[32,1536]{1,0:T(8,128)(2,1)S(1)} %rounded_sum.2), channel_id=1, source_target_pairs={{0,16},{8,24},{16,0},{24,8},{1,17},{9,25},{17,1},{25,9},{2,18},{10... | collective-permute-start | bytes 294920 | tf_op jit(solution)/shard_map/ppermute | solution.py:164
  70.7 1.2 %collective-permute-start.29 = (f32[64,128]{1,0:T(8,128)S(1)}, f32[64,128]{1,0:T(8,128)S(1)}, u32[]{:S(2)}, u32[]{:S(2)}) collective-permute-start(f32[64,128]{1,0:T(8,128)S(1)} %get-tuple-element.80.refs_1_), channel_id=1, source_target_pairs={{0,1},{1,0},{2,3},{3,2},{4,5},{5,4},{6,7},{7,6},{8,9},{9,8},{10,11... | collective-permute-start | bytes 98312 | tf_op jit(solution)/shard_map/ppermute | solution.py:164
  72.1 8.8 %collective-permute-start.30 = (bf16[64,1536]{1,0:T(8,128)(2,1)S(1)}, bf16[64,1536]{1,0:T(8,128)(2,1)S(1)}, u32[]{:S(2)}, u32[]{:S(2)}) collective-permute-start(bf16[64,1536]{1,0:T(8,128)(2,1)S(1)} %normed_rows.1.after_ref.refs_0_), channel_id=1, source_target_pairs={{0,24},{8,16},{16,8},{24,0},{1,25},{9,17},{17,9},{25,1},{2,26},{10... | collective-permute-start | bytes 589832 | tf_op jit(solution)/shard_map/ppermute | solution.py:164
  73.1 10.9 %collective-permute-start.33 = (bf16[64,1536]{1,0:T(8,128)(2,1)S(1)}, bf16[64,1536]{1,0:T(8,128)(2,1)S(1)}, u32[]{:S(2)}, u32[]{:S(2)}) collective-permute-start(bf16[64,1536]{1,0:T(8,128)(2,1)S(1)} %normed_rows.1.after_ref.refs_0_), channel_id=1, source_target_pairs={{0,16},{8,24},{16,0},{24,8},{1,17},{9,25},{17,1},{25,9},{2,18},{10... | collective-permute-start | bytes 589832 | tf_op jit(solution)/shard_map/ppermute | solution.py:164
  73.6 10.4 %collective-permute-start.34 = (bf16[64,1536]{1,0:T(8,128)(2,1)S(1)}, bf16[64,1536]{1,0:T(8,128)(2,1)S(1)}, u32[]{:S(2)}, u32[]{:S(2)}) collective-permute-start(bf16[64,1536]{1,0:T(8,128)(2,1)S(1)} %normed_rows.1.after_ref.refs_0_), channel_id=1, source_target_pairs={{0,8},{8,0},{16,24},{24,16},{1,9},{9,1},{17,25},{25,17},{2,10},{10... | collective-permute-start | bytes 589832 | tf_op jit(solution)/shard_map/ppermute | solution.py:164
  81.7 2.3 %collective-permute-start.32 = (bf16[128,1536]{1,0:T(8,128)(2,1)S(1)}, bf16[128,1536]{1,0:T(8,128)(2,1)S(1)}, u32[]{:S(2)}, u32[]{:S(2)}) collective-permute-start(bf16[128,1536]{1,0:T(8,128)(2,1)S(1)} %up_projected.5.refs_0_), channel_id=1, source_target_pairs={{0,1},{1,0},{2,3},{3,2},{4,5},{5,4},{6,7},{7,6},{8,9},{9,8},{10,11... | collective-permute-start | bytes 1179656 | tf_op jit(solution)/shard_map/ppermute | solution.py:164
  82.6 2.4 %collective-permute-start.31 = (bf16[128,1536]{1,0:T(8,128)(2,1)S(1)}, bf16[128,1536]{1,0:T(8,128)(2,1)S(1)}, u32[]{:S(2)}, u32[]{:S(2)}) collective-permute-start(bf16[128,1536]{1,0:T(8,128)(2,1)S(1)} %up_projected.4.refs_0_), channel_id=1, source_target_pairs={{0,1},{1,0},{2,3},{3,2},{4,5},{5,4},{6,7},{7,6},{8,9},{9,8},{10,11... | collective-permute-start | bytes 1179656 | tf_op jit(solution)/shard_map/ppermute | solution.py:164
  86.6 2.6 %collective-permute-start.36 = (bf16[128,1536]{1,0:T(8,128)(2,1)S(1)}, bf16[128,1536]{1,0:T(8,128)(2,1)S(1)}, u32[]{:S(2)}, u32[]{:S(2)}) collective-permute-start(bf16[128,1536]{1,0:T(8,128)(2,1)S(1)} %up_projected.7.refs_0_), channel_id=1, source_target_pairs={{0,1},{1,0},{2,3},{3,2},{4,5},{5,4},{6,7},{7,6},{8,9},{9,8},{10,11... | collective-permute-start | bytes 1179656 | tf_op jit(solution)/shard_map/ppermute | solution.py:164
  87.5 2.6 %collective-permute-start.35 = (bf16[128,1536]{1,0:T(8,128)(2,1)S(1)}, bf16[128,1536]{1,0:T(8,128)(2,1)S(1)}, u32[]{:S(2)}, u32[]{:S(2)}) collective-permute-start(bf16[128,1536]{1,0:T(8,128)(2,1)S(1)} %up_projected.6.refs_0_), channel_id=1, source_target_pairs={{0,1},{1,0},{2,3},{3,2},{4,5},{5,4},{6,7},{7,6},{8,9},{9,8},{10,11... | collective-permute-start | bytes 1179656 | tf_op jit(solution)/shard_map/ppermute | solution.py:164
  88.1 8.7 %collective-permute-start.39 = (bf16[64,1536]{1,0:T(8,128)(2,1)S(1)}, bf16[64,1536]{1,0:T(8,128)(2,1)S(1)}, u32[]{:S(2)}, u32[]{:S(2)}) collective-permute-start(bf16[64,1536]{1,0:T(8,128)(2,1)S(1)} %get-tuple-element.84), channel_id=1, source_target_pairs={{0,24},{8,16},{16,8},{24,0},{1,25},{9,17},{17,9},{25,1},{2,26},{10... | collective-permute-start | bytes 589832 | tf_op jit(solution)/shard_map/ppermute | solution.py:164
  90.1 10.8 %copy-start.1 = (bf16[3072,576]{0,1:T(8,128)(2,1)S(1)}, bf16[3072,576]{0,1:T(8,128)(2,1)}, u32[]{:S(2)}) copy-start(bf16[3072,576]{0,1:T(8,128)(2,1)} %param.11) | copy-start | bytes 10616836
  91.1 8.4 %collective-permute-start.37 = (bf16[64,1536]{1,0:T(8,128)(2,1)S(1)}, bf16[64,1536]{1,0:T(8,128)(2,1)S(1)}, u32[]{:S(2)}, u32[]{:S(2)}) collective-permute-start(bf16[64,1536]{1,0:T(8,128)(2,1)S(1)} %get-tuple-element.82), channel_id=1, source_target_pairs={{0,8},{8,0},{16,24},{24,16},{1,9},{9,1},{17,25},{25,17},{2,10},{10... | collective-permute-start | bytes 589832 | tf_op jit(solution)/shard_map/ppermute | solution.py:164
  92.3 7.7 %collective-permute-start.38 = (bf16[64,1536]{1,0:T(8,128)(2,1)S(1)}, bf16[64,1536]{1,0:T(8,128)(2,1)S(1)}, u32[]{:S(2)}, u32[]{:S(2)}) collective-permute-start(bf16[64,1536]{1,0:T(8,128)(2,1)S(1)} %get-tuple-element.83), channel_id=1, source_target_pairs={{0,16},{8,24},{16,0},{24,8},{1,17},{9,25},{17,1},{25,9},{2,18},{10... | collective-permute-start | bytes 589832 | tf_op jit(solution)/shard_map/ppermute | solution.py:164
